TPU v7x, 32 devices: a whole 2x2x4 slice. The times are simulated.
32 devices in a mesh: expert: 8 (over z, y), context: 2 (over core), dp: 2 (over x).
Axes of the slice: x: 2, y: 2, z: 4, core: 2. Of those that a mesh axis runs over, the one named last changes fastest.
Arguments:
- residual: bfloat16 [2, 2, 256, 4096], P('dp', 'context', 'expert'), may hold values from -6 to 6
- x_raw: bfloat16 [2, 2, 256, 8192], P('dp', 'context', None, 'expert'), may hold values from -6 to 6
- z_gate: bfloat16 [2, 2, 256, 8192], P('dp', 'context', None, 'expert'), may hold values from -6 to 6
- conv_w: float32 [4, 8192], P(None, 'expert'), may hold values from -3 to 3
- conv_b: float32 [8192], P('expert'), may hold values from -0.5 to 0.5
- xproj_w: bfloat16 [8192, 288], P('expert'), may hold values from -0.0625 to 0.0625
- dtproj_w: bfloat16 [256, 8192], P(None, 'expert'), may hold values from -0.375 to 0.375
- dt_bias: float32 [8192], P('expert'), may hold values from -4 to -1
- a_rate: float32 [16, 8192], P(None, 'expert'), may hold values from 0.02 to 2
- skip_gain: float32 [8192], P('expert'), may hold values from 0.5 to 1.5
- out_w: bfloat16 [8192, 4096], P('expert'), may hold values from -0.0625 to 0.0625
- norm_gain: float32 [4096], replicated, may hold values from 0.5 to 1.5
- route_ids: int32 [2, 2, 256, 2], P('dp', 'context', 'expert'), may hold values from 0 to 3, all different within a row; in each aligned block of 32 rows (0 to 31, 32 to 63, ..., all dimensions but the last counted through in order) at most 24 rows name the same one
- route_w: float32 [2, 2, 256, 2], P('dp', 'context', 'expert'), may hold values from 0.2 to 1
- w_gate: bfloat16 [8, 4096, 6144], P('expert', None, ('context', 'dp')), may hold values from -0.09375 to 0.09375
- w_up: bfloat16 [8, 4096, 6144], P('expert', None, ('context', 'dp')), may hold values from -0.09375 to 0.09375
- w_down: bfloat16 [8, 6144, 4096], P('expert', ('context', 'dp')), may hold values from -0.0546875 to 0.0546875
Outputs:
- mixed: bfloat16 [2, 2, 256, 4096], P('dp', 'context', 'expert')
Inputs may be any that keep to these rules, and one draw needn't show every extreme that they name: `route_ids`: each row names 2 different experts; in each aligned block of 32 rows no expert is named by more than 24 rows, a bound that some block reaches.
All inputs are finite; a program needn't handle non-finite values.
Results may differ from a plain program's by a relative error of at most 0.018.
Values may be sent and summed in bfloat16 or wider, within the bound.
No kernel may reach another device: no remote copies, remote signals or barrier semaphores. Data moves between devices by JAX's collectives and lax.ppermute only.
A program may use at most 192 MiB of HBM per device.

v0:
```python
import functools

import jax
import jax.numpy as jnp
from jax import lax
from jax.experimental import pallas as pl
from jax.experimental.pallas import tpu as pltpu
from jax.sharding import PartitionSpec as P

NSTATE = 16
DT_RANK = 256
CONV = 4
TOP = 2
LANES = 128
SUB = 8
F32 = jnp.float32
BF16 = jnp.bfloat16
MIB = 1 << 20


def from_behind(block, axis, distance):
    devices = range(lax.axis_size(axis))
    route = [(i - distance, i) for i in devices if i - distance in devices]
    return lax.ppermute(block, axis, route)


def shift(block, axis, distance):
    size = lax.axis_size(axis)
    return lax.ppermute(block, axis, [(i, (i + distance) % size) for i in range(size)])


def swap_pair(block):
    size = lax.axis_size("expert")
    return lax.ppermute(block, "expert", [(i, i ^ 1) for i in range(size)])


def cost(flops, bytes_accessed, transcendentals=0):
    return pl.CostEstimate(
        flops=int(flops), bytes_accessed=int(bytes_accessed), transcendentals=int(transcendentals)
    )


def spread_rows(values, wide_ref):
    length, count = values.shape
    col = lax.broadcasted_iota(jnp.int32, (count, count * LANES), 1)
    row = lax.broadcasted_iota(jnp.int32, (count, count * LANES), 0)
    ones = jnp.where((col >= row * LANES) & (col < (row + 1) * LANES), 1.0, 0.0).astype(BF16)
    out = jnp.dot(values, ones, preferred_element_type=F32)
    for n in range(count):
        wide_ref[pl.ds(n * length, length), :] = out[:, n * LANES : (n + 1) * LANES]


def scan_kernel(groups, line, place_ref, *refs):
    pieces, refs = refs[:line], refs[line:]
    w_ref, bias_ref, neg_ref, x_ref, y_ref, sum_ref, end_ref, bc_ref = refs[:8]
    low_ref, step_ref, drive_ref, wide_ref = refs[8:]
    length = x_ref.shape[0]
    share = length // line
    for s in range(line):
        start = pl.multiple_of((place_ref[0] + (line - s)) % line * share, share)
        low_ref[pl.ds(start, share), :] = pieces[s][:, :DT_RANK]
        bc_ref[pl.ds(start, share), :] = pieces[s][:, DT_RANK:]
    spread_rows(bc_ref[...], wide_ref)
    for g in range(SUB):
        rows = pl.ds(g, length, stride=SUB)
        if g >= groups:
            step_ref[rows, :] = jnp.zeros((length, LANES), F32)
            drive_ref[rows, :] = jnp.zeros((length, LANES), F32)
            continue
        cols = pl.ds(g * LANES, LANES)
        raw = jnp.dot(low_ref[...], w_ref[:, cols], preferred_element_type=F32) + bias_ref[:, cols]
        step = jnp.maximum(raw, 0.0) + jnp.log1p(jnp.exp(-jnp.abs(raw)))
        step_ref[rows, :] = step
        drive_ref[rows, :] = step * x_ref[:, cols].astype(F32)

    def block(k, carry):
        states, total = list(carry[0]), carry[1]
        for u in range(SUB):
            t = k * SUB + u
            here = pl.ds(pl.multiple_of(t * SUB, SUB), SUB)
            step, drive = step_ref[here, :], drive_ref[here, :]
            total = total + step
            out = jnp.zeros((SUB, LANES), F32)
            for n in range(NSTATE):
                decay = jnp.exp(step * neg_ref[n])
                b = wide_ref[pl.ds(n * length + t, 1), :]
                c = wide_ref[pl.ds((NSTATE + n) * length + t, 1), :]
                states[n] = states[n] * decay + drive * b
                out = out + states[n] * c
            y_ref[here, :] = out
            sum_ref[here, :] = total
        return tuple(states), total

    zero = jnp.zeros((SUB, LANES), F32)
    states, total = lax.fori_loop(0, length // SUB, block, ((zero,) * NSTATE, zero))
    for n in range(NSTATE):
        end_ref[n] = states[n]


def run_scan(place, pieces, w, bias, neg, x):
    length, channels = x.shape
    vmem = pl.BlockSpec(memory_space=pltpu.VMEM)
    tall = jax.ShapeDtypeStruct((length * SUB, LANES), F32)
    return pl.pallas_call(
        functools.partial(scan_kernel, channels // LANES, len(pieces)),
        out_shape=(
            tall,
            tall,
            jax.ShapeDtypeStruct((NSTATE, SUB, LANES), F32),
            jax.ShapeDtypeStruct((length, 2 * NSTATE), BF16),
        ),
        in_specs=[pl.BlockSpec(memory_space=pltpu.SMEM)] + [vmem] * (len(pieces) + 4),
        out_specs=(vmem,) * 4,
        scratch_shapes=[
            pltpu.VMEM((length, DT_RANK), BF16),
            pltpu.VMEM((length * SUB, LANES), F32),
            pltpu.VMEM((length * SUB, LANES), F32),
            pltpu.VMEM((2 * NSTATE * length, LANES), F32),
        ],
        compiler_params=pltpu.CompilerParams(vmem_limit_bytes=20 * MIB),
        cost_estimate=cost(2e8, 4 * MIB, NSTATE * length * channels),
        name="state_scan",
    )(place, *pieces, w, bias, neg, x)


def out_kernel(groups, line, parts, at_ref, y_ref, sum_ref, enter_ref, bc_ref, neg_ref, x_ref, z_ref,
               skip_ref, w_hbm, *refs):
    kept_refs, sent_refs = refs[:parts], refs[parts : 2 * parts]
    full_ref, wide_ref, gated_ref, order_ref, w_ref, sems = refs[2 * parts :]
    length = x_ref.shape[0]
    part = w_ref.shape[1] // parts

    def fetch(j):
        cols = pl.ds(j * part, part)
        return pltpu.make_async_copy(w_hbm.at[:, cols], w_ref.at[:, cols], sems.at[j])

    for j in range(parts):
        fetch(j).start()
    spread_rows(bc_ref[:, NSTATE:], wide_ref)

    def block(k, carry):
        for u in range(SUB):
            t = k * SUB + u
            here = pl.ds(pl.multiple_of(t * SUB, SUB), SUB)
            total = sum_ref[here, :]
            out = y_ref[here, :]
            for n in range(NSTATE):
                c = wide_ref[pl.ds(n * length + t, 1), :]
                out = out + jnp.exp(total * neg_ref[n]) * enter_ref[n] * c
            full_ref[here, :] = out
        return carry

    lax.fori_loop(0, length // SUB, block, 0)
    for g in range(groups):
        cols = pl.ds(g * LANES, LANES)
        mixed_in = x_ref[:, cols].astype(F32)
        read = full_ref[pl.ds(g, length, stride=SUB), :] + skip_ref[:, cols] * mixed_in
        z = z_ref[:, cols].astype(F32)
        gated_ref[:, cols] = (read * (z / (1.0 + jnp.exp(-z)))).astype(BF16)
    place, half = at_ref[0], at_ref[1]
    count = length // 2
    piece = count // line
    for k in range(line):
        for r in range(2):
            source = pl.multiple_of((2 * ((place + k) % line) + (half ^ r)) * piece, piece)
            order_ref[pl.ds(r * count + k * piece, piece), :] = gated_ref[pl.ds(source, piece), :]
    tile = min(256, part)
    for j in range(parts):
        fetch(j).wait()

        def step(i, carry):
            target = pl.ds(pl.multiple_of(i * tile, tile), tile)
            source = pl.ds(pl.multiple_of(j * part + i * tile, tile), tile)
            out = jnp.dot(order_ref[...], w_ref[:, source], preferred_element_type=F32).astype(BF16)
            kept_refs[j][:, target] = out[:count]
            sent_refs[j][:, target] = out[count:]
            return carry

        lax.fori_loop(0, part // tile, step, 0)


def run_out(at, line, parts, y, total, enter, bc, neg, x, z, skip, w):
    length, channels = x.shape
    wide = w.shape[1]
    vmem = pl.BlockSpec(memory_space=pltpu.VMEM)
    return pl.pallas_call(
        functools.partial(out_kernel, channels // LANES, line, parts),
        out_shape=(jax.ShapeDtypeStruct((length // 2, wide // parts), BF16),) * (2 * parts),
        in_specs=[pl.BlockSpec(memory_space=pltpu.SMEM)] + [vmem] * 8 + [pl.BlockSpec(memory_space=pl.ANY)],
        out_specs=(vmem,) * (2 * parts),
        scratch_shapes=[
            pltpu.VMEM((length * SUB, LANES), F32),
            pltpu.VMEM((NSTATE * length, LANES), F32),
            pltpu.VMEM((length, channels), BF16),
            pltpu.VMEM((length, channels), BF16),
            pltpu.VMEM((channels, wide), BF16),
            pltpu.SemaphoreType.DMA((parts,)),
        ],
        compiler_params=pltpu.CompilerParams(vmem_limit_bytes=48 * MIB),
        cost_estimate=cost(
            2 * length * channels * wide, 2 * channels * wide + 8 * MIB, NSTATE * length * channels
        ),
        name="readout_project",
    )(at, y, total, enter, bc, neg, x, z, skip, w)


def gate_up_kernel(count, tile, *refs):
    pieces, (gate_hbm, up_hbm, out_ref, rows_ref, gate_ref, up_ref, sems) = refs[:count], refs[count:]
    copies, at = [], 0
    for k, piece in enumerate(pieces):
        rows = pl.ds(at, piece.shape[0])
        copies.append(pltpu.make_async_copy(piece, rows_ref.at[rows, :], sems.at[k]))
        at += piece.shape[0]
    steps = out_ref.shape[1] // tile

    def fetch(j, k):
        cols = pl.ds(pl.multiple_of(j * tile, tile), tile)
        source, target = ((gate_hbm, gate_ref), (up_hbm, up_ref))[k]
        sem = sems.at[count + 2 * j + k]
        return pltpu.make_async_copy(source.at[:, cols], target.at[:, cols], sem)

    for copy in copies:
        copy.start()
    for j in range(steps):
        fetch(j, 0).start()
        fetch(j, 1).start()
    for copy in copies:
        copy.wait()

    def step(j, carry):
        cols = pl.ds(pl.multiple_of(j * tile, tile), tile)
        fetch(j, 0).wait()
        gate = jnp.dot(rows_ref[...], gate_ref[:, cols], preferred_element_type=F32)
        fetch(j, 1).wait()
        up = jnp.dot(rows_ref[...], up_ref[:, cols], preferred_element_type=F32)
        out_ref[:, cols] = (gate / (1.0 + jnp.exp(-gate)) * up).astype(BF16)
        return carry

    lax.fori_loop(0, steps, step, 0)


def gate_up(pieces, w_gate, w_up):
    depth, hidden = w_gate.shape
    rows = sum(p.shape[0] for p in pieces)
    tile = min(256, hidden)
    anywhere = pl.BlockSpec(memory_space=pl.ANY)
    return pl.pallas_call(
        functools.partial(gate_up_kernel, len(pieces), tile),
        out_shape=jax.ShapeDtypeStruct((rows, hidden), BF16),
        in_specs=[anywhere] * (len(pieces) + 2),
        out_specs=pl.BlockSpec(memory_space=pltpu.VMEM),
        scratch_shapes=[
            pltpu.VMEM((rows, depth), BF16),
            pltpu.VMEM((depth, hidden), BF16),
            pltpu.VMEM((depth, hidden), BF16),
            pltpu.SemaphoreType.DMA((len(pieces) + 2 * (hidden // tile),)),
        ],
        compiler_params=pltpu.CompilerParams(vmem_limit_bytes=52 * MIB),
        cost_estimate=cost(4 * rows * depth * hidden, 4 * depth * hidden + 2 * rows * depth),
        name="gate_up",
    )(*pieces, w_gate, w_up)


def down_kernel(first, tile, rows_ref, w_hbm, *refs):
    outs, (w_ref, sems) = refs[:-2], refs[-2:]
    width = w_ref.shape[1]

    def fetch(j):
        source = pl.ds(pl.multiple_of(first + j * tile, tile), tile)
        target = pl.ds(pl.multiple_of(j * tile, tile), tile)
        return pltpu.make_async_copy(w_hbm.at[:, source], w_ref.at[:, target], sems.at[j])

    for j in range(width // tile):
        fetch(j).start()

    def step(j, carry):
        cols = pl.ds(pl.multiple_of(j * tile, tile), tile)
        fetch(j).wait()
        out = jnp.dot(rows_ref[...], w_ref[:, cols], preferred_element_type=F32).astype(BF16)
        start = 0
        for ref in outs:
            ref[:, cols] = out[start : start + ref.shape[0]]
            start += ref.shape[0]
        return carry

    lax.fori_loop(0, width // tile, step, 0)


def down(rows, sizes, w_down, first, width):
    hidden = w_down.shape[0]
    tile = min(512, width)
    vmem = pl.BlockSpec(memory_space=pltpu.VMEM)
    return pl.pallas_call(
        functools.partial(down_kernel, first, tile),
        out_shape=tuple(jax.ShapeDtypeStruct((n, width), BF16) for n in sizes),
        in_specs=[vmem, pl.BlockSpec(memory_space=pl.ANY)],
        out_specs=(vmem,) * len(sizes),
        scratch_shapes=[pltpu.VMEM((hidden, width), BF16), pltpu.SemaphoreType.DMA((width // tile,))],
        compiler_params=pltpu.CompilerParams(vmem_limit_bytes=52 * MIB),
        cost_estimate=cost(
            2 * rows.shape[0] * hidden * width, 2 * hidden * width + 2 * rows.shape[0] * (hidden + width)
        ),
        name="down",
    )(rows, w_down)


def add_up(*parts):
    return sum(p.astype(F32) for p in parts)


def along_line(block, distance):
    size = lax.axis_size("expert")
    return lax.ppermute(block, "expert", [(e, (e + 2 * distance) % size) for e in range(size)])


def cross(block, turn):
    owners, dps = lax.axis_size("expert"), lax.axis_size("dp")
    route = []
    for e in range(owners):
        for core in range(2):
            for d in range(dps):
                to = (e ^ 1, core, d) if core == turn else (e, core, d ^ 1)
                route.append(((e * 2 + core) * dps + d, (to[0] * 2 + core) * dps + to[2]))
    return lax.ppermute(block, ("expert", "context", "dp"), route)


def after(blocks, *others):
    return lax.optimization_barrier((blocks, others))[0]


def send_rows(packed, line):
    size = packed.shape[0] // line
    parts = [packed[size * s : size * (s + 1)] for s in range(line)]
    return [parts[0]] + [along_line(parts[s], s) for s in range(1, line)]


def send_home(result, line):
    size = result.shape[0] // line
    parts = [result[size * s : size * (s + 1)] for s in range(line)]
    came = [parts[0]] + [along_line(parts[s], -s) for s in range(1, line)]
    return jnp.concatenate(came, axis=0)


def plain_experts(packed, line, w_gate, w_up, w_down):
    own = jnp.concatenate(send_rows(packed, line), axis=0)
    rows = jnp.concatenate([own, swap_pair(own)], axis=0)
    rows = lax.all_gather(rows, ("context", "dp"), axis=0, tiled=True)
    hidden = gate_up([rows], w_gate, w_up)
    out = down(hidden, (rows.shape[0],), w_down, 0, w_down.shape[1])[0]
    mine = lax.psum_scatter(out, ("context", "dp"), scatter_dimension=0, tiled=True)
    count = own.shape[0]
    return send_home(add_up(mine[:count], swap_pair(mine[count:])).astype(BF16), line)


def square_experts(early, late, line, w_gate, w_up, w_down):
    width = w_down.shape[1]
    half = width // 2

    def pieces(two, four):
        return [two, four, shift(two, "context", 1), shift(four, "context", 1)]

    def home_first(outs):
        rows = outs[0].shape[0] // 4
        both = add_up(outs[0], shift(outs[1], "context", 1))
        return both[: 2 * rows], both[2 * rows :].astype(BF16)

    def home_second(kept, far):
        rows = kept.shape[0] // 2
        two = add_up(kept, far)
        return two[:rows], two[rows:].astype(BF16)

    early_came = send_rows(early, line)
    late_came = send_rows(after(late, early_came[1]), line)
    early_own = jnp.concatenate(early_came, axis=0)
    early_near = cross(early_own, 0)
    early_two = jnp.concatenate([early_own, early_near], axis=0)
    early_four = cross(early_two, 1)
    late_came[0] = after(late_came[0], early_near)
    late_own = jnp.concatenate(late_came, axis=0)
    late_near = cross(late_own, 0)
    sizes = (4 * early_own.shape[0],) * 2
    early_hidden = gate_up(after(pieces(early_two, early_four), late_own), w_gate, w_up)

    late_two = jnp.concatenate([after(late_own, early_hidden), late_near], axis=0)
    late_four = cross(late_two, 1)
    early_out = down(after(early_hidden, late_two), sizes, w_down, 0, width)
    late_four = after(late_four, early_out)
    early_kept, early_go = home_first(after(early_out, late_four))
    early_far = cross(early_go, 1)
    sizes = (4 * late_own.shape[0],) * 2
    late_hidden = gate_up(after(pieces(late_two, late_four), early_go), w_gate, w_up)

    early_kept, early_go = home_second(after(early_kept, late_hidden), early_far)
    early_far = cross(early_go, 0)
    out_left = down(after(late_hidden, early_go), sizes, w_down, 0, half)
    early_result = add_up(after(early_kept, out_left), early_far).astype(BF16)
    early_back = send_home(early_result, line)
    left = home_first(out_left)
    left_far = cross(left[1], 1)
    out_right = down(after(late_hidden, early_result, left[1]), sizes, w_down, half, half)
    left = home_second(after(left[0], out_right), left_far)
    left_far = cross(left[1], 0)
    right = home_first(out_right)
    right_far = cross(right[1], 1)
    right = home_second(after(right[0], left[1]), right_far)
    right_far = cross(right[1], 0)
    late_back = []
    for kept, far in ((left[0], left_far), (right[0], right_far)):
        late_back.append(send_home(add_up(kept, far).astype(BF16), line))
    return early_back, jnp.concatenate(late_back, axis=1)


def on_device(
    residual,
    x_raw,
    z_gate,
    conv_w,
    conv_b,
    xproj_w,
    dtproj_w,
    dt_bias,
    a_rate,
    skip_gain,
    out_w,
    norm_gain,
    route_ids,
    route_w,
    w_gate,
    w_up,
    w_down,
):
    owners, contexts, dps = (lax.axis_size(a) for a in ("expert", "context", "dp"))
    me = lax.axis_index("expert")
    place, half = me // 2, me % 2
    line = owners // 2
    length, channels = x_raw.shape[2:]
    width = residual.shape[3]
    row_count = residual.shape[2]

    values = x_raw[0, 0]
    prior_rim = from_behind(values[length - (CONV - 1) :], "context", 1)
    padded = jnp.concatenate([prior_rim, values], axis=0).astype(F32)
    conv_sum = conv_b[None, :] + sum(
        (
            conv_w[lag_index][None, :] * padded[lag_index : lag_index + length]
            for lag_index in range(CONV)
        )
    )
    mixed_in = jax.nn.silu(conv_sum).astype(BF16)
    projected = jnp.dot(mixed_in, xproj_w, preferred_element_type=F32).astype(BF16)
    shares = projected.reshape(line, length // line, -1)

    def share_of(s):
        return lax.dynamic_index_in_dim(shares, (place + s) % line, 0, keepdims=False)

    share = add_up(share_of(0), *[along_line(share_of(s), s) for s in range(1, line)]).astype(BF16)
    share = add_up(share, swap_pair(share)).astype(BF16)
    pieces = [share] + [along_line(share, s) for s in range(1, line)]

    neg = -a_rate.reshape(NSTATE, channels // LANES, LANES)
    neg = jnp.pad(neg, ((0, 0), (0, SUB - channels // LANES), (0, 0)))
    where = jnp.stack([place, half]).astype(jnp.int32)
    y, total, end, bc = run_scan(where, pieces, dtproj_w, dt_bias[None, :], neg, mixed_in)
    enter = from_behind(end, "context", 1)
    for step in range(contexts - 2):
        decay = jnp.exp(total[-SUB:][None] * neg)
        enter = from_behind(end + decay * enter, "context", 1)
    parts = 4
    part = width // parts
    cut = run_out(
        where, line, parts, y, total, enter, bc, neg, mixed_in, z_gate[0, 0], skip_gain[None, :], out_w
    )
    kept, sent = cut[:parts], cut[parts:]
    sums, got = [], swap_pair(sent[0])
    for k in range(parts):
        both = add_up(kept[k], got).astype(BF16).reshape(line, row_count, part)
        if k + 1 < parts:
            got = swap_pair(after(sent[k + 1], got))
        sums.append(add_up(both[0], *[along_line(both[s], s) for s in range(1, line)]))
    mixer_out = jnp.concatenate(sums, axis=1)

    stream_f = (residual[0, 0].astype(F32) + mixer_out).astype(BF16).astype(F32)
    normed = (
        stream_f
        * lax.rsqrt(jnp.mean(stream_f * stream_f, axis=1, keepdims=True) + 1e-05)
        * norm_gain[None, :]
    ).astype(BF16)
    ids, weights = route_ids[0, 0], route_w[0, 0]
    capacity = min(row_count, 8 * ((3 * row_count * TOP + 16 * line - 1) // (16 * line)))
    cuts = (0, 8, capacity) if contexts == 2 and dps == 2 and capacity > 8 else (0, capacity)
    named = jnp.any(ids[:, :, None] == jnp.arange(line, dtype=jnp.int32), axis=1)
    rank = jnp.cumsum(named.astype(jnp.int32), axis=0) - 1
    chosen = ids[:, :, None] == jnp.arange(line, dtype=jnp.int32)
    rank_of = jnp.sum(jnp.where(chosen, rank[:, None, :], 0), axis=2)
    away = (ids - place + line) % line
    placing, weighting, packed = [], [], []
    for low, high in zip(cuts[:-1], cuts[1:]):
        inside = (rank_of >= low) & (rank_of < high)
        slot_of = jnp.where(inside, away * (high - low) + rank_of - low, -1)
        hits = slot_of[:, :, None] == jnp.arange(line * (high - low), dtype=jnp.int32)
        placing = jnp.any(hits, axis=1).astype(BF16)
        weighting.append(jnp.sum(jnp.where(hits, weights[:, :, None], 0.0), axis=1))
        rows = lax.dot_general(
            placing, normed, (((0,), (0,)), ((), ())), preferred_element_type=F32
        )
        packed.append(rows.astype(BF16))
    if len(packed) == 2:
        back = square_experts(*packed, line, w_gate[0], w_up[0], w_down[0])
    else:
        back = [plain_experts(packed[0], line, w_gate[0], w_up[0], w_down[0])]
    expert_sum = jnp.dot(
        jnp.concatenate(weighting, axis=1),
        jnp.concatenate(back, axis=0).astype(F32),
        precision=lax.Precision.HIGHEST,
        preferred_element_type=F32,
    )
    mixed = (stream_f + expert_sum).astype(BF16)
    return mixed.reshape(1, 1, row_count, width)


def solution(mesh):
    placed = (
        P("dp", "context", "expert", None),
        P("dp", "context", None, "expert"),
        P("dp", "context", None, "expert"),
        P(None, "expert"),
        P("expert"),
        P("expert", None),
        P(None, "expert"),
        P("expert"),
        P(None, "expert"),
        P("expert"),
        P("expert", None),
        P(),
        P("dp", "context", "expert", None),
        P("dp", "context", "expert", None),
        P("expert", None, ("context", "dp")),
        P("expert", None, ("context", "dp")),
        P("expert", ("context", "dp"), None),
    )
    return jax.shard_map(
        on_device,
        mesh=mesh,
        in_specs=placed,
        out_specs=P("dp", "context", "expert", None),
        check_vma=False,
    )
```

profile of v0, /device:TPU:0, one launch (start us, length us, event | category | flops | bytes accessed | tf_op | source)
XLA Modules:
  0.0 251.6 jit_solution(1192510565233314689)
XLA Ops:
  0.8 2.3 collective-permute-start
  8.9 2.5 collective-permute-start.1
  16.0 2.6 %collective-permute-done.2 = bf16[64,288]{1,0:T(8,128)(2,1)S(1)} collective-permute-done((bf16[64,288]{1,0:T(8,128)(2,1)S(1)}, bf16[64,288]{1,0:T(8,128)(2,1)S(1)}, u32[]{:S(2)}, u32[]{:S(2)}) %collective-permute-start.2) | collective-permute-done | bytes 36896 | tf_op jit(solution)/shard_map/ppermute | solution.py:313
  20.4 2.4 collective-permute-done.4
  22.8 2.3 collective-permute-start.7
  27.8 2.3 collective-permute-done.6.refs_2_
  31.0 6.9 %state_scan.1 = (f32[2048,128]{1,0:T(8,128)S(1)}, f32[2048,128]{1,0:T(8,128)S(1)}, f32[16,8,128]{2,1,0:T(8,128)S(1)}, bf16[256,32]{1,0:T(8,128)(2,1)S(1)}) custom-call(s32[2]{0:T(128)S(1)} %pad_add_fusion.place_ref.at_ref, bf16[64,288]{1,0:T(8,128)(2,1)S(1)} %add_convert_fusion.5.refs_0_, bf16[64,288]{1,0:T(8,128)(2,1)S(1)} %collective-permute-done.5.refs_1_, ...), custom_call_target="tpu_custom_call" | custom-call | flops 200000000 | bytes 4194304 | tf_op jit(solution)/shard_map/state_scan/pallas_call | solution.py:104
  40.1 10.8 %readout_project.1 = (bf16[128,1024]{1,0:T(8,128)(2,1)S(1)}, bf16[128,1024]{1,0:T(8,128)(2,1)S(1)}, bf16[128,1024]{1,0:T(8,128)(2,1)S(1)}, bf16[128,1024]{1,0:T(...) custom-call(s32[2]{0:T(128)S(1)} %pad_add_fusion.place_ref.at_ref, ...), custom_call_target="tpu_custom_call" | custom-call | flops 2147483648 | bytes 16777216 | tf_op jit(solution)/shard_map/readout_project/pallas_call | solution.py:186
  52.6 6.9 %collective-permute-done.9 = bf16[128,1024]{1,0:T(8,128)(2,1)S(1)} collective-permute-done((bf16[128,1024]{1,0:T(8,128)(2,1)S(1)}, bf16[128,1024]{1,0:T(8,128)(2,1)S(1)}, u32[]{:S(2)}, u32[]{:S(2)}) %collective-permute-start.9) | collective-permute-done | bytes 262176 | tf_op jit(solution)/shard_map/ppermute | solution.py:34
  61.2 3.8 %collective-permute-start.12 = (bf16[32,1024]{1,0:T(8,128)(2,1)S(1)}, bf16[32,1024]{1,0:T(8,128)(2,1)S(1)}, u32[]{:S(2)}, u32[]{:S(2)}) collective-permute-start(bf16[32,1024]{1,0:T(8,128)(2,1)S(1)} %get-tuple-element.115), channel_id=1, source_target_pairs={{0,24},{4,28},{8,0},{12,4},{16,8},{20,12},{24,16},{28,20},{1,25},{... | collective-permute-start | bytes 196616 | tf_op jit(solution)/shard_map/ppermute | solution.py:313
  65.0 2.3 collective-permute-done.13
  67.4 3.8 %collective-permute-start.16 = (bf16[32,1024]{1,0:T(8,128)(2,1)S(1)}, bf16[32,1024]{1,0:T(8,128)(2,1)S(1)}, u32[]{:S(2)}, u32[]{:S(2)}) collective-permute-start(bf16[32,1024]{1,0:T(8,128)(2,1)S(1)} %get-tuple-element.118), channel_id=1, source_target_pairs={{0,24},{4,28},{8,0},{12,4},{16,8},{20,12},{24,16},{28,20},{1,25},{... | collective-permute-start | bytes 196616 | tf_op jit(solution)/shard_map/ppermute | solution.py:313
  73.5 2.9 %collective-permute-done.15 = bf16[32,1024]{1,0:T(8,128)(2,1)S(1)} collective-permute-done((bf16[32,1024]{1,0:T(8,128)(2,1)S(1)}, bf16[32,1024]{1,0:T(8,128)(2,1)S(1)}, u32[]{:S(2)}, u32[]{:S(2)}) %collective-permute-start.15) | collective-permute-done | bytes 65568 | tf_op jit(solution)/shard_map/ppermute | solution.py:313
  80.0 3.2 %collective-permute-start.20 = (bf16[32,1024]{1,0:T(8,128)(2,1)S(1)}, bf16[32,1024]{1,0:T(8,128)(2,1)S(1)}, u32[]{:S(2)}, u32[]{:S(2)}) collective-permute-start(bf16[32,1024]{1,0:T(8,128)(2,1)S(1)} %get-tuple-element.121), channel_id=1, source_target_pairs={{0,24},{4,28},{8,0},{12,4},{16,8},{20,12},{24,16},{28,20},{1,25},{... | collective-permute-start | bytes 196616 | tf_op jit(solution)/shard_map/ppermute | solution.py:313
  85.1 3.8 %collective-permute-start.24 = (bf16[32,1024]{1,0:T(8,128)(2,1)S(1)}, bf16[32,1024]{1,0:T(8,128)(2,1)S(1)}, u32[]{:S(2)}, u32[]{:S(2)}) collective-permute-start(bf16[32,1024]{1,0:T(8,128)(2,1)S(1)} %get-tuple-element.124), channel_id=1, source_target_pairs={{0,24},{4,28},{8,0},{12,4},{16,8},{20,12},{24,16},{28,20},{1,25},{... | collective-permute-start | bytes 196616 | tf_op jit(solution)/shard_map/ppermute | solution.py:313
  91.7 2.3 collective-permute-done.23
  95.1 3.9 %collective-permute-start.27 = (bf16[8,4096]{1,0:T(8,128)(2,1)S(1)}, bf16[8,4096]{1,0:T(8,128)(2,1)S(1)}, u32[]{:S(2)}, u32[]{:S(2)}) collective-permute-start(bf16[8,4096]{1,0:T(8,128)(2,1)S(1)} %get-tuple-element.111), channel_id=1, source_target_pairs={{0,24},{4,28},{8,0},{12,4},{16,8},{20,12},{24,16},{28,20},{1,25},{... | collective-permute-start | bytes 196616 | tf_op jit(solution)/shard_map/ppermute | solution.py:313
  98.9 2.5 collective-permute-done.25
  109.2 4.5 %collective-permute-done.28 = bf16[32,4096]{1,0:T(8,128)(2,1)S(1)} collective-permute-done((bf16[32,4096]{1,0:T(8,128)(2,1)S(1)}, bf16[32,4096]{1,0:T(8,128)(2,1)S(1)}, u32[]{:S(2)}, u32[]{:S(2)}) %collective-permute-start.28) | collective-permute-done | bytes 262176 | tf_op jit(solution)/shard_map/ppermute | solution.py:324
  115.5 7.6 %collective-permute-done.29.refs_1_ = bf16[64,4096]{1,0:T(8,128)(2,1)S(1)} collective-permute-done((bf16[64,4096]{1,0:T(8,128)(2,1)S(1)}, bf16[64,4096]{1,0:T(8,128)(2,1)S(1)}, u32[]{:S(2)}, u32[]{:S(2)}) %collective-permute-start.29) | collective-permute-done | bytes 524320 | tf_op jit(solution)/shard_map/ppermute | solution.py:324
  125.9 17.7 %gate_up.2.rows_ref = bf16[256,1536]{1,0:T(8,128)(2,1)} custom-call(bf16[64,4096]{1,0:T(8,128)(2,1)S(1)} %constant_dynamic-update-slice_fusion.refs_0_, bf16[64,4096]{1,0:T(8,128)(2,1)S(1)} %collective-permute-done.29.refs_1_, bf16[64,4096]{1,0:T(8,128)(2,1)S(1)} %collective-permute-done.30.refs_2_, bf16[64,4096]{1,0:T(8,128)(2,1)} %copy-done.7, ...), custom_call_target="tpu_custom_call" | custom-call | flops 6442450944 | bytes 27262976 | tf_op jit(solution)/shard_map/gate_up/pallas_call | solution.py:247
  145.2 7.1 %down.3 = (bf16[128,4096]{1,0:T(8,128)(2,1)S(1)}, bf16[128,4096]{1,0:T(8,128)(2,1)}) custom-call(bf16[256,1536]{1,0:T(8,128)(2,1)S(1)} %copy-done.2, bf16[1536,4096]{1,0:T(8,128)(2,1)} %bitcast.48), custom_call_target="tpu_custom_call" | custom-call | flops 3221225472 | bytes 15466496 | tf_op jit(solution)/shard_map/down/pallas_call | solution.py:293
  152.3 6.2 %collective-permute-done.36.refs_1_ = bf16[128,4096]{1,0:T(8,128)(2,1)S(1)} collective-permute-done((bf16[128,4096]{1,0:T(8,128)(2,1)S(1)}, bf16[128,4096]{1,0:T(8,128)(2,1)S(1)}, u32[]{:S(2)}, u32[]{:S(2)}) %collective-permute-start.36) | collective-permute-done | bytes 1048608 | tf_op jit(solution)/shard_map/ppermute | solution.py:324
  159.1 3.7 %collective-permute-done.37 = bf16[128,4096]{1,0:T(8,128)(2,1)S(1)} collective-permute-done((bf16[128,4096]{1,0:T(8,128)(2,1)}, bf16[128,4096]{1,0:T(8,128)(2,1)S(1)}, u32[]{:S(2)}, u32[]{:S(2)}) %collective-permute-start.37) | collective-permute-done | bytes 1048608 | tf_op jit(solution)/shard_map/ppermute | solution.py:29
  166.8 31.6 %gate_up.3.rows_ref = bf16[512,1536]{1,0:T(8,128)(2,1)} custom-call(bf16[128,4096]{1,0:T(8,128)(2,1)S(1)} %constant_dynamic-update-slice_fusion.9.refs_0_, bf16[128,4096]{1,0:T(8,128)(2,1)} %copy-done.12, bf16[128,4096]{1,0:T(8,128)(2,1)} %copy-done.13, bf16[128,4096]{1,0:T(8,128)(2,1)} %copy-done.14, bf16[4096,1536]{1,0:T(8,128)(2,1)} %bitcast.52, ...), custom_call_target="tpu_custom_call" | custom-call | flops 12884901888 | bytes 29360128 | tf_op jit(solution)/shard_map/gate_up/pallas_call | solution.py:247
  200.5 7.8 %down.4 = (bf16[256,2048]{1,0:T(8,128)(2,1)S(1)}, bf16[256,2048]{1,0:T(8,128)(2,1)}) custom-call(bf16[512,1536]{1,0:T(8,128)(2,1)} %gate_up.3.rows_ref, bf16[1536,4096]{1,0:T(8,128)(2,1)} %bitcast.49), custom_call_target="tpu_custom_call" | custom-call | flops 3221225472 | bytes 9961472 | tf_op jit(solution)/shard_map/down/pallas_call | solution.py:293
  212.3 7.8 %down.5 = (bf16[256,2048]{1,0:T(8,128)(2,1)S(1)}, bf16[256,2048]{1,0:T(8,128)(2,1)}) custom-call(bf16[512,1536]{1,0:T(8,128)(2,1)} %gate_up.3.rows_ref, bf16[1536,4096]{1,0:T(8,128)(2,1)} %bitcast.50), custom_call_target="tpu_custom_call" | custom-call | flops 3221225472 | bytes 9961472 | tf_op jit(solution)/shard_map/down/pallas_call | solution.py:293
  220.3 2.4 collective-permute-start.43
  225.4 3.2 %collective-permute-done.43 = bf16[8,4096]{1,0:T(8,128)(2,1)S(1)} collective-permute-done((bf16[8,4096]{1,0:T(8,128)(2,1)S(1)}, bf16[8,4096]{1,0:T(8,128)(2,1)S(1)}, u32[]{:S(2)}, u32[]{:S(2)}) %collective-permute-start.43) | collective-permute-done | bytes 65568 | tf_op jit(solution)/shard_map/ppermute | solution.py:313
  228.6 3.0 %collective-permute-done.47 = bf16[64,2048]{1,0:T(8,128)(2,1)S(1)} collective-permute-done((bf16[64,2048]{1,0:T(8,128)(2,1)S(1)}, bf16[64,2048]{1,0:T(8,128)(2,1)S(1)}, u32[]{:S(2)}, u32[]{:S(2)}) %collective-permute-start.47) | collective-permute-done | bytes 262176 | tf_op jit(solution)/shard_map/ppermute | solution.py:324
  231.8 2.3 collective-permute-done.52
  247.5 2.9 %collective-permute-done.55 = bf16[16,2048]{1,0:T(8,128)(2,1)S(1)} collective-permute-done((bf16[16,2048]{1,0:T(8,128)(2,1)S(1)}, bf16[16,2048]{1,0:T(8,128)(2,1)S(1)}, u32[]{:S(2)}, u32[]{:S(2)}) %collective-permute-start.55) | collective-permute-done | bytes 65568 | tf_op jit(solution)/shard_map/ppermute | solution.py:313
  (200 shorter events, 75.7 us)
Async XLA Ops:
  8.9 6.9 %collective-permute-start.1 = (bf16[64,288]{1,0:T(8,128)(2,1)S(1)}, bf16[64,288]{1,0:T(8,128)(2,1)S(1)}, u32[]{:S(2)}, u32[]{:S(2)}) collective-permute-start(bf16[64,288]{1,0:T(8,128)(2,1)S(1)} %get-tuple-element.126), channel_id=1, source_target_pairs={{0,8},{4,12},{8,16},{12,20},{16,24},{20,28},{24,0},{28,4},{1,9},{5... | collective-permute-start | bytes 110600 | tf_op jit(solution)/shard_map/ppermute | solution.py:313
  50.9 8.6 %collective-permute-start.9 = (bf16[128,1024]{1,0:T(8,128)(2,1)S(1)}, bf16[128,1024]{1,0:T(8,128)(2,1)S(1)}, u32[]{:S(2)}, u32[]{:S(2)}) collective-permute-start(bf16[128,1024]{1,0:T(8,128)(2,1)S(1)} %get-tuple-element.52), channel_id=1, source_target_pairs={{0,4},{4,0},{8,12},{12,8},{16,20},{20,16},{24,28},{28,24},{1,5},{5... | collective-permute-start | bytes 786440 | tf_op jit(solution)/shard_map/ppermute | solution.py:34
  59.5 7.8 %collective-permute-start.13 = (bf16[128,1024]{1,0:T(8,128)(2,1)S(1)}, bf16[128,1024]{1,0:T(8,128)(2,1)S(1)}, u32[]{:S(2)}, u32[]{:S(2)}) collective-permute-start(bf16[128,1024]{1,0:T(8,128)(2,1)S(1)} %get-tuple-element.55), channel_id=1, source_target_pairs={{0,4},{4,0},{8,12},{12,8},{16,20},{20,16},{24,28},{28,24},{1,5},{5... | collective-permute-start | bytes 786440 | tf_op jit(solution)/shard_map/ppermute | solution.py:34
  61.1 10.1 %collective-permute-start.10 = (bf16[32,1024]{1,0:T(8,128)(2,1)S(1)}, bf16[32,1024]{1,0:T(8,128)(2,1)S(1)}, u32[]{:S(2)}, u32[]{:S(2)}) collective-permute-start(bf16[32,1024]{1,0:T(8,128)(2,1)S(1)} %get-tuple-element.114), channel_id=1, source_target_pairs={{0,8},{4,12},{8,16},{12,20},{16,24},{20,28},{24,0},{28,4},{1,9},{5... | collective-permute-start | bytes 196616 | tf_op jit(solution)/shard_map/ppermute | solution.py:313
  61.2 10.1 %collective-permute-start.12 = (bf16[32,1024]{1,0:T(8,128)(2,1)S(1)}, bf16[32,1024]{1,0:T(8,128)(2,1)S(1)}, u32[]{:S(2)}, u32[]{:S(2)}) collective-permute-start(bf16[32,1024]{1,0:T(8,128)(2,1)S(1)} %get-tuple-element.115), channel_id=1, source_target_pairs={{0,24},{4,28},{8,0},{12,4},{16,8},{20,12},{24,16},{28,20},{1,25},{... | collective-permute-start | bytes 196616 | tf_op jit(solution)/shard_map/ppermute | solution.py:313
  65.0 7.8 %collective-permute-start.11 = (bf16[32,1024]{1,0:T(8,128)(2,1)S(1)}, bf16[32,1024]{1,0:T(8,128)(2,1)S(1)}, u32[]{:S(2)}, u32[]{:S(2)}) collective-permute-start(bf16[32,1024]{1,0:T(8,128)(2,1)S(1)} %get-tuple-element.116), channel_id=1, source_target_pairs={{0,16},{4,20},{8,24},{12,28},{16,0},{20,4},{24,8},{28,12},{1,17},{... | collective-permute-start | bytes 196616 | tf_op jit(solution)/shard_map/ppermute | solution.py:313
  77.7 7.2 %collective-permute-start.21 = (bf16[128,1024]{1,0:T(8,128)(2,1)S(1)}, bf16[128,1024]{1,0:T(8,128)(2,1)S(1)}, u32[]{:S(2)}, u32[]{:S(2)}) collective-permute-start(bf16[128,1024]{1,0:T(8,128)(2,1)S(1)} %get-tuple-element.61), channel_id=1, source_target_pairs={{0,4},{4,0},{8,12},{12,8},{16,20},{20,16},{24,28},{28,24},{1,5},{5... | collective-permute-start | bytes 786440 | tf_op jit(solution)/shard_map/ppermute | solution.py:34
  79.3 9.6 %collective-permute-start.18 = (bf16[32,1024]{1,0:T(8,128)(2,1)S(1)}, bf16[32,1024]{1,0:T(8,128)(2,1)S(1)}, u32[]{:S(2)}, u32[]{:S(2)}) collective-permute-start(bf16[32,1024]{1,0:T(8,128)(2,1)S(1)} %get-tuple-element.120), channel_id=1, source_target_pairs={{0,8},{4,12},{8,16},{12,20},{16,24},{20,28},{24,0},{28,4},{1,9},{5... | collective-permute-start | bytes 196616 | tf_op jit(solution)/shard_map/ppermute | solution.py:313
  80.0 9.8 %collective-permute-start.20 = (bf16[32,1024]{1,0:T(8,128)(2,1)S(1)}, bf16[32,1024]{1,0:T(8,128)(2,1)S(1)}, u32[]{:S(2)}, u32[]{:S(2)}) collective-permute-start(bf16[32,1024]{1,0:T(8,128)(2,1)S(1)} %get-tuple-element.121), channel_id=1, source_target_pairs={{0,24},{4,28},{8,0},{12,4},{16,8},{20,12},{24,16},{28,20},{1,25},{... | collective-permute-start | bytes 196616 | tf_op jit(solution)/shard_map/ppermute | solution.py:313
  83.2 7.2 %collective-permute-start.19 = (bf16[32,1024]{1,0:T(8,128)(2,1)S(1)}, bf16[32,1024]{1,0:T(8,128)(2,1)S(1)}, u32[]{:S(2)}, u32[]{:S(2)}) collective-permute-start(bf16[32,1024]{1,0:T(8,128)(2,1)S(1)} %get-tuple-element.122), channel_id=1, source_target_pairs={{0,16},{4,20},{8,24},{12,28},{16,0},{20,4},{24,8},{28,12},{1,17},{... | collective-permute-start | bytes 196616 | tf_op jit(solution)/shard_map/ppermute | solution.py:313
  95.1 10.5 %collective-permute-start.27 = (bf16[8,4096]{1,0:T(8,128)(2,1)S(1)}, bf16[8,4096]{1,0:T(8,128)(2,1)S(1)}, u32[]{:S(2)}, u32[]{:S(2)}) collective-permute-start(bf16[8,4096]{1,0:T(8,128)(2,1)S(1)} %get-tuple-element.111), channel_id=1, source_target_pairs={{0,24},{4,28},{8,0},{12,4},{16,8},{20,12},{24,16},{28,20},{1,25},{... | collective-permute-start | bytes 196616 | tf_op jit(solution)/shard_map/ppermute | solution.py:313
  98.9 8.4 %collective-permute-start.26 = (bf16[8,4096]{1,0:T(8,128)(2,1)S(1)}, bf16[8,4096]{1,0:T(8,128)(2,1)S(1)}, u32[]{:S(2)}, u32[]{:S(2)}) collective-permute-start(bf16[8,4096]{1,0:T(8,128)(2,1)S(1)} %get-tuple-element.112), channel_id=1, source_target_pairs={{0,16},{4,20},{8,24},{12,28},{16,0},{20,4},{24,8},{28,12},{1,17},{... | collective-permute-start | bytes 196616 | tf_op jit(solution)/shard_map/ppermute | solution.py:313
  101.4 21.7 %collective-permute-start.34 = (bf16[16,4096]{1,0:T(8,128)(2,1)S(1)}, bf16[16,4096]{1,0:T(8,128)(2,1)S(1)}, u32[]{:S(2)}, u32[]{:S(2)}) collective-permute-start(bf16[16,4096]{1,0:T(8,128)(2,1)S(1)} %get-tuple-element.93), channel_id=1, source_target_pairs={{0,24},{4,28},{8,0},{12,4},{16,8},{20,12},{24,16},{28,20},{1,25},{... | collective-permute-start | bytes 393224 | tf_op jit(solution)/shard_map/ppermute | solution.py:313
  101.5 21.6 %collective-permute-start.33 = (bf16[16,4096]{1,0:T(8,128)(2,1)S(1)}, bf16[16,4096]{1,0:T(8,128)(2,1)S(1)}, u32[]{:S(2)}, u32[]{:S(2)}) collective-permute-start(bf16[16,4096]{1,0:T(8,128)(2,1)S(1)} %get-tuple-element.94), channel_id=1, source_target_pairs={{0,16},{4,20},{8,24},{12,28},{16,0},{20,4},{24,8},{28,12},{1,17},{... | collective-permute-start | bytes 393224 | tf_op jit(solution)/shard_map/ppermute | solution.py:313
  103.6 11.8 %collective-permute-start.32 = (bf16[16,4096]{1,0:T(8,128)(2,1)S(1)}, bf16[16,4096]{1,0:T(8,128)(2,1)S(1)}, u32[]{:S(2)}, u32[]{:S(2)}) collective-permute-start(bf16[16,4096]{1,0:T(8,128)(2,1)S(1)} %get-tuple-element.95), channel_id=1, source_target_pairs={{0,8},{4,12},{8,16},{12,20},{16,24},{20,28},{24,0},{28,4},{1,9},{5... | collective-permute-start | bytes 393224 | tf_op jit(solution)/shard_map/ppermute | solution.py:313
  113.8 11.2 %collective-permute-start.30 = (bf16[64,4096]{1,0:T(8,128)(2,1)S(1)}, bf16[64,4096]{1,0:T(8,128)(2,1)S(1)}, u32[]{:S(2)}, u32[]{:S(2)}) collective-permute-start(bf16[64,4096]{1,0:T(8,128)(2,1)S(1)} %constant_dynamic-update-slice_fusion.refs_0_), channel_id=1, source_target_pairs={{0,2},{2,0},{1,3},{3,1},{4,6},{6,4},{5,7},{7,5},{8,10},{10,8},{9,1... | collective-permute-start | bytes 1572872 | tf_op jit(solution)/shard_map/ppermute | solution.py:29
  113.9 9.2 %collective-permute-start.29 = (bf16[64,4096]{1,0:T(8,128)(2,1)S(1)}, bf16[64,4096]{1,0:T(8,128)(2,1)S(1)}, u32[]{:S(2)}, u32[]{:S(2)}) collective-permute-start(bf16[64,4096]{1,0:T(8,128)(2,1)S(1)} %constant_dynamic-update-slice_fusion.refs_0_), channel_id=1, source_target_pairs={{0,1},{1,0},{2,6},{3,7},{4,5},{5,4},{6,2},{7,3},{8,9},{9,8},{10,14... | collective-permute-start | bytes 1572872 | tf_op jit(solution)/shard_map/ppermute | solution.py:324
  123.2 20.4 %collective-permute-start.35 = (bf16[64,4096]{1,0:T(8,128)(2,1)S(1)}, bf16[64,4096]{1,0:T(8,128)(2,1)S(1)}, u32[]{:S(2)}, u32[]{:S(2)}) collective-permute-start(bf16[64,4096]{1,0:T(8,128)(2,1)S(1)} %constant_dynamic-update-slice_fusion.5), channel_id=1, source_target_pairs={{0,4},{1,5},{2,3},{3,2},{4,0},{5,1},{6,7},{7,6},{8,12},{9,13},{10,... | collective-permute-start | bytes 1572872 | tf_op jit(solution)/shard_map/ppermute | solution.py:324
  143.6 14.9 %collective-permute-start.36 = (bf16[128,4096]{1,0:T(8,128)(2,1)S(1)}, bf16[128,4096]{1,0:T(8,128)(2,1)S(1)}, u32[]{:S(2)}, u32[]{:S(2)}) collective-permute-start(bf16[128,4096]{1,0:T(8,128)(2,1)S(1)} %constant_dynamic-update-slice_fusion.9.refs_0_), channel_id=1, source_target_pairs={{0,1},{1,0},{2,6},{3,7},{4,5},{5,4},{6,2},{7,3},{8,9},{9,8},{10,14... | collective-permute-start | bytes 3145736 | tf_op jit(solution)/shard_map/ppermute | solution.py:324
  163.2 35.3 %collective-permute-start.40 = (bf16[64,4096]{1,0:T(8,128)(2,1)S(1)}, bf16[64,4096]{1,0:T(8,128)(2,1)S(1)}, u32[]{:S(2)}, u32[]{:S(2)}) collective-permute-start(bf16[64,4096]{1,0:T(8,128)(2,1)S(1)} %slice.349), channel_id=1, source_target_pairs={{0,1},{1,0},{2,6},{3,7},{4,5},{5,4},{6,2},{7,3},{8,9},{9,8},{10,14... | collective-permute-start | bytes 1572872 | tf_op jit(solution)/shard_map/ppermute | solution.py:324
  198.7 9.7 %collective-permute-start.41 = (bf16[32,4096]{1,0:T(8,128)(2,1)S(1)}, bf16[32,4096]{1,0:T(8,128)(2,1)S(1)}, u32[]{:S(2)}, u32[]{:S(2)}) collective-permute-start(bf16[32,4096]{1,0:T(8,128)(2,1)S(1)} %slice.352), channel_id=1, source_target_pairs={{0,4},{1,5},{2,3},{3,2},{4,0},{5,1},{6,7},{7,6},{8,12},{9,13},{10,... | collective-permute-start | bytes 786440 | tf_op jit(solution)/shard_map/ppermute | solution.py:324
  208.5 14.2 %collective-permute-start.42 = (bf16[8,4096]{1,0:T(8,128)(2,1)S(1)}, bf16[8,4096]{1,0:T(8,128)(2,1)S(1)}, u32[]{:S(2)}, u32[]{:S(2)}) collective-permute-start(bf16[8,4096]{1,0:T(8,128)(2,1)S(1)} %get-tuple-element.107), channel_id=1, source_target_pairs={{0,24},{4,28},{8,0},{12,4},{16,8},{20,12},{24,16},{28,20},{1,25},{... | collective-permute-start | bytes 196616 | tf_op jit(solution)/shard_map/ppermute | solution.py:313
  211.7 11.1 %collective-permute-start.46 = (bf16[128,2048]{1,0:T(8,128)(2,1)S(1)}, bf16[128,2048]{1,0:T(8,128)(2,1)S(1)}, u32[]{:S(2)}, u32[]{:S(2)}) collective-permute-start(bf16[128,2048]{1,0:T(8,128)(2,1)S(1)} %slice.348), channel_id=1, source_target_pairs={{0,1},{1,0},{2,6},{3,7},{4,5},{5,4},{6,2},{7,3},{8,9},{9,8},{10,14... | collective-permute-start | bytes 1572872 | tf_op jit(solution)/shard_map/ppermute | solution.py:324
  220.2 22.5 %collective-permute-start.44 = (bf16[8,4096]{1,0:T(8,128)(2,1)S(1)}, bf16[8,4096]{1,0:T(8,128)(2,1)S(1)}, u32[]{:S(2)}, u32[]{:S(2)}) collective-permute-start(bf16[8,4096]{1,0:T(8,128)(2,1)S(1)} %get-tuple-element.105), channel_id=1, source_target_pairs={{0,8},{4,12},{8,16},{12,20},{16,24},{20,28},{24,0},{28,4},{1,9},{5... | collective-permute-start | bytes 196616 | tf_op jit(solution)/shard_map/ppermute | solution.py:313
  220.3 8.3 %collective-permute-start.43 = (bf16[8,4096]{1,0:T(8,128)(2,1)S(1)}, bf16[8,4096]{1,0:T(8,128)(2,1)S(1)}, u32[]{:S(2)}, u32[]{:S(2)}) collective-permute-start(bf16[8,4096]{1,0:T(8,128)(2,1)S(1)} %get-tuple-element.106), channel_id=1, source_target_pairs={{0,16},{4,20},{8,24},{12,28},{16,0},{20,4},{24,8},{28,12},{1,17},{... | collective-permute-start | bytes 196616 | tf_op jit(solution)/shard_map/ppermute | solution.py:313
  223.0 8.6 %collective-permute-start.47 = (bf16[64,2048]{1,0:T(8,128)(2,1)S(1)}, bf16[64,2048]{1,0:T(8,128)(2,1)S(1)}, u32[]{:S(2)}, u32[]{:S(2)}) collective-permute-start(bf16[64,2048]{1,0:T(8,128)(2,1)S(1)} %slice.351), channel_id=1, source_target_pairs={{0,4},{1,5},{2,3},{3,2},{4,0},{5,1},{6,7},{7,6},{8,12},{9,13},{10,... | collective-permute-start | bytes 786440 | tf_op jit(solution)/shard_map/ppermute | solution.py:324
  224.8 9.2 %collective-permute-start.52 = (bf16[128,2048]{1,0:T(8,128)(2,1)S(1)}, bf16[128,2048]{1,0:T(8,128)(2,1)S(1)}, u32[]{:S(2)}, u32[]{:S(2)}) collective-permute-start(bf16[128,2048]{1,0:T(8,128)(2,1)S(1)} %slice.347), channel_id=1, source_target_pairs={{0,1},{1,0},{2,6},{3,7},{4,5},{5,4},{6,2},{7,3},{8,9},{9,8},{10,14... | collective-permute-start | bytes 1572872 | tf_op jit(solution)/shard_map/ppermute | solution.py:324
  235.1 7.9 %collective-permute-start.50 = (bf16[16,2048]{1,0:T(8,128)(2,1)S(1)}, bf16[16,2048]{1,0:T(8,128)(2,1)S(1)}, u32[]{:S(2)}, u32[]{:S(2)}) collective-permute-start(bf16[16,2048]{1,0:T(8,128)(2,1)S(1)} %get-tuple-element.98), channel_id=1, source_target_pairs={{0,8},{4,12},{8,16},{12,20},{16,24},{20,28},{24,0},{28,4},{1,9},{5... | collective-permute-start | bytes 196616 | tf_op jit(solution)/shard_map/ppermute | solution.py:313
  237.1 8.1 %collective-permute-start.49 = (bf16[16,2048]{1,0:T(8,128)(2,1)S(1)}, bf16[16,2048]{1,0:T(8,128)(2,1)S(1)}, u32[]{:S(2)}, u32[]{:S(2)}) collective-permute-start(bf16[16,2048]{1,0:T(8,128)(2,1)S(1)} %get-tuple-element.99), channel_id=1, source_target_pairs={{0,16},{4,20},{8,24},{12,28},{16,0},{20,4},{24,8},{28,12},{1,17},{... | collective-permute-start | bytes 196616 | tf_op jit(solution)/shard_map/ppermute | solution.py:313
  237.4 7.8 %collective-permute-start.48 = (bf16[16,2048]{1,0:T(8,128)(2,1)S(1)}, bf16[16,2048]{1,0:T(8,128)(2,1)S(1)}, u32[]{:S(2)}, u32[]{:S(2)}) collective-permute-start(bf16[16,2048]{1,0:T(8,128)(2,1)S(1)} %get-tuple-element.100), channel_id=1, source_target_pairs={{0,24},{4,28},{8,0},{12,4},{16,8},{20,12},{24,16},{28,20},{1,25},{... | collective-permute-start | bytes 196616 | tf_op jit(solution)/shard_map/ppermute | solution.py:313
  242.7 7.6 %collective-permute-start.55 = (bf16[16,2048]{1,0:T(8,128)(2,1)S(1)}, bf16[16,2048]{1,0:T(8,128)(2,1)S(1)}, u32[]{:S(2)}, u32[]{:S(2)}) collective-permute-start(bf16[16,2048]{1,0:T(8,128)(2,1)S(1)} %get-tuple-element.103), channel_id=1, source_target_pairs={{0,16},{4,20},{8,24},{12,28},{16,0},{20,4},{24,8},{28,12},{1,17},{... | collective-permute-start | bytes 196616 | tf_op jit(solution)/shard_map/ppermute | solution.py:313
  243.0 7.4 %collective-permute-start.54 = (bf16[16,2048]{1,0:T(8,128)(2,1)S(1)}, bf16[16,2048]{1,0:T(8,128)(2,1)S(1)}, u32[]{:S(2)}, u32[]{:S(2)}) collective-permute-start(bf16[16,2048]{1,0:T(8,128)(2,1)S(1)} %get-tuple-element.104), channel_id=1, source_target_pairs={{0,24},{4,28},{8,0},{12,4},{16,8},{20,12},{24,16},{28,20},{1,25},{... | collective-permute-start | bytes 196616 | tf_op jit(solution)/shard_map/ppermute | solution.py:313
  (40 other events, 295.6 us)
where the time goes:
time: 252 us
  Pallas kernels  89.7 us (36%)
  starting transfers between devices  73.9 us (29%)
  waiting for transfers between devices  72.5 us (29%)
  other arithmetic  6.72 us (3%)
  local copies, waits for them, and re-layouts  5.8 us (2%)
    pallas_call x2, Pallas kernels, gate_up(): pl.pallas_call(functools.partial(gate_up_kernel, len(pieces), tile), out_...  49.3 us
    ppermute x33, starting transfers between devices, along_line(): lax.ppermute(block, 'expert', [(e, (e + 2 * distance) % size) for e in ra...  47.9 us
    ppermute x33, waiting for transfers between devices, along_line(): lax.ppermute(block, 'expert', [(e, (e + 2 * distance) % size) for e in ra...  29.5 us
    ppermute x10, waiting for transfers between devices, cross(): return lax.ppermute(block, ('expert', 'context', 'dp'), route)  24.8 us
    pallas_call x3, Pallas kernels, down(): pl.pallas_call(functools.partial(down_kernel, first, tile), out_shape=tup...  22.7 us
    ppermute x10, starting transfers between devices, cross(): return lax.ppermute(block, ('expert', 'context', 'dp'), route)  13.7 us
    ppermute x5, waiting for transfers between devices, swap_pair(): return lax.ppermute(block, 'expert', [(i, i ^ 1) for i in range(size)])  12.8 us
    pallas_call x1, Pallas kernels, run_out(): pl.pallas_call(functools.partial(out_kernel, channels // LANES, line, par...  10.8 us
  transfers between devices with their start and end apart: 57, of which 30 were waited for; matrix products, arithmetic and copies ran while one was open for 2% of the time, Pallas kernels for 29%

commit v1 on v0

--- a/solution.py
+++ b/solution.py
@@ -128,13 +128,13 @@
     kept_refs, sent_refs = refs[:parts], refs[parts : 2 * parts]
     full_ref, wide_ref, gated_ref, order_ref, w_ref, sems = refs[2 * parts :]
     length = x_ref.shape[0]
-    part = w_ref.shape[1] // parts
+    tiles, _, tile = w_ref.shape
 
     def fetch(j):
-        cols = pl.ds(j * part, part)
-        return pltpu.make_async_copy(w_hbm.at[:, cols], w_ref.at[:, cols], sems.at[j])
-
-    for j in range(parts):
+        cols = pl.ds(pl.multiple_of(j * tile, tile), tile)
+        return pltpu.make_async_copy(w_hbm.at[:, cols], w_ref.at[j], sems.at[j])
+
+    for j in range(tiles):
         fetch(j).start()
     spread_rows(bc_ref[:, NSTATE:], wide_ref)
 
@@ -164,24 +164,24 @@
         for r in range(2):
             source = pl.multiple_of((2 * ((place + k) % line) + (half ^ r)) * piece, piece)
             order_ref[pl.ds(r * count + k * piece, piece), :] = gated_ref[pl.ds(source, piece), :]
-    tile = min(256, part)
     for j in range(parts):
-        fetch(j).wait()
 
         def step(i, carry):
-            target = pl.ds(pl.multiple_of(i * tile, tile), tile)
-            source = pl.ds(pl.multiple_of(j * part + i * tile, tile), tile)
-            out = jnp.dot(order_ref[...], w_ref[:, source], preferred_element_type=F32).astype(BF16)
-            kept_refs[j][:, target] = out[:count]
-            sent_refs[j][:, target] = out[count:]
+            at = j * (tiles // parts) + i
+            fetch(at).wait()
+            cols = pl.ds(pl.multiple_of(i * tile, tile), tile)
+            out = jnp.dot(order_ref[...], w_ref[at], preferred_element_type=F32).astype(BF16)
+            kept_refs[j][:, cols] = out[:count]
+            sent_refs[j][:, cols] = out[count:]
             return carry
 
-        lax.fori_loop(0, part // tile, step, 0)
+        lax.fori_loop(0, tiles // parts, step, 0)
 
 
 def run_out(at, line, parts, y, total, enter, bc, neg, x, z, skip, w):
     length, channels = x.shape
     wide = w.shape[1]
+    tile = min(256, wide // parts)
     vmem = pl.BlockSpec(memory_space=pltpu.VMEM)
     return pl.pallas_call(
         functools.partial(out_kernel, channels // LANES, line, parts),
@@ -193,8 +193,8 @@
             pltpu.VMEM((NSTATE * length, LANES), F32),
             pltpu.VMEM((length, channels), BF16),
             pltpu.VMEM((length, channels), BF16),
-            pltpu.VMEM((channels, wide), BF16),
-            pltpu.SemaphoreType.DMA((parts,)),
+            pltpu.VMEM((wide // tile, channels, tile), BF16),
+            pltpu.SemaphoreType.DMA((wide // tile,)),
         ],
         compiler_params=pltpu.CompilerParams(vmem_limit_bytes=48 * MIB),
         cost_estimate=cost(
@@ -204,20 +204,19 @@
     )(at, y, total, enter, bc, neg, x, z, skip, w)
 
 
-def gate_up_kernel(count, tile, *refs):
+def gate_up_kernel(count, first, *refs):
     pieces, (gate_hbm, up_hbm, out_ref, rows_ref, gate_ref, up_ref, sems) = refs[:count], refs[count:]
     copies, at = [], 0
     for k, piece in enumerate(pieces):
         rows = pl.ds(at, piece.shape[0])
         copies.append(pltpu.make_async_copy(piece, rows_ref.at[rows, :], sems.at[k]))
         at += piece.shape[0]
-    steps = out_ref.shape[1] // tile
+    steps, tile = gate_ref.shape[0], gate_ref.shape[2]
 
     def fetch(j, k):
-        cols = pl.ds(pl.multiple_of(j * tile, tile), tile)
+        cols = pl.ds(pl.multiple_of(first + j * tile, tile), tile)
         source, target = ((gate_hbm, gate_ref), (up_hbm, up_ref))[k]
-        sem = sems.at[count + 2 * j + k]
-        return pltpu.make_async_copy(source.at[:, cols], target.at[:, cols], sem)
+        return pltpu.make_async_copy(source.at[:, cols], target.at[j], sems.at[count + 2 * j + k])
 
     for copy in copies:
         copy.start()
@@ -228,80 +227,87 @@
         copy.wait()
 
     def step(j, carry):
+        fetch(j, 0).wait()
+        gate = jnp.dot(rows_ref[...], gate_ref[j], preferred_element_type=F32)
+        fetch(j, 1).wait()
+        up = jnp.dot(rows_ref[...], up_ref[j], preferred_element_type=F32)
         cols = pl.ds(pl.multiple_of(j * tile, tile), tile)
-        fetch(j, 0).wait()
-        gate = jnp.dot(rows_ref[...], gate_ref[:, cols], preferred_element_type=F32)
-        fetch(j, 1).wait()
-        up = jnp.dot(rows_ref[...], up_ref[:, cols], preferred_element_type=F32)
         out_ref[:, cols] = (gate / (1.0 + jnp.exp(-gate)) * up).astype(BF16)
         return carry
 
     lax.fori_loop(0, steps, step, 0)
 
 
-def gate_up(pieces, w_gate, w_up):
-    depth, hidden = w_gate.shape
+def gate_up(pieces, w_gate, w_up, first, width):
+    depth = w_gate.shape[0]
     rows = sum(p.shape[0] for p in pieces)
-    tile = min(256, hidden)
+    tile = min(256, width)
+    steps = width // tile
     anywhere = pl.BlockSpec(memory_space=pl.ANY)
     return pl.pallas_call(
-        functools.partial(gate_up_kernel, len(pieces), tile),
-        out_shape=jax.ShapeDtypeStruct((rows, hidden), BF16),
+        functools.partial(gate_up_kernel, len(pieces), first),
+        out_shape=jax.ShapeDtypeStruct((rows, width), BF16),
         in_specs=[anywhere] * (len(pieces) + 2),
         out_specs=pl.BlockSpec(memory_space=pltpu.VMEM),
         scratch_shapes=[
             pltpu.VMEM((rows, depth), BF16),
-            pltpu.VMEM((depth, hidden), BF16),
-            pltpu.VMEM((depth, hidden), BF16),
-            pltpu.SemaphoreType.DMA((len(pieces) + 2 * (hidden // tile),)),
+            pltpu.VMEM((steps, depth, tile), BF16),
+            pltpu.VMEM((steps, depth, tile), BF16),
+            pltpu.SemaphoreType.DMA((len(pieces) + 2 * steps,)),
         ],
-        compiler_params=pltpu.CompilerParams(vmem_limit_bytes=52 * MIB),
-        cost_estimate=cost(4 * rows * depth * hidden, 4 * depth * hidden + 2 * rows * depth),
+        compiler_params=pltpu.CompilerParams(vmem_limit_bytes=49 * MIB),
+        cost_estimate=cost(4 * rows * depth * width, 4 * depth * width + 2 * rows * depth),
         name="gate_up",
     )(*pieces, w_gate, w_up)
 
 
-def down_kernel(first, tile, rows_ref, w_hbm, *refs):
-    outs, (w_ref, sems) = refs[:-2], refs[-2:]
-    width = w_ref.shape[1]
+def down_kernel(count, first, *refs):
+    pieces, w_hbm, outs = refs[:count], refs[count], refs[count + 1 : -3]
+    rows_ref, w_ref, sems = refs[-3:]
+    tiles, _, tile = w_ref.shape
 
     def fetch(j):
         source = pl.ds(pl.multiple_of(first + j * tile, tile), tile)
-        target = pl.ds(pl.multiple_of(j * tile, tile), tile)
-        return pltpu.make_async_copy(w_hbm.at[:, source], w_ref.at[:, target], sems.at[j])
-
-    for j in range(width // tile):
+        return pltpu.make_async_copy(w_hbm.at[:, source], w_ref.at[j], sems.at[j])
+
+    for j in range(tiles):
         fetch(j).start()
+    at = 0
+    for piece in pieces:
+        rows_ref[:, pl.ds(at, piece.shape[1])] = piece[...]
+        at += piece.shape[1]
 
     def step(j, carry):
+        fetch(j).wait()
+        out = jnp.dot(rows_ref[...], w_ref[j], preferred_element_type=F32).astype(BF16)
         cols = pl.ds(pl.multiple_of(j * tile, tile), tile)
-        fetch(j).wait()
-        out = jnp.dot(rows_ref[...], w_ref[:, cols], preferred_element_type=F32).astype(BF16)
         start = 0
         for ref in outs:
             ref[:, cols] = out[start : start + ref.shape[0]]
             start += ref.shape[0]
         return carry
 
-    lax.fori_loop(0, width // tile, step, 0)
-
-
-def down(rows, sizes, w_down, first, width):
-    hidden = w_down.shape[0]
-    tile = min(512, width)
+    lax.fori_loop(0, tiles, step, 0)
+
+
+def down(pieces, sizes, w_down, first, width):
+    hidden, rows = w_down.shape[0], pieces[0].shape[0]
+    tile = min(256, width)
     vmem = pl.BlockSpec(memory_space=pltpu.VMEM)
     return pl.pallas_call(
-        functools.partial(down_kernel, first, tile),
+        functools.partial(down_kernel, len(pieces), first),
         out_shape=tuple(jax.ShapeDtypeStruct((n, width), BF16) for n in sizes),
-        in_specs=[vmem, pl.BlockSpec(memory_space=pl.ANY)],
+        in_specs=[vmem] * len(pieces) + [pl.BlockSpec(memory_space=pl.ANY)],
         out_specs=(vmem,) * len(sizes),
-        scratch_shapes=[pltpu.VMEM((hidden, width), BF16), pltpu.SemaphoreType.DMA((width // tile,))],
-        compiler_params=pltpu.CompilerParams(vmem_limit_bytes=52 * MIB),
-        cost_estimate=cost(
-            2 * rows.shape[0] * hidden * width, 2 * hidden * width + 2 * rows.shape[0] * (hidden + width)
-        ),
+        scratch_shapes=[
+            pltpu.VMEM((rows, hidden), BF16),
+            pltpu.VMEM((width // tile, hidden, tile), BF16),
+            pltpu.SemaphoreType.DMA((width // tile,)),
+        ],
+        compiler_params=pltpu.CompilerParams(vmem_limit_bytes=49 * MIB),
+        cost_estimate=cost(2 * rows * hidden * width, 2 * hidden * width + 2 * rows * (hidden + width)),
         name="down",
-    )(rows, w_down)
+    )(*pieces, w_down)
 
 
 def add_up(*parts):
@@ -345,8 +351,8 @@
     own = jnp.concatenate(send_rows(packed, line), axis=0)
     rows = jnp.concatenate([own, swap_pair(own)], axis=0)
     rows = lax.all_gather(rows, ("context", "dp"), axis=0, tiled=True)
-    hidden = gate_up([rows], w_gate, w_up)
-    out = down(hidden, (rows.shape[0],), w_down, 0, w_down.shape[1])[0]
+    hidden = gate_up([rows], w_gate, w_up, 0, w_gate.shape[1])
+    out = down([hidden], (rows.shape[0],), w_down, 0, w_down.shape[1])[0]
     mine = lax.psum_scatter(out, ("context", "dp"), scatter_dimension=0, tiled=True)
     count = own.shape[0]
     return send_home(add_up(mine[:count], swap_pair(mine[count:])).astype(BF16), line)
@@ -355,6 +361,8 @@
 def square_experts(early, late, line, w_gate, w_up, w_down):
     width = w_down.shape[1]
     half = width // 2
+    hidden = w_down.shape[0]
+    most = hidden * 2 // 3
 
     def pieces(two, four):
         return [two, four, shift(two, "context", 1), shift(four, "context", 1)]
@@ -379,25 +387,30 @@
     late_own = jnp.concatenate(late_came, axis=0)
     late_near = cross(late_own, 0)
     sizes = (4 * early_own.shape[0],) * 2
-    early_hidden = gate_up(after(pieces(early_two, early_four), late_own), w_gate, w_up)
-
-    late_two = jnp.concatenate([after(late_own, early_hidden), late_near], axis=0)
+    early_rows = after(pieces(early_two, early_four), late_own)
+    early_first = gate_up(early_rows, w_gate, w_up, 0, most)
+
+    late_two = jnp.concatenate([after(late_own, early_first), late_near], axis=0)
     late_four = cross(late_two, 1)
-    early_out = down(after(early_hidden, late_two), sizes, w_down, 0, width)
+    early_second = gate_up(after(early_rows, late_two), w_gate, w_up, most, hidden - most)
+    early_out = down([early_first, early_second], sizes, w_down, 0, width)
     late_four = after(late_four, early_out)
     early_kept, early_go = home_first(after(early_out, late_four))
     early_far = cross(early_go, 1)
     sizes = (4 * late_own.shape[0],) * 2
-    late_hidden = gate_up(after(pieces(late_two, late_four), early_go), w_gate, w_up)
-
-    early_kept, early_go = home_second(after(early_kept, late_hidden), early_far)
+    late_rows = after(pieces(late_two, late_four), early_go)
+    late_first = gate_up(late_rows, w_gate, w_up, 0, hidden // 2)
+    early_kept, early_go = home_second(after(early_kept, late_first), early_far)
     early_far = cross(early_go, 0)
-    out_left = down(after(late_hidden, early_go), sizes, w_down, 0, half)
-    early_result = add_up(after(early_kept, out_left), early_far).astype(BF16)
+    late_second = gate_up(after(late_rows, early_go), w_gate, w_up, hidden // 2, hidden // 2)
+    early_result = add_up(after(early_kept, late_second), early_far).astype(BF16)
     early_back = send_home(early_result, line)
+    late_hidden = [late_first, late_second]
+    out_left = down(after(late_hidden, early_result), sizes, w_down, 0, half)
     left = home_first(out_left)
     left_far = cross(left[1], 1)
-    out_right = down(after(late_hidden, early_result, left[1]), sizes, w_down, half, half)
+    late_hidden, early_back = lax.optimization_barrier((late_hidden, early_back))
+    out_right = down(after(late_hidden, left[1]), sizes, w_down, half, half)
     left = home_second(after(left[0], out_right), left_far)
     left_far = cross(left[1], 0)
     right = home_first(out_right)

time: 252 us -> 250 us (level)
  waiting for transfers between devices: 72.5 us -> 77.1 us
  Pallas kernels: 89.7 us -> 86.5 us
    ppermute x10, waiting for transfers between devices: 24.8 us -> 29.8 us  [cross(): return lax.ppermute(block, ('expert', 'context', 'dp'), route)]
    pallas_call x5 -> x7, Pallas kernels: 72 us -> 68.9 us  [the longest x4 50 us: gate_up(): pl.pallas_call(functools.partial(gate_up_kernel, len(pieces), first), out...]
  transfers between devices with their start and end apart: 57 -> 57, of which waited for: 30 -> 31; matrix products, arithmetic and copies ran while one was open for 2% -> 2% of each run, Pallas kernels for 29% -> 23%
where the time goes in v1:
time: 250 us
  Pallas kernels  86.5 us (35%)
  waiting for transfers between devices  77.1 us (31%)
  starting transfers between devices  72.9 us (29%)
  other arithmetic  6.05 us (2%)
  local copies, waits for them, and re-layouts  4.18 us (2%)
    pallas_call x4, Pallas kernels, gate_up(): pl.pallas_call(functools.partial(gate_up_kernel, len(pieces), first), out...  50 us
    ppermute x33, starting transfers between devices, along_line(): lax.ppermute(block, 'expert', [(e, (e + 2 * distance) % size) for e in ra...  46.5 us
    ppermute x33, waiting for transfers between devices, along_line(): lax.ppermute(block, 'expert', [(e, (e + 2 * distance) % size) for e in ra...  31.5 us
    ppermute x10, waiting for transfers between devices, cross(): return lax.ppermute(block, ('expert', 'context', 'dp'), route)  29.8 us
    pallas_call x3, Pallas kernels, down(): pl.pallas_call(functools.partial(down_kernel, len(pieces), first), out_sh...  18.9 us
    ppermute x10, starting transfers between devices, cross(): return lax.ppermute(block, ('expert', 'context', 'dp'), route)  13.9 us
    ppermute x5, waiting for transfers between devices, swap_pair(): return lax.ppermute(block, 'expert', [(i, i ^ 1) for i in range(size)])  12.8 us
    pallas_call x1, Pallas kernels, run_out(): pl.pallas_call(functools.partial(out_kernel, channels // LANES, line, par...  10.7 us
  transfers between devices with their start and end apart: 57, of which 31 were waited for; matrix products, arithmetic and copies ran while one was open for 2% of the time, Pallas kernels for 23%

profile of v1, /device:TPU:0, one launch (start us, length us, event | category | flops | bytes accessed | tf_op | source)
XLA Modules:
  0.0 249.7 jit_solution(10158463507708453723)
XLA Ops:
  0.8 2.3 collective-permute-start
  8.3 2.5 collective-permute-start.1
  15.3 2.6 %collective-permute-done.2 = bf16[64,288]{1,0:T(8,128)(2,1)S(1)} collective-permute-done((bf16[64,288]{1,0:T(8,128)(2,1)S(1)}, bf16[64,288]{1,0:T(8,128)(2,1)S(1)}, u32[]{:S(2)}, u32[]{:S(2)}) %collective-permute-start.2) | collective-permute-done | bytes 36896 | tf_op jit(solution)/shard_map/ppermute | solution.py:319
  19.7 2.4 collective-permute-done.4
  22.1 2.3 collective-permute-start.7
  30.3 6.9 %state_scan.1 = (f32[2048,128]{1,0:T(8,128)S(1)}, f32[2048,128]{1,0:T(8,128)S(1)}, f32[16,8,128]{2,1,0:T(8,128)S(1)}, bf16[256,32]{1,0:T(8,128)(2,1)S(1)}) custom-call(s32[2]{0:T(128)S(1)} %pad_add_fusion.place_ref.at_ref, bf16[64,288]{1,0:T(8,128)(2,1)S(1)} %add_convert_fusion.5.refs_0_, bf16[64,288]{1,0:T(8,128)(2,1)S(1)} %collective-permute-done.5.refs_1_, ...), custom_call_target="tpu_custom_call" | custom-call | flops 200000000 | bytes 4194304 | tf_op jit(solution)/shard_map/state_scan/pallas_call | solution.py:104
  39.4 10.7 %readout_project.1 = (bf16[128,1024]{1,0:T(8,128)(2,1)S(1)}, bf16[128,1024]{1,0:T(8,128)(2,1)S(1)}, bf16[128,1024]{1,0:T(8,128)(2,1)S(1)}, bf16[128,1024]{1,0:T(...) custom-call(s32[2]{0:T(128)S(1)} %pad_add_fusion.place_ref.at_ref, ...), custom_call_target="tpu_custom_call" | custom-call | flops 2147483648 | bytes 16777216 | tf_op jit(solution)/shard_map/readout_project/pallas_call | solution.py:186
  51.9 6.9 %collective-permute-done.9 = bf16[128,1024]{1,0:T(8,128)(2,1)S(1)} collective-permute-done((bf16[128,1024]{1,0:T(8,128)(2,1)S(1)}, bf16[128,1024]{1,0:T(8,128)(2,1)S(1)}, u32[]{:S(2)}, u32[]{:S(2)}) %collective-permute-start.9) | collective-permute-done | bytes 262176 | tf_op jit(solution)/shard_map/ppermute | solution.py:34
  60.4 3.8 %collective-permute-start.12 = (bf16[32,1024]{1,0:T(8,128)(2,1)S(1)}, bf16[32,1024]{1,0:T(8,128)(2,1)S(1)}, u32[]{:S(2)}, u32[]{:S(2)}) collective-permute-start(bf16[32,1024]{1,0:T(8,128)(2,1)S(1)} %get-tuple-element.139), channel_id=1, source_target_pairs={{0,24},{4,28},{8,0},{12,4},{16,8},{20,12},{24,16},{28,20},{1,25},{... | collective-permute-start | bytes 196616 | tf_op jit(solution)/shard_map/ppermute | solution.py:319
  64.2 2.3 collective-permute-done.13
  66.6 3.8 %collective-permute-start.16 = (bf16[32,1024]{1,0:T(8,128)(2,1)S(1)}, bf16[32,1024]{1,0:T(8,128)(2,1)S(1)}, u32[]{:S(2)}, u32[]{:S(2)}) collective-permute-start(bf16[32,1024]{1,0:T(8,128)(2,1)S(1)} %get-tuple-element.142), channel_id=1, source_target_pairs={{0,24},{4,28},{8,0},{12,4},{16,8},{20,12},{24,16},{28,20},{1,25},{... | collective-permute-start | bytes 196616 | tf_op jit(solution)/shard_map/ppermute | solution.py:319
  72.7 2.9 %collective-permute-done.15 = bf16[32,1024]{1,0:T(8,128)(2,1)S(1)} collective-permute-done((bf16[32,1024]{1,0:T(8,128)(2,1)S(1)}, bf16[32,1024]{1,0:T(8,128)(2,1)S(1)}, u32[]{:S(2)}, u32[]{:S(2)}) %collective-permute-start.15) | collective-permute-done | bytes 65568 | tf_op jit(solution)/shard_map/ppermute | solution.py:319
  79.2 3.2 %collective-permute-start.20 = (bf16[32,1024]{1,0:T(8,128)(2,1)S(1)}, bf16[32,1024]{1,0:T(8,128)(2,1)S(1)}, u32[]{:S(2)}, u32[]{:S(2)}) collective-permute-start(bf16[32,1024]{1,0:T(8,128)(2,1)S(1)} %get-tuple-element.145), channel_id=1, source_target_pairs={{0,24},{4,28},{8,0},{12,4},{16,8},{20,12},{24,16},{28,20},{1,25},{... | collective-permute-start | bytes 196616 | tf_op jit(solution)/shard_map/ppermute | solution.py:319
  84.3 3.8 %collective-permute-start.24 = (bf16[32,1024]{1,0:T(8,128)(2,1)S(1)}, bf16[32,1024]{1,0:T(8,128)(2,1)S(1)}, u32[]{:S(2)}, u32[]{:S(2)}) collective-permute-start(bf16[32,1024]{1,0:T(8,128)(2,1)S(1)} %get-tuple-element.148), channel_id=1, source_target_pairs={{0,24},{4,28},{8,0},{12,4},{16,8},{20,12},{24,16},{28,20},{1,25},{... | collective-permute-start | bytes 196616 | tf_op jit(solution)/shard_map/ppermute | solution.py:319
  91.0 2.3 collective-permute-done.23
  94.3 3.9 %collective-permute-start.27 = (bf16[8,4096]{1,0:T(8,128)(2,1)S(1)}, bf16[8,4096]{1,0:T(8,128)(2,1)S(1)}, u32[]{:S(2)}, u32[]{:S(2)}) collective-permute-start(bf16[8,4096]{1,0:T(8,128)(2,1)S(1)} %get-tuple-element.134), channel_id=1, source_target_pairs={{0,24},{4,28},{8,0},{12,4},{16,8},{20,12},{24,16},{28,20},{1,25},{... | collective-permute-start | bytes 196616 | tf_op jit(solution)/shard_map/ppermute | solution.py:319
  98.2 2.5 collective-permute-done.25
  108.4 4.5 %collective-permute-done.28 = bf16[32,4096]{1,0:T(8,128)(2,1)S(1)} collective-permute-done((bf16[32,4096]{1,0:T(8,128)(2,1)S(1)}, bf16[32,4096]{1,0:T(8,128)(2,1)S(1)}, u32[]{:S(2)}, u32[]{:S(2)}) %collective-permute-start.28) | collective-permute-done | bytes 262176 | tf_op jit(solution)/shard_map/ppermute | solution.py:330
  114.7 7.6 %collective-permute-done.32.refs_1_ = bf16[64,4096]{1,0:T(8,128)(2,1)S(1)} collective-permute-done((bf16[64,4096]{1,0:T(8,128)(2,1)S(1)}, bf16[64,4096]{1,0:T(8,128)(2,1)S(1)}, u32[]{:S(2)}, u32[]{:S(2)}) %collective-permute-start.32) | collective-permute-done | bytes 524320 | tf_op jit(solution)/shard_map/ppermute | solution.py:330
  124.3 11.7 %gate_up.4.refs_0_ = bf16[256,1024]{1,0:T(8,128)(2,1)S(1)} custom-call(bf16[64,4096]{1,0:T(8,128)(2,1)S(1)} %constant_dynamic-update-slice_fusion.4.refs_0_, bf16[64,4096]{1,0:T(8,128)(2,1)S(1)} %collective-permute-done.32.refs_1_, bf16[64,4096]{1,0:T(8,128)(2,1)S(1)} %collective-permute-done.33.refs_2_, ...), custom_call_target="tpu_custom_call" | custom-call | flops 4294967296 | bytes 18874368 | tf_op jit(solution)/shard_map/gate_up/pallas_call | solution.py:247
  137.6 6.7 %gate_up.5.refs_1_ = bf16[256,512]{1,0:T(8,128)(2,1)S(1)} custom-call(bf16[64,4096]{1,0:T(8,128)(2,1)S(1)} %constant_dynamic-update-slice_fusion.4.refs_0_, bf16[64,4096]{1,0:T(8,128)(2,1)S(1)} %collective-permute-done.32.refs_1_, bf16[64,4096]{1,0:T(8,128)(2,1)S(1)} %collective-permute-done.33.refs_2_, ...), custom_call_target="tpu_custom_call" | custom-call | flops 2147483648 | bytes 10485760 | tf_op jit(solution)/shard_map/gate_up/pallas_call | solution.py:247
  144.3 7.3 %down.3 = (bf16[128,4096]{1,0:T(8,128)(2,1)S(1)}, bf16[128,4096]{1,0:T(8,128)(2,1)S(1)}) custom-call(bf16[256,1024]{1,0:T(8,128)(2,1)S(1)} %gate_up.4.refs_0_, bf16[256,512]{1,0:T(8,128)(2,1)S(1)} %gate_up.5.refs_1_, bf16[1536,4096]{1,0:T(8,128)(2,1)} %bitcast.55), custom_call_target="tpu_custom_call" | custom-call | flops 3221225472 | bytes 15466496 | tf_op jit(solution)/shard_map/down/pallas_call | solution.py:297
  157.3 15.8 %gate_up.6.refs_0_ = bf16[512,768]{1,0:T(8,128)(2,1)S(1)} custom-call(bf16[128,4096]{1,0:T(8,128)(2,1)S(1)} %constant_dynamic-update-slice_fusion.9.refs_0_, bf16[128,4096]{1,0:T(8,128)(2,1)S(1)} %collective-permute-done.36.refs_1_, bf16[128,4096]{1,0:T(8,128)(2,1)S(1)} %collective-permute-done.37.refs_2_, ...), custom_call_target="tpu_custom_call" | custom-call | flops 6442450944 | bytes 16777216 | tf_op jit(solution)/shard_map/gate_up/pallas_call | solution.py:247
  175.1 15.8 %gate_up.7.refs_1_ = bf16[512,768]{1,0:T(8,128)(2,1)S(1)} custom-call(bf16[128,4096]{1,0:T(8,128)(2,1)S(1)} %constant_dynamic-update-slice_fusion.9.refs_0_, bf16[128,4096]{1,0:T(8,128)(2,1)S(1)} %collective-permute-done.36.refs_1_, bf16[128,4096]{1,0:T(8,128)(2,1)S(1)} %collective-permute-done.37.refs_2_, ...), custom_call_target="tpu_custom_call" | custom-call | flops 6442450944 | bytes 16777216 | tf_op jit(solution)/shard_map/gate_up/pallas_call | solution.py:247
  191.1 5.8 %down.4 = (bf16[256,2048]{1,0:T(8,128)(2,1)S(1)}, bf16[256,2048]{1,0:T(8,128)(2,1)S(1)}) custom-call(bf16[512,768]{1,0:T(8,128)(2,1)S(1)} %gate_up.6.refs_0_, bf16[512,768]{1,0:T(8,128)(2,1)S(1)} %gate_up.7.refs_1_, bf16[1536,4096]{1,0:T(8,128)(2,1)} %bitcast.56), custom_call_target="tpu_custom_call" | custom-call | flops 3221225472 | bytes 9961472 | tf_op jit(solution)/shard_map/down/pallas_call | solution.py:297
  197.1 2.4 collective-permute-start.43
  200.9 3.0 %collective-permute-done.44 = bf16[8,4096]{1,0:T(8,128)(2,1)S(1)} collective-permute-done((bf16[8,4096]{1,0:T(8,128)(2,1)S(1)}, bf16[8,4096]{1,0:T(8,128)(2,1)S(1)}, u32[]{:S(2)}, u32[]{:S(2)}) %collective-permute-start.44) | collective-permute-done | bytes 65568 | tf_op jit(solution)/shard_map/ppermute | solution.py:319
  206.2 5.8 %down.5 = (bf16[256,2048]{1,0:T(8,128)(2,1)S(1)}, bf16[256,2048]{1,0:T(8,128)(2,1)S(1)}) custom-call(bf16[512,768]{1,0:T(8,128)(2,1)S(1)} %gate_up.6.refs_0_, bf16[512,768]{1,0:T(8,128)(2,1)S(1)} %gate_up.7.refs_1_, bf16[1536,4096]{1,0:T(8,128)(2,1)} %bitcast.57), custom_call_target="tpu_custom_call" | custom-call | flops 3221225472 | bytes 9961472 | tf_op jit(solution)/shard_map/down/pallas_call | solution.py:297
  213.0 8.4 %collective-permute-done.46 = bf16[128,2048]{1,0:T(8,128)(2,1)S(1)} collective-permute-done((bf16[128,2048]{1,0:T(8,128)(2,1)S(1)}, bf16[128,2048]{1,0:T(8,128)(2,1)S(1)}, u32[]{:S(2)}, u32[]{:S(2)}) %collective-permute-start.46) | collective-permute-done | bytes 524320 | tf_op jit(solution)/shard_map/ppermute | solution.py:330
  224.0 6.7 %collective-permute-done.47 = bf16[64,2048]{1,0:T(8,128)(2,1)S(1)} collective-permute-done((bf16[64,2048]{1,0:T(8,128)(2,1)S(1)}, bf16[64,2048]{1,0:T(8,128)(2,1)S(1)}, u32[]{:S(2)}, u32[]{:S(2)}) %collective-permute-start.47) | collective-permute-done | bytes 262176 | tf_op jit(solution)/shard_map/ppermute | solution.py:330
  243.1 2.6 %collective-permute-done.56 = bf16[16,2048]{1,0:T(8,128)(2,1)S(1)} collective-permute-done((bf16[16,2048]{1,0:T(8,128)(2,1)S(1)}, bf16[16,2048]{1,0:T(8,128)(2,1)S(1)}, u32[]{:S(2)}, u32[]{:S(2)}) %collective-permute-start.56) | collective-permute-done | bytes 65568 | tf_op jit(solution)/shard_map/ppermute | solution.py:319
  245.7 2.7 %collective-permute-done.55 = bf16[16,2048]{1,0:T(8,128)(2,1)S(1)} collective-permute-done((bf16[16,2048]{1,0:T(8,128)(2,1)S(1)}, bf16[16,2048]{1,0:T(8,128)(2,1)S(1)}, u32[]{:S(2)}, u32[]{:S(2)}) %collective-permute-start.55) | collective-permute-done | bytes 65568 | tf_op jit(solution)/shard_map/ppermute | solution.py:319
  (194 shorter events, 77.1 us)
Async XLA Ops:
  8.3 6.9 %collective-permute-start.1 = (bf16[64,288]{1,0:T(8,128)(2,1)S(1)}, bf16[64,288]{1,0:T(8,128)(2,1)S(1)}, u32[]{:S(2)}, u32[]{:S(2)}) collective-permute-start(bf16[64,288]{1,0:T(8,128)(2,1)S(1)} %get-tuple-element.150), channel_id=1, source_target_pairs={{0,8},{4,12},{8,16},{12,20},{16,24},{20,28},{24,0},{28,4},{1,9},{5... | collective-permute-start | bytes 110600 | tf_op jit(solution)/shard_map/ppermute | solution.py:319
  50.1 8.6 %collective-permute-start.9 = (bf16[128,1024]{1,0:T(8,128)(2,1)S(1)}, bf16[128,1024]{1,0:T(8,128)(2,1)S(1)}, u32[]{:S(2)}, u32[]{:S(2)}) collective-permute-start(bf16[128,1024]{1,0:T(8,128)(2,1)S(1)} %get-tuple-element.64), channel_id=1, source_target_pairs={{0,4},{4,0},{8,12},{12,8},{16,20},{20,16},{24,28},{28,24},{1,5},{5... | collective-permute-start | bytes 786440 | tf_op jit(solution)/shard_map/ppermute | solution.py:34
  58.7 7.8 %collective-permute-start.13 = (bf16[128,1024]{1,0:T(8,128)(2,1)S(1)}, bf16[128,1024]{1,0:T(8,128)(2,1)S(1)}, u32[]{:S(2)}, u32[]{:S(2)}) collective-permute-start(bf16[128,1024]{1,0:T(8,128)(2,1)S(1)} %get-tuple-element.67), channel_id=1, source_target_pairs={{0,4},{4,0},{8,12},{12,8},{16,20},{20,16},{24,28},{28,24},{1,5},{5... | collective-permute-start | bytes 786440 | tf_op jit(solution)/shard_map/ppermute | solution.py:34
  60.3 10.1 %collective-permute-start.10 = (bf16[32,1024]{1,0:T(8,128)(2,1)S(1)}, bf16[32,1024]{1,0:T(8,128)(2,1)S(1)}, u32[]{:S(2)}, u32[]{:S(2)}) collective-permute-start(bf16[32,1024]{1,0:T(8,128)(2,1)S(1)} %get-tuple-element.138), channel_id=1, source_target_pairs={{0,8},{4,12},{8,16},{12,20},{16,24},{20,28},{24,0},{28,4},{1,9},{5... | collective-permute-start | bytes 196616 | tf_op jit(solution)/shard_map/ppermute | solution.py:319
  60.4 10.1 %collective-permute-start.12 = (bf16[32,1024]{1,0:T(8,128)(2,1)S(1)}, bf16[32,1024]{1,0:T(8,128)(2,1)S(1)}, u32[]{:S(2)}, u32[]{:S(2)}) collective-permute-start(bf16[32,1024]{1,0:T(8,128)(2,1)S(1)} %get-tuple-element.139), channel_id=1, source_target_pairs={{0,24},{4,28},{8,0},{12,4},{16,8},{20,12},{24,16},{28,20},{1,25},{... | collective-permute-start | bytes 196616 | tf_op jit(solution)/shard_map/ppermute | solution.py:319
  64.2 7.8 %collective-permute-start.11 = (bf16[32,1024]{1,0:T(8,128)(2,1)S(1)}, bf16[32,1024]{1,0:T(8,128)(2,1)S(1)}, u32[]{:S(2)}, u32[]{:S(2)}) collective-permute-start(bf16[32,1024]{1,0:T(8,128)(2,1)S(1)} %get-tuple-element.140), channel_id=1, source_target_pairs={{0,16},{4,20},{8,24},{12,28},{16,0},{20,4},{24,8},{28,12},{1,17},{... | collective-permute-start | bytes 196616 | tf_op jit(solution)/shard_map/ppermute | solution.py:319
  76.9 7.2 %collective-permute-start.21 = (bf16[128,1024]{1,0:T(8,128)(2,1)S(1)}, bf16[128,1024]{1,0:T(8,128)(2,1)S(1)}, u32[]{:S(2)}, u32[]{:S(2)}) collective-permute-start(bf16[128,1024]{1,0:T(8,128)(2,1)S(1)} %get-tuple-element.73), channel_id=1, source_target_pairs={{0,4},{4,0},{8,12},{12,8},{16,20},{20,16},{24,28},{28,24},{1,5},{5... | collective-permute-start | bytes 786440 | tf_op jit(solution)/shard_map/ppermute | solution.py:34
  78.5 9.6 %collective-permute-start.18 = (bf16[32,1024]{1,0:T(8,128)(2,1)S(1)}, bf16[32,1024]{1,0:T(8,128)(2,1)S(1)}, u32[]{:S(2)}, u32[]{:S(2)}) collective-permute-start(bf16[32,1024]{1,0:T(8,128)(2,1)S(1)} %get-tuple-element.144), channel_id=1, source_target_pairs={{0,8},{4,12},{8,16},{12,20},{16,24},{20,28},{24,0},{28,4},{1,9},{5... | collective-permute-start | bytes 196616 | tf_op jit(solution)/shard_map/ppermute | solution.py:319
  79.2 9.8 %collective-permute-start.20 = (bf16[32,1024]{1,0:T(8,128)(2,1)S(1)}, bf16[32,1024]{1,0:T(8,128)(2,1)S(1)}, u32[]{:S(2)}, u32[]{:S(2)}) collective-permute-start(bf16[32,1024]{1,0:T(8,128)(2,1)S(1)} %get-tuple-element.145), channel_id=1, source_target_pairs={{0,24},{4,28},{8,0},{12,4},{16,8},{20,12},{24,16},{28,20},{1,25},{... | collective-permute-start | bytes 196616 | tf_op jit(solution)/shard_map/ppermute | solution.py:319
  82.4 7.2 %collective-permute-start.19 = (bf16[32,1024]{1,0:T(8,128)(2,1)S(1)}, bf16[32,1024]{1,0:T(8,128)(2,1)S(1)}, u32[]{:S(2)}, u32[]{:S(2)}) collective-permute-start(bf16[32,1024]{1,0:T(8,128)(2,1)S(1)} %get-tuple-element.146), channel_id=1, source_target_pairs={{0,16},{4,20},{8,24},{12,28},{16,0},{20,4},{24,8},{28,12},{1,17},{... | collective-permute-start | bytes 196616 | tf_op jit(solution)/shard_map/ppermute | solution.py:319
  94.3 10.5 %collective-permute-start.27 = (bf16[8,4096]{1,0:T(8,128)(2,1)S(1)}, bf16[8,4096]{1,0:T(8,128)(2,1)S(1)}, u32[]{:S(2)}, u32[]{:S(2)}) collective-permute-start(bf16[8,4096]{1,0:T(8,128)(2,1)S(1)} %get-tuple-element.134), channel_id=1, source_target_pairs={{0,24},{4,28},{8,0},{12,4},{16,8},{20,12},{24,16},{28,20},{1,25},{... | collective-permute-start | bytes 196616 | tf_op jit(solution)/shard_map/ppermute | solution.py:319
  98.2 8.4 %collective-permute-start.26 = (bf16[8,4096]{1,0:T(8,128)(2,1)S(1)}, bf16[8,4096]{1,0:T(8,128)(2,1)S(1)}, u32[]{:S(2)}, u32[]{:S(2)}) collective-permute-start(bf16[8,4096]{1,0:T(8,128)(2,1)S(1)} %get-tuple-element.135), channel_id=1, source_target_pairs={{0,16},{4,20},{8,24},{12,28},{16,0},{20,4},{24,8},{28,12},{1,17},{... | collective-permute-start | bytes 196616 | tf_op jit(solution)/shard_map/ppermute | solution.py:319
  100.7 21.7 %collective-permute-start.31 = (bf16[16,4096]{1,0:T(8,128)(2,1)S(1)}, bf16[16,4096]{1,0:T(8,128)(2,1)S(1)}, u32[]{:S(2)}, u32[]{:S(2)}) collective-permute-start(bf16[16,4096]{1,0:T(8,128)(2,1)S(1)} %get-tuple-element.117), channel_id=1, source_target_pairs={{0,24},{4,28},{8,0},{12,4},{16,8},{20,12},{24,16},{28,20},{1,25},{... | collective-permute-start | bytes 393224 | tf_op jit(solution)/shard_map/ppermute | solution.py:319
  100.7 21.6 %collective-permute-start.30 = (bf16[16,4096]{1,0:T(8,128)(2,1)S(1)}, bf16[16,4096]{1,0:T(8,128)(2,1)S(1)}, u32[]{:S(2)}, u32[]{:S(2)}) collective-permute-start(bf16[16,4096]{1,0:T(8,128)(2,1)S(1)} %get-tuple-element.118), channel_id=1, source_target_pairs={{0,16},{4,20},{8,24},{12,28},{16,0},{20,4},{24,8},{28,12},{1,17},{... | collective-permute-start | bytes 393224 | tf_op jit(solution)/shard_map/ppermute | solution.py:319
  102.8 11.8 %collective-permute-start.29 = (bf16[16,4096]{1,0:T(8,128)(2,1)S(1)}, bf16[16,4096]{1,0:T(8,128)(2,1)S(1)}, u32[]{:S(2)}, u32[]{:S(2)}) collective-permute-start(bf16[16,4096]{1,0:T(8,128)(2,1)S(1)} %get-tuple-element.119), channel_id=1, source_target_pairs={{0,8},{4,12},{8,16},{12,20},{16,24},{20,28},{24,0},{28,4},{1,9},{5... | collective-permute-start | bytes 393224 | tf_op jit(solution)/shard_map/ppermute | solution.py:319
  113.0 11.2 %collective-permute-start.33 = (bf16[64,4096]{1,0:T(8,128)(2,1)S(1)}, bf16[64,4096]{1,0:T(8,128)(2,1)S(1)}, u32[]{:S(2)}, u32[]{:S(2)}) collective-permute-start(bf16[64,4096]{1,0:T(8,128)(2,1)S(1)} %constant_dynamic-update-slice_fusion.4.refs_0_), channel_id=1, source_target_pairs={{0,2},{2,0},{1,3},{3,1},{4,6},{6,4},{5,7},{7,5},{8,10},{10,8},{9,1... | collective-permute-start | bytes 1572872 | tf_op jit(solution)/shard_map/ppermute | solution.py:29
  113.1 9.2 %collective-permute-start.32 = (bf16[64,4096]{1,0:T(8,128)(2,1)S(1)}, bf16[64,4096]{1,0:T(8,128)(2,1)S(1)}, u32[]{:S(2)}, u32[]{:S(2)}) collective-permute-start(bf16[64,4096]{1,0:T(8,128)(2,1)S(1)} %constant_dynamic-update-slice_fusion.4.refs_0_), channel_id=1, source_target_pairs={{0,1},{1,0},{2,6},{3,7},{4,5},{5,4},{6,2},{7,3},{8,9},{9,8},{10,14... | collective-permute-start | bytes 1572872 | tf_op jit(solution)/shard_map/ppermute | solution.py:330
  122.4 13.6 %collective-permute-start.35 = (bf16[64,4096]{1,0:T(8,128)(2,1)S(1)}, bf16[64,4096]{1,0:T(8,128)(2,1)S(1)}, u32[]{:S(2)}, u32[]{:S(2)}) collective-permute-start(bf16[64,4096]{1,0:T(8,128)(2,1)S(1)} %constant_dynamic-update-slice_fusion), channel_id=1, source_target_pairs={{0,4},{1,5},{2,3},{3,2},{4,0},{5,1},{6,7},{7,6},{8,12},{9,13},{10,... | collective-permute-start | bytes 1572872 | tf_op jit(solution)/shard_map/ppermute | solution.py:330
  136.0 15.6 %collective-permute-start.36 = (bf16[128,4096]{1,0:T(8,128)(2,1)S(1)}, bf16[128,4096]{1,0:T(8,128)(2,1)S(1)}, u32[]{:S(2)}, u32[]{:S(2)}) collective-permute-start(bf16[128,4096]{1,0:T(8,128)(2,1)S(1)} %constant_dynamic-update-slice_fusion.9.refs_0_), channel_id=1, source_target_pairs={{0,1},{1,0},{2,6},{3,7},{4,5},{5,4},{6,2},{7,3},{8,9},{9,8},{10,14... | collective-permute-start | bytes 3145736 | tf_op jit(solution)/shard_map/ppermute | solution.py:330
  155.9 17.2 %collective-permute-start.40 = (bf16[64,4096]{1,0:T(8,128)(2,1)S(1)}, bf16[64,4096]{1,0:T(8,128)(2,1)S(1)}, u32[]{:S(2)}, u32[]{:S(2)}) collective-permute-start(bf16[64,4096]{1,0:T(8,128)(2,1)S(1)} %slice.348), channel_id=1, source_target_pairs={{0,1},{1,0},{2,6},{3,7},{4,5},{5,4},{6,2},{7,3},{8,9},{9,8},{10,14... | collective-permute-start | bytes 1572872 | tf_op jit(solution)/shard_map/ppermute | solution.py:330
  173.3 17.7 %collective-permute-start.41 = (bf16[32,4096]{1,0:T(8,128)(2,1)S(1)}, bf16[32,4096]{1,0:T(8,128)(2,1)S(1)}, u32[]{:S(2)}, u32[]{:S(2)}) collective-permute-start(bf16[32,4096]{1,0:T(8,128)(2,1)S(1)} %slice.351), channel_id=1, source_target_pairs={{0,4},{1,5},{2,3},{3,2},{4,0},{5,1},{6,7},{7,6},{8,12},{9,13},{10,... | collective-permute-start | bytes 786440 | tf_op jit(solution)/shard_map/ppermute | solution.py:330
  196.9 8.9 %collective-permute-start.45 = (bf16[256,2048]{1,0:T(8,128)(2,1)S(1)}, bf16[256,2048]{1,0:T(8,128)(2,1)S(1)}, u32[]{:S(2)}, u32[]{:S(2)}) collective-permute-start(bf16[256,2048]{1,0:T(8,128)(2,1)S(1)} %get-tuple-element.104), channel_id=1, source_target_pairs={{0,2},{2,0},{1,3},{3,1},{4,6},{6,4},{5,7},{7,5},{8,10},{10,8},{9,1... | collective-permute-start | bytes 3145736 | tf_op jit(solution)/shard_map/ppermute | solution.py:29
  197.0 6.8 %collective-permute-start.44 = (bf16[8,4096]{1,0:T(8,128)(2,1)S(1)}, bf16[8,4096]{1,0:T(8,128)(2,1)S(1)}, u32[]{:S(2)}, u32[]{:S(2)}) collective-permute-start(bf16[8,4096]{1,0:T(8,128)(2,1)S(1)} %get-tuple-element.130), channel_id=1, source_target_pairs={{0,8},{4,12},{8,16},{12,20},{16,24},{20,28},{24,0},{28,4},{1,9},{5... | collective-permute-start | bytes 196616 | tf_op jit(solution)/shard_map/ppermute | solution.py:319
  197.1 8.7 %collective-permute-start.43 = (bf16[8,4096]{1,0:T(8,128)(2,1)S(1)}, bf16[8,4096]{1,0:T(8,128)(2,1)S(1)}, u32[]{:S(2)}, u32[]{:S(2)}) collective-permute-start(bf16[8,4096]{1,0:T(8,128)(2,1)S(1)} %get-tuple-element.131), channel_id=1, source_target_pairs={{0,16},{4,20},{8,24},{12,28},{16,0},{20,4},{24,8},{28,12},{1,17},{... | collective-permute-start | bytes 196616 | tf_op jit(solution)/shard_map/ppermute | solution.py:319
  212.1 10.1 %collective-permute-start.51 = (bf16[256,2048]{1,0:T(8,128)(2,1)S(1)}, bf16[256,2048]{1,0:T(8,128)(2,1)S(1)}, u32[]{:S(2)}, u32[]{:S(2)}) collective-permute-start(bf16[256,2048]{1,0:T(8,128)(2,1)S(1)} %get-tuple-element.110), channel_id=1, source_target_pairs={{0,2},{2,0},{1,3},{3,1},{4,6},{6,4},{5,7},{7,5},{8,10},{10,8},{9,1... | collective-permute-start | bytes 3145736 | tf_op jit(solution)/shard_map/ppermute | solution.py:29
  212.1 9.2 %collective-permute-start.46 = (bf16[128,2048]{1,0:T(8,128)(2,1)S(1)}, bf16[128,2048]{1,0:T(8,128)(2,1)S(1)}, u32[]{:S(2)}, u32[]{:S(2)}) collective-permute-start(bf16[128,2048]{1,0:T(8,128)(2,1)S(1)} %slice.347), channel_id=1, source_target_pairs={{0,1},{1,0},{2,6},{3,7},{4,5},{5,4},{6,2},{7,3},{8,9},{9,8},{10,14... | collective-permute-start | bytes 1572872 | tf_op jit(solution)/shard_map/ppermute | solution.py:330
  221.5 9.2 %collective-permute-start.47 = (bf16[64,2048]{1,0:T(8,128)(2,1)S(1)}, bf16[64,2048]{1,0:T(8,128)(2,1)S(1)}, u32[]{:S(2)}, u32[]{:S(2)}) collective-permute-start(bf16[64,2048]{1,0:T(8,128)(2,1)S(1)} %slice.350), channel_id=1, source_target_pairs={{0,4},{1,5},{2,3},{3,2},{4,0},{5,1},{6,7},{7,6},{8,12},{9,13},{10,... | collective-permute-start | bytes 786440 | tf_op jit(solution)/shard_map/ppermute | solution.py:330
  222.6 9.6 %collective-permute-start.52 = (bf16[128,2048]{1,0:T(8,128)(2,1)S(1)}, bf16[128,2048]{1,0:T(8,128)(2,1)S(1)}, u32[]{:S(2)}, u32[]{:S(2)}) collective-permute-start(bf16[128,2048]{1,0:T(8,128)(2,1)S(1)} %slice.346), channel_id=1, source_target_pairs={{0,1},{1,0},{2,6},{3,7},{4,5},{5,4},{6,2},{7,3},{8,9},{9,8},{10,14... | collective-permute-start | bytes 1572872 | tf_op jit(solution)/shard_map/ppermute | solution.py:330
  233.6 8.5 %collective-permute-start.50 = (bf16[16,2048]{1,0:T(8,128)(2,1)S(1)}, bf16[16,2048]{1,0:T(8,128)(2,1)S(1)}, u32[]{:S(2)}, u32[]{:S(2)}) collective-permute-start(bf16[16,2048]{1,0:T(8,128)(2,1)S(1)} %get-tuple-element.122), channel_id=1, source_target_pairs={{0,8},{4,12},{8,16},{12,20},{16,24},{20,28},{24,0},{28,4},{1,9},{5... | collective-permute-start | bytes 196616 | tf_op jit(solution)/shard_map/ppermute | solution.py:319
  235.2 7.9 %collective-permute-start.49 = (bf16[16,2048]{1,0:T(8,128)(2,1)S(1)}, bf16[16,2048]{1,0:T(8,128)(2,1)S(1)}, u32[]{:S(2)}, u32[]{:S(2)}) collective-permute-start(bf16[16,2048]{1,0:T(8,128)(2,1)S(1)} %get-tuple-element.123), channel_id=1, source_target_pairs={{0,16},{4,20},{8,24},{12,28},{16,0},{20,4},{24,8},{28,12},{1,17},{... | collective-permute-start | bytes 196616 | tf_op jit(solution)/shard_map/ppermute | solution.py:319
  238.9 6.8 %collective-permute-start.56 = (bf16[16,2048]{1,0:T(8,128)(2,1)S(1)}, bf16[16,2048]{1,0:T(8,128)(2,1)S(1)}, u32[]{:S(2)}, u32[]{:S(2)}) collective-permute-start(bf16[16,2048]{1,0:T(8,128)(2,1)S(1)} %get-tuple-element.126), channel_id=1, source_target_pairs={{0,8},{4,12},{8,16},{12,20},{16,24},{20,28},{24,0},{28,4},{1,9},{5... | collective-permute-start | bytes 196616 | tf_op jit(solution)/shard_map/ppermute | solution.py:319
  240.5 7.9 %collective-permute-start.55 = (bf16[16,2048]{1,0:T(8,128)(2,1)S(1)}, bf16[16,2048]{1,0:T(8,128)(2,1)S(1)}, u32[]{:S(2)}, u32[]{:S(2)}) collective-permute-start(bf16[16,2048]{1,0:T(8,128)(2,1)S(1)} %get-tuple-element.127), channel_id=1, source_target_pairs={{0,16},{4,20},{8,24},{12,28},{16,0},{20,4},{24,8},{28,12},{1,17},{... | collective-permute-start | bytes 196616 | tf_op jit(solution)/shard_map/ppermute | solution.py:319
  (38 other events, 273.4 us)

commit v2 on v1

--- a/solution.py
+++ b/solution.py
@@ -123,10 +123,9 @@
     )(place, *pieces, w, bias, neg, x)
 
 
-def out_kernel(groups, line, parts, at_ref, y_ref, sum_ref, enter_ref, bc_ref, neg_ref, x_ref, z_ref,
+def out_kernel(groups, line, first, at_ref, y_ref, sum_ref, enter_ref, bc_ref, neg_ref, x_ref, z_ref,
                skip_ref, w_hbm, *refs):
-    kept_refs, sent_refs = refs[:parts], refs[parts : 2 * parts]
-    full_ref, wide_ref, gated_ref, order_ref, w_ref, sems = refs[2 * parts :]
+    kept_ref, sent_ref, blocks_ref, full_ref, wide_ref, gated_ref, order_ref, w_ref, sems = refs
     length = x_ref.shape[0]
     tiles, _, tile = w_ref.shape
 
@@ -164,30 +163,43 @@
         for r in range(2):
             source = pl.multiple_of((2 * ((place + k) % line) + (half ^ r)) * piece, piece)
             order_ref[pl.ds(r * count + k * piece, piece), :] = gated_ref[pl.ds(source, piece), :]
-    for j in range(parts):
-
-        def step(i, carry):
-            at = j * (tiles // parts) + i
-            fetch(at).wait()
-            cols = pl.ds(pl.multiple_of(i * tile, tile), tile)
-            out = jnp.dot(order_ref[...], w_ref[at], preferred_element_type=F32).astype(BF16)
-            kept_refs[j][:, cols] = out[:count]
-            sent_refs[j][:, cols] = out[count:]
-            return carry
-
-        lax.fori_loop(0, tiles // parts, step, 0)
-
-
-def run_out(at, line, parts, y, total, enter, bc, neg, x, z, skip, w):
+    def project(j):
+        fetch(j).wait()
+        return jnp.dot(order_ref[...], w_ref[j], preferred_element_type=F32).astype(BF16)
+
+    def step(j, carry):
+        cols = pl.ds(pl.multiple_of(j * tile, tile), tile)
+        out = project(j)
+        kept_ref[:, cols] = out[:count]
+        sent_ref[:, cols] = out[count:]
+        return carry
+
+    def block_step(j, carry):
+        cols = pl.ds(pl.multiple_of((j - first) * tile, tile), tile)
+        out = project(j)
+        for k in range(line):
+            for r in range(2):
+                start = r * count + k * piece
+                blocks_ref[k, pl.ds(r * piece, piece), cols] = out[start : start + piece]
+        return carry
+
+    lax.fori_loop(0, first, step, 0)
+    lax.fori_loop(first, tiles, block_step, 0)
+
+
+def run_out(at, line, y, total, enter, bc, neg, x, z, skip, w):
     length, channels = x.shape
     wide = w.shape[1]
-    tile = min(256, wide // parts)
+    tile = min(512, wide)
+    first = (wide // tile * 5 + 4) // 8
     vmem = pl.BlockSpec(memory_space=pltpu.VMEM)
+    part = jax.ShapeDtypeStruct((length // 2, first * tile), BF16)
+    blocks = jax.ShapeDtypeStruct((line, length // line, wide - first * tile), BF16)
     return pl.pallas_call(
-        functools.partial(out_kernel, channels // LANES, line, parts),
-        out_shape=(jax.ShapeDtypeStruct((length // 2, wide // parts), BF16),) * (2 * parts),
+        functools.partial(out_kernel, channels // LANES, line, first),
+        out_shape=(part, part, blocks),
         in_specs=[pl.BlockSpec(memory_space=pltpu.SMEM)] + [vmem] * 8 + [pl.BlockSpec(memory_space=pl.ANY)],
-        out_specs=(vmem,) * (2 * parts),
+        out_specs=(vmem,) * 3,
         scratch_shapes=[
             pltpu.VMEM((length * SUB, LANES), F32),
             pltpu.VMEM((NSTATE * length, LANES), F32),
@@ -228,8 +240,8 @@
 
     def step(j, carry):
         fetch(j, 0).wait()
+        fetch(j, 1).wait()
         gate = jnp.dot(rows_ref[...], gate_ref[j], preferred_element_type=F32)
-        fetch(j, 1).wait()
         up = jnp.dot(rows_ref[...], up_ref[j], preferred_element_type=F32)
         cols = pl.ds(pl.multiple_of(j * tile, tile), tile)
         out_ref[:, cols] = (gate / (1.0 + jnp.exp(-gate)) * up).astype(BF16)
@@ -292,7 +304,7 @@
 
 def down(pieces, sizes, w_down, first, width):
     hidden, rows = w_down.shape[0], pieces[0].shape[0]
-    tile = min(256, width)
+    tile = min(512, width)
     vmem = pl.BlockSpec(memory_space=pltpu.VMEM)
     return pl.pallas_call(
         functools.partial(down_kernel, len(pieces), first),
@@ -404,16 +416,15 @@
     early_far = cross(early_go, 0)
     late_second = gate_up(after(late_rows, early_go), w_gate, w_up, hidden // 2, hidden // 2)
     early_result = add_up(after(early_kept, late_second), early_far).astype(BF16)
-    early_back = send_home(early_result, line)
     late_hidden = [late_first, late_second]
     out_left = down(after(late_hidden, early_result), sizes, w_down, 0, half)
     left = home_first(out_left)
     left_far = cross(left[1], 1)
-    late_hidden, early_back = lax.optimization_barrier((late_hidden, early_back))
-    out_right = down(after(late_hidden, left[1]), sizes, w_down, half, half)
+    out_right = down(after(late_hidden, early_result, left[1]), sizes, w_down, half, half)
     left = home_second(after(left[0], out_right), left_far)
     left_far = cross(left[1], 0)
     right = home_first(out_right)
+    early_back = send_home(after(early_result, right[1]), line)
     right_far = cross(right[1], 1)
     right = home_second(after(right[0], left[1]), right_far)
     right_far = cross(right[1], 0)
@@ -478,18 +489,17 @@
     for step in range(contexts - 2):
         decay = jnp.exp(total[-SUB:][None] * neg)
         enter = from_behind(end + decay * enter, "context", 1)
-    parts = 4
-    part = width // parts
-    cut = run_out(
-        where, line, parts, y, total, enter, bc, neg, mixed_in, z_gate[0, 0], skip_gain[None, :], out_w
+    kept, sent, blocks = run_out(
+        where, line, y, total, enter, bc, neg, mixed_in, z_gate[0, 0], skip_gain[None, :], out_w
     )
-    kept, sent = cut[:parts], cut[parts:]
-    sums, got = [], swap_pair(sent[0])
-    for k in range(parts):
-        both = add_up(kept[k], got).astype(BF16).reshape(line, row_count, part)
-        if k + 1 < parts:
-            got = swap_pair(after(sent[k + 1], got))
-        sums.append(add_up(both[0], *[along_line(both[s], s) for s in range(1, line)]))
+    got = swap_pair(sent)
+    over_z = add_up(blocks[0], *[along_line(blocks[s], s) for s in range(1, line)])
+    both = add_up(kept, got).astype(BF16).reshape(line, row_count, -1)
+    other = swap_pair(over_z[row_count:].astype(BF16))
+    sums = [
+        add_up(both[0], *[along_line(both[s], s) for s in range(1, line)]),
+        add_up(over_z[:row_count], other),
+    ]
     mixer_out = jnp.concatenate(sums, axis=1)
 
     stream_f = (residual[0, 0].astype(F32) + mixer_out).astype(BF16).astype(F32)

time: 250 us -> 224 us (0.90)
  Pallas kernels: 86.5 us -> 64.7 us
  starting transfers between devices: 72.9 us -> 60.8 us
  waiting for transfers between devices: 77.1 us -> 85.6 us
    pallas_call x4, Pallas kernels: 50 us -> 31.9 us  [gate_up(): pl.pallas_call(functools.partial(gate_up_kernel, len(pieces), first), out...]
    ppermute x33 -> x27, waiting for transfers between devices: 31.5 us -> 48.4 us  [along_line(): lax.ppermute(block, 'expert', [(e, (e + 2 * distance) % size) for e in ra...]
    ppermute x5 -> x3, waiting for transfers between devices: 12.8 us -> 2.42 us  [swap_pair(): return lax.ppermute(block, 'expert', [(i, i ^ 1) for i in range(size)])]
    ppermute x33 -> x27, starting transfers between devices: 46.5 us -> 36.6 us  [along_line(): lax.ppermute(block, 'expert', [(e, (e + 2 * distance) % size) for e in ra...]
    ppermute x7, waiting for transfers between devices: 2.14 us -> 5.82 us  [shift(): lax.ppermute(block, axis, [(i, (i + distance) % size) for i in range(size)])]
    ppermute x5 -> x3, starting transfers between devices: 7.92 us -> 4.83 us  [swap_pair(): return lax.ppermute(block, 'expert', [(i, i ^ 1) for i in range(size)])]
  transfers between devices with their start and end apart: 57 -> 49, of which waited for: 31 -> 29; matrix products, arithmetic and copies ran while one was open for 2% -> 2% of each run, Pallas kernels for 23% -> 19%
where the time goes in v2:
time: 224 us
  waiting for transfers between devices  85.6 us (38%)
  Pallas kernels  64.7 us (29%)
  starting transfers between devices  60.8 us (27%)
  other arithmetic  6.71 us (3%)
  local copies, waits for them, and re-layouts  3.01 us (1%)
    ppermute x27, waiting for transfers between devices, along_line(): lax.ppermute(block, 'expert', [(e, (e + 2 * distance) % size) for e in ra...  48.4 us
    ppermute x27, starting transfers between devices, along_line(): lax.ppermute(block, 'expert', [(e, (e + 2 * distance) % size) for e in ra...  36.6 us
    pallas_call x4, Pallas kernels, gate_up(): pl.pallas_call(functools.partial(gate_up_kernel, len(pieces), first), out...  31.9 us
    ppermute x10, waiting for transfers between devices, cross(): return lax.ppermute(block, ('expert', 'context', 'dp'), route)  28.1 us
    pallas_call x3, Pallas kernels, down(): pl.pallas_call(functools.partial(down_kernel, len(pieces), first), out_sh...  16.8 us
    ppermute x10, starting transfers between devices, cross(): return lax.ppermute(block, ('expert', 'context', 'dp'), route)  15 us
    pallas_call x1, Pallas kernels, run_out(): pl.pallas_call(functools.partial(out_kernel, channels // LANES, line, fir...  9.19 us
    pallas_call x1, Pallas kernels, run_scan(): pl.pallas_call(functools.partial(scan_kernel, channels // LANES, len(piec...  6.9 us
  transfers between devices with their start and end apart: 49, of which 29 were waited for; matrix products, arithmetic and copies ran while one was open for 2% of the time, Pallas kernels for 19%

profile of v2, /device:TPU:0, one launch (start us, length us, event | category | flops | bytes accessed | tf_op | source)
XLA Modules:
  0.0 223.9 jit_solution(17315074759017093844)
XLA Ops:
  0.8 2.3 %collective-permute-start = (bf16[3,1024]{1,0:T(4,128)(2,1)S(1)}, bf16[3,1024]{1,0:T(4,128)(2,1)S(1)}, u32[]{:S(2)}, u32[]{:S(2)}) collective-permute-start(bf16[3,1024]{1,0:T(4,128)(2,1)S(1)} %slice_bitcast_fusion.3), channel_id=1, source_target_pairs={{0,2},{1,3},{4,6},{5,7},{8,10},{9,11},{12,14},{13,15},{16,18},{17,... | collective-permute-start | bytes 18440 | tf_op jit(solution)/shard_map/ppermute | solution.py:24
  9.1 2.5 %collective-permute-start.1 = (bf16[64,288]{1,0:T(8,128)(2,1)S(1)}, bf16[64,288]{1,0:T(8,128)(2,1)S(1)}, u32[]{:S(2)}, u32[]{:S(2)}) collective-permute-start(bf16[64,288]{1,0:T(8,128)(2,1)S(1)} %get-tuple-element.124), channel_id=1, source_target_pairs={{0,8},{4,12},{8,16},{12,20},{16,24},{20,28},{24,0},{28,4},{1,9},{5... | collective-permute-start | bytes 110600 | tf_op jit(solution)/shard_map/ppermute | solution.py:331
  16.1 2.6 %collective-permute-done.2 = bf16[64,288]{1,0:T(8,128)(2,1)S(1)} collective-permute-done((bf16[64,288]{1,0:T(8,128)(2,1)S(1)}, bf16[64,288]{1,0:T(8,128)(2,1)S(1)}, u32[]{:S(2)}, u32[]{:S(2)}) %collective-permute-start.2) | collective-permute-done | bytes 36896 | tf_op jit(solution)/shard_map/ppermute | solution.py:331
  20.5 2.4 %collective-permute-done.4 = bf16[64,288]{1,0:T(8,128)(2,1)S(1)} collective-permute-done((bf16[64,288]{1,0:T(8,128)(2,1)S(1)}, bf16[64,288]{1,0:T(8,128)(2,1)S(1)}, u32[]{:S(2)}, u32[]{:S(2)}) %collective-permute-start.4) | collective-permute-done | bytes 36896 | tf_op jit(solution)/shard_map/ppermute | solution.py:34
  22.9 2.3 %collective-permute-start.7 = (bf16[64,288]{1,0:T(8,128)(2,1)S(1)}, bf16[64,288]{1,0:T(8,128)(2,1)S(1)}, u32[]{:S(2)}, u32[]{:S(2)}) collective-permute-start(bf16[64,288]{1,0:T(8,128)(2,1)S(1)} %add_convert_fusion.2.refs_0_), channel_id=1, source_target_pairs={{0,24},{4,28},{8,0},{12,4},{16,8},{20,12},{24,16},{28,20},{1,25},{... | collective-permute-start | bytes 110600 | tf_op jit(solution)/shard_map/ppermute | solution.py:331
  31.1 6.9 %state_scan.1 = (f32[2048,128]{1,0:T(8,128)S(1)}, f32[2048,128]{1,0:T(8,128)S(1)}, f32[16,8,128]{2,1,0:T(8,128)S(1)}, bf16[256,32]{1,0:T(8,128)(2,1)S(1)}) custom-call(s32[2]{0:T(128)S(1)} %pad_add_fusion.place_ref.at_ref, bf16[64,288]{1,0:T(8,128)(2,1)S(1)} %add_convert_fusion.2.refs_0_, bf16[64,288]{1,0:T(8,128)(2,1)S(1)} %collective-permute-done.5.refs_1_, ...), custom_call_target="tpu_custom_call" | custom-call | flops 200000000 | bytes 4194304 | tf_op jit(solution)/shard_map/state_scan/pallas_call | solution.py:104
  40.2 9.2 %readout_project.1 = (bf16[128,2560]{1,0:T(8,128)(2,1)S(1)}, bf16[128,2560]{1,0:T(8,128)(2,1)S(1)}, bf16[4,64,1536]{2,1,0:T(8,128)(2,1)S(1)}) custom-call(s32[2]{0:T(128)S(1)} %pad_add_fusion.place_ref.at_ref, f32[2048,128]{1,0:T(8,128)S(1)} %get-tuple-element.49.y_ref, f32[2048,128]{1,0:T(8,128)S(1)} %get-tuple-element.50.sum_ref, ...), custom_call_target="tpu_custom_call" | custom-call | flops 2147483648 | bytes 16777216 | tf_op jit(solution)/shard_map/readout_project/pallas_call | solution.py:198
  49.5 3.8 %collective-permute-start.15 = (bf16[64,1536]{1,0:T(8,128)(2,1)S(1)}, bf16[64,1536]{1,0:T(8,128)(2,1)S(1)}, u32[]{:S(2)}, u32[]{:S(2)}) collective-permute-start(bf16[64,1536]{1,0:T(8,128)(2,1)S(1)} %get-tuple-element.98), channel_id=1, source_target_pairs={{0,24},{4,28},{8,0},{12,4},{16,8},{20,12},{24,16},{28,20},{1,25},{... | collective-permute-start | bytes 589832 | tf_op jit(solution)/shard_map/ppermute | solution.py:331
  55.1 4.0 %collective-permute-done.13 = bf16[64,1536]{1,0:T(8,128)(2,1)S(1)} collective-permute-done((bf16[64,1536]{1,0:T(8,128)(2,1)S(1)}, bf16[64,1536]{1,0:T(8,128)(2,1)S(1)}, u32[]{:S(2)}, u32[]{:S(2)}) %collective-permute-start.13) | collective-permute-done | bytes 196640 | tf_op jit(solution)/shard_map/ppermute | solution.py:331
  61.1 9.1 %collective-permute-done.14 = bf16[64,1536]{1,0:T(8,128)(2,1)S(1)} collective-permute-done((bf16[64,1536]{1,0:T(8,128)(2,1)S(1)}, bf16[64,1536]{1,0:T(8,128)(2,1)S(1)}, u32[]{:S(2)}, u32[]{:S(2)}) %collective-permute-start.14) | collective-permute-done | bytes 196640 | tf_op jit(solution)/shard_map/ppermute | solution.py:331
  72.2 3.8 %collective-permute-start.12 = (bf16[32,2560]{1,0:T(8,128)(2,1)S(1)}, bf16[32,2560]{1,0:T(8,128)(2,1)S(1)}, u32[]{:S(2)}, u32[]{:S(2)}) collective-permute-start(bf16[32,2560]{1,0:T(8,128)(2,1)S(1)} %get-tuple-element.101), channel_id=1, source_target_pairs={{0,24},{4,28},{8,0},{12,4},{16,8},{20,12},{24,16},{28,20},{1,25},{... | collective-permute-start | bytes 491528 | tf_op jit(solution)/shard_map/ppermute | solution.py:331
  76.0 5.1 %collective-permute-done.10 = bf16[32,2560]{1,0:T(8,128)(2,1)S(1)} collective-permute-done((bf16[32,2560]{1,0:T(8,128)(2,1)S(1)}, bf16[32,2560]{1,0:T(8,128)(2,1)S(1)}, u32[]{:S(2)}, u32[]{:S(2)}) %collective-permute-start.10) | collective-permute-done | bytes 163872 | tf_op jit(solution)/shard_map/ppermute | solution.py:331
  81.6 6.2 %collective-permute-done.11 = bf16[32,2560]{1,0:T(8,128)(2,1)S(1)} collective-permute-done((bf16[32,2560]{1,0:T(8,128)(2,1)S(1)}, bf16[32,2560]{1,0:T(8,128)(2,1)S(1)}, u32[]{:S(2)}, u32[]{:S(2)}) %collective-permute-start.11) | collective-permute-done | bytes 163872 | tf_op jit(solution)/shard_map/ppermute | solution.py:331
  88.9 3.9 %collective-permute-start.19 = (bf16[8,4096]{1,0:T(8,128)(2,1)S(1)}, bf16[8,4096]{1,0:T(8,128)(2,1)S(1)}, u32[]{:S(2)}, u32[]{:S(2)}) collective-permute-start(bf16[8,4096]{1,0:T(8,128)(2,1)S(1)} %get-tuple-element.121), channel_id=1, source_target_pairs={{0,24},{4,28},{8,0},{12,4},{16,8},{20,12},{24,16},{28,20},{1,25},{... | collective-permute-start | bytes 196616 | tf_op jit(solution)/shard_map/ppermute | solution.py:331
  97.8 3.1 %collective-permute-done.18 = bf16[8,4096]{1,0:T(8,128)(2,1)S(1)} collective-permute-done((bf16[8,4096]{1,0:T(8,128)(2,1)S(1)}, bf16[8,4096]{1,0:T(8,128)(2,1)S(1)}, u32[]{:S(2)}, u32[]{:S(2)}) %collective-permute-start.18) | collective-permute-done | bytes 65568 | tf_op jit(solution)/shard_map/ppermute | solution.py:331
  102.9 4.4 %collective-permute-done.20 = bf16[32,4096]{1,0:T(8,128)(2,1)S(1)} collective-permute-done((bf16[32,4096]{1,0:T(8,128)(2,1)S(1)}, bf16[32,4096]{1,0:T(8,128)(2,1)S(1)}, u32[]{:S(2)}, u32[]{:S(2)}) %collective-permute-start.20) | collective-permute-done | bytes 262176 | tf_op jit(solution)/shard_map/ppermute | solution.py:342
  109.0 7.7 %collective-permute-done.21.refs_1_ = bf16[64,4096]{1,0:T(8,128)(2,1)S(1)} collective-permute-done((bf16[64,4096]{1,0:T(8,128)(2,1)S(1)}, bf16[64,4096]{1,0:T(8,128)(2,1)S(1)}, u32[]{:S(2)}, u32[]{:S(2)}) %collective-permute-start.21) | collective-permute-done | bytes 524320 | tf_op jit(solution)/shard_map/ppermute | solution.py:342
  118.7 7.6 %gate_up.4.refs_0_ = bf16[256,1024]{1,0:T(8,128)(2,1)S(1)} custom-call(bf16[64,4096]{1,0:T(8,128)(2,1)S(1)} %constant_dynamic-update-slice_fusion.refs_0_, bf16[64,4096]{1,0:T(8,128)(2,1)S(1)} %collective-permute-done.21.refs_1_, bf16[64,4096]{1,0:T(8,128)(2,1)S(1)} %collective-permute-done.22.refs_2_, bf16[64,4096]{1,0:T(8,128)(2,1)S(1)} %collective-permute-done.23.refs_3_, ...), custom_call_target="tpu_custom_call" | custom-call | flops 4294967296 | bytes 18874368 | tf_op jit(solution)/shard_map/gate_up/pallas_call | solution.py:259
  128.0 5.0 %gate_up.5.refs_1_ = bf16[256,512]{1,0:T(8,128)(2,1)S(1)} custom-call(bf16[64,4096]{1,0:T(8,128)(2,1)S(1)} %constant_dynamic-update-slice_fusion.refs_0_, bf16[64,4096]{1,0:T(8,128)(2,1)S(1)} %collective-permute-done.21.refs_1_, bf16[64,4096]{1,0:T(8,128)(2,1)S(1)} %collective-permute-done.22.refs_2_, bf16[64,4096]{1,0:T(8,128)(2,1)S(1)} %collective-permute-done.23.refs_3_, ...), custom_call_target="tpu_custom_call" | custom-call | flops 2147483648 | bytes 10485760 | tf_op jit(solution)/shard_map/gate_up/pallas_call | solution.py:259
  133.0 6.1 %down.3 = (bf16[128,4096]{1,0:T(8,128)(2,1)S(1)}, bf16[128,4096]{1,0:T(8,128)(2,1)S(1)}) custom-call(bf16[256,1024]{1,0:T(8,128)(2,1)S(1)} %gate_up.4.refs_0_, bf16[256,512]{1,0:T(8,128)(2,1)S(1)} %gate_up.5.refs_1_, bf16[1536,4096]{1,0:T(8,128)(2,1)} %bitcast.65), custom_call_target="tpu_custom_call" | custom-call | flops 3221225472 | bytes 15466496 | tf_op jit(solution)/shard_map/down/pallas_call | solution.py:309
  146.9 9.7 %gate_up.6.refs_0_ = bf16[512,768]{1,0:T(8,128)(2,1)S(1)} custom-call(bf16[128,4096]{1,0:T(8,128)(2,1)S(1)} %constant_dynamic-update-slice_fusion.9.refs_0_, bf16[128,4096]{1,0:T(8,128)(2,1)S(1)} %collective-permute-done.28.refs_1_, bf16[128,4096]{1,0:T(8,128)(2,1)S(1)} %collective-permute-done.30.refs_2_, ...), custom_call_target="tpu_custom_call" | custom-call | flops 6442450944 | bytes 16777216 | tf_op jit(solution)/shard_map/gate_up/pallas_call | solution.py:259
  158.6 9.7 %gate_up.7.refs_1_ = bf16[512,768]{1,0:T(8,128)(2,1)S(1)} custom-call(bf16[128,4096]{1,0:T(8,128)(2,1)S(1)} %constant_dynamic-update-slice_fusion.9.refs_0_, bf16[128,4096]{1,0:T(8,128)(2,1)S(1)} %collective-permute-done.28.refs_1_, bf16[128,4096]{1,0:T(8,128)(2,1)S(1)} %collective-permute-done.30.refs_2_, ...), custom_call_target="tpu_custom_call" | custom-call | flops 6442450944 | bytes 16777216 | tf_op jit(solution)/shard_map/gate_up/pallas_call | solution.py:259
  168.4 5.4 %down.4 = (bf16[256,2048]{1,0:T(8,128)(2,1)S(1)}, bf16[256,2048]{1,0:T(8,128)(2,1)S(1)}) custom-call(bf16[512,768]{1,0:T(8,128)(2,1)S(1)} %gate_up.6.refs_0_, bf16[512,768]{1,0:T(8,128)(2,1)S(1)} %gate_up.7.refs_1_, bf16[1536,4096]{1,0:T(8,128)(2,1)} %bitcast.66), custom_call_target="tpu_custom_call" | custom-call | flops 3221225472 | bytes 9961472 | tf_op jit(solution)/shard_map/down/pallas_call | solution.py:309
  173.8 2.6 %collective-permute-done.34 = bf16[256,2048]{1,0:T(8,128)(2,1)S(1)} collective-permute-done((bf16[256,2048]{1,0:T(8,128)(2,1)S(1)}, bf16[256,2048]{1,0:T(8,128)(2,1)S(1)}, u32[]{:S(2)}, u32[]{:S(2)}) %collective-permute-start.34) | collective-permute-done | bytes 1048608 | tf_op jit(solution)/shard_map/ppermute | solution.py:29
  178.6 5.4 %down.5 = (bf16[256,2048]{1,0:T(8,128)(2,1)S(1)}, bf16[256,2048]{1,0:T(8,128)(2,1)S(1)}) custom-call(bf16[512,768]{1,0:T(8,128)(2,1)S(1)} %gate_up.6.refs_0_, bf16[512,768]{1,0:T(8,128)(2,1)S(1)} %gate_up.7.refs_1_, bf16[1536,4096]{1,0:T(8,128)(2,1)} %bitcast.67), custom_call_target="tpu_custom_call" | custom-call | flops 3221225472 | bytes 9961472 | tf_op jit(solution)/shard_map/down/pallas_call | solution.py:309
  187.5 5.2 %collective-permute-done.40 = bf16[64,2048]{1,0:T(8,128)(2,1)S(1)} collective-permute-done((bf16[64,2048]{1,0:T(8,128)(2,1)S(1)}, bf16[64,2048]{1,0:T(8,128)(2,1)S(1)}, u32[]{:S(2)}, u32[]{:S(2)}) %collective-permute-start.40) | collective-permute-done | bytes 262176 | tf_op jit(solution)/shard_map/ppermute | solution.py:342
  194.8 2.6 %collective-permute-start.36 = (bf16[8,4096]{1,0:T(8,128)(2,1)S(1)}, bf16[8,4096]{1,0:T(8,128)(2,1)S(1)}, u32[]{:S(2)}, u32[]{:S(2)}) collective-permute-start(bf16[8,4096]{1,0:T(8,128)(2,1)S(1)} %get-tuple-element.117), channel_id=1, source_target_pairs={{0,24},{4,28},{8,0},{12,4},{16,8},{20,12},{24,16},{28,20},{1,25},{... | collective-permute-start | bytes 196616 | tf_op jit(solution)/shard_map/ppermute | solution.py:331
  198.1 3.2 %collective-permute-start.41 = (bf16[16,2048]{1,0:T(8,128)(2,1)S(1)}, bf16[16,2048]{1,0:T(8,128)(2,1)S(1)}, u32[]{:S(2)}, u32[]{:S(2)}) collective-permute-start(bf16[16,2048]{1,0:T(8,128)(2,1)S(1)} %get-tuple-element.110), channel_id=1, source_target_pairs={{0,24},{4,28},{8,0},{12,4},{16,8},{20,12},{24,16},{28,20},{1,25},{... | collective-permute-start | bytes 196616 | tf_op jit(solution)/shard_map/ppermute | solution.py:331
  202.5 2.3 %collective-permute-start.37 = (bf16[8,4096]{1,0:T(8,128)(2,1)S(1)}, bf16[8,4096]{1,0:T(8,128)(2,1)S(1)}, u32[]{:S(2)}, u32[]{:S(2)}) collective-permute-start(bf16[8,4096]{1,0:T(8,128)(2,1)S(1)} %get-tuple-element.116), channel_id=1, source_target_pairs={{0,16},{4,20},{8,24},{12,28},{16,0},{20,4},{24,8},{28,12},{1,17},{... | collective-permute-start | bytes 196616 | tf_op jit(solution)/shard_map/ppermute | solution.py:331
  205.0 4.2 %collective-permute-done.37 = bf16[8,4096]{1,0:T(8,128)(2,1)S(1)} collective-permute-done((bf16[8,4096]{1,0:T(8,128)(2,1)S(1)}, bf16[8,4096]{1,0:T(8,128)(2,1)S(1)}, u32[]{:S(2)}, u32[]{:S(2)}) %collective-permute-start.37) | collective-permute-done | bytes 65568 | tf_op jit(solution)/shard_map/ppermute | solution.py:331
  209.5 6.1 %collective-permute-done.45 = bf16[64,2048]{1,0:T(8,128)(2,1)S(1)} collective-permute-done((bf16[64,2048]{1,0:T(8,128)(2,1)S(1)}, bf16[64,2048]{1,0:T(8,128)(2,1)S(1)}, u32[]{:S(2)}, u32[]{:S(2)}) %collective-permute-start.45) | collective-permute-done | bytes 262176 | tf_op jit(solution)/shard_map/ppermute | solution.py:342
  215.8 2.5 %collective-permute-start.47 = (bf16[16,2048]{1,0:T(8,128)(2,1)S(1)}, bf16[16,2048]{1,0:T(8,128)(2,1)S(1)}, u32[]{:S(2)}, u32[]{:S(2)}) collective-permute-start(bf16[16,2048]{1,0:T(8,128)(2,1)S(1)} %get-tuple-element.113), channel_id=1, source_target_pairs={{0,16},{4,20},{8,24},{12,28},{16,0},{20,4},{24,8},{28,12},{1,17},{... | collective-permute-start | bytes 196616 | tf_op jit(solution)/shard_map/ppermute | solution.py:331
  (171 shorter events, 66.2 us)
Async XLA Ops:
  9.1 6.9 %collective-permute-start.1 = (bf16[64,288]{1,0:T(8,128)(2,1)S(1)}, bf16[64,288]{1,0:T(8,128)(2,1)S(1)}, u32[]{:S(2)}, u32[]{:S(2)}) collective-permute-start(bf16[64,288]{1,0:T(8,128)(2,1)S(1)} %get-tuple-element.124), channel_id=1, source_target_pairs={{0,8},{4,12},{8,16},{12,20},{16,24},{20,28},{24,0},{28,4},{1,9},{5... | collective-permute-start | bytes 110600 | tf_op jit(solution)/shard_map/ppermute | solution.py:331
  49.5 9.6 %collective-permute-start.13 = (bf16[64,1536]{1,0:T(8,128)(2,1)S(1)}, bf16[64,1536]{1,0:T(8,128)(2,1)S(1)}, u32[]{:S(2)}, u32[]{:S(2)}) collective-permute-start(bf16[64,1536]{1,0:T(8,128)(2,1)S(1)} %get-tuple-element.97), channel_id=1, source_target_pairs={{0,8},{4,12},{8,16},{12,20},{16,24},{20,28},{24,0},{28,4},{1,9},{5... | collective-permute-start | bytes 589832 | tf_op jit(solution)/shard_map/ppermute | solution.py:331
  49.5 11.5 %collective-permute-start.15 = (bf16[64,1536]{1,0:T(8,128)(2,1)S(1)}, bf16[64,1536]{1,0:T(8,128)(2,1)S(1)}, u32[]{:S(2)}, u32[]{:S(2)}) collective-permute-start(bf16[64,1536]{1,0:T(8,128)(2,1)S(1)} %get-tuple-element.98), channel_id=1, source_target_pairs={{0,24},{4,28},{8,0},{12,4},{16,8},{20,12},{24,16},{28,20},{1,25},{... | collective-permute-start | bytes 589832 | tf_op jit(solution)/shard_map/ppermute | solution.py:331
  53.4 16.8 %collective-permute-start.14 = (bf16[64,1536]{1,0:T(8,128)(2,1)S(1)}, bf16[64,1536]{1,0:T(8,128)(2,1)S(1)}, u32[]{:S(2)}, u32[]{:S(2)}) collective-permute-start(bf16[64,1536]{1,0:T(8,128)(2,1)S(1)} %get-tuple-element.99), channel_id=1, source_target_pairs={{0,16},{4,20},{8,24},{12,28},{16,0},{20,4},{24,8},{28,12},{1,17},{... | collective-permute-start | bytes 589832 | tf_op jit(solution)/shard_map/ppermute | solution.py:331
  53.4 18.5 %collective-permute-start.9 = (bf16[128,2560]{1,0:T(8,128)(2,1)S(1)}, bf16[128,2560]{1,0:T(8,128)(2,1)S(1)}, u32[]{:S(2)}, u32[]{:S(2)}) collective-permute-start(bf16[128,2560]{1,0:T(8,128)(2,1)S(1)} %get-tuple-element.54), channel_id=1, source_target_pairs={{0,4},{4,0},{8,12},{12,8},{16,20},{20,16},{24,28},{28,24},{1,5},{5... | collective-permute-start | bytes 1966088 | tf_op jit(solution)/shard_map/ppermute | solution.py:34
  72.1 9.0 %collective-permute-start.10 = (bf16[32,2560]{1,0:T(8,128)(2,1)S(1)}, bf16[32,2560]{1,0:T(8,128)(2,1)S(1)}, u32[]{:S(2)}, u32[]{:S(2)}) collective-permute-start(bf16[32,2560]{1,0:T(8,128)(2,1)S(1)} %get-tuple-element.100), channel_id=1, source_target_pairs={{0,8},{4,12},{8,16},{12,20},{16,24},{20,28},{24,0},{28,4},{1,9},{5... | collective-permute-start | bytes 491528 | tf_op jit(solution)/shard_map/ppermute | solution.py:331
  72.2 9.4 %collective-permute-start.12 = (bf16[32,2560]{1,0:T(8,128)(2,1)S(1)}, bf16[32,2560]{1,0:T(8,128)(2,1)S(1)}, u32[]{:S(2)}, u32[]{:S(2)}) collective-permute-start(bf16[32,2560]{1,0:T(8,128)(2,1)S(1)} %get-tuple-element.101), channel_id=1, source_target_pairs={{0,24},{4,28},{8,0},{12,4},{16,8},{20,12},{24,16},{28,20},{1,25},{... | collective-permute-start | bytes 491528 | tf_op jit(solution)/shard_map/ppermute | solution.py:331
  76.0 11.8 %collective-permute-start.11 = (bf16[32,2560]{1,0:T(8,128)(2,1)S(1)}, bf16[32,2560]{1,0:T(8,128)(2,1)S(1)}, u32[]{:S(2)}, u32[]{:S(2)}) collective-permute-start(bf16[32,2560]{1,0:T(8,128)(2,1)S(1)} %get-tuple-element.102), channel_id=1, source_target_pairs={{0,16},{4,20},{8,24},{12,28},{16,0},{20,4},{24,8},{28,12},{1,17},{... | collective-permute-start | bytes 491528 | tf_op jit(solution)/shard_map/ppermute | solution.py:331
  88.5 6.2 %collective-permute-start.17 = (bf16[8,4096]{1,0:T(8,128)(2,1)S(1)}, bf16[8,4096]{1,0:T(8,128)(2,1)S(1)}, u32[]{:S(2)}, u32[]{:S(2)}) collective-permute-start(bf16[8,4096]{1,0:T(8,128)(2,1)S(1)} %get-tuple-element.123), channel_id=1, source_target_pairs={{0,8},{4,12},{8,16},{12,20},{16,24},{20,28},{24,0},{28,4},{1,9},{5... | collective-permute-start | bytes 196616 | tf_op jit(solution)/shard_map/ppermute | solution.py:331
  88.9 8.9 %collective-permute-start.19 = (bf16[8,4096]{1,0:T(8,128)(2,1)S(1)}, bf16[8,4096]{1,0:T(8,128)(2,1)S(1)}, u32[]{:S(2)}, u32[]{:S(2)}) collective-permute-start(bf16[8,4096]{1,0:T(8,128)(2,1)S(1)} %get-tuple-element.121), channel_id=1, source_target_pairs={{0,24},{4,28},{8,0},{12,4},{16,8},{20,12},{24,16},{28,20},{1,25},{... | collective-permute-start | bytes 196616 | tf_op jit(solution)/shard_map/ppermute | solution.py:331
  92.8 8.1 %collective-permute-start.18 = (bf16[8,4096]{1,0:T(8,128)(2,1)S(1)}, bf16[8,4096]{1,0:T(8,128)(2,1)S(1)}, u32[]{:S(2)}, u32[]{:S(2)}) collective-permute-start(bf16[8,4096]{1,0:T(8,128)(2,1)S(1)} %get-tuple-element.122), channel_id=1, source_target_pairs={{0,16},{4,20},{8,24},{12,28},{16,0},{20,4},{24,8},{28,12},{1,17},{... | collective-permute-start | bytes 196616 | tf_op jit(solution)/shard_map/ppermute | solution.py:331
  94.7 22.1 %collective-permute-start.26 = (bf16[16,4096]{1,0:T(8,128)(2,1)S(1)}, bf16[16,4096]{1,0:T(8,128)(2,1)S(1)}, u32[]{:S(2)}, u32[]{:S(2)}) collective-permute-start(bf16[16,4096]{1,0:T(8,128)(2,1)S(1)} %get-tuple-element.103), channel_id=1, source_target_pairs={{0,24},{4,28},{8,0},{12,4},{16,8},{20,12},{24,16},{28,20},{1,25},{... | collective-permute-start | bytes 393224 | tf_op jit(solution)/shard_map/ppermute | solution.py:331
  96.6 20.1 %collective-permute-start.25 = (bf16[16,4096]{1,0:T(8,128)(2,1)S(1)}, bf16[16,4096]{1,0:T(8,128)(2,1)S(1)}, u32[]{:S(2)}, u32[]{:S(2)}) collective-permute-start(bf16[16,4096]{1,0:T(8,128)(2,1)S(1)} %get-tuple-element.104), channel_id=1, source_target_pairs={{0,16},{4,20},{8,24},{12,28},{16,0},{20,4},{24,8},{28,12},{1,17},{... | collective-permute-start | bytes 393224 | tf_op jit(solution)/shard_map/ppermute | solution.py:331
  96.6 12.4 %collective-permute-start.24 = (bf16[16,4096]{1,0:T(8,128)(2,1)S(1)}, bf16[16,4096]{1,0:T(8,128)(2,1)S(1)}, u32[]{:S(2)}, u32[]{:S(2)}) collective-permute-start(bf16[16,4096]{1,0:T(8,128)(2,1)S(1)} %get-tuple-element.105), channel_id=1, source_target_pairs={{0,8},{4,12},{8,16},{12,20},{16,24},{20,28},{24,0},{28,4},{1,9},{5... | collective-permute-start | bytes 393224 | tf_op jit(solution)/shard_map/ppermute | solution.py:331
  100.9 6.4 %collective-permute-start.20 = (bf16[32,4096]{1,0:T(8,128)(2,1)S(1)}, bf16[32,4096]{1,0:T(8,128)(2,1)S(1)}, u32[]{:S(2)}, u32[]{:S(2)}) collective-permute-start(bf16[32,4096]{1,0:T(8,128)(2,1)S(1)} %pad_maximum_fusion.6), channel_id=1, source_target_pairs={{0,4},{1,5},{2,3},{3,2},{4,0},{5,1},{6,7},{7,6},{8,12},{9,13},{10,... | collective-permute-start | bytes 786440 | tf_op jit(solution)/shard_map/ppermute | solution.py:342
  107.4 11.3 %collective-permute-start.22 = (bf16[64,4096]{1,0:T(8,128)(2,1)S(1)}, bf16[64,4096]{1,0:T(8,128)(2,1)S(1)}, u32[]{:S(2)}, u32[]{:S(2)}) collective-permute-start(bf16[64,4096]{1,0:T(8,128)(2,1)S(1)} %constant_dynamic-update-slice_fusion.refs_0_), channel_id=1, source_target_pairs={{0,2},{2,0},{1,3},{3,1},{4,6},{6,4},{5,7},{7,5},{8,10},{10,8},{9,1... | collective-permute-start | bytes 1572872 | tf_op jit(solution)/shard_map/ppermute | solution.py:29
  107.5 9.2 %collective-permute-start.21 = (bf16[64,4096]{1,0:T(8,128)(2,1)S(1)}, bf16[64,4096]{1,0:T(8,128)(2,1)S(1)}, u32[]{:S(2)}, u32[]{:S(2)}) collective-permute-start(bf16[64,4096]{1,0:T(8,128)(2,1)S(1)} %constant_dynamic-update-slice_fusion.refs_0_), channel_id=1, source_target_pairs={{0,1},{1,0},{2,6},{3,7},{4,5},{5,4},{6,2},{7,3},{8,9},{9,8},{10,14... | collective-permute-start | bytes 1572872 | tf_op jit(solution)/shard_map/ppermute | solution.py:342
  116.8 9.6 %collective-permute-start.27 = (bf16[64,4096]{1,0:T(8,128)(2,1)S(1)}, bf16[64,4096]{1,0:T(8,128)(2,1)S(1)}, u32[]{:S(2)}, u32[]{:S(2)}) collective-permute-start(bf16[64,4096]{1,0:T(8,128)(2,1)S(1)} %constant_dynamic-update-slice_fusion.5), channel_id=1, source_target_pairs={{0,4},{1,5},{2,3},{3,2},{4,0},{5,1},{6,7},{7,6},{8,12},{9,13},{10,... | collective-permute-start | bytes 1572872 | tf_op jit(solution)/shard_map/ppermute | solution.py:342
  126.4 14.9 %collective-permute-start.28 = (bf16[128,4096]{1,0:T(8,128)(2,1)S(1)}, bf16[128,4096]{1,0:T(8,128)(2,1)S(1)}, u32[]{:S(2)}, u32[]{:S(2)}) collective-permute-start(bf16[128,4096]{1,0:T(8,128)(2,1)S(1)} %constant_dynamic-update-slice_fusion.9.refs_0_), channel_id=1, source_target_pairs={{0,1},{1,0},{2,6},{3,7},{4,5},{5,4},{6,2},{7,3},{8,9},{9,8},{10,14... | collective-permute-start | bytes 3145736 | tf_op jit(solution)/shard_map/ppermute | solution.py:342
  144.3 12.3 %collective-permute-start.32 = (bf16[64,4096]{1,0:T(8,128)(2,1)S(1)}, bf16[64,4096]{1,0:T(8,128)(2,1)S(1)}, u32[]{:S(2)}, u32[]{:S(2)}) collective-permute-start(bf16[64,4096]{1,0:T(8,128)(2,1)S(1)} %slice.303), channel_id=1, source_target_pairs={{0,1},{1,0},{2,6},{3,7},{4,5},{5,4},{6,2},{7,3},{8,9},{9,8},{10,14... | collective-permute-start | bytes 1572872 | tf_op jit(solution)/shard_map/ppermute | solution.py:342
  156.7 11.6 %collective-permute-start.33 = (bf16[32,4096]{1,0:T(8,128)(2,1)S(1)}, bf16[32,4096]{1,0:T(8,128)(2,1)S(1)}, u32[]{:S(2)}, u32[]{:S(2)}) collective-permute-start(bf16[32,4096]{1,0:T(8,128)(2,1)S(1)} %slice.306), channel_id=1, source_target_pairs={{0,4},{1,5},{2,3},{3,2},{4,0},{5,1},{6,7},{7,6},{8,12},{9,13},{10,... | collective-permute-start | bytes 786440 | tf_op jit(solution)/shard_map/ppermute | solution.py:342
  176.9 9.2 %collective-permute-start.39 = (bf16[128,2048]{1,0:T(8,128)(2,1)S(1)}, bf16[128,2048]{1,0:T(8,128)(2,1)S(1)}, u32[]{:S(2)}, u32[]{:S(2)}) collective-permute-start(bf16[128,2048]{1,0:T(8,128)(2,1)S(1)} %slice.302), channel_id=1, source_target_pairs={{0,1},{1,0},{2,6},{3,7},{4,5},{5,4},{6,2},{7,3},{8,9},{9,8},{10,14... | collective-permute-start | bytes 1572872 | tf_op jit(solution)/shard_map/ppermute | solution.py:342
  184.0 8.8 %collective-permute-start.35 = (bf16[256,2048]{1,0:T(8,128)(2,1)S(1)}, bf16[256,2048]{1,0:T(8,128)(2,1)S(1)}, u32[]{:S(2)}, u32[]{:S(2)}) collective-permute-start(bf16[256,2048]{1,0:T(8,128)(2,1)S(1)} %get-tuple-element.89), channel_id=1, source_target_pairs={{0,2},{2,0},{1,3},{3,1},{4,6},{6,4},{5,7},{7,5},{8,10},{10,8},{9,1... | collective-permute-start | bytes 3145736 | tf_op jit(solution)/shard_map/ppermute | solution.py:29
  186.3 6.4 %collective-permute-start.40 = (bf16[64,2048]{1,0:T(8,128)(2,1)S(1)}, bf16[64,2048]{1,0:T(8,128)(2,1)S(1)}, u32[]{:S(2)}, u32[]{:S(2)}) collective-permute-start(bf16[64,2048]{1,0:T(8,128)(2,1)S(1)} %slice.305), channel_id=1, source_target_pairs={{0,4},{1,5},{2,3},{3,2},{4,0},{5,1},{6,7},{7,6},{8,12},{9,13},{10,... | collective-permute-start | bytes 786440 | tf_op jit(solution)/shard_map/ppermute | solution.py:342
  193.2 9.2 %collective-permute-start.44 = (bf16[128,2048]{1,0:T(8,128)(2,1)S(1)}, bf16[128,2048]{1,0:T(8,128)(2,1)S(1)}, u32[]{:S(2)}, u32[]{:S(2)}) collective-permute-start(bf16[128,2048]{1,0:T(8,128)(2,1)S(1)} %slice.301), channel_id=1, source_target_pairs={{0,1},{1,0},{2,6},{3,7},{4,5},{5,4},{6,2},{7,3},{8,9},{9,8},{10,14... | collective-permute-start | bytes 1572872 | tf_op jit(solution)/shard_map/ppermute | solution.py:342
  194.8 6.6 %collective-permute-start.36 = (bf16[8,4096]{1,0:T(8,128)(2,1)S(1)}, bf16[8,4096]{1,0:T(8,128)(2,1)S(1)}, u32[]{:S(2)}, u32[]{:S(2)}) collective-permute-start(bf16[8,4096]{1,0:T(8,128)(2,1)S(1)} %get-tuple-element.117), channel_id=1, source_target_pairs={{0,24},{4,28},{8,0},{12,4},{16,8},{20,12},{24,16},{28,20},{1,25},{... | collective-permute-start | bytes 196616 | tf_op jit(solution)/shard_map/ppermute | solution.py:331
  197.5 18.4 %collective-permute-start.43 = (bf16[16,2048]{1,0:T(8,128)(2,1)S(1)}, bf16[16,2048]{1,0:T(8,128)(2,1)S(1)}, u32[]{:S(2)}, u32[]{:S(2)}) collective-permute-start(bf16[16,2048]{1,0:T(8,128)(2,1)S(1)} %get-tuple-element.108), channel_id=1, source_target_pairs={{0,8},{4,12},{8,16},{12,20},{16,24},{20,28},{24,0},{28,4},{1,9},{5... | collective-permute-start | bytes 196616 | tf_op jit(solution)/shard_map/ppermute | solution.py:331
  197.5 22.1 %collective-permute-start.42 = (bf16[16,2048]{1,0:T(8,128)(2,1)S(1)}, bf16[16,2048]{1,0:T(8,128)(2,1)S(1)}, u32[]{:S(2)}, u32[]{:S(2)}) collective-permute-start(bf16[16,2048]{1,0:T(8,128)(2,1)S(1)} %get-tuple-element.109), channel_id=1, source_target_pairs={{0,16},{4,20},{8,24},{12,28},{16,0},{20,4},{24,8},{28,12},{1,17},{... | collective-permute-start | bytes 196616 | tf_op jit(solution)/shard_map/ppermute | solution.py:331
  198.1 21.5 %collective-permute-start.41 = (bf16[16,2048]{1,0:T(8,128)(2,1)S(1)}, bf16[16,2048]{1,0:T(8,128)(2,1)S(1)}, u32[]{:S(2)}, u32[]{:S(2)}) collective-permute-start(bf16[16,2048]{1,0:T(8,128)(2,1)S(1)} %get-tuple-element.110), channel_id=1, source_target_pairs={{0,24},{4,28},{8,0},{12,4},{16,8},{20,12},{24,16},{28,20},{1,25},{... | collective-permute-start | bytes 196616 | tf_op jit(solution)/shard_map/ppermute | solution.py:331
  201.5 16.9 %collective-permute-start.38 = (bf16[8,4096]{1,0:T(8,128)(2,1)S(1)}, bf16[8,4096]{1,0:T(8,128)(2,1)S(1)}, u32[]{:S(2)}, u32[]{:S(2)}) collective-permute-start(bf16[8,4096]{1,0:T(8,128)(2,1)S(1)} %get-tuple-element.115), channel_id=1, source_target_pairs={{0,8},{4,12},{8,16},{12,20},{16,24},{20,28},{24,0},{28,4},{1,9},{5... | collective-permute-start | bytes 196616 | tf_op jit(solution)/shard_map/ppermute | solution.py:331
  202.5 6.7 %collective-permute-start.37 = (bf16[8,4096]{1,0:T(8,128)(2,1)S(1)}, bf16[8,4096]{1,0:T(8,128)(2,1)S(1)}, u32[]{:S(2)}, u32[]{:S(2)}) collective-permute-start(bf16[8,4096]{1,0:T(8,128)(2,1)S(1)} %get-tuple-element.116), channel_id=1, source_target_pairs={{0,16},{4,20},{8,24},{12,28},{16,0},{20,4},{24,8},{28,12},{1,17},{... | collective-permute-start | bytes 196616 | tf_op jit(solution)/shard_map/ppermute | solution.py:331
  209.2 6.4 %collective-permute-start.45 = (bf16[64,2048]{1,0:T(8,128)(2,1)S(1)}, bf16[64,2048]{1,0:T(8,128)(2,1)S(1)}, u32[]{:S(2)}, u32[]{:S(2)}) collective-permute-start(bf16[64,2048]{1,0:T(8,128)(2,1)S(1)} %slice.304), channel_id=1, source_target_pairs={{0,4},{1,5},{2,3},{3,2},{4,0},{5,1},{6,7},{7,6},{8,12},{9,13},{10,... | collective-permute-start | bytes 786440 | tf_op jit(solution)/shard_map/ppermute | solution.py:342
  (27 other events, 210.2 us)

commit v3 on v2

--- a/solution.py
+++ b/solution.py
@@ -374,24 +374,30 @@
     width = w_down.shape[1]
     half = width // 2
     hidden = w_down.shape[0]
-    most = hidden * 2 // 3
+    most = hidden // 2
 
     def pieces(two, four):
         return [two, four, shift(two, "context", 1), shift(four, "context", 1)]
 
-    def home_first(outs):
-        rows = outs[0].shape[0] // 4
-        both = add_up(outs[0], shift(outs[1], "context", 1))
-        return both[: 2 * rows], both[2 * rows :].astype(BF16)
-
-    def home_second(kept, far):
-        rows = kept.shape[0] // 2
-        two = add_up(kept, far)
-        return two[:rows], two[rows:].astype(BF16)
+    def part(terms, start, stop):
+        return add_up(*[t[start:stop] for t in terms]).astype(BF16)
+
+    def home_first(outs, *others):
+        terms = [after(outs[0], *others), shift(outs[1], "context", 1)]
+        rows = outs[0].shape[0]
+        return terms, part(terms, rows // 2, rows)
+
+    def home_second(terms, far):
+        terms = terms + [far]
+        rows = far.shape[0]
+        return terms, part(terms, rows // 2, rows)
+
+    def home_third(terms, far):
+        return part(terms + [far], 0, far.shape[0])
 
     early_came = send_rows(early, line)
-    late_came = send_rows(after(late, early_came[1]), line)
     early_own = jnp.concatenate(early_came, axis=0)
+    late_came = send_rows(after(late, early_own), line)
     early_near = cross(early_own, 0)
     early_two = jnp.concatenate([early_own, early_near], axis=0)
     early_four = cross(early_two, 1)
@@ -407,7 +413,7 @@
     early_second = gate_up(after(early_rows, late_two), w_gate, w_up, most, hidden - most)
     early_out = down([early_first, early_second], sizes, w_down, 0, width)
     late_four = after(late_four, early_out)
-    early_kept, early_go = home_first(after(early_out, late_four))
+    early_kept, early_go = home_first(early_out, late_four)
     early_far = cross(early_go, 1)
     sizes = (4 * late_own.shape[0],) * 2
     late_rows = after(pieces(late_two, late_four), early_go)
@@ -415,7 +421,7 @@
     early_kept, early_go = home_second(after(early_kept, late_first), early_far)
     early_far = cross(early_go, 0)
     late_second = gate_up(after(late_rows, early_go), w_gate, w_up, hidden // 2, hidden // 2)
-    early_result = add_up(after(early_kept, late_second), early_far).astype(BF16)
+    early_result = home_third(after(early_kept, late_second), early_far)
     late_hidden = [late_first, late_second]
     out_left = down(after(late_hidden, early_result), sizes, w_down, 0, half)
     left = home_first(out_left)
@@ -423,14 +429,15 @@
     out_right = down(after(late_hidden, early_result, left[1]), sizes, w_down, half, half)
     left = home_second(after(left[0], out_right), left_far)
     left_far = cross(left[1], 0)
-    right = home_first(out_right)
+    right = home_first(after(out_right, left[1]))
+    right_far = cross(right[1], 1)
     early_back = send_home(after(early_result, right[1]), line)
-    right_far = cross(right[1], 1)
-    right = home_second(after(right[0], left[1]), right_far)
+    left_kept, early_back = lax.optimization_barrier((left[0], early_back))
+    left_result = home_third(left_kept, left_far)
+    left_back = send_home(left_result, line)
+    right = home_second(after(right[0], left_result), right_far)
     right_far = cross(right[1], 0)
-    late_back = []
-    for kept, far in ((left[0], left_far), (right[0], right_far)):
-        late_back.append(send_home(add_up(kept, far).astype(BF16), line))
+    late_back = [left_back, send_home(home_third(right[0], right_far), line)]
     return early_back, jnp.concatenate(late_back, axis=1)
 
 

time: 224 us -> 214 us (0.955)
  waiting for transfers between devices: 85.6 us -> 74.3 us
  starting transfers between devices: 60.8 us -> 63.7 us
    ppermute x10, waiting for transfers between devices: 28.1 us -> 17.2 us  [cross(): return lax.ppermute(block, ('expert', 'context', 'dp'), route)]
    ppermute x27, starting transfers between devices: 36.6 us -> 44 us  [along_line(): lax.ppermute(block, 'expert', [(e, (e + 2 * distance) % size) for e in ra...]
    ppermute x27, waiting for transfers between devices: 48.4 us -> 44.2 us  [along_line(): lax.ppermute(block, 'expert', [(e, (e + 2 * distance) % size) for e in ra...]
    ppermute x7, waiting for transfers between devices: 5.82 us -> 9.57 us  [shift(): lax.ppermute(block, axis, [(i, (i + distance) % size) for i in range(size)])]
    ppermute x10, starting transfers between devices: 15 us -> 11.5 us  [cross(): return lax.ppermute(block, ('expert', 'context', 'dp'), route)]
  transfers between devices with their start and end apart: 49 -> 49, of which waited for: 29 -> 35; matrix products, arithmetic and copies ran while one was open for 2% -> 2% of each run, Pallas kernels for 19% -> 20%
where the time goes in v3:
time: 214 us
  waiting for transfers between devices  74.3 us (35%)
  Pallas kernels  64.7 us (30%)
  starting transfers between devices  63.7 us (30%)
  other arithmetic  5.66 us (3%)
  local copies, waits for them, and re-layouts  2.46 us (1%)
  matrix products  2.22 us (1%)
    ppermute x27, waiting for transfers between devices, along_line(): lax.ppermute(block, 'expert', [(e, (e + 2 * distance) % size) for e in ra...  44.2 us
    ppermute x27, starting transfers between devices, along_line(): lax.ppermute(block, 'expert', [(e, (e + 2 * distance) % size) for e in ra...  44 us
    pallas_call x4, Pallas kernels, gate_up(): pl.pallas_call(functools.partial(gate_up_kernel, len(pieces), first), out...  31.9 us
    ppermute x10, waiting for transfers between devices, cross(): return lax.ppermute(block, ('expert', 'context', 'dp'), route)  17.2 us
    pallas_call x3, Pallas kernels, down(): pl.pallas_call(functools.partial(down_kernel, len(pieces), first), out_sh...  16.8 us
    ppermute x10, starting transfers between devices, cross(): return lax.ppermute(block, ('expert', 'context', 'dp'), route)  11.5 us
    ppermute x7, waiting for transfers between devices, shift(): lax.ppermute(block, axis, [(i, (i + distance) % size) for i in range(size)])  9.57 us
    pallas_call x1, Pallas kernels, run_out(): pl.pallas_call(functools.partial(out_kernel, channels // LANES, line, fir...  9.19 us
  transfers between devices with their start and end apart: 49, of which 35 were waited for; matrix products, arithmetic and copies ran while one was open for 2% of the time, Pallas kernels for 20%

profile of v3, /device:TPU:0, one launch (start us, length us, event | category | flops | bytes accessed | tf_op | source)
XLA Modules:
  0.0 213.7 jit_solution(12099972476894345187)
XLA Ops:
  0.8 2.3 %collective-permute-start = (bf16[3,1024]{1,0:T(4,128)(2,1)S(1)}, bf16[3,1024]{1,0:T(4,128)(2,1)S(1)}, u32[]{:S(2)}, u32[]{:S(2)}) collective-permute-start(bf16[3,1024]{1,0:T(4,128)(2,1)S(1)} %slice_bitcast_fusion.3), channel_id=1, source_target_pairs={{0,2},{1,3},{4,6},{5,7},{8,10},{9,11},{12,14},{13,15},{16,18},{17,... | collective-permute-start | bytes 18440 | tf_op jit(solution)/shard_map/ppermute | solution.py:24
  8.4 2.5 %collective-permute-start.1 = (bf16[64,288]{1,0:T(8,128)(2,1)S(1)}, bf16[64,288]{1,0:T(8,128)(2,1)S(1)}, u32[]{:S(2)}, u32[]{:S(2)}) collective-permute-start(bf16[64,288]{1,0:T(8,128)(2,1)S(1)} %get-tuple-element.144), channel_id=1, source_target_pairs={{0,8},{4,12},{8,16},{12,20},{16,24},{20,28},{24,0},{28,4},{1,9},{5... | collective-permute-start | bytes 110600 | tf_op jit(solution)/shard_map/ppermute | solution.py:331
  10.9 2.6 %collective-permute-start.2 = (bf16[64,288]{1,0:T(8,128)(2,1)S(1)}, bf16[64,288]{1,0:T(8,128)(2,1)S(1)}, u32[]{:S(2)}, u32[]{:S(2)}) collective-permute-start(bf16[64,288]{1,0:T(8,128)(2,1)S(1)} %get-tuple-element.146), channel_id=1, source_target_pairs={{0,16},{4,20},{8,24},{12,28},{16,0},{20,4},{24,8},{28,12},{1,17},{... | collective-permute-start | bytes 110600 | tf_op jit(solution)/shard_map/ppermute | solution.py:331
  19.2 2.5 %collective-permute-done.4 = bf16[64,288]{1,0:T(8,128)(2,1)S(1)} collective-permute-done((bf16[64,288]{1,0:T(8,128)(2,1)S(1)}, bf16[64,288]{1,0:T(8,128)(2,1)S(1)}, u32[]{:S(2)}, u32[]{:S(2)}) %collective-permute-start.4) | collective-permute-done | bytes 36896 | tf_op jit(solution)/shard_map/ppermute | solution.py:34
  22.4 3.1 %collective-permute-start.6 = (bf16[64,288]{1,0:T(8,128)(2,1)S(1)}, bf16[64,288]{1,0:T(8,128)(2,1)S(1)}, u32[]{:S(2)}, u32[]{:S(2)}) collective-permute-start(bf16[64,288]{1,0:T(8,128)(2,1)S(1)} %add_convert_fusion.10.refs_0_), channel_id=1, source_target_pairs={{0,16},{4,20},{8,24},{12,28},{16,0},{20,4},{24,8},{28,12},{1,17},{... | collective-permute-start | bytes 110600 | tf_op jit(solution)/shard_map/ppermute | solution.py:331
  29.6 6.9 %state_scan.1 = (f32[2048,128]{1,0:T(8,128)S(1)}, f32[2048,128]{1,0:T(8,128)S(1)}, f32[16,8,128]{2,1,0:T(8,128)S(1)}, bf16[256,32]{1,0:T(8,128)(2,1)S(1)}) custom-call(s32[2]{0:T(128)S(1)} %pad_add_fusion.place_ref.at_ref, bf16[64,288]{1,0:T(8,128)(2,1)S(1)} %add_convert_fusion.10.refs_0_, bf16[64,288]{1,0:T(8,128)(2,1)S(1)} %collective-permute-done.5.refs_1_, ...), custom_call_target="tpu_custom_call" | custom-call | flops 200000000 | bytes 4194304 | tf_op jit(solution)/shard_map/state_scan/pallas_call | solution.py:104
  38.7 9.2 %readout_project.1 = (bf16[128,2560]{1,0:T(8,128)(2,1)S(1)}, bf16[128,2560]{1,0:T(8,128)(2,1)S(1)}, bf16[4,64,1536]{2,1,0:T(8,128)(2,1)S(1)}) custom-call(s32[2]{0:T(128)S(1)} %pad_add_fusion.place_ref.at_ref, f32[2048,128]{1,0:T(8,128)S(1)} %get-tuple-element.59.y_ref, f32[2048,128]{1,0:T(8,128)S(1)} %get-tuple-element.60.sum_ref, ...), custom_call_target="tpu_custom_call" | custom-call | flops 2147483648 | bytes 16777216 | tf_op jit(solution)/shard_map/readout_project/pallas_call | solution.py:198
  50.4 2.1 %collective-permute-start.14 = (bf16[64,1536]{1,0:T(8,128)(2,1)S(1)}, bf16[64,1536]{1,0:T(8,128)(2,1)S(1)}, u32[]{:S(2)}, u32[]{:S(2)}) collective-permute-start(bf16[64,1536]{1,0:T(8,128)(2,1)S(1)} %get-tuple-element.119), channel_id=1, source_target_pairs={{0,16},{4,20},{8,24},{12,28},{16,0},{20,4},{24,8},{28,12},{1,17},{... | collective-permute-start | bytes 589832 | tf_op jit(solution)/shard_map/ppermute | solution.py:331
  53.6 5.7 %collective-permute-done.13 = bf16[64,1536]{1,0:T(8,128)(2,1)S(1)} collective-permute-done((bf16[64,1536]{1,0:T(8,128)(2,1)S(1)}, bf16[64,1536]{1,0:T(8,128)(2,1)S(1)}, u32[]{:S(2)}, u32[]{:S(2)}) %collective-permute-start.13) | collective-permute-done | bytes 196640 | tf_op jit(solution)/shard_map/ppermute | solution.py:331
  59.3 7.6 %collective-permute-done.14 = bf16[64,1536]{1,0:T(8,128)(2,1)S(1)} collective-permute-done((bf16[64,1536]{1,0:T(8,128)(2,1)S(1)}, bf16[64,1536]{1,0:T(8,128)(2,1)S(1)}, u32[]{:S(2)}, u32[]{:S(2)}) %collective-permute-start.14) | collective-permute-done | bytes 196640 | tf_op jit(solution)/shard_map/ppermute | solution.py:331
  67.8 4.3 %collective-permute-start.10 = (bf16[32,2560]{1,0:T(8,128)(2,1)S(1)}, bf16[32,2560]{1,0:T(8,128)(2,1)S(1)}, u32[]{:S(2)}, u32[]{:S(2)}) collective-permute-start(bf16[32,2560]{1,0:T(8,128)(2,1)S(1)} %get-tuple-element.120), channel_id=1, source_target_pairs={{0,8},{4,12},{8,16},{12,20},{16,24},{20,28},{24,0},{28,4},{1,9},{5... | collective-permute-start | bytes 491528 | tf_op jit(solution)/shard_map/ppermute | solution.py:331
  74.5 2.2 %collective-permute-done.10 = bf16[32,2560]{1,0:T(8,128)(2,1)S(1)} collective-permute-done((bf16[32,2560]{1,0:T(8,128)(2,1)S(1)}, bf16[32,2560]{1,0:T(8,128)(2,1)S(1)}, u32[]{:S(2)}, u32[]{:S(2)}) %collective-permute-start.10) | collective-permute-done | bytes 163872 | tf_op jit(solution)/shard_map/ppermute | solution.py:331
  76.7 5.6 %collective-permute-done.11 = bf16[32,2560]{1,0:T(8,128)(2,1)S(1)} collective-permute-done((bf16[32,2560]{1,0:T(8,128)(2,1)S(1)}, bf16[32,2560]{1,0:T(8,128)(2,1)S(1)}, u32[]{:S(2)}, u32[]{:S(2)}) %collective-permute-start.11) | collective-permute-done | bytes 163872 | tf_op jit(solution)/shard_map/ppermute | solution.py:331
  83.0 4.0 %collective-permute-start.17 = (bf16[8,4096]{1,0:T(8,128)(2,1)S(1)}, bf16[8,4096]{1,0:T(8,128)(2,1)S(1)}, u32[]{:S(2)}, u32[]{:S(2)}) collective-permute-start(bf16[8,4096]{1,0:T(8,128)(2,1)S(1)} %get-tuple-element.142), channel_id=1, source_target_pairs={{0,8},{4,12},{8,16},{12,20},{16,24},{20,28},{24,0},{28,4},{1,9},{5... | collective-permute-start | bytes 196616 | tf_op jit(solution)/shard_map/ppermute | solution.py:331
  87.0 2.8 %collective-permute-start.18 = (bf16[8,4096]{1,0:T(8,128)(2,1)S(1)}, bf16[8,4096]{1,0:T(8,128)(2,1)S(1)}, u32[]{:S(2)}, u32[]{:S(2)}) collective-permute-start(bf16[8,4096]{1,0:T(8,128)(2,1)S(1)} %get-tuple-element.141), channel_id=1, source_target_pairs={{0,16},{4,20},{8,24},{12,28},{16,0},{20,4},{24,8},{28,12},{1,17},{... | collective-permute-start | bytes 196616 | tf_op jit(solution)/shard_map/ppermute | solution.py:331
  104.4 5.6 %collective-permute-done.24.refs_1_ = bf16[64,4096]{1,0:T(8,128)(2,1)S(1)} collective-permute-done((bf16[64,4096]{1,0:T(8,128)(2,1)S(1)}, bf16[64,4096]{1,0:T(8,128)(2,1)S(1)}, u32[]{:S(2)}, u32[]{:S(2)}) %collective-permute-start.24) | collective-permute-done | bytes 524320 | tf_op jit(solution)/shard_map/ppermute | solution.py:342
  111.9 6.3 %gate_up.4.refs_0_ = bf16[256,768]{1,0:T(8,128)(2,1)S(1)} custom-call(bf16[64,4096]{1,0:T(8,128)(2,1)S(1)} %constant_dynamic-update-slice_fusion.4.refs_0_, bf16[64,4096]{1,0:T(8,128)(2,1)S(1)} %collective-permute-done.24.refs_1_, bf16[64,4096]{1,0:T(8,128)(2,1)S(1)} %collective-permute-done.25.refs_2_, ...), custom_call_target="tpu_custom_call" | custom-call | flops 3221225472 | bytes 14680064 | tf_op jit(solution)/shard_map/gate_up/pallas_call | solution.py:259
  120.9 6.3 %gate_up.5.refs_1_ = bf16[256,768]{1,0:T(8,128)(2,1)S(1)} custom-call(bf16[64,4096]{1,0:T(8,128)(2,1)S(1)} %constant_dynamic-update-slice_fusion.4.refs_0_, bf16[64,4096]{1,0:T(8,128)(2,1)S(1)} %collective-permute-done.24.refs_1_, bf16[64,4096]{1,0:T(8,128)(2,1)S(1)} %collective-permute-done.25.refs_2_, ...), custom_call_target="tpu_custom_call" | custom-call | flops 3221225472 | bytes 14680064 | tf_op jit(solution)/shard_map/gate_up/pallas_call | solution.py:259
  127.2 6.1 %down.3 = (bf16[128,4096]{1,0:T(8,128)(2,1)S(1)}, bf16[128,4096]{1,0:T(8,128)(2,1)S(1)}) custom-call(bf16[256,768]{1,0:T(8,128)(2,1)S(1)} %gate_up.4.refs_0_, bf16[256,768]{1,0:T(8,128)(2,1)S(1)} %gate_up.5.refs_1_, bf16[1536,4096]{1,0:T(8,128)(2,1)} %bitcast.64), custom_call_target="tpu_custom_call" | custom-call | flops 3221225472 | bytes 15466496 | tf_op jit(solution)/shard_map/down/pallas_call | solution.py:309
  139.0 9.7 %gate_up.6.refs_0_ = bf16[512,768]{1,0:T(8,128)(2,1)S(1)} custom-call(bf16[128,4096]{1,0:T(8,128)(2,1)S(1)} %constant_dynamic-update-slice_fusion.9.refs_0_, bf16[128,4096]{1,0:T(8,128)(2,1)S(1)} %collective-permute-done.28.refs_1_, bf16[128,4096]{1,0:T(8,128)(2,1)S(1)} %collective-permute-done.29.refs_2_, ...), custom_call_target="tpu_custom_call" | custom-call | flops 6442450944 | bytes 16777216 | tf_op jit(solution)/shard_map/gate_up/pallas_call | solution.py:259
  150.4 9.7 %gate_up.7.refs_1_ = bf16[512,768]{1,0:T(8,128)(2,1)S(1)} custom-call(bf16[128,4096]{1,0:T(8,128)(2,1)S(1)} %constant_dynamic-update-slice_fusion.9.refs_0_, bf16[128,4096]{1,0:T(8,128)(2,1)S(1)} %collective-permute-done.28.refs_1_, bf16[128,4096]{1,0:T(8,128)(2,1)S(1)} %collective-permute-done.29.refs_2_, ...), custom_call_target="tpu_custom_call" | custom-call | flops 6442450944 | bytes 16777216 | tf_op jit(solution)/shard_map/gate_up/pallas_call | solution.py:259
  160.2 5.4 %down.4 = (bf16[256,2048]{1,0:T(8,128)(2,1)S(1)}, bf16[256,2048]{1,0:T(8,128)(2,1)S(1)}) custom-call(bf16[512,768]{1,0:T(8,128)(2,1)S(1)} %gate_up.6.refs_0_, bf16[512,768]{1,0:T(8,128)(2,1)S(1)} %gate_up.7.refs_1_, bf16[1536,4096]{1,0:T(8,128)(2,1)} %bitcast.65), custom_call_target="tpu_custom_call" | custom-call | flops 3221225472 | bytes 9961472 | tf_op jit(solution)/shard_map/down/pallas_call | solution.py:309
  165.7 2.6 %collective-permute-done.34 = bf16[256,2048]{1,0:T(8,128)(2,1)S(1)} collective-permute-done((bf16[256,2048]{1,0:T(8,128)(2,1)S(1)}, bf16[256,2048]{1,0:T(8,128)(2,1)S(1)}, u32[]{:S(2)}, u32[]{:S(2)}) %collective-permute-start.34) | collective-permute-done | bytes 1048608 | tf_op jit(solution)/shard_map/ppermute | solution.py:29
  169.0 5.4 %down.5 = (bf16[256,2048]{1,0:T(8,128)(2,1)S(1)}, bf16[256,2048]{1,0:T(8,128)(2,1)S(1)}) custom-call(bf16[512,768]{1,0:T(8,128)(2,1)S(1)} %gate_up.6.refs_0_, bf16[512,768]{1,0:T(8,128)(2,1)S(1)} %gate_up.7.refs_1_, bf16[1536,4096]{1,0:T(8,128)(2,1)} %bitcast.66), custom_call_target="tpu_custom_call" | custom-call | flops 3221225472 | bytes 9961472 | tf_op jit(solution)/shard_map/down/pallas_call | solution.py:309
  174.4 3.3 %collective-permute-done.35 = bf16[128,2048]{1,0:T(8,128)(2,1)S(1)} collective-permute-done((bf16[128,2048]{1,0:T(8,128)(2,1)S(1)}, bf16[128,2048]{1,0:T(8,128)(2,1)S(1)}, u32[]{:S(2)}, u32[]{:S(2)}) %collective-permute-start.35) | collective-permute-done | bytes 524320 | tf_op jit(solution)/shard_map/ppermute | solution.py:342
  177.9 2.6 %collective-permute-done.36 = bf16[256,2048]{1,0:T(8,128)(2,1)S(1)} collective-permute-done((bf16[256,2048]{1,0:T(8,128)(2,1)S(1)}, bf16[256,2048]{1,0:T(8,128)(2,1)S(1)}, u32[]{:S(2)}, u32[]{:S(2)}) %collective-permute-start.36) | collective-permute-done | bytes 1048608 | tf_op jit(solution)/shard_map/ppermute | solution.py:29
  180.7 3.1 %collective-permute-start.37 = (bf16[8,4096]{1,0:T(8,128)(2,1)S(1)}, bf16[8,4096]{1,0:T(8,128)(2,1)S(1)}, u32[]{:S(2)}, u32[]{:S(2)}) collective-permute-start(bf16[8,4096]{1,0:T(8,128)(2,1)S(1)} %get-tuple-element.138), channel_id=1, source_target_pairs={{0,24},{4,28},{8,0},{12,4},{16,8},{20,12},{24,16},{28,20},{1,25},{... | collective-permute-start | bytes 196616 | tf_op jit(solution)/shard_map/ppermute | solution.py:331
  186.3 4.1 %collective-permute-done.38 = bf16[8,4096]{1,0:T(8,128)(2,1)S(1)} collective-permute-done((bf16[8,4096]{1,0:T(8,128)(2,1)S(1)}, bf16[8,4096]{1,0:T(8,128)(2,1)S(1)}, u32[]{:S(2)}, u32[]{:S(2)}) %collective-permute-start.38) | collective-permute-done | bytes 65568 | tf_op jit(solution)/shard_map/ppermute | solution.py:331
  190.4 3.4 %collective-permute-done.40 = bf16[64,2048]{1,0:T(8,128)(2,1)S(1)} collective-permute-done((bf16[64,2048]{1,0:T(8,128)(2,1)S(1)}, bf16[64,2048]{1,0:T(8,128)(2,1)S(1)}, u32[]{:S(2)}, u32[]{:S(2)}) %collective-permute-start.40) | collective-permute-done | bytes 262176 | tf_op jit(solution)/shard_map/ppermute | solution.py:342
  196.0 3.2 %collective-permute-start.41 = (bf16[16,2048]{1,0:T(8,128)(2,1)S(1)}, bf16[16,2048]{1,0:T(8,128)(2,1)S(1)}, u32[]{:S(2)}, u32[]{:S(2)}) collective-permute-start(bf16[16,2048]{1,0:T(8,128)(2,1)S(1)} %get-tuple-element.130), channel_id=1, source_target_pairs={{0,24},{4,28},{8,0},{12,4},{16,8},{20,12},{24,16},{28,20},{1,25},{... | collective-permute-start | bytes 196616 | tf_op jit(solution)/shard_map/ppermute | solution.py:331
  201.9 3.2 %collective-permute-start.46 = (bf16[16,2048]{1,0:T(8,128)(2,1)S(1)}, bf16[16,2048]{1,0:T(8,128)(2,1)S(1)}, u32[]{:S(2)}, u32[]{:S(2)}) collective-permute-start(bf16[16,2048]{1,0:T(8,128)(2,1)S(1)} %get-tuple-element.134), channel_id=1, source_target_pairs={{0,24},{4,28},{8,0},{12,4},{16,8},{20,12},{24,16},{28,20},{1,25},{... | collective-permute-start | bytes 196616 | tf_op jit(solution)/shard_map/ppermute | solution.py:331
  208.2 4.2 %collective-permute-done.47 = bf16[16,2048]{1,0:T(8,128)(2,1)S(1)} collective-permute-done((bf16[16,2048]{1,0:T(8,128)(2,1)S(1)}, bf16[16,2048]{1,0:T(8,128)(2,1)S(1)}, u32[]{:S(2)}, u32[]{:S(2)}) %collective-permute-start.47) | collective-permute-done | bytes 65568 | tf_op jit(solution)/shard_map/ppermute | solution.py:331
  (160 shorter events, 65.5 us)
Async XLA Ops:
  8.4 7.2 %collective-permute-start.1 = (bf16[64,288]{1,0:T(8,128)(2,1)S(1)}, bf16[64,288]{1,0:T(8,128)(2,1)S(1)}, u32[]{:S(2)}, u32[]{:S(2)}) collective-permute-start(bf16[64,288]{1,0:T(8,128)(2,1)S(1)} %get-tuple-element.144), channel_id=1, source_target_pairs={{0,8},{4,12},{8,16},{12,20},{16,24},{20,28},{24,0},{28,4},{1,9},{5... | collective-permute-start | bytes 110600 | tf_op jit(solution)/shard_map/ppermute | solution.py:331
  47.9 19.6 %collective-permute-start.9 = (bf16[128,2560]{1,0:T(8,128)(2,1)S(1)}, bf16[128,2560]{1,0:T(8,128)(2,1)S(1)}, u32[]{:S(2)}, u32[]{:S(2)}) collective-permute-start(bf16[128,2560]{1,0:T(8,128)(2,1)S(1)} %get-tuple-element.64), channel_id=1, source_target_pairs={{0,4},{4,0},{8,12},{12,8},{16,20},{20,16},{24,28},{28,24},{1,5},{5... | collective-permute-start | bytes 1966088 | tf_op jit(solution)/shard_map/ppermute | solution.py:34
  49.5 9.8 %collective-permute-start.13 = (bf16[64,1536]{1,0:T(8,128)(2,1)S(1)}, bf16[64,1536]{1,0:T(8,128)(2,1)S(1)}, u32[]{:S(2)}, u32[]{:S(2)}) collective-permute-start(bf16[64,1536]{1,0:T(8,128)(2,1)S(1)} %get-tuple-element.117), channel_id=1, source_target_pairs={{0,8},{4,12},{8,16},{12,20},{16,24},{20,28},{24,0},{28,4},{1,9},{5... | collective-permute-start | bytes 589832 | tf_op jit(solution)/shard_map/ppermute | solution.py:331
  50.4 16.5 %collective-permute-start.14 = (bf16[64,1536]{1,0:T(8,128)(2,1)S(1)}, bf16[64,1536]{1,0:T(8,128)(2,1)S(1)}, u32[]{:S(2)}, u32[]{:S(2)}) collective-permute-start(bf16[64,1536]{1,0:T(8,128)(2,1)S(1)} %get-tuple-element.119), channel_id=1, source_target_pairs={{0,16},{4,20},{8,24},{12,28},{16,0},{20,4},{24,8},{28,12},{1,17},{... | collective-permute-start | bytes 589832 | tf_op jit(solution)/shard_map/ppermute | solution.py:331
  52.5 14.4 %collective-permute-start.15 = (bf16[64,1536]{1,0:T(8,128)(2,1)S(1)}, bf16[64,1536]{1,0:T(8,128)(2,1)S(1)}, u32[]{:S(2)}, u32[]{:S(2)}) collective-permute-start(bf16[64,1536]{1,0:T(8,128)(2,1)S(1)} %get-tuple-element.118), channel_id=1, source_target_pairs={{0,24},{4,28},{8,0},{12,4},{16,8},{20,12},{24,16},{28,20},{1,25},{... | collective-permute-start | bytes 589832 | tf_op jit(solution)/shard_map/ppermute | solution.py:331
  67.0 7.5 %collective-permute-start.16 = (bf16[32,1536]{1,0:T(8,128)(2,1)S(1)}, bf16[32,1536]{1,0:T(8,128)(2,1)S(1)}, u32[]{:S(2)}, u32[]{:S(2)}) collective-permute-start(bf16[32,1536]{1,0:T(8,128)(2,1)S(1)} %slice.351), channel_id=1, source_target_pairs={{0,4},{4,0},{8,12},{12,8},{16,20},{20,16},{24,28},{28,24},{1,5},{5... | collective-permute-start | bytes 294920 | tf_op jit(solution)/shard_map/ppermute | solution.py:34
  67.8 8.9 %collective-permute-start.10 = (bf16[32,2560]{1,0:T(8,128)(2,1)S(1)}, bf16[32,2560]{1,0:T(8,128)(2,1)S(1)}, u32[]{:S(2)}, u32[]{:S(2)}) collective-permute-start(bf16[32,2560]{1,0:T(8,128)(2,1)S(1)} %get-tuple-element.120), channel_id=1, source_target_pairs={{0,8},{4,12},{8,16},{12,20},{16,24},{20,28},{24,0},{28,4},{1,9},{5... | collective-permute-start | bytes 491528 | tf_op jit(solution)/shard_map/ppermute | solution.py:331
  72.1 10.3 %collective-permute-start.11 = (bf16[32,2560]{1,0:T(8,128)(2,1)S(1)}, bf16[32,2560]{1,0:T(8,128)(2,1)S(1)}, u32[]{:S(2)}, u32[]{:S(2)}) collective-permute-start(bf16[32,2560]{1,0:T(8,128)(2,1)S(1)} %get-tuple-element.122), channel_id=1, source_target_pairs={{0,16},{4,20},{8,24},{12,28},{16,0},{20,4},{24,8},{28,12},{1,17},{... | collective-permute-start | bytes 491528 | tf_op jit(solution)/shard_map/ppermute | solution.py:331
  72.5 9.9 %collective-permute-start.12 = (bf16[32,2560]{1,0:T(8,128)(2,1)S(1)}, bf16[32,2560]{1,0:T(8,128)(2,1)S(1)}, u32[]{:S(2)}, u32[]{:S(2)}) collective-permute-start(bf16[32,2560]{1,0:T(8,128)(2,1)S(1)} %get-tuple-element.121), channel_id=1, source_target_pairs={{0,24},{4,28},{8,0},{12,4},{16,8},{20,12},{24,16},{28,20},{1,25},{... | collective-permute-start | bytes 491528 | tf_op jit(solution)/shard_map/ppermute | solution.py:331
  83.0 8.8 %collective-permute-start.17 = (bf16[8,4096]{1,0:T(8,128)(2,1)S(1)}, bf16[8,4096]{1,0:T(8,128)(2,1)S(1)}, u32[]{:S(2)}, u32[]{:S(2)}) collective-permute-start(bf16[8,4096]{1,0:T(8,128)(2,1)S(1)} %get-tuple-element.142), channel_id=1, source_target_pairs={{0,8},{4,12},{8,16},{12,20},{16,24},{20,28},{24,0},{28,4},{1,9},{5... | collective-permute-start | bytes 196616 | tf_op jit(solution)/shard_map/ppermute | solution.py:331
  87.0 6.6 %collective-permute-start.18 = (bf16[8,4096]{1,0:T(8,128)(2,1)S(1)}, bf16[8,4096]{1,0:T(8,128)(2,1)S(1)}, u32[]{:S(2)}, u32[]{:S(2)}) collective-permute-start(bf16[8,4096]{1,0:T(8,128)(2,1)S(1)} %get-tuple-element.141), channel_id=1, source_target_pairs={{0,16},{4,20},{8,24},{12,28},{16,0},{20,4},{24,8},{28,12},{1,17},{... | collective-permute-start | bytes 196616 | tf_op jit(solution)/shard_map/ppermute | solution.py:331
  94.3 6.4 %collective-permute-start.20 = (bf16[32,4096]{1,0:T(8,128)(2,1)S(1)}, bf16[32,4096]{1,0:T(8,128)(2,1)S(1)}, u32[]{:S(2)}, u32[]{:S(2)}) collective-permute-start(bf16[32,4096]{1,0:T(8,128)(2,1)S(1)} %pad_maximum_fusion), channel_id=1, source_target_pairs={{0,4},{1,5},{2,3},{3,2},{4,0},{5,1},{6,7},{7,6},{8,12},{9,13},{10,... | collective-permute-start | bytes 786440 | tf_op jit(solution)/shard_map/ppermute | solution.py:342
  96.0 8.4 %collective-permute-start.21 = (bf16[16,4096]{1,0:T(8,128)(2,1)S(1)}, bf16[16,4096]{1,0:T(8,128)(2,1)S(1)}, u32[]{:S(2)}, u32[]{:S(2)}) collective-permute-start(bf16[16,4096]{1,0:T(8,128)(2,1)S(1)} %get-tuple-element.125), channel_id=1, source_target_pairs={{0,8},{4,12},{8,16},{12,20},{16,24},{20,28},{24,0},{28,4},{1,9},{5... | collective-permute-start | bytes 393224 | tf_op jit(solution)/shard_map/ppermute | solution.py:331
  97.3 12.7 %collective-permute-start.22 = (bf16[16,4096]{1,0:T(8,128)(2,1)S(1)}, bf16[16,4096]{1,0:T(8,128)(2,1)S(1)}, u32[]{:S(2)}, u32[]{:S(2)}) collective-permute-start(bf16[16,4096]{1,0:T(8,128)(2,1)S(1)} %get-tuple-element.124), channel_id=1, source_target_pairs={{0,16},{4,20},{8,24},{12,28},{16,0},{20,4},{24,8},{28,12},{1,17},{... | collective-permute-start | bytes 393224 | tf_op jit(solution)/shard_map/ppermute | solution.py:331
  98.9 11.1 %collective-permute-start.23 = (bf16[16,4096]{1,0:T(8,128)(2,1)S(1)}, bf16[16,4096]{1,0:T(8,128)(2,1)S(1)}, u32[]{:S(2)}, u32[]{:S(2)}) collective-permute-start(bf16[16,4096]{1,0:T(8,128)(2,1)S(1)} %get-tuple-element.123), channel_id=1, source_target_pairs={{0,24},{4,28},{8,0},{12,4},{16,8},{20,12},{24,16},{28,20},{1,25},{... | collective-permute-start | bytes 393224 | tf_op jit(solution)/shard_map/ppermute | solution.py:331
  100.8 9.2 %collective-permute-start.24 = (bf16[64,4096]{1,0:T(8,128)(2,1)S(1)}, bf16[64,4096]{1,0:T(8,128)(2,1)S(1)}, u32[]{:S(2)}, u32[]{:S(2)}) collective-permute-start(bf16[64,4096]{1,0:T(8,128)(2,1)S(1)} %constant_dynamic-update-slice_fusion.4.refs_0_), channel_id=1, source_target_pairs={{0,1},{1,0},{2,6},{3,7},{4,5},{5,4},{6,2},{7,3},{8,9},{9,8},{10,14... | collective-permute-start | bytes 1572872 | tf_op jit(solution)/shard_map/ppermute | solution.py:342
  102.3 9.4 %collective-permute-start.25 = (bf16[64,4096]{1,0:T(8,128)(2,1)S(1)}, bf16[64,4096]{1,0:T(8,128)(2,1)S(1)}, u32[]{:S(2)}, u32[]{:S(2)}) collective-permute-start(bf16[64,4096]{1,0:T(8,128)(2,1)S(1)} %constant_dynamic-update-slice_fusion.4.refs_0_), channel_id=1, source_target_pairs={{0,2},{2,0},{1,3},{3,1},{4,6},{6,4},{5,7},{7,5},{8,10},{10,8},{9,1... | collective-permute-start | bytes 1572872 | tf_op jit(solution)/shard_map/ppermute | solution.py:29
  110.1 9.2 %collective-permute-start.27 = (bf16[64,4096]{1,0:T(8,128)(2,1)S(1)}, bf16[64,4096]{1,0:T(8,128)(2,1)S(1)}, u32[]{:S(2)}, u32[]{:S(2)}) collective-permute-start(bf16[64,4096]{1,0:T(8,128)(2,1)S(1)} %constant_dynamic-update-slice_fusion), channel_id=1, source_target_pairs={{0,4},{1,5},{2,3},{3,2},{4,0},{5,1},{6,7},{7,6},{8,12},{9,13},{10,... | collective-permute-start | bytes 1572872 | tf_op jit(solution)/shard_map/ppermute | solution.py:342
  119.3 14.9 %collective-permute-start.28 = (bf16[128,4096]{1,0:T(8,128)(2,1)S(1)}, bf16[128,4096]{1,0:T(8,128)(2,1)S(1)}, u32[]{:S(2)}, u32[]{:S(2)}) collective-permute-start(bf16[128,4096]{1,0:T(8,128)(2,1)S(1)} %constant_dynamic-update-slice_fusion.9.refs_0_), channel_id=1, source_target_pairs={{0,1},{1,0},{2,6},{3,7},{4,5},{5,4},{6,2},{7,3},{8,9},{9,8},{10,14... | collective-permute-start | bytes 3145736 | tf_op jit(solution)/shard_map/ppermute | solution.py:342
  136.1 12.5 %collective-permute-start.32 = (bf16[64,4096]{1,0:T(8,128)(2,1)S(1)}, bf16[64,4096]{1,0:T(8,128)(2,1)S(1)}, u32[]{:S(2)}, u32[]{:S(2)}) collective-permute-start(bf16[64,4096]{1,0:T(8,128)(2,1)S(1)} %add_convert_fusion.3), channel_id=1, source_target_pairs={{0,1},{1,0},{2,6},{3,7},{4,5},{5,4},{6,2},{7,3},{8,9},{9,8},{10,14... | collective-permute-start | bytes 1572872 | tf_op jit(solution)/shard_map/ppermute | solution.py:342
  148.8 11.3 %collective-permute-start.33 = (bf16[32,4096]{1,0:T(8,128)(2,1)S(1)}, bf16[32,4096]{1,0:T(8,128)(2,1)S(1)}, u32[]{:S(2)}, u32[]{:S(2)}) collective-permute-start(bf16[32,4096]{1,0:T(8,128)(2,1)S(1)} %add_convert_fusion.9), channel_id=1, source_target_pairs={{0,4},{1,5},{2,3},{3,2},{4,0},{5,1},{6,7},{7,6},{8,12},{9,13},{10,... | collective-permute-start | bytes 786440 | tf_op jit(solution)/shard_map/ppermute | solution.py:342
  168.4 9.2 %collective-permute-start.35 = (bf16[128,2048]{1,0:T(8,128)(2,1)S(1)}, bf16[128,2048]{1,0:T(8,128)(2,1)S(1)}, u32[]{:S(2)}, u32[]{:S(2)}) collective-permute-start(bf16[128,2048]{1,0:T(8,128)(2,1)S(1)} %add_convert_fusion.2), channel_id=1, source_target_pairs={{0,1},{1,0},{2,6},{3,7},{4,5},{5,4},{6,2},{7,3},{8,9},{9,8},{10,14... | collective-permute-start | bytes 1572872 | tf_op jit(solution)/shard_map/ppermute | solution.py:342
  183.8 6.6 %collective-permute-start.38 = (bf16[8,4096]{1,0:T(8,128)(2,1)S(1)}, bf16[8,4096]{1,0:T(8,128)(2,1)S(1)}, u32[]{:S(2)}, u32[]{:S(2)}) collective-permute-start(bf16[8,4096]{1,0:T(8,128)(2,1)S(1)} %get-tuple-element.137), channel_id=1, source_target_pairs={{0,16},{4,20},{8,24},{12,28},{16,0},{20,4},{24,8},{28,12},{1,17},{... | collective-permute-start | bytes 196616 | tf_op jit(solution)/shard_map/ppermute | solution.py:331
  183.8 6.6 %collective-permute-start.39 = (bf16[8,4096]{1,0:T(8,128)(2,1)S(1)}, bf16[8,4096]{1,0:T(8,128)(2,1)S(1)}, u32[]{:S(2)}, u32[]{:S(2)}) collective-permute-start(bf16[8,4096]{1,0:T(8,128)(2,1)S(1)} %get-tuple-element.136), channel_id=1, source_target_pairs={{0,8},{4,12},{8,16},{12,20},{16,24},{20,28},{24,0},{28,4},{1,9},{5... | collective-permute-start | bytes 196616 | tf_op jit(solution)/shard_map/ppermute | solution.py:331
  184.5 9.3 %collective-permute-start.40 = (bf16[64,2048]{1,0:T(8,128)(2,1)S(1)}, bf16[64,2048]{1,0:T(8,128)(2,1)S(1)}, u32[]{:S(2)}, u32[]{:S(2)}) collective-permute-start(bf16[64,2048]{1,0:T(8,128)(2,1)S(1)} %add_convert_fusion.7), channel_id=1, source_target_pairs={{0,4},{1,5},{2,3},{3,2},{4,0},{5,1},{6,7},{7,6},{8,12},{9,13},{10,... | collective-permute-start | bytes 786440 | tf_op jit(solution)/shard_map/ppermute | solution.py:342
  185.0 10.1 %collective-permute-start.44 = (bf16[128,2048]{1,0:T(8,128)(2,1)S(1)}, bf16[128,2048]{1,0:T(8,128)(2,1)S(1)}, u32[]{:S(2)}, u32[]{:S(2)}) collective-permute-start(bf16[128,2048]{1,0:T(8,128)(2,1)S(1)} %add_convert_fusion.1), channel_id=1, source_target_pairs={{0,1},{1,0},{2,6},{3,7},{4,5},{5,4},{6,2},{7,3},{8,9},{9,8},{10,14... | collective-permute-start | bytes 1572872 | tf_op jit(solution)/shard_map/ppermute | solution.py:342
  195.3 6.4 %collective-permute-start.45 = (bf16[64,2048]{1,0:T(8,128)(2,1)S(1)}, bf16[64,2048]{1,0:T(8,128)(2,1)S(1)}, u32[]{:S(2)}, u32[]{:S(2)}) collective-permute-start(bf16[64,2048]{1,0:T(8,128)(2,1)S(1)} %add_convert_fusion.5), channel_id=1, source_target_pairs={{0,4},{1,5},{2,3},{3,2},{4,0},{5,1},{6,7},{7,6},{8,12},{9,13},{10,... | collective-permute-start | bytes 786440 | tf_op jit(solution)/shard_map/ppermute | solution.py:342
  196.0 10.0 %collective-permute-start.41 = (bf16[16,2048]{1,0:T(8,128)(2,1)S(1)}, bf16[16,2048]{1,0:T(8,128)(2,1)S(1)}, u32[]{:S(2)}, u32[]{:S(2)}) collective-permute-start(bf16[16,2048]{1,0:T(8,128)(2,1)S(1)} %get-tuple-element.130), channel_id=1, source_target_pairs={{0,24},{4,28},{8,0},{12,4},{16,8},{20,12},{24,16},{28,20},{1,25},{... | collective-permute-start | bytes 196616 | tf_op jit(solution)/shard_map/ppermute | solution.py:331
  199.2 8.5 %collective-permute-start.42 = (bf16[16,2048]{1,0:T(8,128)(2,1)S(1)}, bf16[16,2048]{1,0:T(8,128)(2,1)S(1)}, u32[]{:S(2)}, u32[]{:S(2)}) collective-permute-start(bf16[16,2048]{1,0:T(8,128)(2,1)S(1)} %get-tuple-element.129), channel_id=1, source_target_pairs={{0,16},{4,20},{8,24},{12,28},{16,0},{20,4},{24,8},{28,12},{1,17},{... | collective-permute-start | bytes 196616 | tf_op jit(solution)/shard_map/ppermute | solution.py:331
  200.3 7.4 %collective-permute-start.43 = (bf16[16,2048]{1,0:T(8,128)(2,1)S(1)}, bf16[16,2048]{1,0:T(8,128)(2,1)S(1)}, u32[]{:S(2)}, u32[]{:S(2)}) collective-permute-start(bf16[16,2048]{1,0:T(8,128)(2,1)S(1)} %get-tuple-element.128), channel_id=1, source_target_pairs={{0,8},{4,12},{8,16},{12,20},{16,24},{20,28},{24,0},{28,4},{1,9},{5... | collective-permute-start | bytes 196616 | tf_op jit(solution)/shard_map/ppermute | solution.py:331
  205.1 7.4 %collective-permute-start.47 = (bf16[16,2048]{1,0:T(8,128)(2,1)S(1)}, bf16[16,2048]{1,0:T(8,128)(2,1)S(1)}, u32[]{:S(2)}, u32[]{:S(2)}) collective-permute-start(bf16[16,2048]{1,0:T(8,128)(2,1)S(1)} %get-tuple-element.133), channel_id=1, source_target_pairs={{0,16},{4,20},{8,24},{12,28},{16,0},{20,4},{24,8},{28,12},{1,17},{... | collective-permute-start | bytes 196616 | tf_op jit(solution)/shard_map/ppermute | solution.py:331
  205.9 6.5 %collective-permute-start.48 = (bf16[16,2048]{1,0:T(8,128)(2,1)S(1)}, bf16[16,2048]{1,0:T(8,128)(2,1)S(1)}, u32[]{:S(2)}, u32[]{:S(2)}) collective-permute-start(bf16[16,2048]{1,0:T(8,128)(2,1)S(1)} %get-tuple-element.132), channel_id=1, source_target_pairs={{0,8},{4,12},{8,16},{12,20},{16,24},{20,28},{24,0},{28,4},{1,9},{5... | collective-permute-start | bytes 196616 | tf_op jit(solution)/shard_map/ppermute | solution.py:331
  (28 other events, 198.0 us)

commit v4 on v3

--- a/solution.py
+++ b/solution.py
@@ -273,6 +273,92 @@
     )(*pieces, w_gate, w_up)
 
 
+def finish_kernel(count, first, *refs):
+    pieces, (have_ref, gate_hbm, up_hbm, down_hbm) = refs[:count], refs[count : count + 4]
+    hidden_ref, outs = refs[count + 4], refs[count + 5 : -5]
+    rows_ref, gate_ref, up_ref, down_ref, sems = refs[-5:]
+    done = have_ref.shape[1]
+    steps, tile = gate_ref.shape[0], gate_ref.shape[2]
+    last_steps, last_tile = down_ref.shape[0], down_ref.shape[2]
+
+    def fetch(j, k):
+        cols = pl.ds(pl.multiple_of(done + j * tile, tile), tile)
+        source, target = ((gate_hbm, gate_ref), (up_hbm, up_ref))[k]
+        return pltpu.make_async_copy(source.at[:, cols], target.at[j], sems.at[count + 2 * j + k])
+
+    def last_fetch(j):
+        cols = pl.ds(pl.multiple_of(first + j * last_tile, last_tile), last_tile)
+        sem = sems.at[count + 2 * steps + j]
+        return pltpu.make_async_copy(down_hbm.at[:, cols], down_ref.at[j], sem)
+
+    copies, at = [], 0
+    for k, piece in enumerate(pieces):
+        rows = pl.ds(at, piece.shape[0])
+        copies.append(pltpu.make_async_copy(piece, rows_ref.at[rows, :], sems.at[k]))
+        at += piece.shape[0]
+    for copy in copies:
+        copy.start()
+    for j in range(steps):
+        fetch(j, 0).start()
+        fetch(j, 1).start()
+    for j in range(last_steps):
+        last_fetch(j).start()
+    hidden_ref[:, pl.ds(0, done)] = have_ref[...]
+    for copy in copies:
+        copy.wait()
+
+    def step(j, carry):
+        fetch(j, 0).wait()
+        fetch(j, 1).wait()
+        gate = jnp.dot(rows_ref[...], gate_ref[j], preferred_element_type=F32)
+        up = jnp.dot(rows_ref[...], up_ref[j], preferred_element_type=F32)
+        cols = pl.ds(pl.multiple_of(done + j * tile, tile), tile)
+        hidden_ref[:, cols] = (gate / (1.0 + jnp.exp(-gate)) * up).astype(BF16)
+        return carry
+
+    def last_step(j, carry):
+        last_fetch(j).wait()
+        out = jnp.dot(hidden_ref[...], down_ref[j], preferred_element_type=F32).astype(BF16)
+        cols = pl.ds(pl.multiple_of(j * last_tile, last_tile), last_tile)
+        start = 0
+        for ref in outs:
+            ref[:, cols] = out[start : start + ref.shape[0]]
+            start += ref.shape[0]
+        return carry
+
+    lax.fori_loop(0, steps, step, 0)
+    lax.fori_loop(0, last_steps, last_step, 0)
+
+
+def finish(pieces, have, sizes, w_gate, w_up, w_down, first, width):
+    depth, hidden = w_gate.shape
+    rows, done = have.shape
+    tile, last_tile = min(256, hidden - done), min(512, width)
+    steps, last_steps = (hidden - done) // tile, width // last_tile
+    vmem, anywhere = pl.BlockSpec(memory_space=pltpu.VMEM), pl.BlockSpec(memory_space=pl.ANY)
+    shapes = [(rows, hidden)] + [(n, width) for n in sizes]
+    hidden_out, *outs = pl.pallas_call(
+        functools.partial(finish_kernel, len(pieces), first),
+        out_shape=tuple(jax.ShapeDtypeStruct(shape, BF16) for shape in shapes),
+        in_specs=[anywhere] * len(pieces) + [vmem] + [anywhere] * 3,
+        out_specs=(vmem,) * len(shapes),
+        scratch_shapes=[
+            pltpu.VMEM((rows, depth), BF16),
+            pltpu.VMEM((steps, depth, tile), BF16),
+            pltpu.VMEM((steps, depth, tile), BF16),
+            pltpu.VMEM((last_steps, hidden, last_tile), BF16),
+            pltpu.SemaphoreType.DMA((len(pieces) + 2 * steps + last_steps,)),
+        ],
+        compiler_params=pltpu.CompilerParams(vmem_limit_bytes=49 * MIB),
+        cost_estimate=cost(
+            4 * rows * depth * (hidden - done) + 2 * rows * hidden * width,
+            4 * depth * (hidden - done) + 2 * hidden * width + 2 * rows * (depth + width),
+        ),
+        name="gate_up_down",
+    )(*pieces, have, w_gate, w_up, w_down)
+    return hidden_out, outs
+
+
 def down_kernel(count, first, *refs):
     pieces, w_hbm, outs = refs[:count], refs[count], refs[count + 1 : -3]
     rows_ref, w_ref, sems = refs[-3:]
@@ -346,17 +432,10 @@
     return lax.optimization_barrier((blocks, others))[0]
 
 
-def send_rows(packed, line):
+def send_rows(packed, line, way=1):
     size = packed.shape[0] // line
     parts = [packed[size * s : size * (s + 1)] for s in range(line)]
-    return [parts[0]] + [along_line(parts[s], s) for s in range(1, line)]
-
-
-def send_home(result, line):
-    size = result.shape[0] // line
-    parts = [result[size * s : size * (s + 1)] for s in range(line)]
-    came = [parts[0]] + [along_line(parts[s], -s) for s in range(1, line)]
-    return jnp.concatenate(came, axis=0)
+    return [parts[0]] + [along_line(parts[s], way * s) for s in range(1, line)]
 
 
 def plain_experts(packed, line, w_gate, w_up, w_down):
@@ -367,7 +446,8 @@
     out = down([hidden], (rows.shape[0],), w_down, 0, w_down.shape[1])[0]
     mine = lax.psum_scatter(out, ("context", "dp"), scatter_dimension=0, tiled=True)
     count = own.shape[0]
-    return send_home(add_up(mine[:count], swap_pair(mine[count:])).astype(BF16), line)
+    result = add_up(mine[:count], swap_pair(mine[count:])).astype(BF16)
+    return jnp.concatenate(send_rows(result, line, -1), axis=0)
 
 
 def square_experts(early, late, line, w_gate, w_up, w_down):
@@ -410,8 +490,8 @@
 
     late_two = jnp.concatenate([after(late_own, early_first), late_near], axis=0)
     late_four = cross(late_two, 1)
-    early_second = gate_up(after(early_rows, late_two), w_gate, w_up, most, hidden - most)
-    early_out = down([early_first, early_second], sizes, w_down, 0, width)
+    early_rows = after(early_rows, late_two)
+    early_out = finish(early_rows, early_first, sizes, w_gate, w_up, w_down, 0, width)[1]
     late_four = after(late_four, early_out)
     early_kept, early_go = home_first(early_out, late_four)
     early_far = cross(early_go, 1)
@@ -420,25 +500,31 @@
     late_first = gate_up(late_rows, w_gate, w_up, 0, hidden // 2)
     early_kept, early_go = home_second(after(early_kept, late_first), early_far)
     early_far = cross(early_go, 0)
-    late_second = gate_up(after(late_rows, early_go), w_gate, w_up, hidden // 2, hidden // 2)
-    early_result = home_third(after(early_kept, late_second), early_far)
-    late_hidden = [late_first, late_second]
-    out_left = down(after(late_hidden, early_result), sizes, w_down, 0, half)
+    late_rows = after(late_rows, early_go)
+    late_hidden, out_left = finish(late_rows, late_first, sizes, w_gate, w_up, w_down, 0, half)
+    early_result = home_third(after(early_kept, out_left[0]), early_far)
     left = home_first(out_left)
     left_far = cross(left[1], 1)
-    out_right = down(after(late_hidden, early_result, left[1]), sizes, w_down, half, half)
+    out_right = down([after(late_hidden, left[1])], sizes, w_down, half, half)
     left = home_second(after(left[0], out_right), left_far)
     left_far = cross(left[1], 0)
     right = home_first(after(out_right, left[1]))
     right_far = cross(right[1], 1)
-    early_back = send_home(after(early_result, right[1]), line)
-    left_kept, early_back = lax.optimization_barrier((left[0], early_back))
-    left_result = home_third(left_kept, left_far)
-    left_back = send_home(left_result, line)
+    left_result = home_third(after(left[0], right[1]), left_far)
     right = home_second(after(right[0], left_result), right_far)
     right_far = cross(right[1], 0)
-    late_back = [left_back, send_home(home_third(right[0], right_far), line)]
-    return early_back, jnp.concatenate(late_back, axis=1)
+    few, many = early_result.shape[0] // line, left_result.shape[0] // line
+    packed = []
+    for s in range(line):
+        mine = early_result[few * s : few * (s + 1)]
+        packed += [mine[:, :half], mine[:, half:], left_result[many * s : many * (s + 1)]]
+    left_came = send_rows(jnp.concatenate(packed, axis=0), line, -1)
+    right_result = home_third(right[0], right_far)
+    right_came = send_rows(right_result, line, -1)
+    left_came = after(left_came, right_result)
+    left_rows = [c[:few] for c in left_came] + [c[2 * few :] for c in left_came]
+    right_rows = [c[few : 2 * few] for c in left_came] + right_came
+    return [jnp.concatenate(rows, axis=0) for rows in (left_rows, right_rows)]
 
 
 def on_device(
@@ -538,11 +624,18 @@
         back = square_experts(*packed, line, w_gate[0], w_up[0], w_down[0])
     else:
         back = [plain_experts(packed[0], line, w_gate[0], w_up[0], w_down[0])]
-    expert_sum = jnp.dot(
-        jnp.concatenate(weighting, axis=1),
-        jnp.concatenate(back, axis=0).astype(F32),
-        precision=lax.Precision.HIGHEST,
-        preferred_element_type=F32,
+    weighting = jnp.concatenate(weighting, axis=1)
+    expert_sum = jnp.concatenate(
+        [
+            jnp.dot(
+                weighting,
+                rows.astype(F32),
+                precision=lax.Precision.HIGHEST,
+                preferred_element_type=F32,
+            )
+            for rows in back
+        ],
+        axis=1,
     )
     mixed = (stream_f + expert_sum).astype(BF16)
     return mixed.reshape(1, 1, row_count, width)

time: 214 us -> 210 us (0.981)
    pallas_call x0 -> x2, Pallas kernels: none -> 26.3 us  [finish(): pl.pallas_call(functools.partial(finish_kernel, len(pieces), first), out_...]
    pallas_call x4 -> x2, Pallas kernels: 31.9 us -> 16 us  [gate_up(): pl.pallas_call(functools.partial(gate_up_kernel, len(pieces), first), out...]
    pallas_call x3 -> x1, Pallas kernels: 16.8 us -> 5.36 us  [down(): pl.pallas_call(functools.partial(down_kernel, len(pieces), first), out_sh...]
    ppermute x27 -> x24, waiting for transfers between devices: 44.2 us -> 41.6 us  [along_line(): lax.ppermute(block, 'expert', [(e, (e + 2 * distance) % size) for e in ra...]
    ppermute x10, waiting for transfers between devices: 17.2 us -> 19.4 us  [cross(): return lax.ppermute(block, ('expert', 'context', 'dp'), route)]
    ppermute x27 -> x24, starting transfers between devices: 44 us -> 41.9 us  [along_line(): lax.ppermute(block, 'expert', [(e, (e + 2 * distance) % size) for e in ra...]
  transfers between devices with their start and end apart: 49 -> 46, of which waited for: 35 -> 33; matrix products, arithmetic and copies ran while one was open for 2% -> 3% of each run, Pallas kernels for 20% -> 16%
where the time goes in v4:
time: 210 us
  waiting for transfers between devices  72.2 us (34%)
  Pallas kernels  63.8 us (30%)
  starting transfers between devices  62.3 us (30%)
  other arithmetic  6.47 us (3%)
  local copies, waits for them, and re-layouts  2.54 us (1%)
    ppermute x24, starting transfers between devices, along_line(): lax.ppermute(block, 'expert', [(e, (e + 2 * distance) % size) for e in ra...  41.9 us
    ppermute x24, waiting for transfers between devices, along_line(): lax.ppermute(block, 'expert', [(e, (e + 2 * distance) % size) for e in ra...  41.6 us
    pallas_call x2, Pallas kernels, finish(): pl.pallas_call(functools.partial(finish_kernel, len(pieces), first), out_...  26.3 us
    ppermute x10, waiting for transfers between devices, cross(): return lax.ppermute(block, ('expert', 'context', 'dp'), route)  19.4 us
    pallas_call x2, Pallas kernels, gate_up(): pl.pallas_call(functools.partial(gate_up_kernel, len(pieces), first), out...  16 us
    ppermute x10, starting transfers between devices, cross(): return lax.ppermute(block, ('expert', 'context', 'dp'), route)  12.2 us
    pallas_call x1, Pallas kernels, run_out(): pl.pallas_call(functools.partial(out_kernel, channels // LANES, line, fir...  9.19 us
    ppermute x7, waiting for transfers between devices, shift(): lax.ppermute(block, axis, [(i, (i + distance) % size) for i in range(size)])  7.78 us
  transfers between devices with their start and end apart: 46, of which 33 were waited for; matrix products, arithmetic and copies ran while one was open for 3% of the time, Pallas kernels for 16%

profile of v4, /device:TPU:0, one launch (start us, length us, event | category | flops | bytes accessed | tf_op | source)
XLA Modules:
  0.0 209.7 jit_solution(8379000073332738589)
XLA Ops:
  0.8 2.3 %collective-permute-start = (bf16[3,1024]{1,0:T(4,128)(2,1)S(1)}, bf16[3,1024]{1,0:T(4,128)(2,1)S(1)}, u32[]{:S(2)}, u32[]{:S(2)}) collective-permute-start(bf16[3,1024]{1,0:T(4,128)(2,1)S(1)} %slice_bitcast_fusion.3), channel_id=1, source_target_pairs={{0,2},{1,3},{4,6},{5,7},{8,10},{9,11},{12,14},{13,15},{16,18},{17,... | collective-permute-start | bytes 18440 | tf_op jit(solution)/shard_map/ppermute | solution.py:24
  8.4 2.5 %collective-permute-start.1 = (bf16[64,288]{1,0:T(8,128)(2,1)S(1)}, bf16[64,288]{1,0:T(8,128)(2,1)S(1)}, u32[]{:S(2)}, u32[]{:S(2)}) collective-permute-start(bf16[64,288]{1,0:T(8,128)(2,1)S(1)} %get-tuple-element.148), channel_id=1, source_target_pairs={{0,8},{4,12},{8,16},{12,20},{16,24},{20,28},{24,0},{28,4},{1,9},{5... | collective-permute-start | bytes 110600 | tf_op jit(solution)/shard_map/ppermute | solution.py:417
  10.9 2.6 %collective-permute-start.2 = (bf16[64,288]{1,0:T(8,128)(2,1)S(1)}, bf16[64,288]{1,0:T(8,128)(2,1)S(1)}, u32[]{:S(2)}, u32[]{:S(2)}) collective-permute-start(bf16[64,288]{1,0:T(8,128)(2,1)S(1)} %get-tuple-element.150), channel_id=1, source_target_pairs={{0,16},{4,20},{8,24},{12,28},{16,0},{20,4},{24,8},{28,12},{1,17},{... | collective-permute-start | bytes 110600 | tf_op jit(solution)/shard_map/ppermute | solution.py:417
  19.2 2.5 %collective-permute-done.4 = bf16[64,288]{1,0:T(8,128)(2,1)S(1)} collective-permute-done((bf16[64,288]{1,0:T(8,128)(2,1)S(1)}, bf16[64,288]{1,0:T(8,128)(2,1)S(1)}, u32[]{:S(2)}, u32[]{:S(2)}) %collective-permute-start.4) | collective-permute-done | bytes 36896 | tf_op jit(solution)/shard_map/ppermute | solution.py:34
  22.4 3.1 %collective-permute-start.6 = (bf16[64,288]{1,0:T(8,128)(2,1)S(1)}, bf16[64,288]{1,0:T(8,128)(2,1)S(1)}, u32[]{:S(2)}, u32[]{:S(2)}) collective-permute-start(bf16[64,288]{1,0:T(8,128)(2,1)S(1)} %add_convert_fusion.10.refs_0_), channel_id=1, source_target_pairs={{0,16},{4,20},{8,24},{12,28},{16,0},{20,4},{24,8},{28,12},{1,17},{... | collective-permute-start | bytes 110600 | tf_op jit(solution)/shard_map/ppermute | solution.py:417
  25.8 2.1 collective-permute-done.5.refs_1_
  29.6 6.9 %state_scan.1 = (f32[2048,128]{1,0:T(8,128)S(1)}, f32[2048,128]{1,0:T(8,128)S(1)}, f32[16,8,128]{2,1,0:T(8,128)S(1)}, bf16[256,32]{1,0:T(8,128)(2,1)S(1)}) custom-call(s32[2]{0:T(128)S(1)} %pad_add_fusion.place_ref.at_ref, bf16[64,288]{1,0:T(8,128)(2,1)S(1)} %add_convert_fusion.10.refs_0_, bf16[64,288]{1,0:T(8,128)(2,1)S(1)} %collective-permute-done.5.refs_1_, ...), custom_call_target="tpu_custom_call" | custom-call | flops 200000000 | bytes 4194304 | tf_op jit(solution)/shard_map/state_scan/pallas_call | solution.py:104
  38.7 9.2 %readout_project.1 = (bf16[128,2560]{1,0:T(8,128)(2,1)S(1)}, bf16[128,2560]{1,0:T(8,128)(2,1)S(1)}, bf16[4,64,1536]{2,1,0:T(8,128)(2,1)S(1)}) custom-call(s32[2]{0:T(128)S(1)} %pad_add_fusion.place_ref.at_ref, f32[2048,128]{1,0:T(8,128)S(1)} %get-tuple-element.59.y_ref, f32[2048,128]{1,0:T(8,128)S(1)} %get-tuple-element.60.sum_ref, ...), custom_call_target="tpu_custom_call" | custom-call | flops 2147483648 | bytes 16777216 | tf_op jit(solution)/shard_map/readout_project/pallas_call | solution.py:198
  50.4 2.1 %collective-permute-start.14 = (bf16[64,1536]{1,0:T(8,128)(2,1)S(1)}, bf16[64,1536]{1,0:T(8,128)(2,1)S(1)}, u32[]{:S(2)}, u32[]{:S(2)}) collective-permute-start(bf16[64,1536]{1,0:T(8,128)(2,1)S(1)} %get-tuple-element.119), channel_id=1, source_target_pairs={{0,16},{4,20},{8,24},{12,28},{16,0},{20,4},{24,8},{28,12},{1,17},{... | collective-permute-start | bytes 589832 | tf_op jit(solution)/shard_map/ppermute | solution.py:417
  53.6 5.7 %collective-permute-done.13 = bf16[64,1536]{1,0:T(8,128)(2,1)S(1)} collective-permute-done((bf16[64,1536]{1,0:T(8,128)(2,1)S(1)}, bf16[64,1536]{1,0:T(8,128)(2,1)S(1)}, u32[]{:S(2)}, u32[]{:S(2)}) %collective-permute-start.13) | collective-permute-done | bytes 196640 | tf_op jit(solution)/shard_map/ppermute | solution.py:417
  59.3 7.6 %collective-permute-done.14 = bf16[64,1536]{1,0:T(8,128)(2,1)S(1)} collective-permute-done((bf16[64,1536]{1,0:T(8,128)(2,1)S(1)}, bf16[64,1536]{1,0:T(8,128)(2,1)S(1)}, u32[]{:S(2)}, u32[]{:S(2)}) %collective-permute-start.14) | collective-permute-done | bytes 196640 | tf_op jit(solution)/shard_map/ppermute | solution.py:417
  67.8 4.3 %collective-permute-start.10 = (bf16[32,2560]{1,0:T(8,128)(2,1)S(1)}, bf16[32,2560]{1,0:T(8,128)(2,1)S(1)}, u32[]{:S(2)}, u32[]{:S(2)}) collective-permute-start(bf16[32,2560]{1,0:T(8,128)(2,1)S(1)} %get-tuple-element.120), channel_id=1, source_target_pairs={{0,8},{4,12},{8,16},{12,20},{16,24},{20,28},{24,0},{28,4},{1,9},{5... | collective-permute-start | bytes 491528 | tf_op jit(solution)/shard_map/ppermute | solution.py:417
  74.5 2.2 %collective-permute-done.10 = bf16[32,2560]{1,0:T(8,128)(2,1)S(1)} collective-permute-done((bf16[32,2560]{1,0:T(8,128)(2,1)S(1)}, bf16[32,2560]{1,0:T(8,128)(2,1)S(1)}, u32[]{:S(2)}, u32[]{:S(2)}) %collective-permute-start.10) | collective-permute-done | bytes 163872 | tf_op jit(solution)/shard_map/ppermute | solution.py:417
  76.7 5.6 %collective-permute-done.11 = bf16[32,2560]{1,0:T(8,128)(2,1)S(1)} collective-permute-done((bf16[32,2560]{1,0:T(8,128)(2,1)S(1)}, bf16[32,2560]{1,0:T(8,128)(2,1)S(1)}, u32[]{:S(2)}, u32[]{:S(2)}) %collective-permute-start.11) | collective-permute-done | bytes 163872 | tf_op jit(solution)/shard_map/ppermute | solution.py:417
  83.0 4.0 %collective-permute-start.17 = (bf16[8,4096]{1,0:T(8,128)(2,1)S(1)}, bf16[8,4096]{1,0:T(8,128)(2,1)S(1)}, u32[]{:S(2)}, u32[]{:S(2)}) collective-permute-start(bf16[8,4096]{1,0:T(8,128)(2,1)S(1)} %get-tuple-element.146), channel_id=1, source_target_pairs={{0,8},{4,12},{8,16},{12,20},{16,24},{20,28},{24,0},{28,4},{1,9},{5... | collective-permute-start | bytes 196616 | tf_op jit(solution)/shard_map/ppermute | solution.py:417
  87.1 2.8 %collective-permute-start.18 = (bf16[8,4096]{1,0:T(8,128)(2,1)S(1)}, bf16[8,4096]{1,0:T(8,128)(2,1)S(1)}, u32[]{:S(2)}, u32[]{:S(2)}) collective-permute-start(bf16[8,4096]{1,0:T(8,128)(2,1)S(1)} %get-tuple-element.145), channel_id=1, source_target_pairs={{0,16},{4,20},{8,24},{12,28},{16,0},{20,4},{24,8},{28,12},{1,17},{... | collective-permute-start | bytes 196616 | tf_op jit(solution)/shard_map/ppermute | solution.py:417
  102.4 2.0 collective-permute-done.24
  104.4 5.6 %collective-permute-done.21.refs_1_ = bf16[64,4096]{1,0:T(8,128)(2,1)S(1)} collective-permute-done((bf16[64,4096]{1,0:T(8,128)(2,1)S(1)}, bf16[64,4096]{1,0:T(8,128)(2,1)S(1)}, u32[]{:S(2)}, u32[]{:S(2)}) %collective-permute-start.21) | collective-permute-done | bytes 524320 | tf_op jit(solution)/shard_map/ppermute | solution.py:428
  111.9 6.3 %gate_up.2.refs_4_ = bf16[256,768]{1,0:T(8,128)(2,1)S(1)} custom-call(bf16[64,4096]{1,0:T(8,128)(2,1)S(1)} %constant_dynamic-update-slice_fusion.refs_0_, bf16[64,4096]{1,0:T(8,128)(2,1)S(1)} %collective-permute-done.21.refs_1_, bf16[64,4096]{1,0:T(8,128)(2,1)S(1)} %collective-permute-done.22.refs_2_, bf16[64,4096]{1,0:T(8,128)(2,1)S(1)} %collective-permute-done.23.refs_3_, ...), custom_call_target="tpu_custom_call" | custom-call | flops 3221225472 | bytes 14680064 | tf_op jit(solution)/shard_map/gate_up/pallas_call | solution.py:259
  120.9 11.9 %gate_up_down.2 = (bf16[256,1536]{1,0:T(8,128)(2,1)}, bf16[128,4096]{1,0:T(8,128)(2,1)S(1)}, bf16[128,4096]{1,0:T(8,128)(2,1)}) custom-call(bf16[64,4096]{1,0:T(8,128)(2,1)S(1)} %constant_dynamic-update-slice_fusion.refs_0_, bf16[64,4096]{1,0:T(8,128)(2,1)S(1)} %collective-permute-done.21.refs_1_, bf16[64,4096]{1,0:T(8,128)(2,1)S(1)} %collective-permute-done.22.refs_2_, ...), custom_call_target="tpu_custom_call" | custom-call | flops 6442450944 | bytes 29360128 | tf_op jit(solution)/shard_map/gate_up_down/pallas_call | solution.py:340
  134.2 2.3 %collective-permute-done.29 = bf16[128,4096]{1,0:T(8,128)(2,1)S(1)} collective-permute-done((bf16[128,4096]{1,0:T(8,128)(2,1)}, bf16[128,4096]{1,0:T(8,128)(2,1)S(1)}, u32[]{:S(2)}, u32[]{:S(2)}) %collective-permute-start.29) | collective-permute-done | bytes 1048608 | tf_op jit(solution)/shard_map/ppermute | solution.py:29
  138.6 9.7 %gate_up.3.refs_4_ = bf16[512,768]{1,0:T(8,128)(2,1)S(1)} custom-call(bf16[128,4096]{1,0:T(8,128)(2,1)S(1)} %constant_dynamic-update-slice_fusion.9.refs_0_, bf16[128,4096]{1,0:T(8,128)(2,1)S(1)} %collective-permute-done.28.refs_1_, bf16[128,4096]{1,0:T(8,128)(2,1)S(1)} %collective-permute-done.30.refs_2_, ...), custom_call_target="tpu_custom_call" | custom-call | flops 6442450944 | bytes 16777216 | tf_op jit(solution)/shard_map/gate_up/pallas_call | solution.py:259
  148.5 14.3 %gate_up_down.3 = (bf16[512,1536]{1,0:T(8,128)(2,1)}, bf16[256,2048]{1,0:T(8,128)(2,1)S(1)}, bf16[256,2048]{1,0:T(8,128)(2,1)S(1)}) custom-call(bf16[128,4096]{1,0:T(8,128)(2,1)S(1)} %constant_dynamic-update-slice_fusion.9.refs_0_, bf16[128,4096]{1,0:T(8,128)(2,1)S(1)} %collective-permute-done.28.refs_1_, bf16[128,4096]{1,0:T(8,128)(2,1)} %copy-done.2, ...), custom_call_target="tpu_custom_call" | custom-call | flops 9663676416 | bytes 25165824 | tf_op jit(solution)/shard_map/gate_up_down/pallas_call | solution.py:340
  163.1 2.5 %collective-permute-done.34 = bf16[256,2048]{1,0:T(8,128)(2,1)S(1)} collective-permute-done((bf16[256,2048]{1,0:T(8,128)(2,1)S(1)}, bf16[256,2048]{1,0:T(8,128)(2,1)S(1)}, u32[]{:S(2)}, u32[]{:S(2)}) %collective-permute-start.34) | collective-permute-done | bytes 1048608 | tf_op jit(solution)/shard_map/ppermute | solution.py:29
  168.1 5.4 %down.1 = (bf16[256,2048]{1,0:T(8,128)(2,1)S(1)}, bf16[256,2048]{1,0:T(8,128)(2,1)S(1)}) custom-call(bf16[512,1536]{1,0:T(8,128)(2,1)S(1)} %copy-done.4, bf16[1536,4096]{1,0:T(8,128)(2,1)} %bitcast.75), custom_call_target="tpu_custom_call" | custom-call | flops 3221225472 | bytes 9961472 | tf_op jit(solution)/shard_map/down/pallas_call | solution.py:395
  173.5 4.3 %collective-permute-done.35 = bf16[128,2048]{1,0:T(8,128)(2,1)S(1)} collective-permute-done((bf16[128,2048]{1,0:T(8,128)(2,1)S(1)}, bf16[128,2048]{1,0:T(8,128)(2,1)S(1)}, u32[]{:S(2)}, u32[]{:S(2)}) %collective-permute-start.35) | collective-permute-done | bytes 524320 | tf_op jit(solution)/shard_map/ppermute | solution.py:428
  181.4 4.2 %collective-permute-done.37 = bf16[64,2048]{1,0:T(8,128)(2,1)S(1)} collective-permute-done((bf16[64,2048]{1,0:T(8,128)(2,1)S(1)}, bf16[64,2048]{1,0:T(8,128)(2,1)S(1)}, u32[]{:S(2)}, u32[]{:S(2)}) %collective-permute-start.37) | collective-permute-done | bytes 262176 | tf_op jit(solution)/shard_map/ppermute | solution.py:428
  187.1 2.4 %collective-permute-start.39 = (bf16[32,2048]{1,0:T(8,128)(2,1)S(1)}, bf16[32,2048]{1,0:T(8,128)(2,1)S(1)}, u32[]{:S(2)}, u32[]{:S(2)}) collective-permute-start(bf16[32,2048]{1,0:T(8,128)(2,1)S(1)} %pad_maximum_fusion.3), channel_id=1, source_target_pairs={{0,16},{4,20},{8,24},{12,28},{16,0},{20,4},{24,8},{28,12},{1,17},{... | collective-permute-start | bytes 393224 | tf_op jit(solution)/shard_map/ppermute | solution.py:417
  191.3 3.1 %collective-permute-start.38 = (bf16[32,2048]{1,0:T(8,128)(2,1)S(1)}, bf16[32,2048]{1,0:T(8,128)(2,1)S(1)}, u32[]{:S(2)}, u32[]{:S(2)}) collective-permute-start(bf16[32,2048]{1,0:T(8,128)(2,1)S(1)} %pad_maximum_fusion.2), channel_id=1, source_target_pairs={{0,24},{4,28},{8,0},{12,4},{16,8},{20,12},{24,16},{28,20},{1,25},{... | collective-permute-start | bytes 393224 | tf_op jit(solution)/shard_map/ppermute | solution.py:417
  194.4 2.1 %collective-permute-done.42 = bf16[64,2048]{1,0:T(8,128)(2,1)S(1)} collective-permute-done((bf16[64,2048]{1,0:T(8,128)(2,1)S(1)}, bf16[64,2048]{1,0:T(8,128)(2,1)S(1)}, u32[]{:S(2)}, u32[]{:S(2)}) %collective-permute-start.42) | collective-permute-done | bytes 262176 | tf_op jit(solution)/shard_map/ppermute | solution.py:428
  198.9 2.6 %collective-permute-start.43 = (bf16[16,2048]{1,0:T(8,128)(2,1)S(1)}, bf16[16,2048]{1,0:T(8,128)(2,1)S(1)}, u32[]{:S(2)}, u32[]{:S(2)}) collective-permute-start(bf16[16,2048]{1,0:T(8,128)(2,1)S(1)} %get-tuple-element.129), channel_id=1, source_target_pairs={{0,24},{4,28},{8,0},{12,4},{16,8},{20,12},{24,16},{28,20},{1,25},{... | collective-permute-start | bytes 196616 | tf_op jit(solution)/shard_map/ppermute | solution.py:417
  203.9 4.6 %collective-permute-done.44 = bf16[16,2048]{1,0:T(8,128)(2,1)S(1)} collective-permute-done((bf16[16,2048]{1,0:T(8,128)(2,1)S(1)}, bf16[16,2048]{1,0:T(8,128)(2,1)S(1)}, u32[]{:S(2)}, u32[]{:S(2)}) %collective-permute-start.44) | collective-permute-done | bytes 65568 | tf_op jit(solution)/shard_map/ppermute | solution.py:417
  (174 shorter events, 60.0 us)
Async XLA Ops:
  8.4 7.2 %collective-permute-start.1 = (bf16[64,288]{1,0:T(8,128)(2,1)S(1)}, bf16[64,288]{1,0:T(8,128)(2,1)S(1)}, u32[]{:S(2)}, u32[]{:S(2)}) collective-permute-start(bf16[64,288]{1,0:T(8,128)(2,1)S(1)} %get-tuple-element.148), channel_id=1, source_target_pairs={{0,8},{4,12},{8,16},{12,20},{16,24},{20,28},{24,0},{28,4},{1,9},{5... | collective-permute-start | bytes 110600 | tf_op jit(solution)/shard_map/ppermute | solution.py:417
  10.9 6.2 %collective-permute-start.2 = (bf16[64,288]{1,0:T(8,128)(2,1)S(1)}, bf16[64,288]{1,0:T(8,128)(2,1)S(1)}, u32[]{:S(2)}, u32[]{:S(2)}) collective-permute-start(bf16[64,288]{1,0:T(8,128)(2,1)S(1)} %get-tuple-element.150), channel_id=1, source_target_pairs={{0,16},{4,20},{8,24},{12,28},{16,0},{20,4},{24,8},{28,12},{1,17},{... | collective-permute-start | bytes 110600 | tf_op jit(solution)/shard_map/ppermute | solution.py:417
  22.4 6.2 %collective-permute-start.6 = (bf16[64,288]{1,0:T(8,128)(2,1)S(1)}, bf16[64,288]{1,0:T(8,128)(2,1)S(1)}, u32[]{:S(2)}, u32[]{:S(2)}) collective-permute-start(bf16[64,288]{1,0:T(8,128)(2,1)S(1)} %add_convert_fusion.10.refs_0_), channel_id=1, source_target_pairs={{0,16},{4,20},{8,24},{12,28},{16,0},{20,4},{24,8},{28,12},{1,17},{... | collective-permute-start | bytes 110600 | tf_op jit(solution)/shard_map/ppermute | solution.py:417
  47.9 19.6 %collective-permute-start.9 = (bf16[128,2560]{1,0:T(8,128)(2,1)S(1)}, bf16[128,2560]{1,0:T(8,128)(2,1)S(1)}, u32[]{:S(2)}, u32[]{:S(2)}) collective-permute-start(bf16[128,2560]{1,0:T(8,128)(2,1)S(1)} %get-tuple-element.64), channel_id=1, source_target_pairs={{0,4},{4,0},{8,12},{12,8},{16,20},{20,16},{24,28},{28,24},{1,5},{5... | collective-permute-start | bytes 1966088 | tf_op jit(solution)/shard_map/ppermute | solution.py:34
  49.5 9.8 %collective-permute-start.13 = (bf16[64,1536]{1,0:T(8,128)(2,1)S(1)}, bf16[64,1536]{1,0:T(8,128)(2,1)S(1)}, u32[]{:S(2)}, u32[]{:S(2)}) collective-permute-start(bf16[64,1536]{1,0:T(8,128)(2,1)S(1)} %get-tuple-element.117), channel_id=1, source_target_pairs={{0,8},{4,12},{8,16},{12,20},{16,24},{20,28},{24,0},{28,4},{1,9},{5... | collective-permute-start | bytes 589832 | tf_op jit(solution)/shard_map/ppermute | solution.py:417
  50.4 16.5 %collective-permute-start.14 = (bf16[64,1536]{1,0:T(8,128)(2,1)S(1)}, bf16[64,1536]{1,0:T(8,128)(2,1)S(1)}, u32[]{:S(2)}, u32[]{:S(2)}) collective-permute-start(bf16[64,1536]{1,0:T(8,128)(2,1)S(1)} %get-tuple-element.119), channel_id=1, source_target_pairs={{0,16},{4,20},{8,24},{12,28},{16,0},{20,4},{24,8},{28,12},{1,17},{... | collective-permute-start | bytes 589832 | tf_op jit(solution)/shard_map/ppermute | solution.py:417
  52.5 14.4 %collective-permute-start.15 = (bf16[64,1536]{1,0:T(8,128)(2,1)S(1)}, bf16[64,1536]{1,0:T(8,128)(2,1)S(1)}, u32[]{:S(2)}, u32[]{:S(2)}) collective-permute-start(bf16[64,1536]{1,0:T(8,128)(2,1)S(1)} %get-tuple-element.118), channel_id=1, source_target_pairs={{0,24},{4,28},{8,0},{12,4},{16,8},{20,12},{24,16},{28,20},{1,25},{... | collective-permute-start | bytes 589832 | tf_op jit(solution)/shard_map/ppermute | solution.py:417
  67.0 7.5 %collective-permute-start.16 = (bf16[32,1536]{1,0:T(8,128)(2,1)S(1)}, bf16[32,1536]{1,0:T(8,128)(2,1)S(1)}, u32[]{:S(2)}, u32[]{:S(2)}) collective-permute-start(bf16[32,1536]{1,0:T(8,128)(2,1)S(1)} %slice.456), channel_id=1, source_target_pairs={{0,4},{4,0},{8,12},{12,8},{16,20},{20,16},{24,28},{28,24},{1,5},{5... | collective-permute-start | bytes 294920 | tf_op jit(solution)/shard_map/ppermute | solution.py:34
  67.8 8.9 %collective-permute-start.10 = (bf16[32,2560]{1,0:T(8,128)(2,1)S(1)}, bf16[32,2560]{1,0:T(8,128)(2,1)S(1)}, u32[]{:S(2)}, u32[]{:S(2)}) collective-permute-start(bf16[32,2560]{1,0:T(8,128)(2,1)S(1)} %get-tuple-element.120), channel_id=1, source_target_pairs={{0,8},{4,12},{8,16},{12,20},{16,24},{20,28},{24,0},{28,4},{1,9},{5... | collective-permute-start | bytes 491528 | tf_op jit(solution)/shard_map/ppermute | solution.py:417
  72.1 10.3 %collective-permute-start.11 = (bf16[32,2560]{1,0:T(8,128)(2,1)S(1)}, bf16[32,2560]{1,0:T(8,128)(2,1)S(1)}, u32[]{:S(2)}, u32[]{:S(2)}) collective-permute-start(bf16[32,2560]{1,0:T(8,128)(2,1)S(1)} %get-tuple-element.122), channel_id=1, source_target_pairs={{0,16},{4,20},{8,24},{12,28},{16,0},{20,4},{24,8},{28,12},{1,17},{... | collective-permute-start | bytes 491528 | tf_op jit(solution)/shard_map/ppermute | solution.py:417
  72.5 9.9 %collective-permute-start.12 = (bf16[32,2560]{1,0:T(8,128)(2,1)S(1)}, bf16[32,2560]{1,0:T(8,128)(2,1)S(1)}, u32[]{:S(2)}, u32[]{:S(2)}) collective-permute-start(bf16[32,2560]{1,0:T(8,128)(2,1)S(1)} %get-tuple-element.121), channel_id=1, source_target_pairs={{0,24},{4,28},{8,0},{12,4},{16,8},{20,12},{24,16},{28,20},{1,25},{... | collective-permute-start | bytes 491528 | tf_op jit(solution)/shard_map/ppermute | solution.py:417
  83.0 8.8 %collective-permute-start.17 = (bf16[8,4096]{1,0:T(8,128)(2,1)S(1)}, bf16[8,4096]{1,0:T(8,128)(2,1)S(1)}, u32[]{:S(2)}, u32[]{:S(2)}) collective-permute-start(bf16[8,4096]{1,0:T(8,128)(2,1)S(1)} %get-tuple-element.146), channel_id=1, source_target_pairs={{0,8},{4,12},{8,16},{12,20},{16,24},{20,28},{24,0},{28,4},{1,9},{5... | collective-permute-start | bytes 196616 | tf_op jit(solution)/shard_map/ppermute | solution.py:417
  87.1 6.6 %collective-permute-start.18 = (bf16[8,4096]{1,0:T(8,128)(2,1)S(1)}, bf16[8,4096]{1,0:T(8,128)(2,1)S(1)}, u32[]{:S(2)}, u32[]{:S(2)}) collective-permute-start(bf16[8,4096]{1,0:T(8,128)(2,1)S(1)} %get-tuple-element.145), channel_id=1, source_target_pairs={{0,16},{4,20},{8,24},{12,28},{16,0},{20,4},{24,8},{28,12},{1,17},{... | collective-permute-start | bytes 196616 | tf_op jit(solution)/shard_map/ppermute | solution.py:417
  94.3 6.4 %collective-permute-start.20 = (bf16[32,4096]{1,0:T(8,128)(2,1)S(1)}, bf16[32,4096]{1,0:T(8,128)(2,1)S(1)}, u32[]{:S(2)}, u32[]{:S(2)}) collective-permute-start(bf16[32,4096]{1,0:T(8,128)(2,1)S(1)} %pad_maximum_fusion), channel_id=1, source_target_pairs={{0,4},{1,5},{2,3},{3,2},{4,0},{5,1},{6,7},{7,6},{8,12},{9,13},{10,... | collective-permute-start | bytes 786440 | tf_op jit(solution)/shard_map/ppermute | solution.py:428
  96.0 8.4 %collective-permute-start.24 = (bf16[16,4096]{1,0:T(8,128)(2,1)S(1)}, bf16[16,4096]{1,0:T(8,128)(2,1)S(1)}, u32[]{:S(2)}, u32[]{:S(2)}) collective-permute-start(bf16[16,4096]{1,0:T(8,128)(2,1)S(1)} %get-tuple-element.125), channel_id=1, source_target_pairs={{0,8},{4,12},{8,16},{12,20},{16,24},{20,28},{24,0},{28,4},{1,9},{5... | collective-permute-start | bytes 393224 | tf_op jit(solution)/shard_map/ppermute | solution.py:417
  97.3 12.7 %collective-permute-start.25 = (bf16[16,4096]{1,0:T(8,128)(2,1)S(1)}, bf16[16,4096]{1,0:T(8,128)(2,1)S(1)}, u32[]{:S(2)}, u32[]{:S(2)}) collective-permute-start(bf16[16,4096]{1,0:T(8,128)(2,1)S(1)} %get-tuple-element.124), channel_id=1, source_target_pairs={{0,16},{4,20},{8,24},{12,28},{16,0},{20,4},{24,8},{28,12},{1,17},{... | collective-permute-start | bytes 393224 | tf_op jit(solution)/shard_map/ppermute | solution.py:417
  99.0 11.1 %collective-permute-start.26 = (bf16[16,4096]{1,0:T(8,128)(2,1)S(1)}, bf16[16,4096]{1,0:T(8,128)(2,1)S(1)}, u32[]{:S(2)}, u32[]{:S(2)}) collective-permute-start(bf16[16,4096]{1,0:T(8,128)(2,1)S(1)} %get-tuple-element.123), channel_id=1, source_target_pairs={{0,24},{4,28},{8,0},{12,4},{16,8},{20,12},{24,16},{28,20},{1,25},{... | collective-permute-start | bytes 393224 | tf_op jit(solution)/shard_map/ppermute | solution.py:417
  100.8 9.2 %collective-permute-start.21 = (bf16[64,4096]{1,0:T(8,128)(2,1)S(1)}, bf16[64,4096]{1,0:T(8,128)(2,1)S(1)}, u32[]{:S(2)}, u32[]{:S(2)}) collective-permute-start(bf16[64,4096]{1,0:T(8,128)(2,1)S(1)} %constant_dynamic-update-slice_fusion.refs_0_), channel_id=1, source_target_pairs={{0,1},{1,0},{2,6},{3,7},{4,5},{5,4},{6,2},{7,3},{8,9},{9,8},{10,14... | collective-permute-start | bytes 1572872 | tf_op jit(solution)/shard_map/ppermute | solution.py:428
  102.3 9.4 %collective-permute-start.22 = (bf16[64,4096]{1,0:T(8,128)(2,1)S(1)}, bf16[64,4096]{1,0:T(8,128)(2,1)S(1)}, u32[]{:S(2)}, u32[]{:S(2)}) collective-permute-start(bf16[64,4096]{1,0:T(8,128)(2,1)S(1)} %constant_dynamic-update-slice_fusion.refs_0_), channel_id=1, source_target_pairs={{0,2},{2,0},{1,3},{3,1},{4,6},{6,4},{5,7},{7,5},{8,10},{10,8},{9,1... | collective-permute-start | bytes 1572872 | tf_op jit(solution)/shard_map/ppermute | solution.py:29
  110.1 9.2 %collective-permute-start.27 = (bf16[64,4096]{1,0:T(8,128)(2,1)S(1)}, bf16[64,4096]{1,0:T(8,128)(2,1)S(1)}, u32[]{:S(2)}, u32[]{:S(2)}) collective-permute-start(bf16[64,4096]{1,0:T(8,128)(2,1)S(1)} %constant_dynamic-update-slice_fusion.5), channel_id=1, source_target_pairs={{0,4},{1,5},{2,3},{3,2},{4,0},{5,1},{6,7},{7,6},{8,12},{9,13},{10,... | collective-permute-start | bytes 1572872 | tf_op jit(solution)/shard_map/ppermute | solution.py:428
  119.4 14.9 %collective-permute-start.28 = (bf16[128,4096]{1,0:T(8,128)(2,1)S(1)}, bf16[128,4096]{1,0:T(8,128)(2,1)S(1)}, u32[]{:S(2)}, u32[]{:S(2)}) collective-permute-start(bf16[128,4096]{1,0:T(8,128)(2,1)S(1)} %constant_dynamic-update-slice_fusion.9.refs_0_), channel_id=1, source_target_pairs={{0,1},{1,0},{2,6},{3,7},{4,5},{5,4},{6,2},{7,3},{8,9},{9,8},{10,14... | collective-permute-start | bytes 3145736 | tf_op jit(solution)/shard_map/ppermute | solution.py:428
  136.7 11.7 %collective-permute-start.32 = (bf16[64,4096]{1,0:T(8,128)(2,1)S(1)}, bf16[64,4096]{1,0:T(8,128)(2,1)S(1)}, u32[]{:S(2)}, u32[]{:S(2)}) collective-permute-start(bf16[64,4096]{1,0:T(8,128)(2,1)S(1)} %add_convert_fusion.3), channel_id=1, source_target_pairs={{0,1},{1,0},{2,6},{3,7},{4,5},{5,4},{6,2},{7,3},{8,9},{9,8},{10,14... | collective-permute-start | bytes 1572872 | tf_op jit(solution)/shard_map/ppermute | solution.py:428
  165.7 12.1 %collective-permute-start.35 = (bf16[128,2048]{1,0:T(8,128)(2,1)S(1)}, bf16[128,2048]{1,0:T(8,128)(2,1)S(1)}, u32[]{:S(2)}, u32[]{:S(2)}) collective-permute-start(bf16[128,2048]{1,0:T(8,128)(2,1)S(1)} %add_convert_fusion.2), channel_id=1, source_target_pairs={{0,1},{1,0},{2,6},{3,7},{4,5},{5,4},{6,2},{7,3},{8,9},{9,8},{10,14... | collective-permute-start | bytes 1572872 | tf_op jit(solution)/shard_map/ppermute | solution.py:428
  166.5 11.4 %collective-permute-start.33 = (bf16[32,4096]{1,0:T(8,128)(2,1)S(1)}, bf16[32,4096]{1,0:T(8,128)(2,1)S(1)}, u32[]{:S(2)}, u32[]{:S(2)}) collective-permute-start(bf16[32,4096]{1,0:T(8,128)(2,1)S(1)} %add_convert_fusion.9), channel_id=1, source_target_pairs={{0,4},{1,5},{2,3},{3,2},{4,0},{5,1},{6,7},{7,6},{8,12},{9,13},{10,... | collective-permute-start | bytes 786440 | tf_op jit(solution)/shard_map/ppermute | solution.py:428
  178.1 7.4 %collective-permute-start.37 = (bf16[64,2048]{1,0:T(8,128)(2,1)S(1)}, bf16[64,2048]{1,0:T(8,128)(2,1)S(1)}, u32[]{:S(2)}, u32[]{:S(2)}) collective-permute-start(bf16[64,2048]{1,0:T(8,128)(2,1)S(1)} %add_convert_fusion.7), channel_id=1, source_target_pairs={{0,4},{1,5},{2,3},{3,2},{4,0},{5,1},{6,7},{7,6},{8,12},{9,13},{10,... | collective-permute-start | bytes 786440 | tf_op jit(solution)/shard_map/ppermute | solution.py:428
  180.7 9.2 %collective-permute-start.41 = (bf16[128,2048]{1,0:T(8,128)(2,1)S(1)}, bf16[128,2048]{1,0:T(8,128)(2,1)S(1)}, u32[]{:S(2)}, u32[]{:S(2)}) collective-permute-start(bf16[128,2048]{1,0:T(8,128)(2,1)S(1)} %add_convert_fusion.1), channel_id=1, source_target_pairs={{0,1},{1,0},{2,6},{3,7},{4,5},{5,4},{6,2},{7,3},{8,9},{9,8},{10,14... | collective-permute-start | bytes 1572872 | tf_op jit(solution)/shard_map/ppermute | solution.py:428
  185.7 10.9 %collective-permute-start.40 = (bf16[32,2048]{1,0:T(8,128)(2,1)S(1)}, bf16[32,2048]{1,0:T(8,128)(2,1)S(1)}, u32[]{:S(2)}, u32[]{:S(2)}) collective-permute-start(bf16[32,2048]{1,0:T(8,128)(2,1)S(1)} %pad_maximum_fusion.4), channel_id=1, source_target_pairs={{0,8},{4,12},{8,16},{12,20},{16,24},{20,28},{24,0},{28,4},{1,9},{5... | collective-permute-start | bytes 393224 | tf_op jit(solution)/shard_map/ppermute | solution.py:417
  187.1 10.3 %collective-permute-start.39 = (bf16[32,2048]{1,0:T(8,128)(2,1)S(1)}, bf16[32,2048]{1,0:T(8,128)(2,1)S(1)}, u32[]{:S(2)}, u32[]{:S(2)}) collective-permute-start(bf16[32,2048]{1,0:T(8,128)(2,1)S(1)} %pad_maximum_fusion.3), channel_id=1, source_target_pairs={{0,16},{4,20},{8,24},{12,28},{16,0},{20,4},{24,8},{28,12},{1,17},{... | collective-permute-start | bytes 393224 | tf_op jit(solution)/shard_map/ppermute | solution.py:417
  190.1 6.4 %collective-permute-start.42 = (bf16[64,2048]{1,0:T(8,128)(2,1)S(1)}, bf16[64,2048]{1,0:T(8,128)(2,1)S(1)}, u32[]{:S(2)}, u32[]{:S(2)}) collective-permute-start(bf16[64,2048]{1,0:T(8,128)(2,1)S(1)} %add_convert_fusion.5), channel_id=1, source_target_pairs={{0,4},{1,5},{2,3},{3,2},{4,0},{5,1},{6,7},{7,6},{8,12},{9,13},{10,... | collective-permute-start | bytes 786440 | tf_op jit(solution)/shard_map/ppermute | solution.py:428
  191.3 7.4 %collective-permute-start.38 = (bf16[32,2048]{1,0:T(8,128)(2,1)S(1)}, bf16[32,2048]{1,0:T(8,128)(2,1)S(1)}, u32[]{:S(2)}, u32[]{:S(2)}) collective-permute-start(bf16[32,2048]{1,0:T(8,128)(2,1)S(1)} %pad_maximum_fusion.2), channel_id=1, source_target_pairs={{0,24},{4,28},{8,0},{12,4},{16,8},{20,12},{24,16},{28,20},{1,25},{... | collective-permute-start | bytes 393224 | tf_op jit(solution)/shard_map/ppermute | solution.py:417
  201.5 7.1 %collective-permute-start.44 = (bf16[16,2048]{1,0:T(8,128)(2,1)S(1)}, bf16[16,2048]{1,0:T(8,128)(2,1)S(1)}, u32[]{:S(2)}, u32[]{:S(2)}) collective-permute-start(bf16[16,2048]{1,0:T(8,128)(2,1)S(1)} %get-tuple-element.128), channel_id=1, source_target_pairs={{0,16},{4,20},{8,24},{12,28},{16,0},{20,4},{24,8},{28,12},{1,17},{... | collective-permute-start | bytes 196616 | tf_op jit(solution)/shard_map/ppermute | solution.py:417
  202.3 6.2 %collective-permute-start.45 = (bf16[16,2048]{1,0:T(8,128)(2,1)S(1)}, bf16[16,2048]{1,0:T(8,128)(2,1)S(1)}, u32[]{:S(2)}, u32[]{:S(2)}) collective-permute-start(bf16[16,2048]{1,0:T(8,128)(2,1)S(1)} %get-tuple-element.127), channel_id=1, source_target_pairs={{0,8},{4,12},{8,16},{12,20},{16,24},{20,28},{24,0},{28,4},{1,9},{5... | collective-permute-start | bytes 196616 | tf_op jit(solution)/shard_map/ppermute | solution.py:417
  (28 other events, 203.5 us)

commit v5 on v4

--- a/solution.py
+++ b/solution.py
@@ -232,15 +232,20 @@
 
     for copy in copies:
         copy.start()
-    for j in range(steps):
-        fetch(j, 0).start()
-        fetch(j, 1).start()
+    fetch(0, 0).start()
+    fetch(0, 1).start()
     for copy in copies:
         copy.wait()
 
     def step(j, carry):
         fetch(j, 0).wait()
         fetch(j, 1).wait()
+
+        @pl.when(j + 1 < steps)
+        def _():
+            fetch(j + 1, 0).start()
+            fetch(j + 1, 1).start()
+
         gate = jnp.dot(rows_ref[...], gate_ref[j], preferred_element_type=F32)
         up = jnp.dot(rows_ref[...], up_ref[j], preferred_element_type=F32)
         cols = pl.ds(pl.multiple_of(j * tile, tile), tile)
@@ -298,11 +303,8 @@
         at += piece.shape[0]
     for copy in copies:
         copy.start()
-    for j in range(steps):
-        fetch(j, 0).start()
-        fetch(j, 1).start()
-    for j in range(last_steps):
-        last_fetch(j).start()
+    fetch(0, 0).start()
+    fetch(0, 1).start()
     hidden_ref[:, pl.ds(0, done)] = have_ref[...]
     for copy in copies:
         copy.wait()
@@ -310,6 +312,17 @@
     def step(j, carry):
         fetch(j, 0).wait()
         fetch(j, 1).wait()
+
+        @pl.when(j + 1 < steps)
+        def _():
+            fetch(j + 1, 0).start()
+            fetch(j + 1, 1).start()
+
+        @pl.when(j + 1 == steps)
+        def _():
+            for k in range(last_steps):
+                last_fetch(k).start()
+
         gate = jnp.dot(rows_ref[...], gate_ref[j], preferred_element_type=F32)
         up = jnp.dot(rows_ref[...], up_ref[j], preferred_element_type=F32)
         cols = pl.ds(pl.multiple_of(done + j * tile, tile), tile)
@@ -503,7 +516,7 @@
     late_rows = after(late_rows, early_go)
     late_hidden, out_left = finish(late_rows, late_first, sizes, w_gate, w_up, w_down, 0, half)
     early_result = home_third(after(early_kept, out_left[0]), early_far)
-    left = home_first(out_left)
+    left = home_first(after(out_left, early_result))
     left_far = cross(left[1], 1)
     out_right = down([after(late_hidden, left[1])], sizes, w_down, half, half)
     left = home_second(after(left[0], out_right), left_far)

time: 210 us -> 214 us (1.019)
  Pallas kernels: 63.8 us -> 69.9 us
    pallas_call x2, Pallas kernels: 26.3 us -> 30.4 us  [finish(): pl.pallas_call(functools.partial(finish_kernel, len(pieces), first), out_...]
    ppermute x10, waiting for transfers between devices: 19.4 us -> 17.3 us  [cross(): return lax.ppermute(block, ('expert', 'context', 'dp'), route)]
  transfers between devices with their start and end apart: 46 -> 46, of which waited for: 33 -> 31; matrix products, arithmetic and copies ran while one was open for 3% -> 2% of each run, Pallas kernels for 16% -> 25%
where the time goes in v5:
time: 214 us
  waiting for transfers between devices  70.9 us (33%)
  Pallas kernels  69.9 us (33%)
  starting transfers between devices  61.5 us (29%)
  other arithmetic  6.47 us (3%)
  local copies, waits for them, and re-layouts  2.54 us (1%)
    ppermute x24, starting transfers between devices, along_line(): lax.ppermute(block, 'expert', [(e, (e + 2 * distance) % size) for e in ra...  41.9 us
    ppermute x24, waiting for transfers between devices, along_line(): lax.ppermute(block, 'expert', [(e, (e + 2 * distance) % size) for e in ra...  41.6 us
    pallas_call x2, Pallas kernels, finish(): pl.pallas_call(functools.partial(finish_kernel, len(pieces), first), out_...  30.4 us
    pallas_call x2, Pallas kernels, gate_up(): pl.pallas_call(functools.partial(gate_up_kernel, len(pieces), first), out...  18 us
    ppermute x10, waiting for transfers between devices, cross(): return lax.ppermute(block, ('expert', 'context', 'dp'), route)  17.3 us
    ppermute x10, starting transfers between devices, cross(): return lax.ppermute(block, ('expert', 'context', 'dp'), route)  11.4 us
    pallas_call x1, Pallas kernels, run_out(): pl.pallas_call(functools.partial(out_kernel, channels // LANES, line, fir...  9.19 us
    ppermute x7, waiting for transfers between devices, shift(): lax.ppermute(block, axis, [(i, (i + distance) % size) for i in range(size)])  8.58 us
  transfers between devices with their start and end apart: 46, of which 31 were waited for; matrix products, arithmetic and copies ran while one was open for 2% of the time, Pallas kernels for 25%

profile of v5, /device:TPU:0, one launch (start us, length us, event | category | flops | bytes accessed | tf_op | source)
XLA Modules:
  0.0 213.8 jit_solution(3745967506484344773)
XLA Ops:
  0.8 2.3 %collective-permute-start = (bf16[3,1024]{1,0:T(4,128)(2,1)S(1)}, bf16[3,1024]{1,0:T(4,128)(2,1)S(1)}, u32[]{:S(2)}, u32[]{:S(2)}) collective-permute-start(bf16[3,1024]{1,0:T(4,128)(2,1)S(1)} %slice_bitcast_fusion.3), channel_id=1, source_target_pairs={{0,2},{1,3},{4,6},{5,7},{8,10},{9,11},{12,14},{13,15},{16,18},{17,... | collective-permute-start | bytes 18440 | tf_op jit(solution)/shard_map/ppermute | solution.py:24
  8.4 2.5 %collective-permute-start.1 = (bf16[64,288]{1,0:T(8,128)(2,1)S(1)}, bf16[64,288]{1,0:T(8,128)(2,1)S(1)}, u32[]{:S(2)}, u32[]{:S(2)}) collective-permute-start(bf16[64,288]{1,0:T(8,128)(2,1)S(1)} %get-tuple-element.152), channel_id=1, source_target_pairs={{0,8},{4,12},{8,16},{12,20},{16,24},{20,28},{24,0},{28,4},{1,9},{5... | collective-permute-start | bytes 110600 | tf_op jit(solution)/shard_map/ppermute | solution.py:430
  10.9 2.6 %collective-permute-start.2 = (bf16[64,288]{1,0:T(8,128)(2,1)S(1)}, bf16[64,288]{1,0:T(8,128)(2,1)S(1)}, u32[]{:S(2)}, u32[]{:S(2)}) collective-permute-start(bf16[64,288]{1,0:T(8,128)(2,1)S(1)} %get-tuple-element.154), channel_id=1, source_target_pairs={{0,16},{4,20},{8,24},{12,28},{16,0},{20,4},{24,8},{28,12},{1,17},{... | collective-permute-start | bytes 110600 | tf_op jit(solution)/shard_map/ppermute | solution.py:430
  19.2 2.5 %collective-permute-done.4 = bf16[64,288]{1,0:T(8,128)(2,1)S(1)} collective-permute-done((bf16[64,288]{1,0:T(8,128)(2,1)S(1)}, bf16[64,288]{1,0:T(8,128)(2,1)S(1)}, u32[]{:S(2)}, u32[]{:S(2)}) %collective-permute-start.4) | collective-permute-done | bytes 36896 | tf_op jit(solution)/shard_map/ppermute | solution.py:34
  22.4 3.1 %collective-permute-start.6 = (bf16[64,288]{1,0:T(8,128)(2,1)S(1)}, bf16[64,288]{1,0:T(8,128)(2,1)S(1)}, u32[]{:S(2)}, u32[]{:S(2)}) collective-permute-start(bf16[64,288]{1,0:T(8,128)(2,1)S(1)} %add_convert_fusion.10.refs_0_), channel_id=1, source_target_pairs={{0,16},{4,20},{8,24},{12,28},{16,0},{20,4},{24,8},{28,12},{1,17},{... | collective-permute-start | bytes 110600 | tf_op jit(solution)/shard_map/ppermute | solution.py:430
  25.8 2.1 collective-permute-done.5.refs_1_
  29.6 6.9 %state_scan.1 = (f32[2048,128]{1,0:T(8,128)S(1)}, f32[2048,128]{1,0:T(8,128)S(1)}, f32[16,8,128]{2,1,0:T(8,128)S(1)}, bf16[256,32]{1,0:T(8,128)(2,1)S(1)}) custom-call(s32[2]{0:T(128)S(1)} %pad_add_fusion.place_ref.at_ref, bf16[64,288]{1,0:T(8,128)(2,1)S(1)} %add_convert_fusion.10.refs_0_, bf16[64,288]{1,0:T(8,128)(2,1)S(1)} %collective-permute-done.5.refs_1_, ...), custom_call_target="tpu_custom_call" | custom-call | flops 200000000 | bytes 4194304 | tf_op jit(solution)/shard_map/state_scan/pallas_call | solution.py:104
  38.7 9.2 %readout_project.1 = (bf16[128,2560]{1,0:T(8,128)(2,1)S(1)}, bf16[128,2560]{1,0:T(8,128)(2,1)S(1)}, bf16[4,64,1536]{2,1,0:T(8,128)(2,1)S(1)}) custom-call(s32[2]{0:T(128)S(1)} %pad_add_fusion.place_ref.at_ref, f32[2048,128]{1,0:T(8,128)S(1)} %get-tuple-element.61.y_ref, f32[2048,128]{1,0:T(8,128)S(1)} %get-tuple-element.62.sum_ref, ...), custom_call_target="tpu_custom_call" | custom-call | flops 2147483648 | bytes 16777216 | tf_op jit(solution)/shard_map/readout_project/pallas_call | solution.py:198
  50.4 2.1 %collective-permute-start.14 = (bf16[64,1536]{1,0:T(8,128)(2,1)S(1)}, bf16[64,1536]{1,0:T(8,128)(2,1)S(1)}, u32[]{:S(2)}, u32[]{:S(2)}) collective-permute-start(bf16[64,1536]{1,0:T(8,128)(2,1)S(1)} %get-tuple-element.123), channel_id=1, source_target_pairs={{0,16},{4,20},{8,24},{12,28},{16,0},{20,4},{24,8},{28,12},{1,17},{... | collective-permute-start | bytes 589832 | tf_op jit(solution)/shard_map/ppermute | solution.py:430
  53.6 5.7 %collective-permute-done.13 = bf16[64,1536]{1,0:T(8,128)(2,1)S(1)} collective-permute-done((bf16[64,1536]{1,0:T(8,128)(2,1)S(1)}, bf16[64,1536]{1,0:T(8,128)(2,1)S(1)}, u32[]{:S(2)}, u32[]{:S(2)}) %collective-permute-start.13) | collective-permute-done | bytes 196640 | tf_op jit(solution)/shard_map/ppermute | solution.py:430
  59.3 7.6 %collective-permute-done.14 = bf16[64,1536]{1,0:T(8,128)(2,1)S(1)} collective-permute-done((bf16[64,1536]{1,0:T(8,128)(2,1)S(1)}, bf16[64,1536]{1,0:T(8,128)(2,1)S(1)}, u32[]{:S(2)}, u32[]{:S(2)}) %collective-permute-start.14) | collective-permute-done | bytes 196640 | tf_op jit(solution)/shard_map/ppermute | solution.py:430
  67.8 4.3 %collective-permute-start.10 = (bf16[32,2560]{1,0:T(8,128)(2,1)S(1)}, bf16[32,2560]{1,0:T(8,128)(2,1)S(1)}, u32[]{:S(2)}, u32[]{:S(2)}) collective-permute-start(bf16[32,2560]{1,0:T(8,128)(2,1)S(1)} %get-tuple-element.124), channel_id=1, source_target_pairs={{0,8},{4,12},{8,16},{12,20},{16,24},{20,28},{24,0},{28,4},{1,9},{5... | collective-permute-start | bytes 491528 | tf_op jit(solution)/shard_map/ppermute | solution.py:430
  74.5 2.2 %collective-permute-done.10 = bf16[32,2560]{1,0:T(8,128)(2,1)S(1)} collective-permute-done((bf16[32,2560]{1,0:T(8,128)(2,1)S(1)}, bf16[32,2560]{1,0:T(8,128)(2,1)S(1)}, u32[]{:S(2)}, u32[]{:S(2)}) %collective-permute-start.10) | collective-permute-done | bytes 163872 | tf_op jit(solution)/shard_map/ppermute | solution.py:430
  76.7 5.6 %collective-permute-done.11 = bf16[32,2560]{1,0:T(8,128)(2,1)S(1)} collective-permute-done((bf16[32,2560]{1,0:T(8,128)(2,1)S(1)}, bf16[32,2560]{1,0:T(8,128)(2,1)S(1)}, u32[]{:S(2)}, u32[]{:S(2)}) %collective-permute-start.11) | collective-permute-done | bytes 163872 | tf_op jit(solution)/shard_map/ppermute | solution.py:430
  83.0 4.0 %collective-permute-start.17 = (bf16[8,4096]{1,0:T(8,128)(2,1)S(1)}, bf16[8,4096]{1,0:T(8,128)(2,1)S(1)}, u32[]{:S(2)}, u32[]{:S(2)}) collective-permute-start(bf16[8,4096]{1,0:T(8,128)(2,1)S(1)} %get-tuple-element.150), channel_id=1, source_target_pairs={{0,8},{4,12},{8,16},{12,20},{16,24},{20,28},{24,0},{28,4},{1,9},{5... | collective-permute-start | bytes 196616 | tf_op jit(solution)/shard_map/ppermute | solution.py:430
  87.1 2.8 %collective-permute-start.18 = (bf16[8,4096]{1,0:T(8,128)(2,1)S(1)}, bf16[8,4096]{1,0:T(8,128)(2,1)S(1)}, u32[]{:S(2)}, u32[]{:S(2)}) collective-permute-start(bf16[8,4096]{1,0:T(8,128)(2,1)S(1)} %get-tuple-element.149), channel_id=1, source_target_pairs={{0,16},{4,20},{8,24},{12,28},{16,0},{20,4},{24,8},{28,12},{1,17},{... | collective-permute-start | bytes 196616 | tf_op jit(solution)/shard_map/ppermute | solution.py:430
  102.4 2.0 collective-permute-done.24
  104.4 5.6 %collective-permute-done.21.refs_1_ = bf16[64,4096]{1,0:T(8,128)(2,1)S(1)} collective-permute-done((bf16[64,4096]{1,0:T(8,128)(2,1)S(1)}, bf16[64,4096]{1,0:T(8,128)(2,1)S(1)}, u32[]{:S(2)}, u32[]{:S(2)}) %collective-permute-start.21) | collective-permute-done | bytes 524320 | tf_op jit(solution)/shard_map/ppermute | solution.py:441
  111.9 8.2 %gate_up.2.refs_4_ = bf16[256,768]{1,0:T(8,128)(2,1)S(1)} custom-call(bf16[64,4096]{1,0:T(8,128)(2,1)S(1)} %constant_dynamic-update-slice_fusion.refs_0_, bf16[64,4096]{1,0:T(8,128)(2,1)S(1)} %collective-permute-done.21.refs_1_, bf16[64,4096]{1,0:T(8,128)(2,1)S(1)} %collective-permute-done.22.refs_2_, bf16[64,4096]{1,0:T(8,128)(2,1)S(1)} %collective-permute-done.23.refs_3_, ...), custom_call_target="tpu_custom_call" | custom-call | flops 3221225472 | bytes 14680064 | tf_op jit(solution)/shard_map/gate_up/pallas_call | solution.py:264
  121.8 15.0 %gate_up_down.2 = (bf16[256,1536]{1,0:T(8,128)(2,1)}, bf16[128,4096]{1,0:T(8,128)(2,1)S(1)}, bf16[128,4096]{1,0:T(8,128)(2,1)}) custom-call(bf16[64,4096]{1,0:T(8,128)(2,1)S(1)} %constant_dynamic-update-slice_fusion.refs_0_, bf16[64,4096]{1,0:T(8,128)(2,1)S(1)} %collective-permute-done.21.refs_1_, bf16[64,4096]{1,0:T(8,128)(2,1)S(1)} %collective-permute-done.22.refs_2_, ...), custom_call_target="tpu_custom_call" | custom-call | flops 6442450944 | bytes 29360128 | tf_op jit(solution)/shard_map/gate_up_down/pallas_call | solution.py:353
  137.5 3.0 %collective-permute-done.29 = bf16[128,4096]{1,0:T(8,128)(2,1)S(1)} collective-permute-done((bf16[128,4096]{1,0:T(8,128)(2,1)}, bf16[128,4096]{1,0:T(8,128)(2,1)S(1)}, u32[]{:S(2)}, u32[]{:S(2)}) %collective-permute-start.29) | collective-permute-done | bytes 1048608 | tf_op jit(solution)/shard_map/ppermute | solution.py:29
  142.6 9.8 %gate_up.3.refs_4_ = bf16[512,768]{1,0:T(8,128)(2,1)S(1)} custom-call(bf16[128,4096]{1,0:T(8,128)(2,1)S(1)} %constant_dynamic-update-slice_fusion.9.refs_0_, bf16[128,4096]{1,0:T(8,128)(2,1)S(1)} %collective-permute-done.28.refs_1_, bf16[128,4096]{1,0:T(8,128)(2,1)S(1)} %collective-permute-done.30.refs_2_, ...), custom_call_target="tpu_custom_call" | custom-call | flops 6442450944 | bytes 16777216 | tf_op jit(solution)/shard_map/gate_up/pallas_call | solution.py:264
  154.1 15.4 %gate_up_down.3 = (bf16[512,1536]{1,0:T(8,128)(2,1)}, bf16[256,2048]{1,0:T(8,128)(2,1)S(1)}, bf16[256,2048]{1,0:T(8,128)(2,1)S(1)}) custom-call(bf16[128,4096]{1,0:T(8,128)(2,1)S(1)} %constant_dynamic-update-slice_fusion.9.refs_0_, bf16[128,4096]{1,0:T(8,128)(2,1)S(1)} %collective-permute-done.28.refs_1_, bf16[128,4096]{1,0:T(8,128)(2,1)} %copy-done.2, ...), custom_call_target="tpu_custom_call" | custom-call | flops 9663676416 | bytes 25165824 | tf_op jit(solution)/shard_map/gate_up_down/pallas_call | solution.py:353
  169.7 2.6 %collective-permute-done.34 = bf16[256,2048]{1,0:T(8,128)(2,1)S(1)} collective-permute-done((bf16[256,2048]{1,0:T(8,128)(2,1)S(1)}, bf16[256,2048]{1,0:T(8,128)(2,1)S(1)}, u32[]{:S(2)}, u32[]{:S(2)}) %collective-permute-start.34) | collective-permute-done | bytes 1048608 | tf_op jit(solution)/shard_map/ppermute | solution.py:29
  173.1 5.4 %down.1 = (bf16[256,2048]{1,0:T(8,128)(2,1)S(1)}, bf16[256,2048]{1,0:T(8,128)(2,1)S(1)}) custom-call(bf16[512,1536]{1,0:T(8,128)(2,1)S(1)} %copy-done.4, bf16[1536,4096]{1,0:T(8,128)(2,1)} %bitcast.75), custom_call_target="tpu_custom_call" | custom-call | flops 3221225472 | bytes 9961472 | tf_op jit(solution)/shard_map/down/pallas_call | solution.py:408
  178.5 3.3 %collective-permute-done.35 = bf16[128,2048]{1,0:T(8,128)(2,1)S(1)} collective-permute-done((bf16[128,2048]{1,0:T(8,128)(2,1)S(1)}, bf16[128,2048]{1,0:T(8,128)(2,1)S(1)}, u32[]{:S(2)}, u32[]{:S(2)}) %collective-permute-start.35) | collective-permute-done | bytes 524320 | tf_op jit(solution)/shard_map/ppermute | solution.py:441
  185.3 4.3 %collective-permute-done.37 = bf16[64,2048]{1,0:T(8,128)(2,1)S(1)} collective-permute-done((bf16[64,2048]{1,0:T(8,128)(2,1)S(1)}, bf16[64,2048]{1,0:T(8,128)(2,1)S(1)}, u32[]{:S(2)}, u32[]{:S(2)}) %collective-permute-start.37) | collective-permute-done | bytes 262176 | tf_op jit(solution)/shard_map/ppermute | solution.py:441
  191.1 2.4 %collective-permute-start.39 = (bf16[32,2048]{1,0:T(8,128)(2,1)S(1)}, bf16[32,2048]{1,0:T(8,128)(2,1)S(1)}, u32[]{:S(2)}, u32[]{:S(2)}) collective-permute-start(bf16[32,2048]{1,0:T(8,128)(2,1)S(1)} %pad_maximum_fusion.3), channel_id=1, source_target_pairs={{0,16},{4,20},{8,24},{12,28},{16,0},{20,4},{24,8},{28,12},{1,17},{... | collective-permute-start | bytes 393224 | tf_op jit(solution)/shard_map/ppermute | solution.py:430
  194.6 3.1 %collective-permute-start.38 = (bf16[32,2048]{1,0:T(8,128)(2,1)S(1)}, bf16[32,2048]{1,0:T(8,128)(2,1)S(1)}, u32[]{:S(2)}, u32[]{:S(2)}) collective-permute-start(bf16[32,2048]{1,0:T(8,128)(2,1)S(1)} %pad_maximum_fusion.2), channel_id=1, source_target_pairs={{0,24},{4,28},{8,0},{12,4},{16,8},{20,12},{24,16},{28,20},{1,25},{... | collective-permute-start | bytes 393224 | tf_op jit(solution)/shard_map/ppermute | solution.py:430
  197.7 2.8 %collective-permute-done.42 = bf16[64,2048]{1,0:T(8,128)(2,1)S(1)} collective-permute-done((bf16[64,2048]{1,0:T(8,128)(2,1)S(1)}, bf16[64,2048]{1,0:T(8,128)(2,1)S(1)}, u32[]{:S(2)}, u32[]{:S(2)}) %collective-permute-start.42) | collective-permute-done | bytes 262176 | tf_op jit(solution)/shard_map/ppermute | solution.py:441
  202.8 2.4 %collective-permute-start.43 = (bf16[16,2048]{1,0:T(8,128)(2,1)S(1)}, bf16[16,2048]{1,0:T(8,128)(2,1)S(1)}, u32[]{:S(2)}, u32[]{:S(2)}) collective-permute-start(bf16[16,2048]{1,0:T(8,128)(2,1)S(1)} %get-tuple-element.133), channel_id=1, source_target_pairs={{0,24},{4,28},{8,0},{12,4},{16,8},{20,12},{24,16},{28,20},{1,25},{... | collective-permute-start | bytes 196616 | tf_op jit(solution)/shard_map/ppermute | solution.py:430
  207.8 4.9 %collective-permute-done.44 = bf16[16,2048]{1,0:T(8,128)(2,1)S(1)} collective-permute-done((bf16[16,2048]{1,0:T(8,128)(2,1)S(1)}, bf16[16,2048]{1,0:T(8,128)(2,1)S(1)}, u32[]{:S(2)}, u32[]{:S(2)}) %collective-permute-start.44) | collective-permute-done | bytes 65568 | tf_op jit(solution)/shard_map/ppermute | solution.py:430
  (174 shorter events, 57.4 us)
Async XLA Ops:
  8.4 7.2 %collective-permute-start.1 = (bf16[64,288]{1,0:T(8,128)(2,1)S(1)}, bf16[64,288]{1,0:T(8,128)(2,1)S(1)}, u32[]{:S(2)}, u32[]{:S(2)}) collective-permute-start(bf16[64,288]{1,0:T(8,128)(2,1)S(1)} %get-tuple-element.152), channel_id=1, source_target_pairs={{0,8},{4,12},{8,16},{12,20},{16,24},{20,28},{24,0},{28,4},{1,9},{5... | collective-permute-start | bytes 110600 | tf_op jit(solution)/shard_map/ppermute | solution.py:430
  10.9 6.2 %collective-permute-start.2 = (bf16[64,288]{1,0:T(8,128)(2,1)S(1)}, bf16[64,288]{1,0:T(8,128)(2,1)S(1)}, u32[]{:S(2)}, u32[]{:S(2)}) collective-permute-start(bf16[64,288]{1,0:T(8,128)(2,1)S(1)} %get-tuple-element.154), channel_id=1, source_target_pairs={{0,16},{4,20},{8,24},{12,28},{16,0},{20,4},{24,8},{28,12},{1,17},{... | collective-permute-start | bytes 110600 | tf_op jit(solution)/shard_map/ppermute | solution.py:430
  22.4 6.2 %collective-permute-start.6 = (bf16[64,288]{1,0:T(8,128)(2,1)S(1)}, bf16[64,288]{1,0:T(8,128)(2,1)S(1)}, u32[]{:S(2)}, u32[]{:S(2)}) collective-permute-start(bf16[64,288]{1,0:T(8,128)(2,1)S(1)} %add_convert_fusion.10.refs_0_), channel_id=1, source_target_pairs={{0,16},{4,20},{8,24},{12,28},{16,0},{20,4},{24,8},{28,12},{1,17},{... | collective-permute-start | bytes 110600 | tf_op jit(solution)/shard_map/ppermute | solution.py:430
  47.9 19.6 %collective-permute-start.9 = (bf16[128,2560]{1,0:T(8,128)(2,1)S(1)}, bf16[128,2560]{1,0:T(8,128)(2,1)S(1)}, u32[]{:S(2)}, u32[]{:S(2)}) collective-permute-start(bf16[128,2560]{1,0:T(8,128)(2,1)S(1)} %get-tuple-element.66), channel_id=1, source_target_pairs={{0,4},{4,0},{8,12},{12,8},{16,20},{20,16},{24,28},{28,24},{1,5},{5... | collective-permute-start | bytes 1966088 | tf_op jit(solution)/shard_map/ppermute | solution.py:34
  49.5 9.8 %collective-permute-start.13 = (bf16[64,1536]{1,0:T(8,128)(2,1)S(1)}, bf16[64,1536]{1,0:T(8,128)(2,1)S(1)}, u32[]{:S(2)}, u32[]{:S(2)}) collective-permute-start(bf16[64,1536]{1,0:T(8,128)(2,1)S(1)} %get-tuple-element.121), channel_id=1, source_target_pairs={{0,8},{4,12},{8,16},{12,20},{16,24},{20,28},{24,0},{28,4},{1,9},{5... | collective-permute-start | bytes 589832 | tf_op jit(solution)/shard_map/ppermute | solution.py:430
  50.4 16.5 %collective-permute-start.14 = (bf16[64,1536]{1,0:T(8,128)(2,1)S(1)}, bf16[64,1536]{1,0:T(8,128)(2,1)S(1)}, u32[]{:S(2)}, u32[]{:S(2)}) collective-permute-start(bf16[64,1536]{1,0:T(8,128)(2,1)S(1)} %get-tuple-element.123), channel_id=1, source_target_pairs={{0,16},{4,20},{8,24},{12,28},{16,0},{20,4},{24,8},{28,12},{1,17},{... | collective-permute-start | bytes 589832 | tf_op jit(solution)/shard_map/ppermute | solution.py:430
  52.5 14.4 %collective-permute-start.15 = (bf16[64,1536]{1,0:T(8,128)(2,1)S(1)}, bf16[64,1536]{1,0:T(8,128)(2,1)S(1)}, u32[]{:S(2)}, u32[]{:S(2)}) collective-permute-start(bf16[64,1536]{1,0:T(8,128)(2,1)S(1)} %get-tuple-element.122), channel_id=1, source_target_pairs={{0,24},{4,28},{8,0},{12,4},{16,8},{20,12},{24,16},{28,20},{1,25},{... | collective-permute-start | bytes 589832 | tf_op jit(solution)/shard_map/ppermute | solution.py:430
  67.0 7.5 %collective-permute-start.16 = (bf16[32,1536]{1,0:T(8,128)(2,1)S(1)}, bf16[32,1536]{1,0:T(8,128)(2,1)S(1)}, u32[]{:S(2)}, u32[]{:S(2)}) collective-permute-start(bf16[32,1536]{1,0:T(8,128)(2,1)S(1)} %slice.456), channel_id=1, source_target_pairs={{0,4},{4,0},{8,12},{12,8},{16,20},{20,16},{24,28},{28,24},{1,5},{5... | collective-permute-start | bytes 294920 | tf_op jit(solution)/shard_map/ppermute | solution.py:34
  67.8 8.9 %collective-permute-start.10 = (bf16[32,2560]{1,0:T(8,128)(2,1)S(1)}, bf16[32,2560]{1,0:T(8,128)(2,1)S(1)}, u32[]{:S(2)}, u32[]{:S(2)}) collective-permute-start(bf16[32,2560]{1,0:T(8,128)(2,1)S(1)} %get-tuple-element.124), channel_id=1, source_target_pairs={{0,8},{4,12},{8,16},{12,20},{16,24},{20,28},{24,0},{28,4},{1,9},{5... | collective-permute-start | bytes 491528 | tf_op jit(solution)/shard_map/ppermute | solution.py:430
  72.1 10.3 %collective-permute-start.11 = (bf16[32,2560]{1,0:T(8,128)(2,1)S(1)}, bf16[32,2560]{1,0:T(8,128)(2,1)S(1)}, u32[]{:S(2)}, u32[]{:S(2)}) collective-permute-start(bf16[32,2560]{1,0:T(8,128)(2,1)S(1)} %get-tuple-element.126), channel_id=1, source_target_pairs={{0,16},{4,20},{8,24},{12,28},{16,0},{20,4},{24,8},{28,12},{1,17},{... | collective-permute-start | bytes 491528 | tf_op jit(solution)/shard_map/ppermute | solution.py:430
  72.5 9.9 %collective-permute-start.12 = (bf16[32,2560]{1,0:T(8,128)(2,1)S(1)}, bf16[32,2560]{1,0:T(8,128)(2,1)S(1)}, u32[]{:S(2)}, u32[]{:S(2)}) collective-permute-start(bf16[32,2560]{1,0:T(8,128)(2,1)S(1)} %get-tuple-element.125), channel_id=1, source_target_pairs={{0,24},{4,28},{8,0},{12,4},{16,8},{20,12},{24,16},{28,20},{1,25},{... | collective-permute-start | bytes 491528 | tf_op jit(solution)/shard_map/ppermute | solution.py:430
  83.0 8.8 %collective-permute-start.17 = (bf16[8,4096]{1,0:T(8,128)(2,1)S(1)}, bf16[8,4096]{1,0:T(8,128)(2,1)S(1)}, u32[]{:S(2)}, u32[]{:S(2)}) collective-permute-start(bf16[8,4096]{1,0:T(8,128)(2,1)S(1)} %get-tuple-element.150), channel_id=1, source_target_pairs={{0,8},{4,12},{8,16},{12,20},{16,24},{20,28},{24,0},{28,4},{1,9},{5... | collective-permute-start | bytes 196616 | tf_op jit(solution)/shard_map/ppermute | solution.py:430
  87.1 6.6 %collective-permute-start.18 = (bf16[8,4096]{1,0:T(8,128)(2,1)S(1)}, bf16[8,4096]{1,0:T(8,128)(2,1)S(1)}, u32[]{:S(2)}, u32[]{:S(2)}) collective-permute-start(bf16[8,4096]{1,0:T(8,128)(2,1)S(1)} %get-tuple-element.149), channel_id=1, source_target_pairs={{0,16},{4,20},{8,24},{12,28},{16,0},{20,4},{24,8},{28,12},{1,17},{... | collective-permute-start | bytes 196616 | tf_op jit(solution)/shard_map/ppermute | solution.py:430
  94.3 6.4 %collective-permute-start.20 = (bf16[32,4096]{1,0:T(8,128)(2,1)S(1)}, bf16[32,4096]{1,0:T(8,128)(2,1)S(1)}, u32[]{:S(2)}, u32[]{:S(2)}) collective-permute-start(bf16[32,4096]{1,0:T(8,128)(2,1)S(1)} %pad_maximum_fusion), channel_id=1, source_target_pairs={{0,4},{1,5},{2,3},{3,2},{4,0},{5,1},{6,7},{7,6},{8,12},{9,13},{10,... | collective-permute-start | bytes 786440 | tf_op jit(solution)/shard_map/ppermute | solution.py:441
  96.0 8.4 %collective-permute-start.24 = (bf16[16,4096]{1,0:T(8,128)(2,1)S(1)}, bf16[16,4096]{1,0:T(8,128)(2,1)S(1)}, u32[]{:S(2)}, u32[]{:S(2)}) collective-permute-start(bf16[16,4096]{1,0:T(8,128)(2,1)S(1)} %get-tuple-element.129), channel_id=1, source_target_pairs={{0,8},{4,12},{8,16},{12,20},{16,24},{20,28},{24,0},{28,4},{1,9},{5... | collective-permute-start | bytes 393224 | tf_op jit(solution)/shard_map/ppermute | solution.py:430
  97.3 12.7 %collective-permute-start.25 = (bf16[16,4096]{1,0:T(8,128)(2,1)S(1)}, bf16[16,4096]{1,0:T(8,128)(2,1)S(1)}, u32[]{:S(2)}, u32[]{:S(2)}) collective-permute-start(bf16[16,4096]{1,0:T(8,128)(2,1)S(1)} %get-tuple-element.128), channel_id=1, source_target_pairs={{0,16},{4,20},{8,24},{12,28},{16,0},{20,4},{24,8},{28,12},{1,17},{... | collective-permute-start | bytes 393224 | tf_op jit(solution)/shard_map/ppermute | solution.py:430
  99.0 11.1 %collective-permute-start.26 = (bf16[16,4096]{1,0:T(8,128)(2,1)S(1)}, bf16[16,4096]{1,0:T(8,128)(2,1)S(1)}, u32[]{:S(2)}, u32[]{:S(2)}) collective-permute-start(bf16[16,4096]{1,0:T(8,128)(2,1)S(1)} %get-tuple-element.127), channel_id=1, source_target_pairs={{0,24},{4,28},{8,0},{12,4},{16,8},{20,12},{24,16},{28,20},{1,25},{... | collective-permute-start | bytes 393224 | tf_op jit(solution)/shard_map/ppermute | solution.py:430
  100.8 9.2 %collective-permute-start.21 = (bf16[64,4096]{1,0:T(8,128)(2,1)S(1)}, bf16[64,4096]{1,0:T(8,128)(2,1)S(1)}, u32[]{:S(2)}, u32[]{:S(2)}) collective-permute-start(bf16[64,4096]{1,0:T(8,128)(2,1)S(1)} %constant_dynamic-update-slice_fusion.refs_0_), channel_id=1, source_target_pairs={{0,1},{1,0},{2,6},{3,7},{4,5},{5,4},{6,2},{7,3},{8,9},{9,8},{10,14... | collective-permute-start | bytes 1572872 | tf_op jit(solution)/shard_map/ppermute | solution.py:441
  102.3 9.4 %collective-permute-start.22 = (bf16[64,4096]{1,0:T(8,128)(2,1)S(1)}, bf16[64,4096]{1,0:T(8,128)(2,1)S(1)}, u32[]{:S(2)}, u32[]{:S(2)}) collective-permute-start(bf16[64,4096]{1,0:T(8,128)(2,1)S(1)} %constant_dynamic-update-slice_fusion.refs_0_), channel_id=1, source_target_pairs={{0,2},{2,0},{1,3},{3,1},{4,6},{6,4},{5,7},{7,5},{8,10},{10,8},{9,1... | collective-permute-start | bytes 1572872 | tf_op jit(solution)/shard_map/ppermute | solution.py:29
  110.1 10.1 %collective-permute-start.27 = (bf16[64,4096]{1,0:T(8,128)(2,1)S(1)}, bf16[64,4096]{1,0:T(8,128)(2,1)S(1)}, u32[]{:S(2)}, u32[]{:S(2)}) collective-permute-start(bf16[64,4096]{1,0:T(8,128)(2,1)S(1)} %constant_dynamic-update-slice_fusion.5), channel_id=1, source_target_pairs={{0,4},{1,5},{2,3},{3,2},{4,0},{5,1},{6,7},{7,6},{8,12},{9,13},{10,... | collective-permute-start | bytes 1572872 | tf_op jit(solution)/shard_map/ppermute | solution.py:441
  120.3 17.2 %collective-permute-start.28 = (bf16[128,4096]{1,0:T(8,128)(2,1)S(1)}, bf16[128,4096]{1,0:T(8,128)(2,1)S(1)}, u32[]{:S(2)}, u32[]{:S(2)}) collective-permute-start(bf16[128,4096]{1,0:T(8,128)(2,1)S(1)} %constant_dynamic-update-slice_fusion.9.refs_0_), channel_id=1, source_target_pairs={{0,1},{1,0},{2,6},{3,7},{4,5},{5,4},{6,2},{7,3},{8,9},{9,8},{10,14... | collective-permute-start | bytes 3145736 | tf_op jit(solution)/shard_map/ppermute | solution.py:441
  140.6 11.7 %collective-permute-start.32 = (bf16[64,4096]{1,0:T(8,128)(2,1)S(1)}, bf16[64,4096]{1,0:T(8,128)(2,1)S(1)}, u32[]{:S(2)}, u32[]{:S(2)}) collective-permute-start(bf16[64,4096]{1,0:T(8,128)(2,1)S(1)} %add_convert_fusion.3), channel_id=1, source_target_pairs={{0,1},{1,0},{2,6},{3,7},{4,5},{5,4},{6,2},{7,3},{8,9},{9,8},{10,14... | collective-permute-start | bytes 1572872 | tf_op jit(solution)/shard_map/ppermute | solution.py:441
  152.5 17.0 %collective-permute-start.33 = (bf16[32,4096]{1,0:T(8,128)(2,1)S(1)}, bf16[32,4096]{1,0:T(8,128)(2,1)S(1)}, u32[]{:S(2)}, u32[]{:S(2)}) collective-permute-start(bf16[32,4096]{1,0:T(8,128)(2,1)S(1)} %add_convert_fusion.9), channel_id=1, source_target_pairs={{0,4},{1,5},{2,3},{3,2},{4,0},{5,1},{6,7},{7,6},{8,12},{9,13},{10,... | collective-permute-start | bytes 786440 | tf_op jit(solution)/shard_map/ppermute | solution.py:441
  172.5 9.2 %collective-permute-start.35 = (bf16[128,2048]{1,0:T(8,128)(2,1)S(1)}, bf16[128,2048]{1,0:T(8,128)(2,1)S(1)}, u32[]{:S(2)}, u32[]{:S(2)}) collective-permute-start(bf16[128,2048]{1,0:T(8,128)(2,1)S(1)} %add_convert_fusion.2), channel_id=1, source_target_pairs={{0,1},{1,0},{2,6},{3,7},{4,5},{5,4},{6,2},{7,3},{8,9},{9,8},{10,14... | collective-permute-start | bytes 1572872 | tf_op jit(solution)/shard_map/ppermute | solution.py:441
  182.2 7.5 %collective-permute-start.37 = (bf16[64,2048]{1,0:T(8,128)(2,1)S(1)}, bf16[64,2048]{1,0:T(8,128)(2,1)S(1)}, u32[]{:S(2)}, u32[]{:S(2)}) collective-permute-start(bf16[64,2048]{1,0:T(8,128)(2,1)S(1)} %add_convert_fusion.7), channel_id=1, source_target_pairs={{0,4},{1,5},{2,3},{3,2},{4,0},{5,1},{6,7},{7,6},{8,12},{9,13},{10,... | collective-permute-start | bytes 786440 | tf_op jit(solution)/shard_map/ppermute | solution.py:441
  184.7 9.2 %collective-permute-start.41 = (bf16[128,2048]{1,0:T(8,128)(2,1)S(1)}, bf16[128,2048]{1,0:T(8,128)(2,1)S(1)}, u32[]{:S(2)}, u32[]{:S(2)}) collective-permute-start(bf16[128,2048]{1,0:T(8,128)(2,1)S(1)} %add_convert_fusion.1), channel_id=1, source_target_pairs={{0,1},{1,0},{2,6},{3,7},{4,5},{5,4},{6,2},{7,3},{8,9},{9,8},{10,14... | collective-permute-start | bytes 1572872 | tf_op jit(solution)/shard_map/ppermute | solution.py:441
  189.8 10.8 %collective-permute-start.40 = (bf16[32,2048]{1,0:T(8,128)(2,1)S(1)}, bf16[32,2048]{1,0:T(8,128)(2,1)S(1)}, u32[]{:S(2)}, u32[]{:S(2)}) collective-permute-start(bf16[32,2048]{1,0:T(8,128)(2,1)S(1)} %pad_maximum_fusion.4), channel_id=1, source_target_pairs={{0,8},{4,12},{8,16},{12,20},{16,24},{20,28},{24,0},{28,4},{1,9},{5... | collective-permute-start | bytes 393224 | tf_op jit(solution)/shard_map/ppermute | solution.py:430
  191.1 10.3 %collective-permute-start.39 = (bf16[32,2048]{1,0:T(8,128)(2,1)S(1)}, bf16[32,2048]{1,0:T(8,128)(2,1)S(1)}, u32[]{:S(2)}, u32[]{:S(2)}) collective-permute-start(bf16[32,2048]{1,0:T(8,128)(2,1)S(1)} %pad_maximum_fusion.3), channel_id=1, source_target_pairs={{0,16},{4,20},{8,24},{12,28},{16,0},{20,4},{24,8},{28,12},{1,17},{... | collective-permute-start | bytes 393224 | tf_op jit(solution)/shard_map/ppermute | solution.py:430
  194.1 6.4 %collective-permute-start.42 = (bf16[64,2048]{1,0:T(8,128)(2,1)S(1)}, bf16[64,2048]{1,0:T(8,128)(2,1)S(1)}, u32[]{:S(2)}, u32[]{:S(2)}) collective-permute-start(bf16[64,2048]{1,0:T(8,128)(2,1)S(1)} %add_convert_fusion.5), channel_id=1, source_target_pairs={{0,4},{1,5},{2,3},{3,2},{4,0},{5,1},{6,7},{7,6},{8,12},{9,13},{10,... | collective-permute-start | bytes 786440 | tf_op jit(solution)/shard_map/ppermute | solution.py:441
  194.6 8.1 %collective-permute-start.38 = (bf16[32,2048]{1,0:T(8,128)(2,1)S(1)}, bf16[32,2048]{1,0:T(8,128)(2,1)S(1)}, u32[]{:S(2)}, u32[]{:S(2)}) collective-permute-start(bf16[32,2048]{1,0:T(8,128)(2,1)S(1)} %pad_maximum_fusion.2), channel_id=1, source_target_pairs={{0,24},{4,28},{8,0},{12,4},{16,8},{20,12},{24,16},{28,20},{1,25},{... | collective-permute-start | bytes 393224 | tf_op jit(solution)/shard_map/ppermute | solution.py:430
  205.2 7.4 %collective-permute-start.44 = (bf16[16,2048]{1,0:T(8,128)(2,1)S(1)}, bf16[16,2048]{1,0:T(8,128)(2,1)S(1)}, u32[]{:S(2)}, u32[]{:S(2)}) collective-permute-start(bf16[16,2048]{1,0:T(8,128)(2,1)S(1)} %get-tuple-element.132), channel_id=1, source_target_pairs={{0,16},{4,20},{8,24},{12,28},{16,0},{20,4},{24,8},{28,12},{1,17},{... | collective-permute-start | bytes 196616 | tf_op jit(solution)/shard_map/ppermute | solution.py:430
  206.4 6.3 %collective-permute-start.45 = (bf16[16,2048]{1,0:T(8,128)(2,1)S(1)}, bf16[16,2048]{1,0:T(8,128)(2,1)S(1)}, u32[]{:S(2)}, u32[]{:S(2)}) collective-permute-start(bf16[16,2048]{1,0:T(8,128)(2,1)S(1)} %get-tuple-element.131), channel_id=1, source_target_pairs={{0,8},{4,12},{8,16},{12,20},{16,24},{20,28},{24,0},{28,4},{1,9},{5... | collective-permute-start | bytes 196616 | tf_op jit(solution)/shard_map/ppermute | solution.py:430
  (28 other events, 208.1 us)

commit v6 on v4

--- a/solution.py
+++ b/solution.py
@@ -52,8 +52,8 @@
 
 def scan_kernel(groups, line, place_ref, *refs):
     pieces, refs = refs[:line], refs[line:]
-    w_ref, bias_ref, neg_ref, x_ref, y_ref, sum_ref, end_ref, bc_ref = refs[:8]
-    low_ref, step_ref, drive_ref, wide_ref = refs[8:]
+    w_ref, bias_ref, rate_ref, x_ref, y_ref, sum_ref, end_ref, bc_ref, neg_ref = refs[:9]
+    low_ref, step_ref, drive_ref, wide_ref = refs[9:]
     length = x_ref.shape[0]
     share = length // line
     for s in range(line):
@@ -66,8 +66,10 @@
         if g >= groups:
             step_ref[rows, :] = jnp.zeros((length, LANES), F32)
             drive_ref[rows, :] = jnp.zeros((length, LANES), F32)
+            neg_ref[pl.ds(g, NSTATE, stride=SUB), :] = jnp.zeros((NSTATE, LANES), F32)
             continue
         cols = pl.ds(g * LANES, LANES)
+        neg_ref[pl.ds(g, NSTATE, stride=SUB), :] = -rate_ref[:, cols]
         raw = jnp.dot(low_ref[...], w_ref[:, cols], preferred_element_type=F32) + bias_ref[:, cols]
         step = jnp.maximum(raw, 0.0) + jnp.log1p(jnp.exp(-jnp.abs(raw)))
         step_ref[rows, :] = step
@@ -82,7 +84,7 @@
             total = total + step
             out = jnp.zeros((SUB, LANES), F32)
             for n in range(NSTATE):
-                decay = jnp.exp(step * neg_ref[n])
+                decay = jnp.exp(step * neg_ref[pl.ds(n * SUB, SUB), :])
                 b = wide_ref[pl.ds(n * length + t, 1), :]
                 c = wide_ref[pl.ds((NSTATE + n) * length + t, 1), :]
                 states[n] = states[n] * decay + drive * b
@@ -97,7 +99,7 @@
         end_ref[n] = states[n]
 
 
-def run_scan(place, pieces, w, bias, neg, x):
+def run_scan(place, pieces, w, bias, rate, x):
     length, channels = x.shape
     vmem = pl.BlockSpec(memory_space=pltpu.VMEM)
     tall = jax.ShapeDtypeStruct((length * SUB, LANES), F32)
@@ -108,9 +110,10 @@
             tall,
             jax.ShapeDtypeStruct((NSTATE, SUB, LANES), F32),
             jax.ShapeDtypeStruct((length, 2 * NSTATE), BF16),
+            jax.ShapeDtypeStruct((NSTATE * SUB, LANES), F32),
         ),
         in_specs=[pl.BlockSpec(memory_space=pltpu.SMEM)] + [vmem] * (len(pieces) + 4),
-        out_specs=(vmem,) * 4,
+        out_specs=(vmem,) * 5,
         scratch_shapes=[
             pltpu.VMEM((length, DT_RANK), BF16),
             pltpu.VMEM((length * SUB, LANES), F32),
@@ -120,7 +123,7 @@
         compiler_params=pltpu.CompilerParams(vmem_limit_bytes=20 * MIB),
         cost_estimate=cost(2e8, 4 * MIB, NSTATE * length * channels),
         name="state_scan",
-    )(place, *pieces, w, bias, neg, x)
+    )(place, *pieces, w, bias, rate, x)
 
 
 def out_kernel(groups, line, first, at_ref, y_ref, sum_ref, enter_ref, bc_ref, neg_ref, x_ref, z_ref,
@@ -145,7 +148,7 @@
             out = y_ref[here, :]
             for n in range(NSTATE):
                 c = wide_ref[pl.ds(n * length + t, 1), :]
-                out = out + jnp.exp(total * neg_ref[n]) * enter_ref[n] * c
+                out = out + jnp.exp(total * neg_ref[pl.ds(n * SUB, SUB), :]) * enter_ref[n] * c
             full_ref[here, :] = out
         return carry
 
@@ -503,7 +506,7 @@
     late_rows = after(late_rows, early_go)
     late_hidden, out_left = finish(late_rows, late_first, sizes, w_gate, w_up, w_down, 0, half)
     early_result = home_third(after(early_kept, out_left[0]), early_far)
-    left = home_first(out_left)
+    left = home_first(after(out_left, early_result))
     left_far = cross(left[1], 1)
     out_right = down([after(late_hidden, left[1])], sizes, w_down, half, half)
     left = home_second(after(left[0], out_right), left_far)
@@ -574,13 +577,13 @@
     share = add_up(share, swap_pair(share)).astype(BF16)
     pieces = [share] + [along_line(share, s) for s in range(1, line)]
 
-    neg = -a_rate.reshape(NSTATE, channels // LANES, LANES)
-    neg = jnp.pad(neg, ((0, 0), (0, SUB - channels // LANES), (0, 0)))
     where = jnp.stack([place, half]).astype(jnp.int32)
-    y, total, end, bc = run_scan(where, pieces, dtproj_w, dt_bias[None, :], neg, mixed_in)
+    y, total, end, bc, neg = run_scan(
+        where, pieces, dtproj_w, dt_bias[None, :], a_rate, mixed_in
+    )
     enter = from_behind(end, "context", 1)
     for step in range(contexts - 2):
-        decay = jnp.exp(total[-SUB:][None] * neg)
+        decay = jnp.exp(total[-SUB:][None] * neg.reshape(end.shape))
         enter = from_behind(end + decay * enter, "context", 1)
     kept, sent, blocks = run_out(
         where, line, y, total, enter, bc, neg, mixed_in, z_gate[0, 0], skip_gain[None, :], out_w
@@ -601,7 +604,7 @@
         * lax.rsqrt(jnp.mean(stream_f * stream_f, axis=1, keepdims=True) + 1e-05)
         * norm_gain[None, :]
     ).astype(BF16)
-    ids, weights = route_ids[0, 0], route_w[0, 0]
+    ids, weights = after((route_ids[0, 0], route_w[0, 0]), kept)
     capacity = min(row_count, 8 * ((3 * row_count * TOP + 16 * line - 1) // (16 * line)))
     cuts = (0, 8, capacity) if contexts == 2 and dps == 2 and capacity > 8 else (0, capacity)
     named = jnp.any(ids[:, :, None] == jnp.arange(line, dtype=jnp.int32), axis=1)

time: 210 us -> 210 us (level)
  transfers between devices with their start and end apart: 46 -> 46, of which waited for: 33 -> 34; matrix products, arithmetic and copies ran while one was open for 3% -> 2% of each run, Pallas kernels for 16% -> 23%
where the time goes in v6:
time: 210 us; the launch traced here: 209 us
  waiting for transfers between devices  72.5 us (35%)
  Pallas kernels  63.8 us (30%)
  starting transfers between devices  61.5 us (29%)
  other arithmetic  5.8 us (3%)
  local copies, waits for them, and re-layouts  3.29 us (2%)
    ppermute x24, starting transfers between devices, along_line(): lax.ppermute(block, 'expert', [(e, (e + 2 * distance) % size) for e in ra...  43.1 us
    ppermute x24, waiting for transfers between devices, along_line(): lax.ppermute(block, 'expert', [(e, (e + 2 * distance) % size) for e in ra...  41.2 us
    pallas_call x2, Pallas kernels, finish(): pl.pallas_call(functools.partial(finish_kernel, len(pieces), first), out_...  26.3 us
    ppermute x10, waiting for transfers between devices, cross(): return lax.ppermute(block, ('expert', 'context', 'dp'), route)  18.9 us
    pallas_call x2, Pallas kernels, gate_up(): pl.pallas_call(functools.partial(gate_up_kernel, len(pieces), first), out...  16 us
    ppermute x10, starting transfers between devices, cross(): return lax.ppermute(block, ('expert', 'context', 'dp'), route)  10.3 us
    pallas_call x1, Pallas kernels, run_out(): pl.pallas_call(functools.partial(out_kernel, channels // LANES, line, fir...  9.19 us
    ppermute x7, waiting for transfers between devices, shift(): lax.ppermute(block, axis, [(i, (i + distance) % size) for i in range(size)])  8.93 us
  transfers between devices with their start and end apart: 46, of which 34 were waited for; matrix products, arithmetic and copies ran while one was open for 2% of the time, Pallas kernels for 23%

profile of v6, /device:TPU:0, one launch (start us, length us, event | category | flops | bytes accessed | tf_op | source)
XLA Modules:
  0.0 209.2 jit_solution(18439801029354145800)
XLA Ops:
  0.8 2.3 %collective-permute-start = (bf16[3,1024]{1,0:T(4,128)(2,1)S(1)}, bf16[3,1024]{1,0:T(4,128)(2,1)S(1)}, u32[]{:S(2)}, u32[]{:S(2)}) collective-permute-start(bf16[3,1024]{1,0:T(4,128)(2,1)S(1)} %slice_bitcast_fusion.3), channel_id=1, source_target_pairs={{0,2},{1,3},{4,6},{5,7},{8,10},{9,11},{12,14},{13,15},{16,18},{17,... | collective-permute-start | bytes 18440 | tf_op jit(solution)/shard_map/ppermute | solution.py:24
  6.6 2.5 %collective-permute-start.1 = (bf16[64,288]{1,0:T(8,128)(2,1)S(1)}, bf16[64,288]{1,0:T(8,128)(2,1)S(1)}, u32[]{:S(2)}, u32[]{:S(2)}) collective-permute-start(bf16[64,288]{1,0:T(8,128)(2,1)S(1)} %get-tuple-element.158), channel_id=1, source_target_pairs={{0,8},{4,12},{8,16},{12,20},{16,24},{20,28},{24,0},{28,4},{1,9},{5... | collective-permute-start | bytes 110600 | tf_op jit(solution)/shard_map/ppermute | solution.py:420
  9.1 2.6 %collective-permute-start.2 = (bf16[64,288]{1,0:T(8,128)(2,1)S(1)}, bf16[64,288]{1,0:T(8,128)(2,1)S(1)}, u32[]{:S(2)}, u32[]{:S(2)}) collective-permute-start(bf16[64,288]{1,0:T(8,128)(2,1)S(1)} %get-tuple-element.160), channel_id=1, source_target_pairs={{0,16},{4,20},{8,24},{12,28},{16,0},{20,4},{24,8},{28,12},{1,17},{... | collective-permute-start | bytes 110600 | tf_op jit(solution)/shard_map/ppermute | solution.py:420
  13.3 2.3 %collective-permute-done.2 = bf16[64,288]{1,0:T(8,128)(2,1)S(1)} collective-permute-done((bf16[64,288]{1,0:T(8,128)(2,1)S(1)}, bf16[64,288]{1,0:T(8,128)(2,1)S(1)}, u32[]{:S(2)}, u32[]{:S(2)}) %collective-permute-start.2) | collective-permute-done | bytes 36896 | tf_op jit(solution)/shard_map/ppermute | solution.py:420
  17.6 2.6 %collective-permute-done.4 = bf16[64,288]{1,0:T(8,128)(2,1)S(1)} collective-permute-done((bf16[64,288]{1,0:T(8,128)(2,1)S(1)}, bf16[64,288]{1,0:T(8,128)(2,1)S(1)}, u32[]{:S(2)}, u32[]{:S(2)}) %collective-permute-start.4) | collective-permute-done | bytes 36896 | tf_op jit(solution)/shard_map/ppermute | solution.py:34
  21.2 2.6 %collective-permute-start.6 = (bf16[64,288]{1,0:T(8,128)(2,1)S(1)}, bf16[64,288]{1,0:T(8,128)(2,1)S(1)}, u32[]{:S(2)}, u32[]{:S(2)}) collective-permute-start(bf16[64,288]{1,0:T(8,128)(2,1)S(1)} %add_convert_fusion.10.refs_0_), channel_id=1, source_target_pairs={{0,16},{4,20},{8,24},{12,28},{16,0},{20,4},{24,8},{28,12},{1,17},{... | collective-permute-start | bytes 110600 | tf_op jit(solution)/shard_map/ppermute | solution.py:420
  27.9 6.9 %state_scan.1 = (f32[2048,128]{1,0:T(8,128)S(1)}, f32[2048,128]{1,0:T(8,128)S(1)}, f32[16,8,128]{2,1,0:T(8,128)S(1)}, bf16[256,32]{1,0:T(8,128)(2,1)S(1)}, f32[128,128]{1,0:T(8,128)S(1)}) custom-call(s32[2]{0:T(128)S(1)} %pad_add_fusion.place_ref.at_ref, bf16[64,288]{1,0:T(8,128)(2,1)S(1)} %add_convert_fusion.10.refs_0_, ...), custom_call_target="tpu_custom_call" | custom-call | flops 200000000 | bytes 4194304 | tf_op jit(solution)/shard_map/state_scan/pallas_call | solution.py:106
  37.0 9.2 %readout_project.1 = (bf16[128,2560]{1,0:T(8,128)(2,1)S(1)}, bf16[128,2560]{1,0:T(8,128)(2,1)S(1)}, bf16[4,64,1536]{2,1,0:T(8,128)(2,1)S(1)}) custom-call(s32[2]{0:T(128)S(1)} %pad_add_fusion.place_ref.at_ref, f32[2048,128]{1,0:T(8,128)S(1)} %get-tuple-element.64.y_ref, f32[2048,128]{1,0:T(8,128)S(1)} %get-tuple-element.65.sum_ref, ...), custom_call_target="tpu_custom_call" | custom-call | flops 2147483648 | bytes 16777216 | tf_op jit(solution)/shard_map/readout_project/pallas_call | solution.py:201
  49.4 2.2 %collective-permute-start.14 = (bf16[64,1536]{1,0:T(8,128)(2,1)}, bf16[64,1536]{1,0:T(8,128)(2,1)S(1)}, u32[]{:S(2)}, u32[]{:S(2)}) collective-permute-start(bf16[64,1536]{1,0:T(8,128)(2,1)} %get-tuple-element.129), channel_id=1, source_target_pairs={{0,16},{4,20},{8,24},{12,28},{16,0},{20,4},{24,8},{28,12},{1,17},{... | collective-permute-start | bytes 589832 | tf_op jit(solution)/shard_map/ppermute | solution.py:420
  52.8 5.6 %collective-permute-done.13 = bf16[64,1536]{1,0:T(8,128)(2,1)S(1)} collective-permute-done((bf16[64,1536]{1,0:T(8,128)(2,1)}, bf16[64,1536]{1,0:T(8,128)(2,1)S(1)}, u32[]{:S(2)}, u32[]{:S(2)}) %collective-permute-start.13) | collective-permute-done | bytes 196640 | tf_op jit(solution)/shard_map/ppermute | solution.py:420
  58.4 7.6 %collective-permute-done.14 = bf16[64,1536]{1,0:T(8,128)(2,1)S(1)} collective-permute-done((bf16[64,1536]{1,0:T(8,128)(2,1)}, bf16[64,1536]{1,0:T(8,128)(2,1)S(1)}, u32[]{:S(2)}, u32[]{:S(2)}) %collective-permute-start.14) | collective-permute-done | bytes 196640 | tf_op jit(solution)/shard_map/ppermute | solution.py:420
  67.8 4.5 %collective-permute-start.10 = (bf16[32,2560]{1,0:T(8,128)(2,1)S(1)}, bf16[32,2560]{1,0:T(8,128)(2,1)S(1)}, u32[]{:S(2)}, u32[]{:S(2)}) collective-permute-start(bf16[32,2560]{1,0:T(8,128)(2,1)S(1)} %get-tuple-element.130), channel_id=1, source_target_pairs={{0,8},{4,12},{8,16},{12,20},{16,24},{20,28},{24,0},{28,4},{1,9},{5... | collective-permute-start | bytes 491528 | tf_op jit(solution)/shard_map/ppermute | solution.py:420
  72.5 2.3 %collective-permute-start.12 = (bf16[32,2560]{1,0:T(8,128)(2,1)S(1)}, bf16[32,2560]{1,0:T(8,128)(2,1)S(1)}, u32[]{:S(2)}, u32[]{:S(2)}) collective-permute-start(bf16[32,2560]{1,0:T(8,128)(2,1)S(1)} %get-tuple-element.131), channel_id=1, source_target_pairs={{0,24},{4,28},{8,0},{12,4},{16,8},{20,12},{24,16},{28,20},{1,25},{... | collective-permute-start | bytes 491528 | tf_op jit(solution)/shard_map/ppermute | solution.py:420
  74.8 2.2 %collective-permute-done.10 = bf16[32,2560]{1,0:T(8,128)(2,1)S(1)} collective-permute-done((bf16[32,2560]{1,0:T(8,128)(2,1)S(1)}, bf16[32,2560]{1,0:T(8,128)(2,1)S(1)}, u32[]{:S(2)}, u32[]{:S(2)}) %collective-permute-start.10) | collective-permute-done | bytes 163872 | tf_op jit(solution)/shard_map/ppermute | solution.py:420
  77.0 5.4 %collective-permute-done.11 = bf16[32,2560]{1,0:T(8,128)(2,1)S(1)} collective-permute-done((bf16[32,2560]{1,0:T(8,128)(2,1)S(1)}, bf16[32,2560]{1,0:T(8,128)(2,1)S(1)}, u32[]{:S(2)}, u32[]{:S(2)}) %collective-permute-start.11) | collective-permute-done | bytes 163872 | tf_op jit(solution)/shard_map/ppermute | solution.py:420
  83.1 4.0 %collective-permute-start.17 = (bf16[8,4096]{1,0:T(8,128)(2,1)S(1)}, bf16[8,4096]{1,0:T(8,128)(2,1)S(1)}, u32[]{:S(2)}, u32[]{:S(2)}) collective-permute-start(bf16[8,4096]{1,0:T(8,128)(2,1)S(1)} %get-tuple-element.156), channel_id=1, source_target_pairs={{0,8},{4,12},{8,16},{12,20},{16,24},{20,28},{24,0},{28,4},{1,9},{5... | collective-permute-start | bytes 196616 | tf_op jit(solution)/shard_map/ppermute | solution.py:420
  87.0 3.2 %collective-permute-start.18 = (bf16[8,4096]{1,0:T(8,128)(2,1)S(1)}, bf16[8,4096]{1,0:T(8,128)(2,1)S(1)}, u32[]{:S(2)}, u32[]{:S(2)}) collective-permute-start(bf16[8,4096]{1,0:T(8,128)(2,1)S(1)} %get-tuple-element.155), channel_id=1, source_target_pairs={{0,16},{4,20},{8,24},{12,28},{16,0},{20,4},{24,8},{28,12},{1,17},{... | collective-permute-start | bytes 196616 | tf_op jit(solution)/shard_map/ppermute | solution.py:420
  104.7 5.7 %collective-permute-done.21.refs_1_ = bf16[64,4096]{1,0:T(8,128)(2,1)S(1)} collective-permute-done((bf16[64,4096]{1,0:T(8,128)(2,1)S(1)}, bf16[64,4096]{1,0:T(8,128)(2,1)S(1)}, u32[]{:S(2)}, u32[]{:S(2)}) %collective-permute-start.21) | collective-permute-done | bytes 524320 | tf_op jit(solution)/shard_map/ppermute | solution.py:431
  112.4 6.3 %gate_up.2.refs_4_ = bf16[256,768]{1,0:T(8,128)(2,1)S(1)} custom-call(bf16[64,4096]{1,0:T(8,128)(2,1)S(1)} %constant_dynamic-update-slice_fusion.refs_0_, bf16[64,4096]{1,0:T(8,128)(2,1)S(1)} %collective-permute-done.21.refs_1_, bf16[64,4096]{1,0:T(8,128)(2,1)S(1)} %collective-permute-done.22.refs_2_, bf16[64,4096]{1,0:T(8,128)(2,1)S(1)} %collective-permute-done.23.refs_3_, ...), custom_call_target="tpu_custom_call" | custom-call | flops 3221225472 | bytes 14680064 | tf_op jit(solution)/shard_map/gate_up/pallas_call | solution.py:262
  121.3 12.0 %gate_up_down.2 = (bf16[256,1536]{1,0:T(8,128)(2,1)}, bf16[128,4096]{1,0:T(8,128)(2,1)S(1)}, bf16[128,4096]{1,0:T(8,128)(2,1)}) custom-call(bf16[64,4096]{1,0:T(8,128)(2,1)S(1)} %constant_dynamic-update-slice_fusion.refs_0_, bf16[64,4096]{1,0:T(8,128)(2,1)S(1)} %collective-permute-done.21.refs_1_, bf16[64,4096]{1,0:T(8,128)(2,1)S(1)} %collective-permute-done.22.refs_2_, ...), custom_call_target="tpu_custom_call" | custom-call | flops 6442450944 | bytes 29360128 | tf_op jit(solution)/shard_map/gate_up_down/pallas_call | solution.py:343
  134.7 2.3 %collective-permute-done.29 = bf16[128,4096]{1,0:T(8,128)(2,1)S(1)} collective-permute-done((bf16[128,4096]{1,0:T(8,128)(2,1)}, bf16[128,4096]{1,0:T(8,128)(2,1)S(1)}, u32[]{:S(2)}, u32[]{:S(2)}) %collective-permute-start.29) | collective-permute-done | bytes 1048608 | tf_op jit(solution)/shard_map/ppermute | solution.py:29
  139.0 9.7 %gate_up.3.refs_4_ = bf16[512,768]{1,0:T(8,128)(2,1)S(1)} custom-call(bf16[128,4096]{1,0:T(8,128)(2,1)S(1)} %constant_dynamic-update-slice_fusion.9.refs_0_, bf16[128,4096]{1,0:T(8,128)(2,1)S(1)} %collective-permute-done.28.refs_1_, bf16[128,4096]{1,0:T(8,128)(2,1)S(1)} %collective-permute-done.30.refs_2_, ...), custom_call_target="tpu_custom_call" | custom-call | flops 6442450944 | bytes 16777216 | tf_op jit(solution)/shard_map/gate_up/pallas_call | solution.py:262
  150.5 14.3 %gate_up_down.3 = (bf16[512,1536]{1,0:T(8,128)(2,1)}, bf16[256,2048]{1,0:T(8,128)(2,1)S(1)}, bf16[256,2048]{1,0:T(8,128)(2,1)S(1)}) custom-call(bf16[128,4096]{1,0:T(8,128)(2,1)S(1)} %constant_dynamic-update-slice_fusion.9.refs_0_, bf16[128,4096]{1,0:T(8,128)(2,1)S(1)} %collective-permute-done.28.refs_1_, bf16[128,4096]{1,0:T(8,128)(2,1)} %copy-done.2, ...), custom_call_target="tpu_custom_call" | custom-call | flops 9663676416 | bytes 25165824 | tf_op jit(solution)/shard_map/gate_up_down/pallas_call | solution.py:343
  165.1 2.6 %collective-permute-done.34 = bf16[256,2048]{1,0:T(8,128)(2,1)S(1)} collective-permute-done((bf16[256,2048]{1,0:T(8,128)(2,1)S(1)}, bf16[256,2048]{1,0:T(8,128)(2,1)S(1)}, u32[]{:S(2)}, u32[]{:S(2)}) %collective-permute-start.34) | collective-permute-done | bytes 1048608 | tf_op jit(solution)/shard_map/ppermute | solution.py:29
  168.5 5.4 %down.1 = (bf16[256,2048]{1,0:T(8,128)(2,1)S(1)}, bf16[256,2048]{1,0:T(8,128)(2,1)S(1)}) custom-call(bf16[512,1536]{1,0:T(8,128)(2,1)S(1)} %copy-done.4, bf16[1536,4096]{1,0:T(8,128)(2,1)} %bitcast.68), custom_call_target="tpu_custom_call" | custom-call | flops 3221225472 | bytes 9961472 | tf_op jit(solution)/shard_map/down/pallas_call | solution.py:398
  173.9 3.3 %collective-permute-done.35 = bf16[128,2048]{1,0:T(8,128)(2,1)S(1)} collective-permute-done((bf16[128,2048]{1,0:T(8,128)(2,1)S(1)}, bf16[128,2048]{1,0:T(8,128)(2,1)S(1)}, u32[]{:S(2)}, u32[]{:S(2)}) %collective-permute-start.35) | collective-permute-done | bytes 524320 | tf_op jit(solution)/shard_map/ppermute | solution.py:431
  180.7 4.3 %collective-permute-done.37 = bf16[64,2048]{1,0:T(8,128)(2,1)S(1)} collective-permute-done((bf16[64,2048]{1,0:T(8,128)(2,1)S(1)}, bf16[64,2048]{1,0:T(8,128)(2,1)S(1)}, u32[]{:S(2)}, u32[]{:S(2)}) %collective-permute-start.37) | collective-permute-done | bytes 262176 | tf_op jit(solution)/shard_map/ppermute | solution.py:431
  186.0 3.0 %collective-permute-start.39 = (bf16[32,2048]{1,0:T(8,128)(2,1)S(1)}, bf16[32,2048]{1,0:T(8,128)(2,1)S(1)}, u32[]{:S(2)}, u32[]{:S(2)}) collective-permute-start(bf16[32,2048]{1,0:T(8,128)(2,1)S(1)} %pad_maximum_fusion.3), channel_id=1, source_target_pairs={{0,16},{4,20},{8,24},{12,28},{16,0},{20,4},{24,8},{28,12},{1,17},{... | collective-permute-start | bytes 393224 | tf_op jit(solution)/shard_map/ppermute | solution.py:420
  190.0 3.3 %collective-permute-start.38 = (bf16[32,2048]{1,0:T(8,128)(2,1)S(1)}, bf16[32,2048]{1,0:T(8,128)(2,1)S(1)}, u32[]{:S(2)}, u32[]{:S(2)}) collective-permute-start(bf16[32,2048]{1,0:T(8,128)(2,1)S(1)} %pad_maximum_fusion.2), channel_id=1, source_target_pairs={{0,24},{4,28},{8,0},{12,4},{16,8},{20,12},{24,16},{28,20},{1,25},{... | collective-permute-start | bytes 393224 | tf_op jit(solution)/shard_map/ppermute | solution.py:420
  193.3 2.6 %collective-permute-done.42 = bf16[64,2048]{1,0:T(8,128)(2,1)S(1)} collective-permute-done((bf16[64,2048]{1,0:T(8,128)(2,1)S(1)}, bf16[64,2048]{1,0:T(8,128)(2,1)S(1)}, u32[]{:S(2)}, u32[]{:S(2)}) %collective-permute-start.42) | collective-permute-done | bytes 262176 | tf_op jit(solution)/shard_map/ppermute | solution.py:431
  198.2 2.6 %collective-permute-start.43 = (bf16[16,2048]{1,0:T(8,128)(2,1)S(1)}, bf16[16,2048]{1,0:T(8,128)(2,1)S(1)}, u32[]{:S(2)}, u32[]{:S(2)}) collective-permute-start(bf16[16,2048]{1,0:T(8,128)(2,1)S(1)} %get-tuple-element.139), channel_id=1, source_target_pairs={{0,24},{4,28},{8,0},{12,4},{16,8},{20,12},{24,16},{28,20},{1,25},{... | collective-permute-start | bytes 196616 | tf_op jit(solution)/shard_map/ppermute | solution.py:420
  203.3 4.8 %collective-permute-done.44 = bf16[16,2048]{1,0:T(8,128)(2,1)S(1)} collective-permute-done((bf16[16,2048]{1,0:T(8,128)(2,1)S(1)}, bf16[16,2048]{1,0:T(8,128)(2,1)S(1)}, u32[]{:S(2)}, u32[]{:S(2)}) %collective-permute-start.44) | collective-permute-done | bytes 65568 | tf_op jit(solution)/shard_map/ppermute | solution.py:420
  (174 shorter events, 58.7 us)
Async XLA Ops:
  6.6 6.6 %collective-permute-start.1 = (bf16[64,288]{1,0:T(8,128)(2,1)S(1)}, bf16[64,288]{1,0:T(8,128)(2,1)S(1)}, u32[]{:S(2)}, u32[]{:S(2)}) collective-permute-start(bf16[64,288]{1,0:T(8,128)(2,1)S(1)} %get-tuple-element.158), channel_id=1, source_target_pairs={{0,8},{4,12},{8,16},{12,20},{16,24},{20,28},{24,0},{28,4},{1,9},{5... | collective-permute-start | bytes 110600 | tf_op jit(solution)/shard_map/ppermute | solution.py:420
  9.1 6.5 %collective-permute-start.2 = (bf16[64,288]{1,0:T(8,128)(2,1)S(1)}, bf16[64,288]{1,0:T(8,128)(2,1)S(1)}, u32[]{:S(2)}, u32[]{:S(2)}) collective-permute-start(bf16[64,288]{1,0:T(8,128)(2,1)S(1)} %get-tuple-element.160), channel_id=1, source_target_pairs={{0,16},{4,20},{8,24},{12,28},{16,0},{20,4},{24,8},{28,12},{1,17},{... | collective-permute-start | bytes 110600 | tf_op jit(solution)/shard_map/ppermute | solution.py:420
  20.2 6.0 %collective-permute-start.5 = (bf16[64,288]{1,0:T(8,128)(2,1)S(1)}, bf16[64,288]{1,0:T(8,128)(2,1)S(1)}, u32[]{:S(2)}, u32[]{:S(2)}) collective-permute-start(bf16[64,288]{1,0:T(8,128)(2,1)S(1)} %add_convert_fusion.10.refs_0_), channel_id=1, source_target_pairs={{0,8},{4,12},{8,16},{12,20},{16,24},{20,28},{24,0},{28,4},{1,9},{5... | collective-permute-start | bytes 110600 | tf_op jit(solution)/shard_map/ppermute | solution.py:420
  46.2 21.5 %collective-permute-start.9 = (bf16[128,2560]{1,0:T(8,128)(2,1)S(1)}, bf16[128,2560]{1,0:T(8,128)(2,1)S(1)}, u32[]{:S(2)}, u32[]{:S(2)}) collective-permute-start(bf16[128,2560]{1,0:T(8,128)(2,1)S(1)} %get-tuple-element.70), channel_id=1, source_target_pairs={{0,4},{4,0},{8,12},{12,8},{16,20},{20,16},{24,28},{28,24},{1,5},{5... | collective-permute-start | bytes 1966088 | tf_op jit(solution)/shard_map/ppermute | solution.py:34
  48.5 9.9 %collective-permute-start.13 = (bf16[64,1536]{1,0:T(8,128)(2,1)}, bf16[64,1536]{1,0:T(8,128)(2,1)S(1)}, u32[]{:S(2)}, u32[]{:S(2)}) collective-permute-start(bf16[64,1536]{1,0:T(8,128)(2,1)} %get-tuple-element.127), channel_id=1, source_target_pairs={{0,8},{4,12},{8,16},{12,20},{16,24},{20,28},{24,0},{28,4},{1,9},{5... | collective-permute-start | bytes 589832 | tf_op jit(solution)/shard_map/ppermute | solution.py:420
  49.4 16.6 %collective-permute-start.14 = (bf16[64,1536]{1,0:T(8,128)(2,1)}, bf16[64,1536]{1,0:T(8,128)(2,1)S(1)}, u32[]{:S(2)}, u32[]{:S(2)}) collective-permute-start(bf16[64,1536]{1,0:T(8,128)(2,1)} %get-tuple-element.129), channel_id=1, source_target_pairs={{0,16},{4,20},{8,24},{12,28},{16,0},{20,4},{24,8},{28,12},{1,17},{... | collective-permute-start | bytes 589832 | tf_op jit(solution)/shard_map/ppermute | solution.py:420
  51.5 14.5 %collective-permute-start.15 = (bf16[64,1536]{1,0:T(8,128)(2,1)S(1)}, bf16[64,1536]{1,0:T(8,128)(2,1)}, u32[]{:S(2)}, u32[]{:S(2)}) collective-permute-start(bf16[64,1536]{1,0:T(8,128)(2,1)S(1)} %get-tuple-element.128), channel_id=1, source_target_pairs={{0,24},{4,28},{8,0},{12,4},{16,8},{20,12},{24,16},{28,20},{1,25},{... | collective-permute-start | bytes 589832 | tf_op jit(solution)/shard_map/ppermute | solution.py:420
  67.0 7.7 %collective-permute-start.16 = (bf16[32,1536]{1,0:T(8,128)(2,1)S(1)}, bf16[32,1536]{1,0:T(8,128)(2,1)S(1)}, u32[]{:S(2)}, u32[]{:S(2)}) collective-permute-start(bf16[32,1536]{1,0:T(8,128)(2,1)S(1)} %slice.456), channel_id=1, source_target_pairs={{0,4},{4,0},{8,12},{12,8},{16,20},{20,16},{24,28},{28,24},{1,5},{5... | collective-permute-start | bytes 294920 | tf_op jit(solution)/shard_map/ppermute | solution.py:34
  67.8 9.2 %collective-permute-start.10 = (bf16[32,2560]{1,0:T(8,128)(2,1)S(1)}, bf16[32,2560]{1,0:T(8,128)(2,1)S(1)}, u32[]{:S(2)}, u32[]{:S(2)}) collective-permute-start(bf16[32,2560]{1,0:T(8,128)(2,1)S(1)} %get-tuple-element.130), channel_id=1, source_target_pairs={{0,8},{4,12},{8,16},{12,20},{16,24},{20,28},{24,0},{28,4},{1,9},{5... | collective-permute-start | bytes 491528 | tf_op jit(solution)/shard_map/ppermute | solution.py:420
  72.3 10.0 %collective-permute-start.11 = (bf16[32,2560]{1,0:T(8,128)(2,1)S(1)}, bf16[32,2560]{1,0:T(8,128)(2,1)S(1)}, u32[]{:S(2)}, u32[]{:S(2)}) collective-permute-start(bf16[32,2560]{1,0:T(8,128)(2,1)S(1)} %get-tuple-element.132), channel_id=1, source_target_pairs={{0,16},{4,20},{8,24},{12,28},{16,0},{20,4},{24,8},{28,12},{1,17},{... | collective-permute-start | bytes 491528 | tf_op jit(solution)/shard_map/ppermute | solution.py:420
  72.5 9.9 %collective-permute-start.12 = (bf16[32,2560]{1,0:T(8,128)(2,1)S(1)}, bf16[32,2560]{1,0:T(8,128)(2,1)S(1)}, u32[]{:S(2)}, u32[]{:S(2)}) collective-permute-start(bf16[32,2560]{1,0:T(8,128)(2,1)S(1)} %get-tuple-element.131), channel_id=1, source_target_pairs={{0,24},{4,28},{8,0},{12,4},{16,8},{20,12},{24,16},{28,20},{1,25},{... | collective-permute-start | bytes 491528 | tf_op jit(solution)/shard_map/ppermute | solution.py:420
  83.1 9.4 %collective-permute-start.17 = (bf16[8,4096]{1,0:T(8,128)(2,1)S(1)}, bf16[8,4096]{1,0:T(8,128)(2,1)S(1)}, u32[]{:S(2)}, u32[]{:S(2)}) collective-permute-start(bf16[8,4096]{1,0:T(8,128)(2,1)S(1)} %get-tuple-element.156), channel_id=1, source_target_pairs={{0,8},{4,12},{8,16},{12,20},{16,24},{20,28},{24,0},{28,4},{1,9},{5... | collective-permute-start | bytes 196616 | tf_op jit(solution)/shard_map/ppermute | solution.py:420
  87.0 7.2 %collective-permute-start.18 = (bf16[8,4096]{1,0:T(8,128)(2,1)S(1)}, bf16[8,4096]{1,0:T(8,128)(2,1)S(1)}, u32[]{:S(2)}, u32[]{:S(2)}) collective-permute-start(bf16[8,4096]{1,0:T(8,128)(2,1)S(1)} %get-tuple-element.155), channel_id=1, source_target_pairs={{0,16},{4,20},{8,24},{12,28},{16,0},{20,4},{24,8},{28,12},{1,17},{... | collective-permute-start | bytes 196616 | tf_op jit(solution)/shard_map/ppermute | solution.py:420
  94.8 6.4 %collective-permute-start.20 = (bf16[32,4096]{1,0:T(8,128)(2,1)S(1)}, bf16[32,4096]{1,0:T(8,128)(2,1)S(1)}, u32[]{:S(2)}, u32[]{:S(2)}) collective-permute-start(bf16[32,4096]{1,0:T(8,128)(2,1)S(1)} %pad_maximum_fusion), channel_id=1, source_target_pairs={{0,4},{1,5},{2,3},{3,2},{4,0},{5,1},{6,7},{7,6},{8,12},{9,13},{10,... | collective-permute-start | bytes 786440 | tf_op jit(solution)/shard_map/ppermute | solution.py:431
  96.4 8.4 %collective-permute-start.24 = (bf16[16,4096]{1,0:T(8,128)(2,1)S(1)}, bf16[16,4096]{1,0:T(8,128)(2,1)S(1)}, u32[]{:S(2)}, u32[]{:S(2)}) collective-permute-start(bf16[16,4096]{1,0:T(8,128)(2,1)S(1)} %get-tuple-element.135), channel_id=1, source_target_pairs={{0,8},{4,12},{8,16},{12,20},{16,24},{20,28},{24,0},{28,4},{1,9},{5... | collective-permute-start | bytes 393224 | tf_op jit(solution)/shard_map/ppermute | solution.py:420
  97.3 13.2 %collective-permute-start.25 = (bf16[16,4096]{1,0:T(8,128)(2,1)S(1)}, bf16[16,4096]{1,0:T(8,128)(2,1)S(1)}, u32[]{:S(2)}, u32[]{:S(2)}) collective-permute-start(bf16[16,4096]{1,0:T(8,128)(2,1)S(1)} %get-tuple-element.134), channel_id=1, source_target_pairs={{0,16},{4,20},{8,24},{12,28},{16,0},{20,4},{24,8},{28,12},{1,17},{... | collective-permute-start | bytes 393224 | tf_op jit(solution)/shard_map/ppermute | solution.py:420
  99.3 11.2 %collective-permute-start.26 = (bf16[16,4096]{1,0:T(8,128)(2,1)S(1)}, bf16[16,4096]{1,0:T(8,128)(2,1)S(1)}, u32[]{:S(2)}, u32[]{:S(2)}) collective-permute-start(bf16[16,4096]{1,0:T(8,128)(2,1)S(1)} %get-tuple-element.133), channel_id=1, source_target_pairs={{0,24},{4,28},{8,0},{12,4},{16,8},{20,12},{24,16},{28,20},{1,25},{... | collective-permute-start | bytes 393224 | tf_op jit(solution)/shard_map/ppermute | solution.py:420
  101.2 9.2 %collective-permute-start.21 = (bf16[64,4096]{1,0:T(8,128)(2,1)S(1)}, bf16[64,4096]{1,0:T(8,128)(2,1)S(1)}, u32[]{:S(2)}, u32[]{:S(2)}) collective-permute-start(bf16[64,4096]{1,0:T(8,128)(2,1)S(1)} %constant_dynamic-update-slice_fusion.refs_0_), channel_id=1, source_target_pairs={{0,1},{1,0},{2,6},{3,7},{4,5},{5,4},{6,2},{7,3},{8,9},{9,8},{10,14... | collective-permute-start | bytes 1572872 | tf_op jit(solution)/shard_map/ppermute | solution.py:431
  102.8 9.3 %collective-permute-start.22 = (bf16[64,4096]{1,0:T(8,128)(2,1)S(1)}, bf16[64,4096]{1,0:T(8,128)(2,1)S(1)}, u32[]{:S(2)}, u32[]{:S(2)}) collective-permute-start(bf16[64,4096]{1,0:T(8,128)(2,1)S(1)} %constant_dynamic-update-slice_fusion.refs_0_), channel_id=1, source_target_pairs={{0,2},{2,0},{1,3},{3,1},{4,6},{6,4},{5,7},{7,5},{8,10},{10,8},{9,1... | collective-permute-start | bytes 1572872 | tf_op jit(solution)/shard_map/ppermute | solution.py:29
  110.5 9.2 %collective-permute-start.27 = (bf16[64,4096]{1,0:T(8,128)(2,1)S(1)}, bf16[64,4096]{1,0:T(8,128)(2,1)S(1)}, u32[]{:S(2)}, u32[]{:S(2)}) collective-permute-start(bf16[64,4096]{1,0:T(8,128)(2,1)S(1)} %constant_dynamic-update-slice_fusion.5), channel_id=1, source_target_pairs={{0,4},{1,5},{2,3},{3,2},{4,0},{5,1},{6,7},{7,6},{8,12},{9,13},{10,... | collective-permute-start | bytes 1572872 | tf_op jit(solution)/shard_map/ppermute | solution.py:431
  119.8 14.9 %collective-permute-start.28 = (bf16[128,4096]{1,0:T(8,128)(2,1)S(1)}, bf16[128,4096]{1,0:T(8,128)(2,1)S(1)}, u32[]{:S(2)}, u32[]{:S(2)}) collective-permute-start(bf16[128,4096]{1,0:T(8,128)(2,1)S(1)} %constant_dynamic-update-slice_fusion.9.refs_0_), channel_id=1, source_target_pairs={{0,1},{1,0},{2,6},{3,7},{4,5},{5,4},{6,2},{7,3},{8,9},{9,8},{10,14... | collective-permute-start | bytes 3145736 | tf_op jit(solution)/shard_map/ppermute | solution.py:431
  137.1 11.7 %collective-permute-start.32 = (bf16[64,4096]{1,0:T(8,128)(2,1)S(1)}, bf16[64,4096]{1,0:T(8,128)(2,1)S(1)}, u32[]{:S(2)}, u32[]{:S(2)}) collective-permute-start(bf16[64,4096]{1,0:T(8,128)(2,1)S(1)} %add_convert_fusion.3), channel_id=1, source_target_pairs={{0,1},{1,0},{2,6},{3,7},{4,5},{5,4},{6,2},{7,3},{8,9},{9,8},{10,14... | collective-permute-start | bytes 1572872 | tf_op jit(solution)/shard_map/ppermute | solution.py:431
  148.9 15.9 %collective-permute-start.33 = (bf16[32,4096]{1,0:T(8,128)(2,1)S(1)}, bf16[32,4096]{1,0:T(8,128)(2,1)S(1)}, u32[]{:S(2)}, u32[]{:S(2)}) collective-permute-start(bf16[32,4096]{1,0:T(8,128)(2,1)S(1)} %add_convert_fusion.9), channel_id=1, source_target_pairs={{0,4},{1,5},{2,3},{3,2},{4,0},{5,1},{6,7},{7,6},{8,12},{9,13},{10,... | collective-permute-start | bytes 786440 | tf_op jit(solution)/shard_map/ppermute | solution.py:431
  167.9 9.2 %collective-permute-start.35 = (bf16[128,2048]{1,0:T(8,128)(2,1)S(1)}, bf16[128,2048]{1,0:T(8,128)(2,1)S(1)}, u32[]{:S(2)}, u32[]{:S(2)}) collective-permute-start(bf16[128,2048]{1,0:T(8,128)(2,1)S(1)} %add_convert_fusion.2), channel_id=1, source_target_pairs={{0,1},{1,0},{2,6},{3,7},{4,5},{5,4},{6,2},{7,3},{8,9},{9,8},{10,14... | collective-permute-start | bytes 1572872 | tf_op jit(solution)/shard_map/ppermute | solution.py:431
  177.5 7.5 %collective-permute-start.37 = (bf16[64,2048]{1,0:T(8,128)(2,1)S(1)}, bf16[64,2048]{1,0:T(8,128)(2,1)S(1)}, u32[]{:S(2)}, u32[]{:S(2)}) collective-permute-start(bf16[64,2048]{1,0:T(8,128)(2,1)S(1)} %add_convert_fusion.7), channel_id=1, source_target_pairs={{0,4},{1,5},{2,3},{3,2},{4,0},{5,1},{6,7},{7,6},{8,12},{9,13},{10,... | collective-permute-start | bytes 786440 | tf_op jit(solution)/shard_map/ppermute | solution.py:431
  180.1 9.2 %collective-permute-start.41 = (bf16[128,2048]{1,0:T(8,128)(2,1)S(1)}, bf16[128,2048]{1,0:T(8,128)(2,1)S(1)}, u32[]{:S(2)}, u32[]{:S(2)}) collective-permute-start(bf16[128,2048]{1,0:T(8,128)(2,1)S(1)} %add_convert_fusion.1), channel_id=1, source_target_pairs={{0,1},{1,0},{2,6},{3,7},{4,5},{5,4},{6,2},{7,3},{8,9},{9,8},{10,14... | collective-permute-start | bytes 1572872 | tf_op jit(solution)/shard_map/ppermute | solution.py:431
  185.1 10.8 %collective-permute-start.40 = (bf16[32,2048]{1,0:T(8,128)(2,1)S(1)}, bf16[32,2048]{1,0:T(8,128)(2,1)S(1)}, u32[]{:S(2)}, u32[]{:S(2)}) collective-permute-start(bf16[32,2048]{1,0:T(8,128)(2,1)S(1)} %pad_maximum_fusion.4), channel_id=1, source_target_pairs={{0,8},{4,12},{8,16},{12,20},{16,24},{20,28},{24,0},{28,4},{1,9},{5... | collective-permute-start | bytes 393224 | tf_op jit(solution)/shard_map/ppermute | solution.py:420
  186.0 10.7 %collective-permute-start.39 = (bf16[32,2048]{1,0:T(8,128)(2,1)S(1)}, bf16[32,2048]{1,0:T(8,128)(2,1)S(1)}, u32[]{:S(2)}, u32[]{:S(2)}) collective-permute-start(bf16[32,2048]{1,0:T(8,128)(2,1)S(1)} %pad_maximum_fusion.3), channel_id=1, source_target_pairs={{0,16},{4,20},{8,24},{12,28},{16,0},{20,4},{24,8},{28,12},{1,17},{... | collective-permute-start | bytes 393224 | tf_op jit(solution)/shard_map/ppermute | solution.py:420
  189.4 6.4 %collective-permute-start.42 = (bf16[64,2048]{1,0:T(8,128)(2,1)S(1)}, bf16[64,2048]{1,0:T(8,128)(2,1)S(1)}, u32[]{:S(2)}, u32[]{:S(2)}) collective-permute-start(bf16[64,2048]{1,0:T(8,128)(2,1)S(1)} %add_convert_fusion.5), channel_id=1, source_target_pairs={{0,4},{1,5},{2,3},{3,2},{4,0},{5,1},{6,7},{7,6},{8,12},{9,13},{10,... | collective-permute-start | bytes 786440 | tf_op jit(solution)/shard_map/ppermute | solution.py:431
  190.0 8.0 %collective-permute-start.38 = (bf16[32,2048]{1,0:T(8,128)(2,1)S(1)}, bf16[32,2048]{1,0:T(8,128)(2,1)S(1)}, u32[]{:S(2)}, u32[]{:S(2)}) collective-permute-start(bf16[32,2048]{1,0:T(8,128)(2,1)S(1)} %pad_maximum_fusion.2), channel_id=1, source_target_pairs={{0,24},{4,28},{8,0},{12,4},{16,8},{20,12},{24,16},{28,20},{1,25},{... | collective-permute-start | bytes 393224 | tf_op jit(solution)/shard_map/ppermute | solution.py:420
  200.7 7.4 %collective-permute-start.44 = (bf16[16,2048]{1,0:T(8,128)(2,1)S(1)}, bf16[16,2048]{1,0:T(8,128)(2,1)S(1)}, u32[]{:S(2)}, u32[]{:S(2)}) collective-permute-start(bf16[16,2048]{1,0:T(8,128)(2,1)S(1)} %get-tuple-element.138), channel_id=1, source_target_pairs={{0,16},{4,20},{8,24},{12,28},{16,0},{20,4},{24,8},{28,12},{1,17},{... | collective-permute-start | bytes 196616 | tf_op jit(solution)/shard_map/ppermute | solution.py:420
  201.7 6.4 %collective-permute-start.45 = (bf16[16,2048]{1,0:T(8,128)(2,1)S(1)}, bf16[16,2048]{1,0:T(8,128)(2,1)S(1)}, u32[]{:S(2)}, u32[]{:S(2)}) collective-permute-start(bf16[16,2048]{1,0:T(8,128)(2,1)S(1)} %get-tuple-element.137), channel_id=1, source_target_pairs={{0,8},{4,12},{8,16},{12,20},{16,24},{20,28},{24,0},{28,4},{1,9},{5... | collective-permute-start | bytes 196616 | tf_op jit(solution)/shard_map/ppermute | solution.py:420
  (29 other events, 232.5 us)

commit v7 on v6

--- a/solution.py
+++ b/solution.py
@@ -455,9 +455,7 @@
 
 def square_experts(early, late, line, w_gate, w_up, w_down):
     width = w_down.shape[1]
-    half = width // 2
     hidden = w_down.shape[0]
-    most = hidden // 2
 
     def pieces(two, four):
         return [two, four, shift(two, "context", 1), shift(four, "context", 1)]
@@ -489,45 +487,30 @@
     late_near = cross(late_own, 0)
     sizes = (4 * early_own.shape[0],) * 2
     early_rows = after(pieces(early_two, early_four), late_own)
-    early_first = gate_up(early_rows, w_gate, w_up, 0, most)
+    early_first = gate_up(early_rows, w_gate, w_up, 0, hidden // 2)
 
     late_two = jnp.concatenate([after(late_own, early_first), late_near], axis=0)
     late_four = cross(late_two, 1)
     early_rows = after(early_rows, late_two)
     early_out = finish(early_rows, early_first, sizes, w_gate, w_up, w_down, 0, width)[1]
     late_four = after(late_four, early_out)
-    early_kept, early_go = home_first(early_out, late_four)
+    early_kept, early_go = home_first(after(early_out, late_four))
     early_far = cross(early_go, 1)
     sizes = (4 * late_own.shape[0],) * 2
     late_rows = after(pieces(late_two, late_four), early_go)
-    late_first = gate_up(late_rows, w_gate, w_up, 0, hidden // 2)
-    early_kept, early_go = home_second(after(early_kept, late_first), early_far)
+    late_hidden = gate_up(late_rows, w_gate, w_up, 0, hidden)
+    early_kept, early_go = home_second(after(early_kept, late_hidden), early_far)
     early_far = cross(early_go, 0)
-    late_rows = after(late_rows, early_go)
-    late_hidden, out_left = finish(late_rows, late_first, sizes, w_gate, w_up, w_down, 0, half)
-    early_result = home_third(after(early_kept, out_left[0]), early_far)
-    left = home_first(after(out_left, early_result))
-    left_far = cross(left[1], 1)
-    out_right = down([after(late_hidden, left[1])], sizes, w_down, half, half)
-    left = home_second(after(left[0], out_right), left_far)
-    left_far = cross(left[1], 0)
-    right = home_first(after(out_right, left[1]))
-    right_far = cross(right[1], 1)
-    left_result = home_third(after(left[0], right[1]), left_far)
-    right = home_second(after(right[0], left_result), right_far)
-    right_far = cross(right[1], 0)
-    few, many = early_result.shape[0] // line, left_result.shape[0] // line
-    packed = []
-    for s in range(line):
-        mine = early_result[few * s : few * (s + 1)]
-        packed += [mine[:, :half], mine[:, half:], left_result[many * s : many * (s + 1)]]
-    left_came = send_rows(jnp.concatenate(packed, axis=0), line, -1)
-    right_result = home_third(right[0], right_far)
-    right_came = send_rows(right_result, line, -1)
-    left_came = after(left_came, right_result)
-    left_rows = [c[:few] for c in left_came] + [c[2 * few :] for c in left_came]
-    right_rows = [c[few : 2 * few] for c in left_came] + right_came
-    return [jnp.concatenate(rows, axis=0) for rows in (left_rows, right_rows)]
+    late_out = down([after(late_hidden, early_go)], sizes, w_down, 0, width)
+    early_result = home_third(after(early_kept, late_out), early_far)
+    early_came = send_rows(early_result, line, -1)
+    late_kept, late_go = home_first(after(late_out, early_result))
+    late_far = cross(late_go, 1)
+    late_kept, late_go = home_second(after(late_kept, early_came[1]), late_far)
+    late_far = cross(late_go, 0)
+    late_result = home_third(after(late_kept, early_came[2:]), late_far)
+    late_came = send_rows(late_result, line, -1)
+    return [jnp.concatenate(came, axis=0) for came in (early_came, late_came)]
 
 
 def on_device(
@@ -606,7 +589,8 @@
     ).astype(BF16)
     ids, weights = after((route_ids[0, 0], route_w[0, 0]), kept)
     capacity = min(row_count, 8 * ((3 * row_count * TOP + 16 * line - 1) // (16 * line)))
-    cuts = (0, 8, capacity) if contexts == 2 and dps == 2 and capacity > 8 else (0, capacity)
+    square = contexts == 2 and dps == 2 and capacity > 8
+    cuts = (0, capacity - 8, capacity) if square else (0, capacity)
     named = jnp.any(ids[:, :, None] == jnp.arange(line, dtype=jnp.int32), axis=1)
     rank = jnp.cumsum(named.astype(jnp.int32), axis=0) - 1
     chosen = ids[:, :, None] == jnp.arange(line, dtype=jnp.int32)
@@ -627,18 +611,11 @@
         back = square_experts(*packed, line, w_gate[0], w_up[0], w_down[0])
     else:
         back = [plain_experts(packed[0], line, w_gate[0], w_up[0], w_down[0])]
-    weighting = jnp.concatenate(weighting, axis=1)
-    expert_sum = jnp.concatenate(
-        [
-            jnp.dot(
-                weighting,
-                rows.astype(F32),
-                precision=lax.Precision.HIGHEST,
-                preferred_element_type=F32,
-            )
-            for rows in back
-        ],
-        axis=1,
+    expert_sum = sum(
+        jnp.dot(
+            w, rows.astype(F32), precision=lax.Precision.HIGHEST, preferred_element_type=F32
+        )
+        for w, rows in zip(weighting, back)
     )
     mixed = (stream_f + expert_sum).astype(BF16)
     return mixed.reshape(1, 1, row_count, width)

time: 210 us -> 223 us (1.062)
  waiting for transfers between devices: 72.5 us -> 83.6 us
  starting transfers between devices: 61.5 us -> 64.7 us
  Pallas kernels: 63.8 us -> 61.4 us
    ppermute x24, waiting for transfers between devices: 41.2 us -> 49.8 us  [along_line(): lax.ppermute(block, 'expert', [(e, (e + 2 * distance) % size) for e in ra...]
    pallas_call x2 -> x1, Pallas kernels: 26.3 us -> 19.5 us  [finish(): pl.pallas_call(functools.partial(finish_kernel, len(pieces), first), out_...]
    pallas_call x2, Pallas kernels: 16 us -> 19.8 us  [gate_up(): pl.pallas_call(functools.partial(gate_up_kernel, len(pieces), first), out...]
    ppermute x10 -> x8, waiting for transfers between devices: 18.9 us -> 21.3 us  [cross(): return lax.ppermute(block, ('expert', 'context', 'dp'), route)]
    ppermute x10 -> x8, starting transfers between devices: 10.3 us -> 11.5 us  [cross(): return lax.ppermute(block, ('expert', 'context', 'dp'), route)]
    ppermute x7 -> x6, waiting for transfers between devices: 8.93 us -> 8.95 us  [shift(): lax.ppermute(block, axis, [(i, (i + distance) % size) for i in range(size)])]
  transfers between devices with their start and end apart: 46 -> 43, of which waited for: 34 -> 28; matrix products, arithmetic and copies ran while one was open for 2% -> 2% of each run, Pallas kernels for 23% -> 20%
where the time goes in v7:
time: 223 us
  waiting for transfers between devices  83.6 us (37%)
  starting transfers between devices  64.7 us (29%)
  Pallas kernels  61.4 us (28%)
  other arithmetic  6.89 us (3%)
  local copies, waits for them, and re-layouts  3.17 us (1%)
  matrix products  2.45 us (1%)
    ppermute x24, waiting for transfers between devices, along_line(): lax.ppermute(block, 'expert', [(e, (e + 2 * distance) % size) for e in ra...  49.8 us
    ppermute x24, starting transfers between devices, along_line(): lax.ppermute(block, 'expert', [(e, (e + 2 * distance) % size) for e in ra...  45 us
    ppermute x8, waiting for transfers between devices, cross(): return lax.ppermute(block, ('expert', 'context', 'dp'), route)  21.3 us
    pallas_call x2, Pallas kernels, gate_up(): pl.pallas_call(functools.partial(gate_up_kernel, len(pieces), first), out...  19.8 us
    pallas_call x1, Pallas kernels, finish(): pl.pallas_call(functools.partial(finish_kernel, len(pieces), first), out_...  19.5 us
    ppermute x8, starting transfers between devices, cross(): return lax.ppermute(block, ('expert', 'context', 'dp'), route)  11.5 us
    pallas_call x1, Pallas kernels, run_out(): pl.pallas_call(functools.partial(out_kernel, channels // LANES, line, fir...  9.19 us
    ppermute x6, waiting for transfers between devices, shift(): lax.ppermute(block, axis, [(i, (i + distance) % size) for i in range(size)])  8.95 us
  transfers between devices with their start and end apart: 43, of which 28 were waited for; matrix products, arithmetic and copies ran while one was open for 2% of the time, Pallas kernels for 20%

profile of v7, /device:TPU:0, one launch (start us, length us, event | category | flops | bytes accessed | tf_op | source)
XLA Modules:
  0.0 222.7 jit_solution(16927837181957334369)
XLA Ops:
  0.8 2.3 %collective-permute-start = (bf16[3,1024]{1,0:T(4,128)(2,1)S(1)}, bf16[3,1024]{1,0:T(4,128)(2,1)S(1)}, u32[]{:S(2)}, u32[]{:S(2)}) collective-permute-start(bf16[3,1024]{1,0:T(4,128)(2,1)S(1)} %slice_bitcast_fusion.3), channel_id=1, source_target_pairs={{0,2},{1,3},{4,6},{5,7},{8,10},{9,11},{12,14},{13,15},{16,18},{17,... | collective-permute-start | bytes 18440 | tf_op jit(solution)/shard_map/ppermute | solution.py:24
  7.3 2.5 %collective-permute-start.1 = (bf16[64,288]{1,0:T(8,128)(2,1)S(1)}, bf16[64,288]{1,0:T(8,128)(2,1)S(1)}, u32[]{:S(2)}, u32[]{:S(2)}) collective-permute-start(bf16[64,288]{1,0:T(8,128)(2,1)S(1)} %get-tuple-element.122), channel_id=1, source_target_pairs={{0,8},{4,12},{8,16},{12,20},{16,24},{20,28},{24,0},{28,4},{1,9},{5... | collective-permute-start | bytes 110600 | tf_op jit(solution)/shard_map/ppermute | solution.py:420
  9.7 2.6 %collective-permute-start.2 = (bf16[64,288]{1,0:T(8,128)(2,1)S(1)}, bf16[64,288]{1,0:T(8,128)(2,1)S(1)}, u32[]{:S(2)}, u32[]{:S(2)}) collective-permute-start(bf16[64,288]{1,0:T(8,128)(2,1)S(1)} %get-tuple-element.124), channel_id=1, source_target_pairs={{0,16},{4,20},{8,24},{12,28},{16,0},{20,4},{24,8},{28,12},{1,17},{... | collective-permute-start | bytes 110600 | tf_op jit(solution)/shard_map/ppermute | solution.py:420
  13.9 2.3 %collective-permute-done.2 = bf16[64,288]{1,0:T(8,128)(2,1)S(1)} collective-permute-done((bf16[64,288]{1,0:T(8,128)(2,1)S(1)}, bf16[64,288]{1,0:T(8,128)(2,1)S(1)}, u32[]{:S(2)}, u32[]{:S(2)}) %collective-permute-start.2) | collective-permute-done | bytes 36896 | tf_op jit(solution)/shard_map/ppermute | solution.py:420
  18.2 2.6 %collective-permute-done.4 = bf16[64,288]{1,0:T(8,128)(2,1)S(1)} collective-permute-done((bf16[64,288]{1,0:T(8,128)(2,1)S(1)}, bf16[64,288]{1,0:T(8,128)(2,1)S(1)}, u32[]{:S(2)}, u32[]{:S(2)}) %collective-permute-start.4) | collective-permute-done | bytes 36896 | tf_op jit(solution)/shard_map/ppermute | solution.py:34
  21.8 2.6 %collective-permute-start.6 = (bf16[64,288]{1,0:T(8,128)(2,1)S(1)}, bf16[64,288]{1,0:T(8,128)(2,1)S(1)}, u32[]{:S(2)}, u32[]{:S(2)}) collective-permute-start(bf16[64,288]{1,0:T(8,128)(2,1)S(1)} %add_convert_fusion.7.refs_0_), channel_id=1, source_target_pairs={{0,16},{4,20},{8,24},{12,28},{16,0},{20,4},{24,8},{28,12},{1,17},{... | collective-permute-start | bytes 110600 | tf_op jit(solution)/shard_map/ppermute | solution.py:420
  28.5 6.9 %state_scan.1 = (f32[2048,128]{1,0:T(8,128)S(1)}, f32[2048,128]{1,0:T(8,128)S(1)}, f32[16,8,128]{2,1,0:T(8,128)S(1)}, bf16[256,32]{1,0:T(8,128)(2,1)S(1)}, f32[128,128]{1,0:T(8,128)S(1)}) custom-call(s32[2]{0:T(128)S(1)} %pad_add_fusion.place_ref.at_ref, bf16[64,288]{1,0:T(8,128)(2,1)S(1)} %add_convert_fusion.7.refs_0_, ...), custom_call_target="tpu_custom_call" | custom-call | flops 200000000 | bytes 4194304 | tf_op jit(solution)/shard_map/state_scan/pallas_call | solution.py:106
  37.6 9.2 %readout_project.1 = (bf16[128,2560]{1,0:T(8,128)(2,1)S(1)}, bf16[128,2560]{1,0:T(8,128)(2,1)S(1)}, bf16[4,64,1536]{2,1,0:T(8,128)(2,1)S(1)}) custom-call(s32[2]{0:T(128)S(1)} %pad_add_fusion.place_ref.at_ref, f32[2048,128]{1,0:T(8,128)S(1)} %get-tuple-element.50.y_ref, f32[2048,128]{1,0:T(8,128)S(1)} %get-tuple-element.51.sum_ref, ...), custom_call_target="tpu_custom_call" | custom-call | flops 2147483648 | bytes 16777216 | tf_op jit(solution)/shard_map/readout_project/pallas_call | solution.py:201
  53.5 5.6 %collective-permute-done.13 = bf16[64,1536]{1,0:T(8,128)(2,1)S(1)} collective-permute-done((bf16[64,1536]{1,0:T(8,128)(2,1)}, bf16[64,1536]{1,0:T(8,128)(2,1)S(1)}, u32[]{:S(2)}, u32[]{:S(2)}) %collective-permute-start.13) | collective-permute-done | bytes 196640 | tf_op jit(solution)/shard_map/ppermute | solution.py:420
  59.1 7.6 %collective-permute-done.14 = bf16[64,1536]{1,0:T(8,128)(2,1)S(1)} collective-permute-done((bf16[64,1536]{1,0:T(8,128)(2,1)}, bf16[64,1536]{1,0:T(8,128)(2,1)S(1)}, u32[]{:S(2)}, u32[]{:S(2)}) %collective-permute-start.14) | collective-permute-done | bytes 196640 | tf_op jit(solution)/shard_map/ppermute | solution.py:420
  68.5 4.5 %collective-permute-start.10 = (bf16[32,2560]{1,0:T(8,128)(2,1)S(1)}, bf16[32,2560]{1,0:T(8,128)(2,1)S(1)}, u32[]{:S(2)}, u32[]{:S(2)}) collective-permute-start(bf16[32,2560]{1,0:T(8,128)(2,1)S(1)} %get-tuple-element.102), channel_id=1, source_target_pairs={{0,8},{4,12},{8,16},{12,20},{16,24},{20,28},{24,0},{28,4},{1,9},{5... | collective-permute-start | bytes 491528 | tf_op jit(solution)/shard_map/ppermute | solution.py:420
  73.2 2.2 %collective-permute-start.12 = (bf16[32,2560]{1,0:T(8,128)(2,1)S(1)}, bf16[32,2560]{1,0:T(8,128)(2,1)S(1)}, u32[]{:S(2)}, u32[]{:S(2)}) collective-permute-start(bf16[32,2560]{1,0:T(8,128)(2,1)S(1)} %get-tuple-element.103), channel_id=1, source_target_pairs={{0,24},{4,28},{8,0},{12,4},{16,8},{20,12},{24,16},{28,20},{1,25},{... | collective-permute-start | bytes 491528 | tf_op jit(solution)/shard_map/ppermute | solution.py:420
  75.5 2.2 collective-permute-done.10
  77.6 5.4 %collective-permute-done.11 = bf16[32,2560]{1,0:T(8,128)(2,1)S(1)} collective-permute-done((bf16[32,2560]{1,0:T(8,128)(2,1)S(1)}, bf16[32,2560]{1,0:T(8,128)(2,1)S(1)}, u32[]{:S(2)}, u32[]{:S(2)}) %collective-permute-start.11) | collective-permute-done | bytes 163872 | tf_op jit(solution)/shard_map/ppermute | solution.py:420
  83.8 4.0 %collective-permute-start.17 = (bf16[16,4096]{1,0:T(8,128)(2,1)S(1)}, bf16[16,4096]{1,0:T(8,128)(2,1)S(1)}, u32[]{:S(2)}, u32[]{:S(2)}) collective-permute-start(bf16[16,4096]{1,0:T(8,128)(2,1)S(1)} %get-tuple-element.112), channel_id=1, source_target_pairs={{0,8},{4,12},{8,16},{12,20},{16,24},{20,28},{24,0},{28,4},{1,9},{5... | collective-permute-start | bytes 393224 | tf_op jit(solution)/shard_map/ppermute | solution.py:420
  87.8 3.2 %collective-permute-start.18 = (bf16[16,4096]{1,0:T(8,128)(2,1)S(1)}, bf16[16,4096]{1,0:T(8,128)(2,1)S(1)}, u32[]{:S(2)}, u32[]{:S(2)}) collective-permute-start(bf16[16,4096]{1,0:T(8,128)(2,1)S(1)} %get-tuple-element.111), channel_id=1, source_target_pairs={{0,16},{4,20},{8,24},{12,28},{16,0},{20,4},{24,8},{28,12},{1,17},{... | collective-permute-start | bytes 393224 | tf_op jit(solution)/shard_map/ppermute | solution.py:420
  91.3 3.7 %collective-permute-done.17 = bf16[16,4096]{1,0:T(8,128)(2,1)S(1)} collective-permute-done((bf16[16,4096]{1,0:T(8,128)(2,1)S(1)}, bf16[16,4096]{1,0:T(8,128)(2,1)S(1)}, u32[]{:S(2)}, u32[]{:S(2)}) %collective-permute-start.17) | collective-permute-done | bytes 131104 | tf_op jit(solution)/shard_map/ppermute | solution.py:420
  94.9 3.7 %collective-permute-done.18 = bf16[16,4096]{1,0:T(8,128)(2,1)S(1)} collective-permute-done((bf16[16,4096]{1,0:T(8,128)(2,1)S(1)}, bf16[16,4096]{1,0:T(8,128)(2,1)S(1)}, u32[]{:S(2)}, u32[]{:S(2)}) %collective-permute-start.18) | collective-permute-done | bytes 131104 | tf_op jit(solution)/shard_map/ppermute | solution.py:420
  100.4 7.6 %collective-permute-done.20 = bf16[64,4096]{1,0:T(8,128)(2,1)S(1)} collective-permute-done((bf16[64,4096]{1,0:T(8,128)(2,1)S(1)}, bf16[64,4096]{1,0:T(8,128)(2,1)S(1)}, u32[]{:S(2)}, u32[]{:S(2)}) %collective-permute-start.20) | collective-permute-done | bytes 524320 | tf_op jit(solution)/shard_map/ppermute | solution.py:431
  109.6 3.2 %collective-permute-start.24 = (bf16[8,4096]{1,0:T(8,128)(2,1)S(1)}, bf16[8,4096]{1,0:T(8,128)(2,1)S(1)}, u32[]{:S(2)}, u32[]{:S(2)}) collective-permute-start(bf16[8,4096]{1,0:T(8,128)(2,1)S(1)} %get-tuple-element.120), channel_id=1, source_target_pairs={{0,8},{4,12},{8,16},{12,20},{16,24},{20,28},{24,0},{28,4},{1,9},{5... | collective-permute-start | bytes 196616 | tf_op jit(solution)/shard_map/ppermute | solution.py:420
  115.3 7.6 %collective-permute-done.21.refs_1_ = bf16[128,4096]{1,0:T(8,128)(2,1)S(1)} collective-permute-done((bf16[128,4096]{1,0:T(8,128)(2,1)S(1)}, bf16[128,4096]{1,0:T(8,128)(2,1)S(1)}, u32[]{:S(2)}, u32[]{:S(2)}) %collective-permute-start.21) | collective-permute-done | bytes 1048608 | tf_op jit(solution)/shard_map/ppermute | solution.py:431
  125.6 9.7 %gate_up.2.refs_4_ = bf16[512,768]{1,0:T(8,128)(2,1)S(1)} custom-call(bf16[128,4096]{1,0:T(8,128)(2,1)S(1)} %constant_dynamic-update-slice_fusion.refs_0_, bf16[128,4096]{1,0:T(8,128)(2,1)S(1)} %collective-permute-done.21.refs_1_, bf16[128,4096]{1,0:T(8,128)(2,1)S(1)} %collective-permute-done.22.refs_2_, ...), custom_call_target="tpu_custom_call" | custom-call | flops 6442450944 | bytes 16777216 | tf_op jit(solution)/shard_map/gate_up/pallas_call | solution.py:262
  136.9 19.5 %gate_up_down.1 = (bf16[512,1536]{1,0:T(8,128)(2,1)}, bf16[256,4096]{1,0:T(8,128)(2,1)}, bf16[256,4096]{1,0:T(8,128)(2,1)}) custom-call(bf16[128,4096]{1,0:T(8,128)(2,1)S(1)} %constant_dynamic-update-slice_fusion.refs_0_, bf16[128,4096]{1,0:T(8,128)(2,1)S(1)} %collective-permute-done.21.refs_1_, bf16[128,4096]{1,0:T(8,128)(2,1)S(1)} %collective-permute-done.22.refs_2_, ...), custom_call_target="tpu_custom_call" | custom-call | flops 12884901888 | bytes 33554432 | tf_op jit(solution)/shard_map/gate_up_down/pallas_call | solution.py:343
  157.0 5.3 %collective-permute-done.29 = bf16[256,4096]{1,0:T(8,128)(2,1)S(1)} collective-permute-done((bf16[256,4096]{1,0:T(8,128)(2,1)}, bf16[256,4096]{1,0:T(8,128)(2,1)S(1)}, u32[]{:S(2)}, u32[]{:S(2)}) %collective-permute-start.29) | collective-permute-done | bytes 2097184 | tf_op jit(solution)/shard_map/ppermute | solution.py:29
  164.8 10.1 %gate_up.3.refs_0_ = bf16[256,1536]{1,0:T(8,128)(2,1)S(1)} custom-call(bf16[64,4096]{1,0:T(8,128)(2,1)S(1)} %constant_dynamic-update-slice_fusion.9.refs_0_, bf16[64,4096]{1,0:T(8,128)(2,1)S(1)} %collective-permute-done.28.refs_1_, bf16[64,4096]{1,0:T(8,128)(2,1)S(1)} %collective-permute-done.30.refs_2_, ...), custom_call_target="tpu_custom_call" | custom-call | flops 6442450944 | bytes 27262976 | tf_op jit(solution)/shard_map/gate_up/pallas_call | solution.py:262
  175.0 3.6 %collective-permute-done.32 = bf16[128,4096]{1,0:T(8,128)(2,1)S(1)} collective-permute-done((bf16[128,4096]{1,0:T(8,128)(2,1)S(1)}, bf16[128,4096]{1,0:T(8,128)(2,1)S(1)}, u32[]{:S(2)}, u32[]{:S(2)}) %collective-permute-start.32) | collective-permute-done | bytes 1048608 | tf_op jit(solution)/shard_map/ppermute | solution.py:431
  180.4 6.1 %down.1 = (bf16[128,4096]{1,0:T(8,128)(2,1)S(1)}, bf16[128,4096]{1,0:T(8,128)(2,1)S(1)}) custom-call(bf16[256,1536]{1,0:T(8,128)(2,1)S(1)} %gate_up.3.refs_0_, bf16[1536,4096]{1,0:T(8,128)(2,1)} %bitcast.58), custom_call_target="tpu_custom_call" | custom-call | flops 3221225472 | bytes 15466496 | tf_op jit(solution)/shard_map/down/pallas_call | solution.py:398
  188.4 2.6 %collective-permute-done.37 = bf16[128,4096]{1,0:T(8,128)(2,1)S(1)} collective-permute-done((bf16[128,4096]{1,0:T(8,128)(2,1)S(1)}, bf16[128,4096]{1,0:T(8,128)(2,1)S(1)}, u32[]{:S(2)}, u32[]{:S(2)}) %collective-permute-start.37) | collective-permute-done | bytes 1048608 | tf_op jit(solution)/shard_map/ppermute | solution.py:29
  192.3 3.6 %collective-permute-start.34 = (bf16[16,4096]{1,0:T(8,128)(2,1)S(1)}, bf16[16,4096]{1,0:T(8,128)(2,1)S(1)}, u32[]{:S(2)}, u32[]{:S(2)}) collective-permute-start(bf16[16,4096]{1,0:T(8,128)(2,1)S(1)} %get-tuple-element.108), channel_id=1, source_target_pairs={{0,24},{4,28},{8,0},{12,4},{16,8},{20,12},{24,16},{28,20},{1,25},{... | collective-permute-start | bytes 393224 | tf_op jit(solution)/shard_map/ppermute | solution.py:420
  195.9 3.7 %collective-permute-done.34 = bf16[16,4096]{1,0:T(8,128)(2,1)S(1)} collective-permute-done((bf16[16,4096]{1,0:T(8,128)(2,1)S(1)}, bf16[16,4096]{1,0:T(8,128)(2,1)S(1)}, u32[]{:S(2)}, u32[]{:S(2)}) %collective-permute-start.34) | collective-permute-done | bytes 131104 | tf_op jit(solution)/shard_map/ppermute | solution.py:420
  202.1 2.2 collective-permute-start.35
  206.3 7.4 %collective-permute-done.35 = bf16[16,4096]{1,0:T(8,128)(2,1)S(1)} collective-permute-done((bf16[16,4096]{1,0:T(8,128)(2,1)S(1)}, bf16[16,4096]{1,0:T(8,128)(2,1)S(1)}, u32[]{:S(2)}, u32[]{:S(2)}) %collective-permute-start.35) | collective-permute-done | bytes 131104 | tf_op jit(solution)/shard_map/ppermute | solution.py:420
  (141 shorter events, 57.0 us)
Async XLA Ops:
  7.3 6.6 %collective-permute-start.1 = (bf16[64,288]{1,0:T(8,128)(2,1)S(1)}, bf16[64,288]{1,0:T(8,128)(2,1)S(1)}, u32[]{:S(2)}, u32[]{:S(2)}) collective-permute-start(bf16[64,288]{1,0:T(8,128)(2,1)S(1)} %get-tuple-element.122), channel_id=1, source_target_pairs={{0,8},{4,12},{8,16},{12,20},{16,24},{20,28},{24,0},{28,4},{1,9},{5... | collective-permute-start | bytes 110600 | tf_op jit(solution)/shard_map/ppermute | solution.py:420
  9.7 6.5 %collective-permute-start.2 = (bf16[64,288]{1,0:T(8,128)(2,1)S(1)}, bf16[64,288]{1,0:T(8,128)(2,1)S(1)}, u32[]{:S(2)}, u32[]{:S(2)}) collective-permute-start(bf16[64,288]{1,0:T(8,128)(2,1)S(1)} %get-tuple-element.124), channel_id=1, source_target_pairs={{0,16},{4,20},{8,24},{12,28},{16,0},{20,4},{24,8},{28,12},{1,17},{... | collective-permute-start | bytes 110600 | tf_op jit(solution)/shard_map/ppermute | solution.py:420
  20.8 6.0 %collective-permute-start.5 = (bf16[64,288]{1,0:T(8,128)(2,1)S(1)}, bf16[64,288]{1,0:T(8,128)(2,1)S(1)}, u32[]{:S(2)}, u32[]{:S(2)}) collective-permute-start(bf16[64,288]{1,0:T(8,128)(2,1)S(1)} %add_convert_fusion.7.refs_0_), channel_id=1, source_target_pairs={{0,8},{4,12},{8,16},{12,20},{16,24},{20,28},{24,0},{28,4},{1,9},{5... | collective-permute-start | bytes 110600 | tf_op jit(solution)/shard_map/ppermute | solution.py:420
  46.8 21.5 %collective-permute-start.9 = (bf16[128,2560]{1,0:T(8,128)(2,1)S(1)}, bf16[128,2560]{1,0:T(8,128)(2,1)S(1)}, u32[]{:S(2)}, u32[]{:S(2)}) collective-permute-start(bf16[128,2560]{1,0:T(8,128)(2,1)S(1)} %get-tuple-element.56), channel_id=1, source_target_pairs={{0,4},{4,0},{8,12},{12,8},{16,20},{20,16},{24,28},{28,24},{1,5},{5... | collective-permute-start | bytes 1966088 | tf_op jit(solution)/shard_map/ppermute | solution.py:34
  49.2 9.9 %collective-permute-start.13 = (bf16[64,1536]{1,0:T(8,128)(2,1)}, bf16[64,1536]{1,0:T(8,128)(2,1)S(1)}, u32[]{:S(2)}, u32[]{:S(2)}) collective-permute-start(bf16[64,1536]{1,0:T(8,128)(2,1)} %get-tuple-element.99), channel_id=1, source_target_pairs={{0,8},{4,12},{8,16},{12,20},{16,24},{20,28},{24,0},{28,4},{1,9},{5... | collective-permute-start | bytes 589832 | tf_op jit(solution)/shard_map/ppermute | solution.py:420
  50.0 16.6 %collective-permute-start.14 = (bf16[64,1536]{1,0:T(8,128)(2,1)}, bf16[64,1536]{1,0:T(8,128)(2,1)S(1)}, u32[]{:S(2)}, u32[]{:S(2)}) collective-permute-start(bf16[64,1536]{1,0:T(8,128)(2,1)} %get-tuple-element.101), channel_id=1, source_target_pairs={{0,16},{4,20},{8,24},{12,28},{16,0},{20,4},{24,8},{28,12},{1,17},{... | collective-permute-start | bytes 589832 | tf_op jit(solution)/shard_map/ppermute | solution.py:420
  52.2 14.5 %collective-permute-start.15 = (bf16[64,1536]{1,0:T(8,128)(2,1)S(1)}, bf16[64,1536]{1,0:T(8,128)(2,1)}, u32[]{:S(2)}, u32[]{:S(2)}) collective-permute-start(bf16[64,1536]{1,0:T(8,128)(2,1)S(1)} %get-tuple-element.100), channel_id=1, source_target_pairs={{0,24},{4,28},{8,0},{12,4},{16,8},{20,12},{24,16},{28,20},{1,25},{... | collective-permute-start | bytes 589832 | tf_op jit(solution)/shard_map/ppermute | solution.py:420
  67.7 7.7 %collective-permute-start.16 = (bf16[32,1536]{1,0:T(8,128)(2,1)S(1)}, bf16[32,1536]{1,0:T(8,128)(2,1)S(1)}, u32[]{:S(2)}, u32[]{:S(2)}) collective-permute-start(bf16[32,1536]{1,0:T(8,128)(2,1)S(1)} %slice.292), channel_id=1, source_target_pairs={{0,4},{4,0},{8,12},{12,8},{16,20},{20,16},{24,28},{28,24},{1,5},{5... | collective-permute-start | bytes 294920 | tf_op jit(solution)/shard_map/ppermute | solution.py:34
  68.5 9.1 %collective-permute-start.10 = (bf16[32,2560]{1,0:T(8,128)(2,1)S(1)}, bf16[32,2560]{1,0:T(8,128)(2,1)S(1)}, u32[]{:S(2)}, u32[]{:S(2)}) collective-permute-start(bf16[32,2560]{1,0:T(8,128)(2,1)S(1)} %get-tuple-element.102), channel_id=1, source_target_pairs={{0,8},{4,12},{8,16},{12,20},{16,24},{20,28},{24,0},{28,4},{1,9},{5... | collective-permute-start | bytes 491528 | tf_op jit(solution)/shard_map/ppermute | solution.py:420
  73.0 10.1 %collective-permute-start.11 = (bf16[32,2560]{1,0:T(8,128)(2,1)S(1)}, bf16[32,2560]{1,0:T(8,128)(2,1)S(1)}, u32[]{:S(2)}, u32[]{:S(2)}) collective-permute-start(bf16[32,2560]{1,0:T(8,128)(2,1)S(1)} %get-tuple-element.104), channel_id=1, source_target_pairs={{0,16},{4,20},{8,24},{12,28},{16,0},{20,4},{24,8},{28,12},{1,17},{... | collective-permute-start | bytes 491528 | tf_op jit(solution)/shard_map/ppermute | solution.py:420
  73.2 9.9 %collective-permute-start.12 = (bf16[32,2560]{1,0:T(8,128)(2,1)S(1)}, bf16[32,2560]{1,0:T(8,128)(2,1)S(1)}, u32[]{:S(2)}, u32[]{:S(2)}) collective-permute-start(bf16[32,2560]{1,0:T(8,128)(2,1)S(1)} %get-tuple-element.103), channel_id=1, source_target_pairs={{0,24},{4,28},{8,0},{12,4},{16,8},{20,12},{24,16},{28,20},{1,25},{... | collective-permute-start | bytes 491528 | tf_op jit(solution)/shard_map/ppermute | solution.py:420
  83.8 11.1 %collective-permute-start.17 = (bf16[16,4096]{1,0:T(8,128)(2,1)S(1)}, bf16[16,4096]{1,0:T(8,128)(2,1)S(1)}, u32[]{:S(2)}, u32[]{:S(2)}) collective-permute-start(bf16[16,4096]{1,0:T(8,128)(2,1)S(1)} %get-tuple-element.112), channel_id=1, source_target_pairs={{0,8},{4,12},{8,16},{12,20},{16,24},{20,28},{24,0},{28,4},{1,9},{5... | collective-permute-start | bytes 393224 | tf_op jit(solution)/shard_map/ppermute | solution.py:420
  87.8 10.9 %collective-permute-start.18 = (bf16[16,4096]{1,0:T(8,128)(2,1)S(1)}, bf16[16,4096]{1,0:T(8,128)(2,1)S(1)}, u32[]{:S(2)}, u32[]{:S(2)}) collective-permute-start(bf16[16,4096]{1,0:T(8,128)(2,1)S(1)} %get-tuple-element.111), channel_id=1, source_target_pairs={{0,16},{4,20},{8,24},{12,28},{16,0},{20,4},{24,8},{28,12},{1,17},{... | collective-permute-start | bytes 393224 | tf_op jit(solution)/shard_map/ppermute | solution.py:420
  91.0 7.8 %collective-permute-start.19 = (bf16[16,4096]{1,0:T(8,128)(2,1)S(1)}, bf16[16,4096]{1,0:T(8,128)(2,1)S(1)}, u32[]{:S(2)}, u32[]{:S(2)}) collective-permute-start(bf16[16,4096]{1,0:T(8,128)(2,1)S(1)} %get-tuple-element.110), channel_id=1, source_target_pairs={{0,24},{4,28},{8,0},{12,4},{16,8},{20,12},{24,16},{28,20},{1,25},{... | collective-permute-start | bytes 393224 | tf_op jit(solution)/shard_map/ppermute | solution.py:420
  98.8 9.2 %collective-permute-start.20 = (bf16[64,4096]{1,0:T(8,128)(2,1)S(1)}, bf16[64,4096]{1,0:T(8,128)(2,1)S(1)}, u32[]{:S(2)}, u32[]{:S(2)}) collective-permute-start(bf16[64,4096]{1,0:T(8,128)(2,1)S(1)} %pad_maximum_fusion), channel_id=1, source_target_pairs={{0,4},{1,5},{2,3},{3,2},{4,0},{5,1},{6,7},{7,6},{8,12},{9,13},{10,... | collective-permute-start | bytes 1572872 | tf_op jit(solution)/shard_map/ppermute | solution.py:431
  108.1 14.9 %collective-permute-start.21 = (bf16[128,4096]{1,0:T(8,128)(2,1)S(1)}, bf16[128,4096]{1,0:T(8,128)(2,1)S(1)}, u32[]{:S(2)}, u32[]{:S(2)}) collective-permute-start(bf16[128,4096]{1,0:T(8,128)(2,1)S(1)} %constant_dynamic-update-slice_fusion.refs_0_), channel_id=1, source_target_pairs={{0,1},{1,0},{2,6},{3,7},{4,5},{5,4},{6,2},{7,3},{8,9},{9,8},{10,14... | collective-permute-start | bytes 3145736 | tf_op jit(solution)/shard_map/ppermute | solution.py:431
  109.6 13.3 %collective-permute-start.24 = (bf16[8,4096]{1,0:T(8,128)(2,1)S(1)}, bf16[8,4096]{1,0:T(8,128)(2,1)S(1)}, u32[]{:S(2)}, u32[]{:S(2)}) collective-permute-start(bf16[8,4096]{1,0:T(8,128)(2,1)S(1)} %get-tuple-element.120), channel_id=1, source_target_pairs={{0,8},{4,12},{8,16},{12,20},{16,24},{20,28},{24,0},{28,4},{1,9},{5... | collective-permute-start | bytes 196616 | tf_op jit(solution)/shard_map/ppermute | solution.py:420
  112.9 10.1 %collective-permute-start.25 = (bf16[8,4096]{1,0:T(8,128)(2,1)S(1)}, bf16[8,4096]{1,0:T(8,128)(2,1)S(1)}, u32[]{:S(2)}, u32[]{:S(2)}) collective-permute-start(bf16[8,4096]{1,0:T(8,128)(2,1)S(1)} %get-tuple-element.119), channel_id=1, source_target_pairs={{0,16},{4,20},{8,24},{12,28},{16,0},{20,4},{24,8},{28,12},{1,17},{... | collective-permute-start | bytes 196616 | tf_op jit(solution)/shard_map/ppermute | solution.py:420
  113.8 9.2 %collective-permute-start.26 = (bf16[8,4096]{1,0:T(8,128)(2,1)S(1)}, bf16[8,4096]{1,0:T(8,128)(2,1)S(1)}, u32[]{:S(2)}, u32[]{:S(2)}) collective-permute-start(bf16[8,4096]{1,0:T(8,128)(2,1)S(1)} %get-tuple-element.118), channel_id=1, source_target_pairs={{0,24},{4,28},{8,0},{12,4},{16,8},{20,12},{24,16},{28,20},{1,25},{... | collective-permute-start | bytes 196616 | tf_op jit(solution)/shard_map/ppermute | solution.py:420
  115.3 9.3 %collective-permute-start.22 = (bf16[128,4096]{1,0:T(8,128)(2,1)S(1)}, bf16[128,4096]{1,0:T(8,128)(2,1)S(1)}, u32[]{:S(2)}, u32[]{:S(2)}) collective-permute-start(bf16[128,4096]{1,0:T(8,128)(2,1)S(1)} %constant_dynamic-update-slice_fusion.refs_0_), channel_id=1, source_target_pairs={{0,2},{2,0},{1,3},{3,1},{4,6},{6,4},{5,7},{7,5},{8,10},{10,8},{9,1... | collective-permute-start | bytes 3145736 | tf_op jit(solution)/shard_map/ppermute | solution.py:29
  123.0 12.3 %collective-permute-start.27 = (bf16[32,4096]{1,0:T(8,128)(2,1)S(1)}, bf16[32,4096]{1,0:T(8,128)(2,1)S(1)}, u32[]{:S(2)}, u32[]{:S(2)}) collective-permute-start(bf16[32,4096]{1,0:T(8,128)(2,1)S(1)} %constant_dynamic-update-slice_fusion.5), channel_id=1, source_target_pairs={{0,4},{1,5},{2,3},{3,2},{4,0},{5,1},{6,7},{7,6},{8,12},{9,13},{10,... | collective-permute-start | bytes 786440 | tf_op jit(solution)/shard_map/ppermute | solution.py:431
  135.3 21.0 %collective-permute-start.28 = (bf16[64,4096]{1,0:T(8,128)(2,1)S(1)}, bf16[64,4096]{1,0:T(8,128)(2,1)S(1)}, u32[]{:S(2)}, u32[]{:S(2)}) collective-permute-start(bf16[64,4096]{1,0:T(8,128)(2,1)S(1)} %constant_dynamic-update-slice_fusion.9.refs_0_), channel_id=1, source_target_pairs={{0,1},{1,0},{2,6},{3,7},{4,5},{5,4},{6,2},{7,3},{8,9},{9,8},{10,14... | collective-permute-start | bytes 1572872 | tf_op jit(solution)/shard_map/ppermute | solution.py:431
  156.4 8.4 %collective-permute-start.30 = (bf16[64,4096]{1,0:T(8,128)(2,1)S(1)}, bf16[64,4096]{1,0:T(8,128)(2,1)S(1)}, u32[]{:S(2)}, u32[]{:S(2)}) collective-permute-start(bf16[64,4096]{1,0:T(8,128)(2,1)S(1)} %constant_dynamic-update-slice_fusion.9.refs_0_), channel_id=1, source_target_pairs={{0,2},{2,0},{1,3},{3,1},{4,6},{6,4},{5,7},{7,5},{8,10},{10,8},{9,1... | collective-permute-start | bytes 1572872 | tf_op jit(solution)/shard_map/ppermute | solution.py:29
  156.9 7.9 %collective-permute-start.31 = (bf16[64,4096]{1,0:T(8,128)(2,1)S(1)}, bf16[64,4096]{1,0:T(8,128)(2,1)S(1)}, u32[]{:S(2)}, u32[]{:S(2)}) collective-permute-start(bf16[64,4096]{1,0:T(8,128)(2,1)S(1)} %collective-permute-done.28.refs_1_), channel_id=1, source_target_pairs={{0,2},{2,0},{1,3},{3,1},{4,6},{6,4},{5,7},{7,5},{8,10},{10,8},{9,1... | collective-permute-start | bytes 1572872 | tf_op jit(solution)/shard_map/ppermute | solution.py:29
  163.8 14.9 %collective-permute-start.32 = (bf16[128,4096]{1,0:T(8,128)(2,1)S(1)}, bf16[128,4096]{1,0:T(8,128)(2,1)S(1)}, u32[]{:S(2)}, u32[]{:S(2)}) collective-permute-start(bf16[128,4096]{1,0:T(8,128)(2,1)S(1)} %add_convert_fusion), channel_id=1, source_target_pairs={{0,1},{1,0},{2,6},{3,7},{4,5},{5,4},{6,2},{7,3},{8,9},{9,8},{10,14... | collective-permute-start | bytes 3145736 | tf_op jit(solution)/shard_map/ppermute | solution.py:431
  178.8 9.2 %collective-permute-start.33 = (bf16[64,4096]{1,0:T(8,128)(2,1)S(1)}, bf16[64,4096]{1,0:T(8,128)(2,1)S(1)}, u32[]{:S(2)}, u32[]{:S(2)}) collective-permute-start(bf16[64,4096]{1,0:T(8,128)(2,1)S(1)} %add_convert_fusion.4), channel_id=1, source_target_pairs={{0,4},{1,5},{2,3},{3,2},{4,0},{5,1},{6,7},{7,6},{8,12},{9,13},{10,... | collective-permute-start | bytes 1572872 | tf_op jit(solution)/shard_map/ppermute | solution.py:431
  191.2 9.2 %collective-permute-start.38 = (bf16[64,4096]{1,0:T(8,128)(2,1)S(1)}, bf16[64,4096]{1,0:T(8,128)(2,1)S(1)}, u32[]{:S(2)}, u32[]{:S(2)}) collective-permute-start(bf16[64,4096]{1,0:T(8,128)(2,1)S(1)} %add_convert_fusion.2), channel_id=1, source_target_pairs={{0,1},{1,0},{2,6},{3,7},{4,5},{5,4},{6,2},{7,3},{8,9},{9,8},{10,14... | collective-permute-start | bytes 1572872 | tf_op jit(solution)/shard_map/ppermute | solution.py:431
  192.3 7.3 %collective-permute-start.34 = (bf16[16,4096]{1,0:T(8,128)(2,1)S(1)}, bf16[16,4096]{1,0:T(8,128)(2,1)S(1)}, u32[]{:S(2)}, u32[]{:S(2)}) collective-permute-start(bf16[16,4096]{1,0:T(8,128)(2,1)S(1)} %get-tuple-element.108), channel_id=1, source_target_pairs={{0,24},{4,28},{8,0},{12,4},{16,8},{20,12},{24,16},{28,20},{1,25},{... | collective-permute-start | bytes 393224 | tf_op jit(solution)/shard_map/ppermute | solution.py:420
  200.6 13.2 %collective-permute-start.39 = (bf16[32,4096]{1,0:T(8,128)(2,1)S(1)}, bf16[32,4096]{1,0:T(8,128)(2,1)S(1)}, u32[]{:S(2)}, u32[]{:S(2)}) collective-permute-start(bf16[32,4096]{1,0:T(8,128)(2,1)S(1)} %add_convert_fusion.6), channel_id=1, source_target_pairs={{0,4},{1,5},{2,3},{3,2},{4,0},{5,1},{6,7},{7,6},{8,12},{9,13},{10,... | collective-permute-start | bytes 786440 | tf_op jit(solution)/shard_map/ppermute | solution.py:431
  202.1 11.6 %collective-permute-start.35 = (bf16[16,4096]{1,0:T(8,128)(2,1)S(1)}, bf16[16,4096]{1,0:T(8,128)(2,1)S(1)}, u32[]{:S(2)}, u32[]{:S(2)}) collective-permute-start(bf16[16,4096]{1,0:T(8,128)(2,1)S(1)} %get-tuple-element.107), channel_id=1, source_target_pairs={{0,16},{4,20},{8,24},{12,28},{16,0},{20,4},{24,8},{28,12},{1,17},{... | collective-permute-start | bytes 393224 | tf_op jit(solution)/shard_map/ppermute | solution.py:420
  204.3 9.4 %collective-permute-start.36 = (bf16[16,4096]{1,0:T(8,128)(2,1)S(1)}, bf16[16,4096]{1,0:T(8,128)(2,1)S(1)}, u32[]{:S(2)}, u32[]{:S(2)}) collective-permute-start(bf16[16,4096]{1,0:T(8,128)(2,1)S(1)} %get-tuple-element.106), channel_id=1, source_target_pairs={{0,8},{4,12},{8,16},{12,20},{16,24},{20,28},{24,0},{28,4},{1,9},{5... | collective-permute-start | bytes 393224 | tf_op jit(solution)/shard_map/ppermute | solution.py:420
  215.0 6.2 %collective-permute-start.42 = (bf16[8,4096]{1,0:T(8,128)(2,1)S(1)}, bf16[8,4096]{1,0:T(8,128)(2,1)S(1)}, u32[]{:S(2)}, u32[]{:S(2)}) collective-permute-start(bf16[8,4096]{1,0:T(8,128)(2,1)S(1)} %get-tuple-element.115), channel_id=1, source_target_pairs={{0,8},{4,12},{8,16},{12,20},{16,24},{20,28},{24,0},{28,4},{1,9},{5... | collective-permute-start | bytes 196616 | tf_op jit(solution)/shard_map/ppermute | solution.py:420
  (23 other events, 230.7 us)

commit v8 on v6

--- a/solution.py
+++ b/solution.py
@@ -128,7 +128,8 @@
 
 def out_kernel(groups, line, first, at_ref, y_ref, sum_ref, enter_ref, bc_ref, neg_ref, x_ref, z_ref,
                skip_ref, w_hbm, *refs):
-    kept_ref, sent_ref, blocks_ref, full_ref, wide_ref, gated_ref, order_ref, w_ref, sems = refs
+    kept_ref, sent_ref, block_refs = refs[0], refs[1], refs[2 : 2 + line]
+    full_ref, wide_ref, gated_ref, order_ref, w_ref, sems = refs[2 + line :]
     length = x_ref.shape[0]
     tiles, _, tile = w_ref.shape
 
@@ -183,7 +184,7 @@
         for k in range(line):
             for r in range(2):
                 start = r * count + k * piece
-                blocks_ref[k, pl.ds(r * piece, piece), cols] = out[start : start + piece]
+                block_refs[k][pl.ds(r * piece, piece), cols] = out[start : start + piece]
         return carry
 
     lax.fori_loop(0, first, step, 0)
@@ -197,12 +198,12 @@
     first = (wide // tile * 5 + 4) // 8
     vmem = pl.BlockSpec(memory_space=pltpu.VMEM)
     part = jax.ShapeDtypeStruct((length // 2, first * tile), BF16)
-    blocks = jax.ShapeDtypeStruct((line, length // line, wide - first * tile), BF16)
+    block = jax.ShapeDtypeStruct((length // line, wide - first * tile), BF16)
     return pl.pallas_call(
         functools.partial(out_kernel, channels // LANES, line, first),
-        out_shape=(part, part, blocks),
+        out_shape=(part, part) + (block,) * line,
         in_specs=[pl.BlockSpec(memory_space=pltpu.SMEM)] + [vmem] * 8 + [pl.BlockSpec(memory_space=pl.ANY)],
-        out_specs=(vmem,) * 3,
+        out_specs=(vmem,) * (2 + line),
         scratch_shapes=[
             pltpu.VMEM((length * SUB, LANES), F32),
             pltpu.VMEM((NSTATE * length, LANES), F32),
@@ -219,6 +220,27 @@
     )(at, y, total, enter, bc, neg, x, z, skip, w)
 
 
+class Fetch:
+    def __init__(self, source, cols, target, sems, first):
+        rows = target.shape[0] // 2
+        self.copies = [
+            pltpu.make_async_copy(
+                source.at[pl.ds(h * rows, rows), cols],
+                target.at[pl.ds(h * rows, rows), :],
+                sems.at[first + h],
+            )
+            for h in range(2)
+        ]
+
+    def start(self):
+        for copy in self.copies:
+            copy.start()
+
+    def wait(self):
+        for copy in self.copies:
+            copy.wait()
+
+
 def gate_up_kernel(count, first, *refs):
     pieces, (gate_hbm, up_hbm, out_ref, rows_ref, gate_ref, up_ref, sems) = refs[:count], refs[count:]
     copies, at = [], 0
@@ -231,7 +253,7 @@
     def fetch(j, k):
         cols = pl.ds(pl.multiple_of(first + j * tile, tile), tile)
         source, target = ((gate_hbm, gate_ref), (up_hbm, up_ref))[k]
-        return pltpu.make_async_copy(source.at[:, cols], target.at[j], sems.at[count + 2 * j + k])
+        return Fetch(source, cols, target.at[j], sems, count + 4 * j + 2 * k)
 
     for copy in copies:
         copy.start()
@@ -268,7 +290,7 @@
             pltpu.VMEM((rows, depth), BF16),
             pltpu.VMEM((steps, depth, tile), BF16),
             pltpu.VMEM((steps, depth, tile), BF16),
-            pltpu.SemaphoreType.DMA((len(pieces) + 2 * steps,)),
+            pltpu.SemaphoreType.DMA((len(pieces) + 4 * steps,)),
         ],
         compiler_params=pltpu.CompilerParams(vmem_limit_bytes=49 * MIB),
         cost_estimate=cost(4 * rows * depth * width, 4 * depth * width + 2 * rows * depth),
@@ -287,12 +309,11 @@
     def fetch(j, k):
         cols = pl.ds(pl.multiple_of(done + j * tile, tile), tile)
         source, target = ((gate_hbm, gate_ref), (up_hbm, up_ref))[k]
-        return pltpu.make_async_copy(source.at[:, cols], target.at[j], sems.at[count + 2 * j + k])
+        return Fetch(source, cols, target.at[j], sems, count + 4 * j + 2 * k)
 
     def last_fetch(j):
         cols = pl.ds(pl.multiple_of(first + j * last_tile, last_tile), last_tile)
-        sem = sems.at[count + 2 * steps + j]
-        return pltpu.make_async_copy(down_hbm.at[:, cols], down_ref.at[j], sem)
+        return Fetch(down_hbm, cols, down_ref.at[j], sems, count + 4 * steps + 2 * j)
 
     copies, at = [], 0
     for k, piece in enumerate(pieces):
@@ -350,7 +371,7 @@
             pltpu.VMEM((steps, depth, tile), BF16),
             pltpu.VMEM((steps, depth, tile), BF16),
             pltpu.VMEM((last_steps, hidden, last_tile), BF16),
-            pltpu.SemaphoreType.DMA((len(pieces) + 2 * steps + last_steps,)),
+            pltpu.SemaphoreType.DMA((len(pieces) + 4 * steps + 2 * last_steps,)),
         ],
         compiler_params=pltpu.CompilerParams(vmem_limit_bytes=49 * MIB),
         cost_estimate=cost(
@@ -369,7 +390,7 @@
 
     def fetch(j):
         source = pl.ds(pl.multiple_of(first + j * tile, tile), tile)
-        return pltpu.make_async_copy(w_hbm.at[:, source], w_ref.at[j], sems.at[j])
+        return Fetch(w_hbm, source, w_ref.at[j], sems, 2 * j)
 
     for j in range(tiles):
         fetch(j).start()
@@ -403,7 +424,7 @@
         scratch_shapes=[
             pltpu.VMEM((rows, hidden), BF16),
             pltpu.VMEM((width // tile, hidden, tile), BF16),
-            pltpu.SemaphoreType.DMA((width // tile,)),
+            pltpu.SemaphoreType.DMA((2 * (width // tile),)),
         ],
         compiler_params=pltpu.CompilerParams(vmem_limit_bytes=49 * MIB),
         cost_estimate=cost(2 * rows * hidden * width, 2 * hidden * width + 2 * rows * (hidden + width)),
@@ -568,6 +589,7 @@
     )
     mixed_in = jax.nn.silu(conv_sum).astype(BF16)
     projected = jnp.dot(mixed_in, xproj_w, preferred_element_type=F32).astype(BF16)
+    ids, weights = after((route_ids[0, 0], route_w[0, 0]), projected)
     shares = projected.reshape(line, length // line, -1)
 
     def share_of(s):
@@ -585,7 +607,7 @@
     for step in range(contexts - 2):
         decay = jnp.exp(total[-SUB:][None] * neg.reshape(end.shape))
         enter = from_behind(end + decay * enter, "context", 1)
-    kept, sent, blocks = run_out(
+    kept, sent, *blocks = run_out(
         where, line, y, total, enter, bc, neg, mixed_in, z_gate[0, 0], skip_gain[None, :], out_w
     )
     got = swap_pair(sent)
@@ -604,7 +626,6 @@
         * lax.rsqrt(jnp.mean(stream_f * stream_f, axis=1, keepdims=True) + 1e-05)
         * norm_gain[None, :]
     ).astype(BF16)
-    ids, weights = after((route_ids[0, 0], route_w[0, 0]), kept)
     capacity = min(row_count, 8 * ((3 * row_count * TOP + 16 * line - 1) // (16 * line)))
     cuts = (0, 8, capacity) if contexts == 2 and dps == 2 and capacity > 8 else (0, capacity)
     named = jnp.any(ids[:, :, None] == jnp.arange(line, dtype=jnp.int32), axis=1)

time: 210 us -> 208 us (level)
  transfers between devices with their start and end apart: 46 -> 46, of which waited for: 34 -> 33; matrix products, arithmetic and copies ran while one was open for 2% -> 2% of each run, Pallas kernels for 23% -> 23%
where the time goes in v8:
time: 208 us
  waiting for transfers between devices  72.5 us (35%)
  Pallas kernels  64.1 us (31%)
  starting transfers between devices  61.1 us (29%)
  other arithmetic  4.94 us (2%)
  local copies, waits for them, and re-layouts  2.5 us (1%)
    ppermute x24, starting transfers between devices, along_line(): lax.ppermute(block, 'expert', [(e, (e + 2 * distance) % size) for e in ra...  42.7 us
    ppermute x24, waiting for transfers between devices, along_line(): lax.ppermute(block, 'expert', [(e, (e + 2 * distance) % size) for e in ra...  41.2 us
    pallas_call x2, Pallas kernels, finish(): pl.pallas_call(functools.partial(finish_kernel, len(pieces), first), out_...  26.5 us
    ppermute x10, waiting for transfers between devices, cross(): return lax.ppermute(block, ('expert', 'context', 'dp'), route)  18.7 us
    pallas_call x2, Pallas kernels, gate_up(): pl.pallas_call(functools.partial(gate_up_kernel, len(pieces), first), out...  16.1 us
    ppermute x10, starting transfers between devices, cross(): return lax.ppermute(block, ('expert', 'context', 'dp'), route)  10.3 us
    pallas_call x1, Pallas kernels, run_out(): pl.pallas_call(functools.partial(out_kernel, channels // LANES, line, fir...  9.18 us
    ppermute x7, waiting for transfers between devices, shift(): lax.ppermute(block, axis, [(i, (i + distance) % size) for i in range(size)])  9.09 us
  transfers between devices with their start and end apart: 46, of which 33 were waited for; matrix products, arithmetic and copies ran while one was open for 2% of the time, Pallas kernels for 23%

profile of v8, /device:TPU:0, one launch (start us, length us, event | category | flops | bytes accessed | tf_op | source)
XLA Modules:
  0.0 207.5 jit_solution(13636119148745500805)
XLA Ops:
  0.8 2.3 %collective-permute-start = (bf16[3,1024]{1,0:T(4,128)(2,1)S(1)}, bf16[3,1024]{1,0:T(4,128)(2,1)S(1)}, u32[]{:S(2)}, u32[]{:S(2)}) collective-permute-start(bf16[3,1024]{1,0:T(4,128)(2,1)S(1)} %slice_bitcast_fusion), channel_id=1, source_target_pairs={{0,2},{1,3},{4,6},{5,7},{8,10},{9,11},{12,14},{13,15},{16,18},{17,... | collective-permute-start | bytes 18440 | tf_op jit(solution)/shard_map/ppermute | solution.py:24
  6.7 2.5 %collective-permute-start.1 = (bf16[64,288]{1,0:T(8,128)(2,1)S(1)}, bf16[64,288]{1,0:T(8,128)(2,1)S(1)}, u32[]{:S(2)}, u32[]{:S(2)}) collective-permute-start(bf16[64,288]{1,0:T(8,128)(2,1)S(1)} %get-tuple-element.161), channel_id=1, source_target_pairs={{0,8},{4,12},{8,16},{12,20},{16,24},{20,28},{24,0},{28,4},{1,9},{5... | collective-permute-start | bytes 110600 | tf_op jit(solution)/shard_map/ppermute | solution.py:441
  9.2 2.6 %collective-permute-start.2 = (bf16[64,288]{1,0:T(8,128)(2,1)S(1)}, bf16[64,288]{1,0:T(8,128)(2,1)S(1)}, u32[]{:S(2)}, u32[]{:S(2)}) collective-permute-start(bf16[64,288]{1,0:T(8,128)(2,1)S(1)} %get-tuple-element.163), channel_id=1, source_target_pairs={{0,16},{4,20},{8,24},{12,28},{16,0},{20,4},{24,8},{28,12},{1,17},{... | collective-permute-start | bytes 110600 | tf_op jit(solution)/shard_map/ppermute | solution.py:441
  13.4 2.3 %collective-permute-done.2 = bf16[64,288]{1,0:T(8,128)(2,1)S(1)} collective-permute-done((bf16[64,288]{1,0:T(8,128)(2,1)S(1)}, bf16[64,288]{1,0:T(8,128)(2,1)S(1)}, u32[]{:S(2)}, u32[]{:S(2)}) %collective-permute-start.2) | collective-permute-done | bytes 36896 | tf_op jit(solution)/shard_map/ppermute | solution.py:441
  17.6 2.6 %collective-permute-done.4 = bf16[64,288]{1,0:T(8,128)(2,1)S(1)} collective-permute-done((bf16[64,288]{1,0:T(8,128)(2,1)S(1)}, bf16[64,288]{1,0:T(8,128)(2,1)S(1)}, u32[]{:S(2)}, u32[]{:S(2)}) %collective-permute-start.4) | collective-permute-done | bytes 36896 | tf_op jit(solution)/shard_map/ppermute | solution.py:34
  21.2 2.6 %collective-permute-start.6 = (bf16[64,288]{1,0:T(8,128)(2,1)S(1)}, bf16[64,288]{1,0:T(8,128)(2,1)S(1)}, u32[]{:S(2)}, u32[]{:S(2)}) collective-permute-start(bf16[64,288]{1,0:T(8,128)(2,1)S(1)} %add_convert_fusion.10.refs_0_), channel_id=1, source_target_pairs={{0,16},{4,20},{8,24},{12,28},{16,0},{20,4},{24,8},{28,12},{1,17},{... | collective-permute-start | bytes 110600 | tf_op jit(solution)/shard_map/ppermute | solution.py:441
  27.9 6.9 %state_scan.1 = (f32[2048,128]{1,0:T(8,128)S(1)}, f32[2048,128]{1,0:T(8,128)S(1)}, f32[16,8,128]{2,1,0:T(8,128)S(1)}, bf16[256,32]{1,0:T(8,128)(2,1)S(1)}, f32[128,128]{1,0:T(8,128)S(1)}) custom-call(s32[2]{0:T(128)S(1)} %pad_add_fusion.place_ref.at_ref, bf16[64,288]{1,0:T(8,128)(2,1)S(1)} %add_convert_fusion.10.refs_0_, ...), custom_call_target="tpu_custom_call" | custom-call | flops 200000000 | bytes 4194304 | tf_op jit(solution)/shard_map/state_scan/pallas_call | solution.py:106
  37.0 9.2 %readout_project.1 = (bf16[128,2560]{1,0:T(8,128)(2,1)S(1)}, bf16[128,2560]{1,0:T(8,128)(2,1)S(1)}, bf16[64,1536]{1,0:T(8,128)(2,1)S(1)}, bf16[64,1536]{1,0:T(8,...) custom-call(s32[2]{0:T(128)S(1)} %pad_add_fusion.place_ref.at_ref, ...), custom_call_target="tpu_custom_call" | custom-call | flops 2147483648 | bytes 16777216 | tf_op jit(solution)/shard_map/readout_project/pallas_call | solution.py:202
  48.6 2.1 %collective-permute-start.14 = (bf16[64,1536]{1,0:T(8,128)(2,1)S(1)}, bf16[64,1536]{1,0:T(8,128)(2,1)S(1)}, u32[]{:S(2)}, u32[]{:S(2)}) collective-permute-start(bf16[64,1536]{1,0:T(8,128)(2,1)S(1)} %get-tuple-element.76), channel_id=1, source_target_pairs={{0,16},{4,20},{8,24},{12,28},{16,0},{20,4},{24,8},{28,12},{1,17},{... | collective-permute-start | bytes 589832 | tf_op jit(solution)/shard_map/ppermute | solution.py:441
  51.8 5.7 %collective-permute-done.13 = bf16[64,1536]{1,0:T(8,128)(2,1)S(1)} collective-permute-done((bf16[64,1536]{1,0:T(8,128)(2,1)S(1)}, bf16[64,1536]{1,0:T(8,128)(2,1)S(1)}, u32[]{:S(2)}, u32[]{:S(2)}) %collective-permute-start.13) | collective-permute-done | bytes 196640 | tf_op jit(solution)/shard_map/ppermute | solution.py:441
  57.5 7.6 %collective-permute-done.14 = bf16[64,1536]{1,0:T(8,128)(2,1)S(1)} collective-permute-done((bf16[64,1536]{1,0:T(8,128)(2,1)S(1)}, bf16[64,1536]{1,0:T(8,128)(2,1)S(1)}, u32[]{:S(2)}, u32[]{:S(2)}) %collective-permute-start.14) | collective-permute-done | bytes 196640 | tf_op jit(solution)/shard_map/ppermute | solution.py:441
  66.0 4.4 %collective-permute-start.10 = (bf16[32,2560]{1,0:T(8,128)(2,1)S(1)}, bf16[32,2560]{1,0:T(8,128)(2,1)S(1)}, u32[]{:S(2)}, u32[]{:S(2)}) collective-permute-start(bf16[32,2560]{1,0:T(8,128)(2,1)S(1)} %get-tuple-element.133), channel_id=1, source_target_pairs={{0,8},{4,12},{8,16},{12,20},{16,24},{20,28},{24,0},{28,4},{1,9},{5... | collective-permute-start | bytes 491528 | tf_op jit(solution)/shard_map/ppermute | solution.py:441
  70.7 2.1 %collective-permute-start.12 = (bf16[32,2560]{1,0:T(8,128)(2,1)S(1)}, bf16[32,2560]{1,0:T(8,128)(2,1)S(1)}, u32[]{:S(2)}, u32[]{:S(2)}) collective-permute-start(bf16[32,2560]{1,0:T(8,128)(2,1)S(1)} %get-tuple-element.134), channel_id=1, source_target_pairs={{0,24},{4,28},{8,0},{12,4},{16,8},{20,12},{24,16},{28,20},{1,25},{... | collective-permute-start | bytes 491528 | tf_op jit(solution)/shard_map/ppermute | solution.py:441
  72.9 2.2 %collective-permute-done.10 = bf16[32,2560]{1,0:T(8,128)(2,1)S(1)} collective-permute-done((bf16[32,2560]{1,0:T(8,128)(2,1)S(1)}, bf16[32,2560]{1,0:T(8,128)(2,1)S(1)}, u32[]{:S(2)}, u32[]{:S(2)}) %collective-permute-start.10) | collective-permute-done | bytes 163872 | tf_op jit(solution)/shard_map/ppermute | solution.py:441
  75.1 5.5 %collective-permute-done.11 = bf16[32,2560]{1,0:T(8,128)(2,1)S(1)} collective-permute-done((bf16[32,2560]{1,0:T(8,128)(2,1)S(1)}, bf16[32,2560]{1,0:T(8,128)(2,1)S(1)}, u32[]{:S(2)}, u32[]{:S(2)}) %collective-permute-start.11) | collective-permute-done | bytes 163872 | tf_op jit(solution)/shard_map/ppermute | solution.py:441
  81.2 4.0 %collective-permute-start.17 = (bf16[8,4096]{1,0:T(8,128)(2,1)S(1)}, bf16[8,4096]{1,0:T(8,128)(2,1)S(1)}, u32[]{:S(2)}, u32[]{:S(2)}) collective-permute-start(bf16[8,4096]{1,0:T(8,128)(2,1)S(1)} %get-tuple-element.159), channel_id=1, source_target_pairs={{0,8},{4,12},{8,16},{12,20},{16,24},{20,28},{24,0},{28,4},{1,9},{5... | collective-permute-start | bytes 196616 | tf_op jit(solution)/shard_map/ppermute | solution.py:441
  85.3 3.0 %collective-permute-start.18 = (bf16[8,4096]{1,0:T(8,128)(2,1)S(1)}, bf16[8,4096]{1,0:T(8,128)(2,1)S(1)}, u32[]{:S(2)}, u32[]{:S(2)}) collective-permute-start(bf16[8,4096]{1,0:T(8,128)(2,1)S(1)} %get-tuple-element.158), channel_id=1, source_target_pairs={{0,16},{4,20},{8,24},{12,28},{16,0},{20,4},{24,8},{28,12},{1,17},{... | collective-permute-start | bytes 196616 | tf_op jit(solution)/shard_map/ppermute | solution.py:441
  102.8 5.7 %collective-permute-done.21.refs_1_ = bf16[64,4096]{1,0:T(8,128)(2,1)S(1)} collective-permute-done((bf16[64,4096]{1,0:T(8,128)(2,1)S(1)}, bf16[64,4096]{1,0:T(8,128)(2,1)S(1)}, u32[]{:S(2)}, u32[]{:S(2)}) %collective-permute-start.21) | collective-permute-done | bytes 524320 | tf_op jit(solution)/shard_map/ppermute | solution.py:452
  110.4 6.3 %gate_up.2.refs_4_ = bf16[256,768]{1,0:T(8,128)(2,1)S(1)} custom-call(bf16[64,4096]{1,0:T(8,128)(2,1)S(1)} %constant_dynamic-update-slice_fusion.refs_0_, bf16[64,4096]{1,0:T(8,128)(2,1)S(1)} %collective-permute-done.21.refs_1_, bf16[64,4096]{1,0:T(8,128)(2,1)S(1)} %collective-permute-done.22.refs_2_, bf16[64,4096]{1,0:T(8,128)(2,1)S(1)} %collective-permute-done.23.refs_3_, ...), custom_call_target="tpu_custom_call" | custom-call | flops 3221225472 | bytes 14680064 | tf_op jit(solution)/shard_map/gate_up/pallas_call | solution.py:284
  119.4 12.1 %gate_up_down.2 = (bf16[256,1536]{1,0:T(8,128)(2,1)}, bf16[128,4096]{1,0:T(8,128)(2,1)S(1)}, bf16[128,4096]{1,0:T(8,128)(2,1)}) custom-call(bf16[64,4096]{1,0:T(8,128)(2,1)S(1)} %constant_dynamic-update-slice_fusion.refs_0_, bf16[64,4096]{1,0:T(8,128)(2,1)S(1)} %collective-permute-done.21.refs_1_, bf16[64,4096]{1,0:T(8,128)(2,1)S(1)} %collective-permute-done.22.refs_2_, ...), custom_call_target="tpu_custom_call" | custom-call | flops 6442450944 | bytes 29360128 | tf_op jit(solution)/shard_map/gate_up_down/pallas_call | solution.py:364
  132.7 2.4 %collective-permute-done.29 = bf16[128,4096]{1,0:T(8,128)(2,1)S(1)} collective-permute-done((bf16[128,4096]{1,0:T(8,128)(2,1)}, bf16[128,4096]{1,0:T(8,128)(2,1)S(1)}, u32[]{:S(2)}, u32[]{:S(2)}) %collective-permute-start.29) | collective-permute-done | bytes 1048608 | tf_op jit(solution)/shard_map/ppermute | solution.py:29
  137.2 9.8 %gate_up.3.refs_4_ = bf16[512,768]{1,0:T(8,128)(2,1)S(1)} custom-call(bf16[128,4096]{1,0:T(8,128)(2,1)S(1)} %constant_dynamic-update-slice_fusion.9.refs_0_, bf16[128,4096]{1,0:T(8,128)(2,1)S(1)} %collective-permute-done.28.refs_1_, bf16[128,4096]{1,0:T(8,128)(2,1)S(1)} %collective-permute-done.30.refs_2_, ...), custom_call_target="tpu_custom_call" | custom-call | flops 6442450944 | bytes 16777216 | tf_op jit(solution)/shard_map/gate_up/pallas_call | solution.py:284
  148.7 14.4 %gate_up_down.3 = (bf16[512,1536]{1,0:T(8,128)(2,1)}, bf16[256,2048]{1,0:T(8,128)(2,1)S(1)}, bf16[256,2048]{1,0:T(8,128)(2,1)S(1)}) custom-call(bf16[128,4096]{1,0:T(8,128)(2,1)S(1)} %constant_dynamic-update-slice_fusion.9.refs_0_, bf16[128,4096]{1,0:T(8,128)(2,1)S(1)} %collective-permute-done.28.refs_1_, bf16[128,4096]{1,0:T(8,128)(2,1)} %copy-done.2, ...), custom_call_target="tpu_custom_call" | custom-call | flops 9663676416 | bytes 25165824 | tf_op jit(solution)/shard_map/gate_up_down/pallas_call | solution.py:364
  163.4 2.6 %collective-permute-done.34 = bf16[256,2048]{1,0:T(8,128)(2,1)S(1)} collective-permute-done((bf16[256,2048]{1,0:T(8,128)(2,1)S(1)}, bf16[256,2048]{1,0:T(8,128)(2,1)S(1)}, u32[]{:S(2)}, u32[]{:S(2)}) %collective-permute-start.34) | collective-permute-done | bytes 1048608 | tf_op jit(solution)/shard_map/ppermute | solution.py:29
  166.8 5.4 %down.1 = (bf16[256,2048]{1,0:T(8,128)(2,1)S(1)}, bf16[256,2048]{1,0:T(8,128)(2,1)S(1)}) custom-call(bf16[512,1536]{1,0:T(8,128)(2,1)S(1)} %copy-done.4, bf16[1536,4096]{1,0:T(8,128)(2,1)} %bitcast.59), custom_call_target="tpu_custom_call" | custom-call | flops 3221225472 | bytes 9961472 | tf_op jit(solution)/shard_map/down/pallas_call | solution.py:419
  172.1 3.3 %collective-permute-done.35 = bf16[128,2048]{1,0:T(8,128)(2,1)S(1)} collective-permute-done((bf16[128,2048]{1,0:T(8,128)(2,1)S(1)}, bf16[128,2048]{1,0:T(8,128)(2,1)S(1)}, u32[]{:S(2)}, u32[]{:S(2)}) %collective-permute-start.35) | collective-permute-done | bytes 524320 | tf_op jit(solution)/shard_map/ppermute | solution.py:452
  179.0 4.3 %collective-permute-done.37 = bf16[64,2048]{1,0:T(8,128)(2,1)S(1)} collective-permute-done((bf16[64,2048]{1,0:T(8,128)(2,1)S(1)}, bf16[64,2048]{1,0:T(8,128)(2,1)S(1)}, u32[]{:S(2)}, u32[]{:S(2)}) %collective-permute-start.37) | collective-permute-done | bytes 262176 | tf_op jit(solution)/shard_map/ppermute | solution.py:452
  184.5 2.8 %collective-permute-start.39 = (bf16[32,2048]{1,0:T(8,128)(2,1)S(1)}, bf16[32,2048]{1,0:T(8,128)(2,1)S(1)}, u32[]{:S(2)}, u32[]{:S(2)}) collective-permute-start(bf16[32,2048]{1,0:T(8,128)(2,1)S(1)} %pad_maximum_fusion.3), channel_id=1, source_target_pairs={{0,16},{4,20},{8,24},{12,28},{16,0},{20,4},{24,8},{28,12},{1,17},{... | collective-permute-start | bytes 393224 | tf_op jit(solution)/shard_map/ppermute | solution.py:441
  188.3 3.2 %collective-permute-start.38 = (bf16[32,2048]{1,0:T(8,128)(2,1)S(1)}, bf16[32,2048]{1,0:T(8,128)(2,1)S(1)}, u32[]{:S(2)}, u32[]{:S(2)}) collective-permute-start(bf16[32,2048]{1,0:T(8,128)(2,1)S(1)} %pad_maximum_fusion.2), channel_id=1, source_target_pairs={{0,24},{4,28},{8,0},{12,4},{16,8},{20,12},{24,16},{28,20},{1,25},{... | collective-permute-start | bytes 393224 | tf_op jit(solution)/shard_map/ppermute | solution.py:441
  191.5 2.6 %collective-permute-done.42 = bf16[64,2048]{1,0:T(8,128)(2,1)S(1)} collective-permute-done((bf16[64,2048]{1,0:T(8,128)(2,1)S(1)}, bf16[64,2048]{1,0:T(8,128)(2,1)S(1)}, u32[]{:S(2)}, u32[]{:S(2)}) %collective-permute-start.42) | collective-permute-done | bytes 262176 | tf_op jit(solution)/shard_map/ppermute | solution.py:452
  196.5 2.5 %collective-permute-start.43 = (bf16[16,2048]{1,0:T(8,128)(2,1)S(1)}, bf16[16,2048]{1,0:T(8,128)(2,1)S(1)}, u32[]{:S(2)}, u32[]{:S(2)}) collective-permute-start(bf16[16,2048]{1,0:T(8,128)(2,1)S(1)} %get-tuple-element.142), channel_id=1, source_target_pairs={{0,24},{4,28},{8,0},{12,4},{16,8},{20,12},{24,16},{28,20},{1,25},{... | collective-permute-start | bytes 196616 | tf_op jit(solution)/shard_map/ppermute | solution.py:441
  201.5 4.9 %collective-permute-done.44 = bf16[16,2048]{1,0:T(8,128)(2,1)S(1)} collective-permute-done((bf16[16,2048]{1,0:T(8,128)(2,1)S(1)}, bf16[16,2048]{1,0:T(8,128)(2,1)S(1)}, u32[]{:S(2)}, u32[]{:S(2)}) %collective-permute-start.44) | collective-permute-done | bytes 65568 | tf_op jit(solution)/shard_map/ppermute | solution.py:441
  (173 shorter events, 56.9 us)
Async XLA Ops:
  6.7 6.7 %collective-permute-start.1 = (bf16[64,288]{1,0:T(8,128)(2,1)S(1)}, bf16[64,288]{1,0:T(8,128)(2,1)S(1)}, u32[]{:S(2)}, u32[]{:S(2)}) collective-permute-start(bf16[64,288]{1,0:T(8,128)(2,1)S(1)} %get-tuple-element.161), channel_id=1, source_target_pairs={{0,8},{4,12},{8,16},{12,20},{16,24},{20,28},{24,0},{28,4},{1,9},{5... | collective-permute-start | bytes 110600 | tf_op jit(solution)/shard_map/ppermute | solution.py:441
  9.2 6.5 %collective-permute-start.2 = (bf16[64,288]{1,0:T(8,128)(2,1)S(1)}, bf16[64,288]{1,0:T(8,128)(2,1)S(1)}, u32[]{:S(2)}, u32[]{:S(2)}) collective-permute-start(bf16[64,288]{1,0:T(8,128)(2,1)S(1)} %get-tuple-element.163), channel_id=1, source_target_pairs={{0,16},{4,20},{8,24},{12,28},{16,0},{20,4},{24,8},{28,12},{1,17},{... | collective-permute-start | bytes 110600 | tf_op jit(solution)/shard_map/ppermute | solution.py:441
  20.2 6.0 %collective-permute-start.5 = (bf16[64,288]{1,0:T(8,128)(2,1)S(1)}, bf16[64,288]{1,0:T(8,128)(2,1)S(1)}, u32[]{:S(2)}, u32[]{:S(2)}) collective-permute-start(bf16[64,288]{1,0:T(8,128)(2,1)S(1)} %add_convert_fusion.10.refs_0_), channel_id=1, source_target_pairs={{0,8},{4,12},{8,16},{12,20},{16,24},{20,28},{24,0},{28,4},{1,9},{5... | collective-permute-start | bytes 110600 | tf_op jit(solution)/shard_map/ppermute | solution.py:441
  46.2 19.5 %collective-permute-start.9 = (bf16[128,2560]{1,0:T(8,128)(2,1)S(1)}, bf16[128,2560]{1,0:T(8,128)(2,1)S(1)}, u32[]{:S(2)}, u32[]{:S(2)}) collective-permute-start(bf16[128,2560]{1,0:T(8,128)(2,1)S(1)} %get-tuple-element.73), channel_id=1, source_target_pairs={{0,4},{4,0},{8,12},{12,8},{16,20},{20,16},{24,28},{28,24},{1,5},{5... | collective-permute-start | bytes 1966088 | tf_op jit(solution)/shard_map/ppermute | solution.py:34
  47.8 9.7 %collective-permute-start.13 = (bf16[64,1536]{1,0:T(8,128)(2,1)S(1)}, bf16[64,1536]{1,0:T(8,128)(2,1)S(1)}, u32[]{:S(2)}, u32[]{:S(2)}) collective-permute-start(bf16[64,1536]{1,0:T(8,128)(2,1)S(1)} %get-tuple-element.75), channel_id=1, source_target_pairs={{0,8},{4,12},{8,16},{12,20},{16,24},{20,28},{24,0},{28,4},{1,9},{5... | collective-permute-start | bytes 589832 | tf_op jit(solution)/shard_map/ppermute | solution.py:441
  48.6 16.4 %collective-permute-start.14 = (bf16[64,1536]{1,0:T(8,128)(2,1)S(1)}, bf16[64,1536]{1,0:T(8,128)(2,1)S(1)}, u32[]{:S(2)}, u32[]{:S(2)}) collective-permute-start(bf16[64,1536]{1,0:T(8,128)(2,1)S(1)} %get-tuple-element.76), channel_id=1, source_target_pairs={{0,16},{4,20},{8,24},{12,28},{16,0},{20,4},{24,8},{28,12},{1,17},{... | collective-permute-start | bytes 589832 | tf_op jit(solution)/shard_map/ppermute | solution.py:441
  50.8 14.3 %collective-permute-start.15 = (bf16[64,1536]{1,0:T(8,128)(2,1)S(1)}, bf16[64,1536]{1,0:T(8,128)(2,1)S(1)}, u32[]{:S(2)}, u32[]{:S(2)}) collective-permute-start(bf16[64,1536]{1,0:T(8,128)(2,1)S(1)} %get-tuple-element.77), channel_id=1, source_target_pairs={{0,24},{4,28},{8,0},{12,4},{16,8},{20,12},{24,16},{28,20},{1,25},{... | collective-permute-start | bytes 589832 | tf_op jit(solution)/shard_map/ppermute | solution.py:441
  65.2 7.7 %collective-permute-start.16 = (bf16[32,1536]{1,0:T(8,128)(2,1)S(1)}, bf16[32,1536]{1,0:T(8,128)(2,1)S(1)}, u32[]{:S(2)}, u32[]{:S(2)}) collective-permute-start(bf16[32,1536]{1,0:T(8,128)(2,1)S(1)} %slice.436), channel_id=1, source_target_pairs={{0,4},{4,0},{8,12},{12,8},{16,20},{20,16},{24,28},{28,24},{1,5},{5... | collective-permute-start | bytes 294920 | tf_op jit(solution)/shard_map/ppermute | solution.py:34
  66.0 9.0 %collective-permute-start.10 = (bf16[32,2560]{1,0:T(8,128)(2,1)S(1)}, bf16[32,2560]{1,0:T(8,128)(2,1)S(1)}, u32[]{:S(2)}, u32[]{:S(2)}) collective-permute-start(bf16[32,2560]{1,0:T(8,128)(2,1)S(1)} %get-tuple-element.133), channel_id=1, source_target_pairs={{0,8},{4,12},{8,16},{12,20},{16,24},{20,28},{24,0},{28,4},{1,9},{5... | collective-permute-start | bytes 491528 | tf_op jit(solution)/shard_map/ppermute | solution.py:441
  70.4 10.2 %collective-permute-start.11 = (bf16[32,2560]{1,0:T(8,128)(2,1)S(1)}, bf16[32,2560]{1,0:T(8,128)(2,1)S(1)}, u32[]{:S(2)}, u32[]{:S(2)}) collective-permute-start(bf16[32,2560]{1,0:T(8,128)(2,1)S(1)} %get-tuple-element.135), channel_id=1, source_target_pairs={{0,16},{4,20},{8,24},{12,28},{16,0},{20,4},{24,8},{28,12},{1,17},{... | collective-permute-start | bytes 491528 | tf_op jit(solution)/shard_map/ppermute | solution.py:441
  70.7 9.9 %collective-permute-start.12 = (bf16[32,2560]{1,0:T(8,128)(2,1)S(1)}, bf16[32,2560]{1,0:T(8,128)(2,1)S(1)}, u32[]{:S(2)}, u32[]{:S(2)}) collective-permute-start(bf16[32,2560]{1,0:T(8,128)(2,1)S(1)} %get-tuple-element.134), channel_id=1, source_target_pairs={{0,24},{4,28},{8,0},{12,4},{16,8},{20,12},{24,16},{28,20},{1,25},{... | collective-permute-start | bytes 491528 | tf_op jit(solution)/shard_map/ppermute | solution.py:441
  81.2 9.2 %collective-permute-start.17 = (bf16[8,4096]{1,0:T(8,128)(2,1)S(1)}, bf16[8,4096]{1,0:T(8,128)(2,1)S(1)}, u32[]{:S(2)}, u32[]{:S(2)}) collective-permute-start(bf16[8,4096]{1,0:T(8,128)(2,1)S(1)} %get-tuple-element.159), channel_id=1, source_target_pairs={{0,8},{4,12},{8,16},{12,20},{16,24},{20,28},{24,0},{28,4},{1,9},{5... | collective-permute-start | bytes 196616 | tf_op jit(solution)/shard_map/ppermute | solution.py:441
  85.3 7.0 %collective-permute-start.18 = (bf16[8,4096]{1,0:T(8,128)(2,1)S(1)}, bf16[8,4096]{1,0:T(8,128)(2,1)S(1)}, u32[]{:S(2)}, u32[]{:S(2)}) collective-permute-start(bf16[8,4096]{1,0:T(8,128)(2,1)S(1)} %get-tuple-element.158), channel_id=1, source_target_pairs={{0,16},{4,20},{8,24},{12,28},{16,0},{20,4},{24,8},{28,12},{1,17},{... | collective-permute-start | bytes 196616 | tf_op jit(solution)/shard_map/ppermute | solution.py:441
  92.8 6.4 %collective-permute-start.20 = (bf16[32,4096]{1,0:T(8,128)(2,1)S(1)}, bf16[32,4096]{1,0:T(8,128)(2,1)S(1)}, u32[]{:S(2)}, u32[]{:S(2)}) collective-permute-start(bf16[32,4096]{1,0:T(8,128)(2,1)S(1)} %pad_maximum_fusion), channel_id=1, source_target_pairs={{0,4},{1,5},{2,3},{3,2},{4,0},{5,1},{6,7},{7,6},{8,12},{9,13},{10,... | collective-permute-start | bytes 786440 | tf_op jit(solution)/shard_map/ppermute | solution.py:452
  94.4 8.4 %collective-permute-start.24 = (bf16[16,4096]{1,0:T(8,128)(2,1)S(1)}, bf16[16,4096]{1,0:T(8,128)(2,1)S(1)}, u32[]{:S(2)}, u32[]{:S(2)}) collective-permute-start(bf16[16,4096]{1,0:T(8,128)(2,1)S(1)} %get-tuple-element.138), channel_id=1, source_target_pairs={{0,8},{4,12},{8,16},{12,20},{16,24},{20,28},{24,0},{28,4},{1,9},{5... | collective-permute-start | bytes 393224 | tf_op jit(solution)/shard_map/ppermute | solution.py:441
  95.5 13.0 %collective-permute-start.25 = (bf16[16,4096]{1,0:T(8,128)(2,1)S(1)}, bf16[16,4096]{1,0:T(8,128)(2,1)S(1)}, u32[]{:S(2)}, u32[]{:S(2)}) collective-permute-start(bf16[16,4096]{1,0:T(8,128)(2,1)S(1)} %get-tuple-element.137), channel_id=1, source_target_pairs={{0,16},{4,20},{8,24},{12,28},{16,0},{20,4},{24,8},{28,12},{1,17},{... | collective-permute-start | bytes 393224 | tf_op jit(solution)/shard_map/ppermute | solution.py:441
  97.3 11.2 %collective-permute-start.26 = (bf16[16,4096]{1,0:T(8,128)(2,1)S(1)}, bf16[16,4096]{1,0:T(8,128)(2,1)S(1)}, u32[]{:S(2)}, u32[]{:S(2)}) collective-permute-start(bf16[16,4096]{1,0:T(8,128)(2,1)S(1)} %get-tuple-element.136), channel_id=1, source_target_pairs={{0,24},{4,28},{8,0},{12,4},{16,8},{20,12},{24,16},{28,20},{1,25},{... | collective-permute-start | bytes 393224 | tf_op jit(solution)/shard_map/ppermute | solution.py:441
  99.2 9.2 %collective-permute-start.21 = (bf16[64,4096]{1,0:T(8,128)(2,1)S(1)}, bf16[64,4096]{1,0:T(8,128)(2,1)S(1)}, u32[]{:S(2)}, u32[]{:S(2)}) collective-permute-start(bf16[64,4096]{1,0:T(8,128)(2,1)S(1)} %constant_dynamic-update-slice_fusion.refs_0_), channel_id=1, source_target_pairs={{0,1},{1,0},{2,6},{3,7},{4,5},{5,4},{6,2},{7,3},{8,9},{9,8},{10,14... | collective-permute-start | bytes 1572872 | tf_op jit(solution)/shard_map/ppermute | solution.py:452
  100.8 9.3 %collective-permute-start.22 = (bf16[64,4096]{1,0:T(8,128)(2,1)S(1)}, bf16[64,4096]{1,0:T(8,128)(2,1)S(1)}, u32[]{:S(2)}, u32[]{:S(2)}) collective-permute-start(bf16[64,4096]{1,0:T(8,128)(2,1)S(1)} %constant_dynamic-update-slice_fusion.refs_0_), channel_id=1, source_target_pairs={{0,2},{2,0},{1,3},{3,1},{4,6},{6,4},{5,7},{7,5},{8,10},{10,8},{9,1... | collective-permute-start | bytes 1572872 | tf_op jit(solution)/shard_map/ppermute | solution.py:29
  108.5 9.2 %collective-permute-start.27 = (bf16[64,4096]{1,0:T(8,128)(2,1)S(1)}, bf16[64,4096]{1,0:T(8,128)(2,1)S(1)}, u32[]{:S(2)}, u32[]{:S(2)}) collective-permute-start(bf16[64,4096]{1,0:T(8,128)(2,1)S(1)} %constant_dynamic-update-slice_fusion.5), channel_id=1, source_target_pairs={{0,4},{1,5},{2,3},{3,2},{4,0},{5,1},{6,7},{7,6},{8,12},{9,13},{10,... | collective-permute-start | bytes 1572872 | tf_op jit(solution)/shard_map/ppermute | solution.py:452
  117.8 14.9 %collective-permute-start.28 = (bf16[128,4096]{1,0:T(8,128)(2,1)S(1)}, bf16[128,4096]{1,0:T(8,128)(2,1)S(1)}, u32[]{:S(2)}, u32[]{:S(2)}) collective-permute-start(bf16[128,4096]{1,0:T(8,128)(2,1)S(1)} %constant_dynamic-update-slice_fusion.9.refs_0_), channel_id=1, source_target_pairs={{0,1},{1,0},{2,6},{3,7},{4,5},{5,4},{6,2},{7,3},{8,9},{9,8},{10,14... | collective-permute-start | bytes 3145736 | tf_op jit(solution)/shard_map/ppermute | solution.py:452
  135.3 11.8 %collective-permute-start.32 = (bf16[64,4096]{1,0:T(8,128)(2,1)S(1)}, bf16[64,4096]{1,0:T(8,128)(2,1)S(1)}, u32[]{:S(2)}, u32[]{:S(2)}) collective-permute-start(bf16[64,4096]{1,0:T(8,128)(2,1)S(1)} %add_convert_fusion.3), channel_id=1, source_target_pairs={{0,1},{1,0},{2,6},{3,7},{4,5},{5,4},{6,2},{7,3},{8,9},{9,8},{10,14... | collective-permute-start | bytes 1572872 | tf_op jit(solution)/shard_map/ppermute | solution.py:452
  147.1 16.0 %collective-permute-start.33 = (bf16[32,4096]{1,0:T(8,128)(2,1)S(1)}, bf16[32,4096]{1,0:T(8,128)(2,1)S(1)}, u32[]{:S(2)}, u32[]{:S(2)}) collective-permute-start(bf16[32,4096]{1,0:T(8,128)(2,1)S(1)} %add_convert_fusion.9), channel_id=1, source_target_pairs={{0,4},{1,5},{2,3},{3,2},{4,0},{5,1},{6,7},{7,6},{8,12},{9,13},{10,... | collective-permute-start | bytes 786440 | tf_op jit(solution)/shard_map/ppermute | solution.py:452
  166.2 9.2 %collective-permute-start.35 = (bf16[128,2048]{1,0:T(8,128)(2,1)S(1)}, bf16[128,2048]{1,0:T(8,128)(2,1)S(1)}, u32[]{:S(2)}, u32[]{:S(2)}) collective-permute-start(bf16[128,2048]{1,0:T(8,128)(2,1)S(1)} %add_convert_fusion.2), channel_id=1, source_target_pairs={{0,1},{1,0},{2,6},{3,7},{4,5},{5,4},{6,2},{7,3},{8,9},{9,8},{10,14... | collective-permute-start | bytes 1572872 | tf_op jit(solution)/shard_map/ppermute | solution.py:452
  175.8 7.5 %collective-permute-start.37 = (bf16[64,2048]{1,0:T(8,128)(2,1)S(1)}, bf16[64,2048]{1,0:T(8,128)(2,1)S(1)}, u32[]{:S(2)}, u32[]{:S(2)}) collective-permute-start(bf16[64,2048]{1,0:T(8,128)(2,1)S(1)} %add_convert_fusion.7), channel_id=1, source_target_pairs={{0,4},{1,5},{2,3},{3,2},{4,0},{5,1},{6,7},{7,6},{8,12},{9,13},{10,... | collective-permute-start | bytes 786440 | tf_op jit(solution)/shard_map/ppermute | solution.py:452
  178.4 9.2 %collective-permute-start.41 = (bf16[128,2048]{1,0:T(8,128)(2,1)S(1)}, bf16[128,2048]{1,0:T(8,128)(2,1)S(1)}, u32[]{:S(2)}, u32[]{:S(2)}) collective-permute-start(bf16[128,2048]{1,0:T(8,128)(2,1)S(1)} %add_convert_fusion.1), channel_id=1, source_target_pairs={{0,1},{1,0},{2,6},{3,7},{4,5},{5,4},{6,2},{7,3},{8,9},{9,8},{10,14... | collective-permute-start | bytes 1572872 | tf_op jit(solution)/shard_map/ppermute | solution.py:452
  183.4 10.8 %collective-permute-start.40 = (bf16[32,2048]{1,0:T(8,128)(2,1)S(1)}, bf16[32,2048]{1,0:T(8,128)(2,1)S(1)}, u32[]{:S(2)}, u32[]{:S(2)}) collective-permute-start(bf16[32,2048]{1,0:T(8,128)(2,1)S(1)} %pad_maximum_fusion.4), channel_id=1, source_target_pairs={{0,8},{4,12},{8,16},{12,20},{16,24},{20,28},{24,0},{28,4},{1,9},{5... | collective-permute-start | bytes 393224 | tf_op jit(solution)/shard_map/ppermute | solution.py:441
  184.5 10.6 %collective-permute-start.39 = (bf16[32,2048]{1,0:T(8,128)(2,1)S(1)}, bf16[32,2048]{1,0:T(8,128)(2,1)S(1)}, u32[]{:S(2)}, u32[]{:S(2)}) collective-permute-start(bf16[32,2048]{1,0:T(8,128)(2,1)S(1)} %pad_maximum_fusion.3), channel_id=1, source_target_pairs={{0,16},{4,20},{8,24},{12,28},{16,0},{20,4},{24,8},{28,12},{1,17},{... | collective-permute-start | bytes 393224 | tf_op jit(solution)/shard_map/ppermute | solution.py:441
  187.7 6.4 %collective-permute-start.42 = (bf16[64,2048]{1,0:T(8,128)(2,1)S(1)}, bf16[64,2048]{1,0:T(8,128)(2,1)S(1)}, u32[]{:S(2)}, u32[]{:S(2)}) collective-permute-start(bf16[64,2048]{1,0:T(8,128)(2,1)S(1)} %add_convert_fusion.5), channel_id=1, source_target_pairs={{0,4},{1,5},{2,3},{3,2},{4,0},{5,1},{6,7},{7,6},{8,12},{9,13},{10,... | collective-permute-start | bytes 786440 | tf_op jit(solution)/shard_map/ppermute | solution.py:452
  188.3 8.0 %collective-permute-start.38 = (bf16[32,2048]{1,0:T(8,128)(2,1)S(1)}, bf16[32,2048]{1,0:T(8,128)(2,1)S(1)}, u32[]{:S(2)}, u32[]{:S(2)}) collective-permute-start(bf16[32,2048]{1,0:T(8,128)(2,1)S(1)} %pad_maximum_fusion.2), channel_id=1, source_target_pairs={{0,24},{4,28},{8,0},{12,4},{16,8},{20,12},{24,16},{28,20},{1,25},{... | collective-permute-start | bytes 393224 | tf_op jit(solution)/shard_map/ppermute | solution.py:441
  199.0 7.4 %collective-permute-start.44 = (bf16[16,2048]{1,0:T(8,128)(2,1)S(1)}, bf16[16,2048]{1,0:T(8,128)(2,1)S(1)}, u32[]{:S(2)}, u32[]{:S(2)}) collective-permute-start(bf16[16,2048]{1,0:T(8,128)(2,1)S(1)} %get-tuple-element.141), channel_id=1, source_target_pairs={{0,16},{4,20},{8,24},{12,28},{16,0},{20,4},{24,8},{28,12},{1,17},{... | collective-permute-start | bytes 196616 | tf_op jit(solution)/shard_map/ppermute | solution.py:441
  200.0 6.4 %collective-permute-start.45 = (bf16[16,2048]{1,0:T(8,128)(2,1)S(1)}, bf16[16,2048]{1,0:T(8,128)(2,1)S(1)}, u32[]{:S(2)}, u32[]{:S(2)}) collective-permute-start(bf16[16,2048]{1,0:T(8,128)(2,1)S(1)} %get-tuple-element.140), channel_id=1, source_target_pairs={{0,8},{4,12},{8,16},{12,20},{16,24},{20,28},{24,0},{28,4},{1,9},{5... | collective-permute-start | bytes 196616 | tf_op jit(solution)/shard_map/ppermute | solution.py:441
  (29 other events, 224.5 us)

commit v9 on v8

--- a/solution.py
+++ b/solution.py
@@ -521,11 +521,11 @@
     early_far = cross(early_go, 1)
     sizes = (4 * late_own.shape[0],) * 2
     late_rows = after(pieces(late_two, late_four), early_go)
-    late_first = gate_up(late_rows, w_gate, w_up, 0, hidden // 2)
-    early_kept, early_go = home_second(after(early_kept, late_first), early_far)
+    late_hidden = gate_up(late_rows, w_gate, w_up, 0, hidden)
+    early_kept, early_go = home_second(after(early_kept, late_hidden), early_far)
     early_far = cross(early_go, 0)
-    late_rows = after(late_rows, early_go)
-    late_hidden, out_left = finish(late_rows, late_first, sizes, w_gate, w_up, w_down, 0, half)
+    late_hidden = after(late_hidden, early_go)
+    out_left = down([late_hidden], sizes, w_down, 0, half)
     early_result = home_third(after(early_kept, out_left[0]), early_far)
     left = home_first(after(out_left, early_result))
     left_far = cross(left[1], 1)

time: 208 us -> 208 us (level)
    pallas_call x2 -> x1, Pallas kernels: 26.5 us -> 12.1 us  [finish(): pl.pallas_call(functools.partial(finish_kernel, len(pieces), first), out_...]
    pallas_call x2, Pallas kernels: 16.1 us -> 24.4 us  [gate_up(): pl.pallas_call(functools.partial(gate_up_kernel, len(pieces), first), out...]
    pallas_call x1 -> x2, Pallas kernels: 5.38 us -> 10.7 us  [down(): pl.pallas_call(functools.partial(down_kernel, len(pieces), first), out_sh...]
where the time goes in v9:
time: 208 us
  waiting for transfers between devices  72.3 us (35%)
  Pallas kernels  63.3 us (30%)
  starting transfers between devices  61.1 us (29%)
  other arithmetic  4.93 us (2%)
  local copies, waits for them, and re-layouts  3.9 us (2%)
    ppermute x24, starting transfers between devices, along_line(): lax.ppermute(block, 'expert', [(e, (e + 2 * distance) % size) for e in ra...  42.7 us
    ppermute x24, waiting for transfers between devices, along_line(): lax.ppermute(block, 'expert', [(e, (e + 2 * distance) % size) for e in ra...  41 us
    pallas_call x2, Pallas kernels, gate_up(): pl.pallas_call(functools.partial(gate_up_kernel, len(pieces), first), out...  24.4 us
    ppermute x10, waiting for transfers between devices, cross(): return lax.ppermute(block, ('expert', 'context', 'dp'), route)  18.8 us
    pallas_call x1, Pallas kernels, finish(): pl.pallas_call(functools.partial(finish_kernel, len(pieces), first), out_...  12.1 us
    pallas_call x2, Pallas kernels, down(): pl.pallas_call(functools.partial(down_kernel, len(pieces), first), out_sh...  10.7 us
    ppermute x10, starting transfers between devices, cross(): return lax.ppermute(block, ('expert', 'context', 'dp'), route)  10.3 us
    pallas_call x1, Pallas kernels, run_out(): pl.pallas_call(functools.partial(out_kernel, channels // LANES, line, fir...  9.18 us
  transfers between devices with their start and end apart: 46, of which 33 were waited for; matrix products, arithmetic and copies ran while one was open for 2% of the time, Pallas kernels for 23%

profile of v9, /device:TPU:0, one launch (start us, length us, event | category | flops | bytes accessed | tf_op | source)
XLA Modules:
  0.0 207.9 jit_solution(17091025067385584165)
XLA Ops:
  0.8 2.3 %collective-permute-start = (bf16[3,1024]{1,0:T(4,128)(2,1)S(1)}, bf16[3,1024]{1,0:T(4,128)(2,1)S(1)}, u32[]{:S(2)}, u32[]{:S(2)}) collective-permute-start(bf16[3,1024]{1,0:T(4,128)(2,1)S(1)} %slice_bitcast_fusion), channel_id=1, source_target_pairs={{0,2},{1,3},{4,6},{5,7},{8,10},{9,11},{12,14},{13,15},{16,18},{17,... | collective-permute-start | bytes 18440 | tf_op jit(solution)/shard_map/ppermute | solution.py:24
  6.7 2.5 %collective-permute-start.1 = (bf16[64,288]{1,0:T(8,128)(2,1)S(1)}, bf16[64,288]{1,0:T(8,128)(2,1)S(1)}, u32[]{:S(2)}, u32[]{:S(2)}) collective-permute-start(bf16[64,288]{1,0:T(8,128)(2,1)S(1)} %get-tuple-element.153), channel_id=1, source_target_pairs={{0,8},{4,12},{8,16},{12,20},{16,24},{20,28},{24,0},{28,4},{1,9},{5... | collective-permute-start | bytes 110600 | tf_op jit(solution)/shard_map/ppermute | solution.py:441
  9.2 2.6 %collective-permute-start.2 = (bf16[64,288]{1,0:T(8,128)(2,1)S(1)}, bf16[64,288]{1,0:T(8,128)(2,1)S(1)}, u32[]{:S(2)}, u32[]{:S(2)}) collective-permute-start(bf16[64,288]{1,0:T(8,128)(2,1)S(1)} %get-tuple-element.155), channel_id=1, source_target_pairs={{0,16},{4,20},{8,24},{12,28},{16,0},{20,4},{24,8},{28,12},{1,17},{... | collective-permute-start | bytes 110600 | tf_op jit(solution)/shard_map/ppermute | solution.py:441
  13.4 2.3 %collective-permute-done.2 = bf16[64,288]{1,0:T(8,128)(2,1)S(1)} collective-permute-done((bf16[64,288]{1,0:T(8,128)(2,1)S(1)}, bf16[64,288]{1,0:T(8,128)(2,1)S(1)}, u32[]{:S(2)}, u32[]{:S(2)}) %collective-permute-start.2) | collective-permute-done | bytes 36896 | tf_op jit(solution)/shard_map/ppermute | solution.py:441
  17.6 2.6 %collective-permute-done.4 = bf16[64,288]{1,0:T(8,128)(2,1)S(1)} collective-permute-done((bf16[64,288]{1,0:T(8,128)(2,1)S(1)}, bf16[64,288]{1,0:T(8,128)(2,1)S(1)}, u32[]{:S(2)}, u32[]{:S(2)}) %collective-permute-start.4) | collective-permute-done | bytes 36896 | tf_op jit(solution)/shard_map/ppermute | solution.py:34
  21.2 2.6 %collective-permute-start.6 = (bf16[64,288]{1,0:T(8,128)(2,1)S(1)}, bf16[64,288]{1,0:T(8,128)(2,1)S(1)}, u32[]{:S(2)}, u32[]{:S(2)}) collective-permute-start(bf16[64,288]{1,0:T(8,128)(2,1)S(1)} %add_convert_fusion.10.refs_0_), channel_id=1, source_target_pairs={{0,16},{4,20},{8,24},{12,28},{16,0},{20,4},{24,8},{28,12},{1,17},{... | collective-permute-start | bytes 110600 | tf_op jit(solution)/shard_map/ppermute | solution.py:441
  27.9 6.9 %state_scan.1 = (f32[2048,128]{1,0:T(8,128)S(1)}, f32[2048,128]{1,0:T(8,128)S(1)}, f32[16,8,128]{2,1,0:T(8,128)S(1)}, bf16[256,32]{1,0:T(8,128)(2,1)S(1)}, f32[128,128]{1,0:T(8,128)S(1)}) custom-call(s32[2]{0:T(128)S(1)} %pad_add_fusion.place_ref.at_ref, bf16[64,288]{1,0:T(8,128)(2,1)S(1)} %add_convert_fusion.10.refs_0_, ...), custom_call_target="tpu_custom_call" | custom-call | flops 200000000 | bytes 4194304 | tf_op jit(solution)/shard_map/state_scan/pallas_call | solution.py:106
  37.0 9.2 %readout_project.1 = (bf16[128,2560]{1,0:T(8,128)(2,1)S(1)}, bf16[128,2560]{1,0:T(8,128)(2,1)S(1)}, bf16[64,1536]{1,0:T(8,128)(2,1)S(1)}, bf16[64,1536]{1,0:T(8,...) custom-call(s32[2]{0:T(128)S(1)} %pad_add_fusion.place_ref.at_ref, ...), custom_call_target="tpu_custom_call" | custom-call | flops 2147483648 | bytes 16777216 | tf_op jit(solution)/shard_map/readout_project/pallas_call | solution.py:202
  48.6 2.1 %collective-permute-start.14 = (bf16[64,1536]{1,0:T(8,128)(2,1)S(1)}, bf16[64,1536]{1,0:T(8,128)(2,1)S(1)}, u32[]{:S(2)}, u32[]{:S(2)}) collective-permute-start(bf16[64,1536]{1,0:T(8,128)(2,1)S(1)} %get-tuple-element.72), channel_id=1, source_target_pairs={{0,16},{4,20},{8,24},{12,28},{16,0},{20,4},{24,8},{28,12},{1,17},{... | collective-permute-start | bytes 589832 | tf_op jit(solution)/shard_map/ppermute | solution.py:441
  51.8 5.7 %collective-permute-done.13 = bf16[64,1536]{1,0:T(8,128)(2,1)S(1)} collective-permute-done((bf16[64,1536]{1,0:T(8,128)(2,1)S(1)}, bf16[64,1536]{1,0:T(8,128)(2,1)S(1)}, u32[]{:S(2)}, u32[]{:S(2)}) %collective-permute-start.13) | collective-permute-done | bytes 196640 | tf_op jit(solution)/shard_map/ppermute | solution.py:441
  57.5 7.6 %collective-permute-done.14 = bf16[64,1536]{1,0:T(8,128)(2,1)S(1)} collective-permute-done((bf16[64,1536]{1,0:T(8,128)(2,1)S(1)}, bf16[64,1536]{1,0:T(8,128)(2,1)S(1)}, u32[]{:S(2)}, u32[]{:S(2)}) %collective-permute-start.14) | collective-permute-done | bytes 196640 | tf_op jit(solution)/shard_map/ppermute | solution.py:441
  66.0 4.4 %collective-permute-start.10 = (bf16[32,2560]{1,0:T(8,128)(2,1)S(1)}, bf16[32,2560]{1,0:T(8,128)(2,1)S(1)}, u32[]{:S(2)}, u32[]{:S(2)}) collective-permute-start(bf16[32,2560]{1,0:T(8,128)(2,1)S(1)} %get-tuple-element.125), channel_id=1, source_target_pairs={{0,8},{4,12},{8,16},{12,20},{16,24},{20,28},{24,0},{28,4},{1,9},{5... | collective-permute-start | bytes 491528 | tf_op jit(solution)/shard_map/ppermute | solution.py:441
  70.7 2.1 %collective-permute-start.12 = (bf16[32,2560]{1,0:T(8,128)(2,1)S(1)}, bf16[32,2560]{1,0:T(8,128)(2,1)S(1)}, u32[]{:S(2)}, u32[]{:S(2)}) collective-permute-start(bf16[32,2560]{1,0:T(8,128)(2,1)S(1)} %get-tuple-element.126), channel_id=1, source_target_pairs={{0,24},{4,28},{8,0},{12,4},{16,8},{20,12},{24,16},{28,20},{1,25},{... | collective-permute-start | bytes 491528 | tf_op jit(solution)/shard_map/ppermute | solution.py:441
  72.9 2.2 %collective-permute-done.10 = bf16[32,2560]{1,0:T(8,128)(2,1)S(1)} collective-permute-done((bf16[32,2560]{1,0:T(8,128)(2,1)S(1)}, bf16[32,2560]{1,0:T(8,128)(2,1)S(1)}, u32[]{:S(2)}, u32[]{:S(2)}) %collective-permute-start.10) | collective-permute-done | bytes 163872 | tf_op jit(solution)/shard_map/ppermute | solution.py:441
  75.1 5.5 %collective-permute-done.11 = bf16[32,2560]{1,0:T(8,128)(2,1)S(1)} collective-permute-done((bf16[32,2560]{1,0:T(8,128)(2,1)S(1)}, bf16[32,2560]{1,0:T(8,128)(2,1)S(1)}, u32[]{:S(2)}, u32[]{:S(2)}) %collective-permute-start.11) | collective-permute-done | bytes 163872 | tf_op jit(solution)/shard_map/ppermute | solution.py:441
  81.2 4.0 %collective-permute-start.17 = (bf16[8,4096]{1,0:T(8,128)(2,1)S(1)}, bf16[8,4096]{1,0:T(8,128)(2,1)S(1)}, u32[]{:S(2)}, u32[]{:S(2)}) collective-permute-start(bf16[8,4096]{1,0:T(8,128)(2,1)S(1)} %get-tuple-element.151), channel_id=1, source_target_pairs={{0,8},{4,12},{8,16},{12,20},{16,24},{20,28},{24,0},{28,4},{1,9},{5... | collective-permute-start | bytes 196616 | tf_op jit(solution)/shard_map/ppermute | solution.py:441
  85.3 3.0 %collective-permute-start.18 = (bf16[8,4096]{1,0:T(8,128)(2,1)S(1)}, bf16[8,4096]{1,0:T(8,128)(2,1)S(1)}, u32[]{:S(2)}, u32[]{:S(2)}) collective-permute-start(bf16[8,4096]{1,0:T(8,128)(2,1)S(1)} %get-tuple-element.150), channel_id=1, source_target_pairs={{0,16},{4,20},{8,24},{12,28},{16,0},{20,4},{24,8},{28,12},{1,17},{... | collective-permute-start | bytes 196616 | tf_op jit(solution)/shard_map/ppermute | solution.py:441
  102.8 5.7 %collective-permute-done.21.refs_1_ = bf16[64,4096]{1,0:T(8,128)(2,1)S(1)} collective-permute-done((bf16[64,4096]{1,0:T(8,128)(2,1)S(1)}, bf16[64,4096]{1,0:T(8,128)(2,1)S(1)}, u32[]{:S(2)}, u32[]{:S(2)}) %collective-permute-start.21) | collective-permute-done | bytes 524320 | tf_op jit(solution)/shard_map/ppermute | solution.py:452
  110.4 6.3 %gate_up.2.refs_4_ = bf16[256,768]{1,0:T(8,128)(2,1)S(1)} custom-call(bf16[64,4096]{1,0:T(8,128)(2,1)S(1)} %constant_dynamic-update-slice_fusion.refs_0_, bf16[64,4096]{1,0:T(8,128)(2,1)S(1)} %collective-permute-done.21.refs_1_, bf16[64,4096]{1,0:T(8,128)(2,1)S(1)} %collective-permute-done.22.refs_2_, bf16[64,4096]{1,0:T(8,128)(2,1)S(1)} %collective-permute-done.23.refs_3_, ...), custom_call_target="tpu_custom_call" | custom-call | flops 3221225472 | bytes 14680064 | tf_op jit(solution)/shard_map/gate_up/pallas_call | solution.py:284
  119.4 12.1 %gate_up_down.1 = (bf16[256,1536]{1,0:T(8,128)(2,1)}, bf16[128,4096]{1,0:T(8,128)(2,1)S(1)}, bf16[128,4096]{1,0:T(8,128)(2,1)}) custom-call(bf16[64,4096]{1,0:T(8,128)(2,1)S(1)} %constant_dynamic-update-slice_fusion.refs_0_, bf16[64,4096]{1,0:T(8,128)(2,1)S(1)} %collective-permute-done.21.refs_1_, bf16[64,4096]{1,0:T(8,128)(2,1)S(1)} %collective-permute-done.22.refs_2_, ...), custom_call_target="tpu_custom_call" | custom-call | flops 6442450944 | bytes 29360128 | tf_op jit(solution)/shard_map/gate_up_down/pallas_call | solution.py:364
  132.7 2.4 %collective-permute-done.29 = bf16[128,4096]{1,0:T(8,128)(2,1)S(1)} collective-permute-done((bf16[128,4096]{1,0:T(8,128)(2,1)}, bf16[128,4096]{1,0:T(8,128)(2,1)S(1)}, u32[]{:S(2)}, u32[]{:S(2)}) %collective-permute-start.29) | collective-permute-done | bytes 1048608 | tf_op jit(solution)/shard_map/ppermute | solution.py:29
  137.2 18.0 %gate_up.3.refs_0_ = bf16[512,1536]{1,0:T(8,128)(2,1)} custom-call(bf16[128,4096]{1,0:T(8,128)(2,1)S(1)} %constant_dynamic-update-slice_fusion.9.refs_0_, bf16[128,4096]{1,0:T(8,128)(2,1)S(1)} %collective-permute-done.28.refs_1_, bf16[128,4096]{1,0:T(8,128)(2,1)S(1)} %collective-permute-done.30.refs_2_, ...), custom_call_target="tpu_custom_call" | custom-call | flops 12884901888 | bytes 29360128 | tf_op jit(solution)/shard_map/gate_up/pallas_call | solution.py:284
  158.3 5.4 %down.2 = (bf16[256,2048]{1,0:T(8,128)(2,1)S(1)}, bf16[256,2048]{1,0:T(8,128)(2,1)S(1)}) custom-call(bf16[512,1536]{1,0:T(8,128)(2,1)S(1)} %copy-done.2, bf16[1536,4096]{1,0:T(8,128)(2,1)} %bitcast.50), custom_call_target="tpu_custom_call" | custom-call | flops 3221225472 | bytes 9961472 | tf_op jit(solution)/shard_map/down/pallas_call | solution.py:419
  163.9 2.6 %collective-permute-done.34 = bf16[256,2048]{1,0:T(8,128)(2,1)S(1)} collective-permute-done((bf16[256,2048]{1,0:T(8,128)(2,1)S(1)}, bf16[256,2048]{1,0:T(8,128)(2,1)S(1)}, u32[]{:S(2)}, u32[]{:S(2)}) %collective-permute-start.34) | collective-permute-done | bytes 1048608 | tf_op jit(solution)/shard_map/ppermute | solution.py:29
  167.3 5.4 %down.3 = (bf16[256,2048]{1,0:T(8,128)(2,1)S(1)}, bf16[256,2048]{1,0:T(8,128)(2,1)S(1)}) custom-call(bf16[512,1536]{1,0:T(8,128)(2,1)S(1)} %copy-done.2, bf16[1536,4096]{1,0:T(8,128)(2,1)} %bitcast.51), custom_call_target="tpu_custom_call" | custom-call | flops 3221225472 | bytes 9961472 | tf_op jit(solution)/shard_map/down/pallas_call | solution.py:419
  172.7 3.3 %collective-permute-done.35 = bf16[128,2048]{1,0:T(8,128)(2,1)S(1)} collective-permute-done((bf16[128,2048]{1,0:T(8,128)(2,1)S(1)}, bf16[128,2048]{1,0:T(8,128)(2,1)S(1)}, u32[]{:S(2)}, u32[]{:S(2)}) %collective-permute-start.35) | collective-permute-done | bytes 524320 | tf_op jit(solution)/shard_map/ppermute | solution.py:452
  179.5 4.3 %collective-permute-done.37 = bf16[64,2048]{1,0:T(8,128)(2,1)S(1)} collective-permute-done((bf16[64,2048]{1,0:T(8,128)(2,1)S(1)}, bf16[64,2048]{1,0:T(8,128)(2,1)S(1)}, u32[]{:S(2)}, u32[]{:S(2)}) %collective-permute-start.37) | collective-permute-done | bytes 262176 | tf_op jit(solution)/shard_map/ppermute | solution.py:452
  185.1 2.8 %collective-permute-start.39 = (bf16[32,2048]{1,0:T(8,128)(2,1)S(1)}, bf16[32,2048]{1,0:T(8,128)(2,1)S(1)}, u32[]{:S(2)}, u32[]{:S(2)}) collective-permute-start(bf16[32,2048]{1,0:T(8,128)(2,1)S(1)} %pad_maximum_fusion.3), channel_id=1, source_target_pairs={{0,16},{4,20},{8,24},{12,28},{16,0},{20,4},{24,8},{28,12},{1,17},{... | collective-permute-start | bytes 393224 | tf_op jit(solution)/shard_map/ppermute | solution.py:441
  188.9 3.2 %collective-permute-start.38 = (bf16[32,2048]{1,0:T(8,128)(2,1)S(1)}, bf16[32,2048]{1,0:T(8,128)(2,1)S(1)}, u32[]{:S(2)}, u32[]{:S(2)}) collective-permute-start(bf16[32,2048]{1,0:T(8,128)(2,1)S(1)} %pad_maximum_fusion.2), channel_id=1, source_target_pairs={{0,24},{4,28},{8,0},{12,4},{16,8},{20,12},{24,16},{28,20},{1,25},{... | collective-permute-start | bytes 393224 | tf_op jit(solution)/shard_map/ppermute | solution.py:441
  192.1 2.6 %collective-permute-done.42 = bf16[64,2048]{1,0:T(8,128)(2,1)S(1)} collective-permute-done((bf16[64,2048]{1,0:T(8,128)(2,1)S(1)}, bf16[64,2048]{1,0:T(8,128)(2,1)S(1)}, u32[]{:S(2)}, u32[]{:S(2)}) %collective-permute-start.42) | collective-permute-done | bytes 262176 | tf_op jit(solution)/shard_map/ppermute | solution.py:452
  197.0 2.3 %collective-permute-start.43 = (bf16[16,2048]{1,0:T(8,128)(2,1)S(1)}, bf16[16,2048]{1,0:T(8,128)(2,1)S(1)}, u32[]{:S(2)}, u32[]{:S(2)}) collective-permute-start(bf16[16,2048]{1,0:T(8,128)(2,1)S(1)} %get-tuple-element.134), channel_id=1, source_target_pairs={{0,24},{4,28},{8,0},{12,4},{16,8},{20,12},{24,16},{28,20},{1,25},{... | collective-permute-start | bytes 196616 | tf_op jit(solution)/shard_map/ppermute | solution.py:441
  201.9 4.9 %collective-permute-done.44 = bf16[16,2048]{1,0:T(8,128)(2,1)S(1)} collective-permute-done((bf16[16,2048]{1,0:T(8,128)(2,1)S(1)}, bf16[16,2048]{1,0:T(8,128)(2,1)S(1)}, u32[]{:S(2)}, u32[]{:S(2)}) %collective-permute-start.44) | collective-permute-done | bytes 65568 | tf_op jit(solution)/shard_map/ppermute | solution.py:441
  (169 shorter events, 58.3 us)
Async XLA Ops:
  6.7 6.7 %collective-permute-start.1 = (bf16[64,288]{1,0:T(8,128)(2,1)S(1)}, bf16[64,288]{1,0:T(8,128)(2,1)S(1)}, u32[]{:S(2)}, u32[]{:S(2)}) collective-permute-start(bf16[64,288]{1,0:T(8,128)(2,1)S(1)} %get-tuple-element.153), channel_id=1, source_target_pairs={{0,8},{4,12},{8,16},{12,20},{16,24},{20,28},{24,0},{28,4},{1,9},{5... | collective-permute-start | bytes 110600 | tf_op jit(solution)/shard_map/ppermute | solution.py:441
  9.2 6.5 %collective-permute-start.2 = (bf16[64,288]{1,0:T(8,128)(2,1)S(1)}, bf16[64,288]{1,0:T(8,128)(2,1)S(1)}, u32[]{:S(2)}, u32[]{:S(2)}) collective-permute-start(bf16[64,288]{1,0:T(8,128)(2,1)S(1)} %get-tuple-element.155), channel_id=1, source_target_pairs={{0,16},{4,20},{8,24},{12,28},{16,0},{20,4},{24,8},{28,12},{1,17},{... | collective-permute-start | bytes 110600 | tf_op jit(solution)/shard_map/ppermute | solution.py:441
  20.2 6.0 %collective-permute-start.5 = (bf16[64,288]{1,0:T(8,128)(2,1)S(1)}, bf16[64,288]{1,0:T(8,128)(2,1)S(1)}, u32[]{:S(2)}, u32[]{:S(2)}) collective-permute-start(bf16[64,288]{1,0:T(8,128)(2,1)S(1)} %add_convert_fusion.10.refs_0_), channel_id=1, source_target_pairs={{0,8},{4,12},{8,16},{12,20},{16,24},{20,28},{24,0},{28,4},{1,9},{5... | collective-permute-start | bytes 110600 | tf_op jit(solution)/shard_map/ppermute | solution.py:441
  46.2 19.5 %collective-permute-start.9 = (bf16[128,2560]{1,0:T(8,128)(2,1)S(1)}, bf16[128,2560]{1,0:T(8,128)(2,1)S(1)}, u32[]{:S(2)}, u32[]{:S(2)}) collective-permute-start(bf16[128,2560]{1,0:T(8,128)(2,1)S(1)} %get-tuple-element.69), channel_id=1, source_target_pairs={{0,4},{4,0},{8,12},{12,8},{16,20},{20,16},{24,28},{28,24},{1,5},{5... | collective-permute-start | bytes 1966088 | tf_op jit(solution)/shard_map/ppermute | solution.py:34
  47.8 9.7 %collective-permute-start.13 = (bf16[64,1536]{1,0:T(8,128)(2,1)S(1)}, bf16[64,1536]{1,0:T(8,128)(2,1)S(1)}, u32[]{:S(2)}, u32[]{:S(2)}) collective-permute-start(bf16[64,1536]{1,0:T(8,128)(2,1)S(1)} %get-tuple-element.71), channel_id=1, source_target_pairs={{0,8},{4,12},{8,16},{12,20},{16,24},{20,28},{24,0},{28,4},{1,9},{5... | collective-permute-start | bytes 589832 | tf_op jit(solution)/shard_map/ppermute | solution.py:441
  48.6 16.4 %collective-permute-start.14 = (bf16[64,1536]{1,0:T(8,128)(2,1)S(1)}, bf16[64,1536]{1,0:T(8,128)(2,1)S(1)}, u32[]{:S(2)}, u32[]{:S(2)}) collective-permute-start(bf16[64,1536]{1,0:T(8,128)(2,1)S(1)} %get-tuple-element.72), channel_id=1, source_target_pairs={{0,16},{4,20},{8,24},{12,28},{16,0},{20,4},{24,8},{28,12},{1,17},{... | collective-permute-start | bytes 589832 | tf_op jit(solution)/shard_map/ppermute | solution.py:441
  50.8 14.3 %collective-permute-start.15 = (bf16[64,1536]{1,0:T(8,128)(2,1)S(1)}, bf16[64,1536]{1,0:T(8,128)(2,1)S(1)}, u32[]{:S(2)}, u32[]{:S(2)}) collective-permute-start(bf16[64,1536]{1,0:T(8,128)(2,1)S(1)} %get-tuple-element.73), channel_id=1, source_target_pairs={{0,24},{4,28},{8,0},{12,4},{16,8},{20,12},{24,16},{28,20},{1,25},{... | collective-permute-start | bytes 589832 | tf_op jit(solution)/shard_map/ppermute | solution.py:441
  65.2 7.7 %collective-permute-start.16 = (bf16[32,1536]{1,0:T(8,128)(2,1)S(1)}, bf16[32,1536]{1,0:T(8,128)(2,1)S(1)}, u32[]{:S(2)}, u32[]{:S(2)}) collective-permute-start(bf16[32,1536]{1,0:T(8,128)(2,1)S(1)} %slice.436), channel_id=1, source_target_pairs={{0,4},{4,0},{8,12},{12,8},{16,20},{20,16},{24,28},{28,24},{1,5},{5... | collective-permute-start | bytes 294920 | tf_op jit(solution)/shard_map/ppermute | solution.py:34
  66.0 9.0 %collective-permute-start.10 = (bf16[32,2560]{1,0:T(8,128)(2,1)S(1)}, bf16[32,2560]{1,0:T(8,128)(2,1)S(1)}, u32[]{:S(2)}, u32[]{:S(2)}) collective-permute-start(bf16[32,2560]{1,0:T(8,128)(2,1)S(1)} %get-tuple-element.125), channel_id=1, source_target_pairs={{0,8},{4,12},{8,16},{12,20},{16,24},{20,28},{24,0},{28,4},{1,9},{5... | collective-permute-start | bytes 491528 | tf_op jit(solution)/shard_map/ppermute | solution.py:441
  70.4 10.2 %collective-permute-start.11 = (bf16[32,2560]{1,0:T(8,128)(2,1)S(1)}, bf16[32,2560]{1,0:T(8,128)(2,1)S(1)}, u32[]{:S(2)}, u32[]{:S(2)}) collective-permute-start(bf16[32,2560]{1,0:T(8,128)(2,1)S(1)} %get-tuple-element.127), channel_id=1, source_target_pairs={{0,16},{4,20},{8,24},{12,28},{16,0},{20,4},{24,8},{28,12},{1,17},{... | collective-permute-start | bytes 491528 | tf_op jit(solution)/shard_map/ppermute | solution.py:441
  70.7 9.9 %collective-permute-start.12 = (bf16[32,2560]{1,0:T(8,128)(2,1)S(1)}, bf16[32,2560]{1,0:T(8,128)(2,1)S(1)}, u32[]{:S(2)}, u32[]{:S(2)}) collective-permute-start(bf16[32,2560]{1,0:T(8,128)(2,1)S(1)} %get-tuple-element.126), channel_id=1, source_target_pairs={{0,24},{4,28},{8,0},{12,4},{16,8},{20,12},{24,16},{28,20},{1,25},{... | collective-permute-start | bytes 491528 | tf_op jit(solution)/shard_map/ppermute | solution.py:441
  81.2 9.2 %collective-permute-start.17 = (bf16[8,4096]{1,0:T(8,128)(2,1)S(1)}, bf16[8,4096]{1,0:T(8,128)(2,1)S(1)}, u32[]{:S(2)}, u32[]{:S(2)}) collective-permute-start(bf16[8,4096]{1,0:T(8,128)(2,1)S(1)} %get-tuple-element.151), channel_id=1, source_target_pairs={{0,8},{4,12},{8,16},{12,20},{16,24},{20,28},{24,0},{28,4},{1,9},{5... | collective-permute-start | bytes 196616 | tf_op jit(solution)/shard_map/ppermute | solution.py:441
  85.3 7.0 %collective-permute-start.18 = (bf16[8,4096]{1,0:T(8,128)(2,1)S(1)}, bf16[8,4096]{1,0:T(8,128)(2,1)S(1)}, u32[]{:S(2)}, u32[]{:S(2)}) collective-permute-start(bf16[8,4096]{1,0:T(8,128)(2,1)S(1)} %get-tuple-element.150), channel_id=1, source_target_pairs={{0,16},{4,20},{8,24},{12,28},{16,0},{20,4},{24,8},{28,12},{1,17},{... | collective-permute-start | bytes 196616 | tf_op jit(solution)/shard_map/ppermute | solution.py:441
  92.8 6.4 %collective-permute-start.20 = (bf16[32,4096]{1,0:T(8,128)(2,1)S(1)}, bf16[32,4096]{1,0:T(8,128)(2,1)S(1)}, u32[]{:S(2)}, u32[]{:S(2)}) collective-permute-start(bf16[32,4096]{1,0:T(8,128)(2,1)S(1)} %pad_maximum_fusion), channel_id=1, source_target_pairs={{0,4},{1,5},{2,3},{3,2},{4,0},{5,1},{6,7},{7,6},{8,12},{9,13},{10,... | collective-permute-start | bytes 786440 | tf_op jit(solution)/shard_map/ppermute | solution.py:452
  94.4 8.4 %collective-permute-start.24 = (bf16[16,4096]{1,0:T(8,128)(2,1)S(1)}, bf16[16,4096]{1,0:T(8,128)(2,1)S(1)}, u32[]{:S(2)}, u32[]{:S(2)}) collective-permute-start(bf16[16,4096]{1,0:T(8,128)(2,1)S(1)} %get-tuple-element.130), channel_id=1, source_target_pairs={{0,8},{4,12},{8,16},{12,20},{16,24},{20,28},{24,0},{28,4},{1,9},{5... | collective-permute-start | bytes 393224 | tf_op jit(solution)/shard_map/ppermute | solution.py:441
  95.5 13.0 %collective-permute-start.25 = (bf16[16,4096]{1,0:T(8,128)(2,1)S(1)}, bf16[16,4096]{1,0:T(8,128)(2,1)S(1)}, u32[]{:S(2)}, u32[]{:S(2)}) collective-permute-start(bf16[16,4096]{1,0:T(8,128)(2,1)S(1)} %get-tuple-element.129), channel_id=1, source_target_pairs={{0,16},{4,20},{8,24},{12,28},{16,0},{20,4},{24,8},{28,12},{1,17},{... | collective-permute-start | bytes 393224 | tf_op jit(solution)/shard_map/ppermute | solution.py:441
  97.3 11.2 %collective-permute-start.26 = (bf16[16,4096]{1,0:T(8,128)(2,1)S(1)}, bf16[16,4096]{1,0:T(8,128)(2,1)S(1)}, u32[]{:S(2)}, u32[]{:S(2)}) collective-permute-start(bf16[16,4096]{1,0:T(8,128)(2,1)S(1)} %get-tuple-element.128), channel_id=1, source_target_pairs={{0,24},{4,28},{8,0},{12,4},{16,8},{20,12},{24,16},{28,20},{1,25},{... | collective-permute-start | bytes 393224 | tf_op jit(solution)/shard_map/ppermute | solution.py:441
  99.2 9.2 %collective-permute-start.21 = (bf16[64,4096]{1,0:T(8,128)(2,1)S(1)}, bf16[64,4096]{1,0:T(8,128)(2,1)S(1)}, u32[]{:S(2)}, u32[]{:S(2)}) collective-permute-start(bf16[64,4096]{1,0:T(8,128)(2,1)S(1)} %constant_dynamic-update-slice_fusion.refs_0_), channel_id=1, source_target_pairs={{0,1},{1,0},{2,6},{3,7},{4,5},{5,4},{6,2},{7,3},{8,9},{9,8},{10,14... | collective-permute-start | bytes 1572872 | tf_op jit(solution)/shard_map/ppermute | solution.py:452
  100.8 9.3 %collective-permute-start.22 = (bf16[64,4096]{1,0:T(8,128)(2,1)S(1)}, bf16[64,4096]{1,0:T(8,128)(2,1)S(1)}, u32[]{:S(2)}, u32[]{:S(2)}) collective-permute-start(bf16[64,4096]{1,0:T(8,128)(2,1)S(1)} %constant_dynamic-update-slice_fusion.refs_0_), channel_id=1, source_target_pairs={{0,2},{2,0},{1,3},{3,1},{4,6},{6,4},{5,7},{7,5},{8,10},{10,8},{9,1... | collective-permute-start | bytes 1572872 | tf_op jit(solution)/shard_map/ppermute | solution.py:29
  108.5 9.2 %collective-permute-start.27 = (bf16[64,4096]{1,0:T(8,128)(2,1)S(1)}, bf16[64,4096]{1,0:T(8,128)(2,1)S(1)}, u32[]{:S(2)}, u32[]{:S(2)}) collective-permute-start(bf16[64,4096]{1,0:T(8,128)(2,1)S(1)} %constant_dynamic-update-slice_fusion.5), channel_id=1, source_target_pairs={{0,4},{1,5},{2,3},{3,2},{4,0},{5,1},{6,7},{7,6},{8,12},{9,13},{10,... | collective-permute-start | bytes 1572872 | tf_op jit(solution)/shard_map/ppermute | solution.py:452
  117.8 14.9 %collective-permute-start.28 = (bf16[128,4096]{1,0:T(8,128)(2,1)S(1)}, bf16[128,4096]{1,0:T(8,128)(2,1)S(1)}, u32[]{:S(2)}, u32[]{:S(2)}) collective-permute-start(bf16[128,4096]{1,0:T(8,128)(2,1)S(1)} %constant_dynamic-update-slice_fusion.9.refs_0_), channel_id=1, source_target_pairs={{0,1},{1,0},{2,6},{3,7},{4,5},{5,4},{6,2},{7,3},{8,9},{9,8},{10,14... | collective-permute-start | bytes 3145736 | tf_op jit(solution)/shard_map/ppermute | solution.py:452
  135.2 20.0 %collective-permute-start.32 = (bf16[64,4096]{1,0:T(8,128)(2,1)S(1)}, bf16[64,4096]{1,0:T(8,128)(2,1)S(1)}, u32[]{:S(2)}, u32[]{:S(2)}) collective-permute-start(bf16[64,4096]{1,0:T(8,128)(2,1)S(1)} %add_convert_fusion.3), channel_id=1, source_target_pairs={{0,1},{1,0},{2,6},{3,7},{4,5},{5,4},{6,2},{7,3},{8,9},{9,8},{10,14... | collective-permute-start | bytes 1572872 | tf_op jit(solution)/shard_map/ppermute | solution.py:452
  155.3 8.4 %collective-permute-start.33 = (bf16[32,4096]{1,0:T(8,128)(2,1)S(1)}, bf16[32,4096]{1,0:T(8,128)(2,1)S(1)}, u32[]{:S(2)}, u32[]{:S(2)}) collective-permute-start(bf16[32,4096]{1,0:T(8,128)(2,1)S(1)} %add_convert_fusion.9), channel_id=1, source_target_pairs={{0,4},{1,5},{2,3},{3,2},{4,0},{5,1},{6,7},{7,6},{8,12},{9,13},{10,... | collective-permute-start | bytes 786440 | tf_op jit(solution)/shard_map/ppermute | solution.py:452
  166.7 9.2 %collective-permute-start.35 = (bf16[128,2048]{1,0:T(8,128)(2,1)S(1)}, bf16[128,2048]{1,0:T(8,128)(2,1)S(1)}, u32[]{:S(2)}, u32[]{:S(2)}) collective-permute-start(bf16[128,2048]{1,0:T(8,128)(2,1)S(1)} %add_convert_fusion.2), channel_id=1, source_target_pairs={{0,1},{1,0},{2,6},{3,7},{4,5},{5,4},{6,2},{7,3},{8,9},{9,8},{10,14... | collective-permute-start | bytes 1572872 | tf_op jit(solution)/shard_map/ppermute | solution.py:452
  176.4 7.5 %collective-permute-start.37 = (bf16[64,2048]{1,0:T(8,128)(2,1)S(1)}, bf16[64,2048]{1,0:T(8,128)(2,1)S(1)}, u32[]{:S(2)}, u32[]{:S(2)}) collective-permute-start(bf16[64,2048]{1,0:T(8,128)(2,1)S(1)} %add_convert_fusion.7), channel_id=1, source_target_pairs={{0,4},{1,5},{2,3},{3,2},{4,0},{5,1},{6,7},{7,6},{8,12},{9,13},{10,... | collective-permute-start | bytes 786440 | tf_op jit(solution)/shard_map/ppermute | solution.py:452
  178.9 9.2 %collective-permute-start.41 = (bf16[128,2048]{1,0:T(8,128)(2,1)S(1)}, bf16[128,2048]{1,0:T(8,128)(2,1)S(1)}, u32[]{:S(2)}, u32[]{:S(2)}) collective-permute-start(bf16[128,2048]{1,0:T(8,128)(2,1)S(1)} %add_convert_fusion.1), channel_id=1, source_target_pairs={{0,1},{1,0},{2,6},{3,7},{4,5},{5,4},{6,2},{7,3},{8,9},{9,8},{10,14... | collective-permute-start | bytes 1572872 | tf_op jit(solution)/shard_map/ppermute | solution.py:452
  184.0 10.9 %collective-permute-start.40 = (bf16[32,2048]{1,0:T(8,128)(2,1)S(1)}, bf16[32,2048]{1,0:T(8,128)(2,1)S(1)}, u32[]{:S(2)}, u32[]{:S(2)}) collective-permute-start(bf16[32,2048]{1,0:T(8,128)(2,1)S(1)} %pad_maximum_fusion.4), channel_id=1, source_target_pairs={{0,8},{4,12},{8,16},{12,20},{16,24},{20,28},{24,0},{28,4},{1,9},{5... | collective-permute-start | bytes 393224 | tf_op jit(solution)/shard_map/ppermute | solution.py:441
  185.1 10.6 %collective-permute-start.39 = (bf16[32,2048]{1,0:T(8,128)(2,1)S(1)}, bf16[32,2048]{1,0:T(8,128)(2,1)S(1)}, u32[]{:S(2)}, u32[]{:S(2)}) collective-permute-start(bf16[32,2048]{1,0:T(8,128)(2,1)S(1)} %pad_maximum_fusion.3), channel_id=1, source_target_pairs={{0,16},{4,20},{8,24},{12,28},{16,0},{20,4},{24,8},{28,12},{1,17},{... | collective-permute-start | bytes 393224 | tf_op jit(solution)/shard_map/ppermute | solution.py:441
  188.3 6.4 %collective-permute-start.42 = (bf16[64,2048]{1,0:T(8,128)(2,1)S(1)}, bf16[64,2048]{1,0:T(8,128)(2,1)S(1)}, u32[]{:S(2)}, u32[]{:S(2)}) collective-permute-start(bf16[64,2048]{1,0:T(8,128)(2,1)S(1)} %add_convert_fusion.5), channel_id=1, source_target_pairs={{0,4},{1,5},{2,3},{3,2},{4,0},{5,1},{6,7},{7,6},{8,12},{9,13},{10,... | collective-permute-start | bytes 786440 | tf_op jit(solution)/shard_map/ppermute | solution.py:452
  188.9 8.0 %collective-permute-start.38 = (bf16[32,2048]{1,0:T(8,128)(2,1)S(1)}, bf16[32,2048]{1,0:T(8,128)(2,1)S(1)}, u32[]{:S(2)}, u32[]{:S(2)}) collective-permute-start(bf16[32,2048]{1,0:T(8,128)(2,1)S(1)} %pad_maximum_fusion.2), channel_id=1, source_target_pairs={{0,24},{4,28},{8,0},{12,4},{16,8},{20,12},{24,16},{28,20},{1,25},{... | collective-permute-start | bytes 393224 | tf_op jit(solution)/shard_map/ppermute | solution.py:441
  199.3 7.4 %collective-permute-start.44 = (bf16[16,2048]{1,0:T(8,128)(2,1)S(1)}, bf16[16,2048]{1,0:T(8,128)(2,1)S(1)}, u32[]{:S(2)}, u32[]{:S(2)}) collective-permute-start(bf16[16,2048]{1,0:T(8,128)(2,1)S(1)} %get-tuple-element.133), channel_id=1, source_target_pairs={{0,16},{4,20},{8,24},{12,28},{16,0},{20,4},{24,8},{28,12},{1,17},{... | collective-permute-start | bytes 196616 | tf_op jit(solution)/shard_map/ppermute | solution.py:441
  200.5 6.2 %collective-permute-start.45 = (bf16[16,2048]{1,0:T(8,128)(2,1)S(1)}, bf16[16,2048]{1,0:T(8,128)(2,1)S(1)}, u32[]{:S(2)}, u32[]{:S(2)}) collective-permute-start(bf16[16,2048]{1,0:T(8,128)(2,1)S(1)} %get-tuple-element.132), channel_id=1, source_target_pairs={{0,8},{4,12},{8,16},{12,20},{16,24},{20,28},{24,0},{28,4},{1,9},{5... | collective-permute-start | bytes 196616 | tf_op jit(solution)/shard_map/ppermute | solution.py:441
  (27 other events, 201.5 us)
